TPU v7x, 32 devices: a whole 2x2x4 slice. The times are simulated.
32 devices in a mesh: section: 8 (over y, x, core), tp: 4 (over z).
Axes of the slice: x: 2, y: 2, z: 4, core: 2. Of those that a mesh axis runs over, the one named last changes fastest.
Arguments:
- block_weights: bfloat16 [8, 3072, 4, 2048], P(None, 'section', None, 'tp'), may hold values from -0.109375 to 0.109375
- modulation: float32 [8, 3, 3072], P('section'), may hold values from -4 to 4
- inflow: bfloat16 [8, 512, 3072], P('section', None, 'tp'), may hold values from -6 to 6
- stale_cache: bfloat16 [8, 2, 2048, 2048], P('section', None, None, 'tp'), may hold values from -120 to 120
- patch_index: int32 [8], P('section'), may hold values from 0 to 3
- assignment: int32 [8], replicated, may hold values from 0 to 7, each once
Outputs:
- outflow: bfloat16 [8, 512, 3072], P('section', None, 'tp')
All inputs are finite; a program needn't handle non-finite values.
Results may differ from a plain program's by a relative error of at most 0.022.
Values may be sent and summed in bfloat16 or wider, within the bound.
No kernel may reach another device: no remote copies, remote signals or barrier semaphores. Data moves between devices by JAX's collectives and lax.ppermute only.
A program may use at most 128 MiB of HBM per device.

v0:
```python
import jax
import jax.numpy as jnp
from jax import lax
from jax.sharding import PartitionSpec as P

HD = 128


def passed_along(block, axis, distance):
    devices = range(lax.axis_size(axis))
    route = [((i - distance) % len(devices), i) for i in devices]
    return lax.ppermute(block, axis, route)


def local(block_weights, modulation, inflow, stale_cache, patch_index, assignment):
    blocks = assignment.shape[0]
    section_ids = jnp.arange(blocks, dtype=jnp.int32)
    owner_table = (assignment[None, :] == section_ids[:, None]).astype(jnp.int32)
    inverse = jnp.sum(owner_table * section_ids[None, :], axis=1)
    ordered = jnp.take(block_weights, inverse, axis=0)
    resident = lax.all_to_all(ordered, "section", split_axis=0, concat_axis=1, tiled=True)[0]
    width = resident.shape[0]
    inner_dev = resident.shape[2]
    heads_dev = inner_dev // HD
    patch = inflow.shape[1]
    seq_len = stale_cache.shape[2]
    tokens = lax.all_gather(inflow, "tp", axis=2, tiled=True)[0].astype(jnp.float32)
    center = jnp.mean(tokens, axis=1, keepdims=True)
    spread = jnp.mean((tokens - center) ** 2, axis=1, keepdims=True)
    normed = (tokens - center) * lax.rsqrt(spread + 1e-06)
    normed = (normed * (1.0 + modulation[0, 0]) + modulation[0, 1]).astype(jnp.bfloat16)
    projected = jnp.dot(
        normed, resident[:, :3, :].reshape(width, 3 * inner_dev), preferred_element_type=jnp.float32
    )
    projected = projected.astype(jnp.bfloat16).reshape(patch, 3, inner_dev)
    start = patch_index[0] * patch
    zero_index = jnp.zeros((), jnp.int32)
    keys_all = lax.dynamic_update_slice(stale_cache[0, 0], projected[:, 1], (start, zero_index))
    values_all = lax.dynamic_update_slice(stale_cache[0, 1], projected[:, 2], (start, zero_index))
    query = projected[:, 0].reshape(patch, heads_dev, HD)
    scores = jnp.einsum(
        "phd,shd->hps",
        query,
        keys_all.reshape(seq_len, heads_dev, HD),
        preferred_element_type=jnp.float32,
    )
    scores = scores / jnp.sqrt(jnp.float32(HD))
    highest = jnp.max(scores, axis=2, keepdims=True)
    expo = jnp.exp(scores - highest)
    probabilities = (expo / jnp.sum(expo, axis=2, keepdims=True)).astype(jnp.bfloat16)
    attended = jnp.einsum(
        "hps,shd->phd",
        probabilities,
        values_all.reshape(seq_len, heads_dev, HD),
        preferred_element_type=jnp.float32,
    )
    attended = attended.astype(jnp.bfloat16).reshape(patch, inner_dev)
    partial_value = jnp.dot(attended, resident[:, 3, :].T, preferred_element_type=jnp.float32)
    share = width // lax.axis_size("tp")
    offset = lax.axis_index("tp") * share
    summed = lax.psum(partial_value.astype(jnp.bfloat16), "tp").astype(jnp.float32)
    mixed = lax.dynamic_slice_in_dim(summed, offset, share, 1)
    gate_part = lax.dynamic_slice_in_dim(modulation[0, 2], offset, share, 0)
    result = (inflow[0].astype(jnp.float32) + gate_part * mixed).astype(jnp.bfloat16)
    return passed_along(result[None], "section", 1)


def solution(mesh):
    placed = (
        P(None, "section", None, "tp"),
        P("section", None, None),
        P("section", None, "tp"),
        P("section", None, None, "tp"),
        P("section"),
        P(),
    )
    return jax.shard_map(
        local, mesh=mesh, in_specs=placed, out_specs=P("section", None, "tp"), check_vma=False
    )
```

profile of v0, /device:TPU:0, one launch (start us, length us, event | category | flops | bytes accessed | tf_op | source)
XLA Modules:
  0.0 422.1 jit_solution(15683631897601338189)
XLA Ops:
  6.5 0.8 select_reduce_fusion
  7.3 17.1 %gather_fusion = bf16[8,384,4,512]{3,2,1,0:T(4,128)(2,1)} fusion(bf16[8,384,4,512]{3,2,1,0:T(4,128)(2,1)} %param.6, s32[1024]{0:T(1024)S(1)} %pad_clamp_fusion), kind=kCustom, calls=%fused_computation | custom fusion | bytes 25165856 | tf_op jit(solution)/shard_map/jit(_take)/gather | solution.py:20
  24.4 11.6 %broadcast_select_fusion = bf16[8,384,4,512]{3,2,1,0:T(4,128)(2,1)} fusion(bf16[8,384,4,512]{3,2,1,0:T(4,128)(2,1)} %gather_fusion, pred[8]{0:T(512)(128)(4,1)S(1)} %compare_and_fusion), kind=kLoop, calls=%fused_computation.6 | loop fusion | flops 6291456 | bytes 25165832 | tf_op jit(solution)/shard_map/jit(_take)/select_n | solution.py:20
  36.1 5.3 %all-to-all-start = ((bf16[8,384,4,512]{3,2,1,0:T(4,128)(2,1)}), bf16[8,384,4,512]{3,2,1,0:T(4,128)(2,1)}, u32[]{:S(2)}, u32[]{:S(2)}) async-start(bf16[8,384,4,512]{3,2,1,0:T(4,128)(2,1)} %broadcast_select_fusion), calls=%async_computation | async-start | bytes 25165824 | tf_op jit(solution)/shard_map/all_to_all | solution.py:21
  41.4 0.0 copy-start.2
  41.5 0.0 all-gather.2.cloned.1.call-start
  41.5 0.7 all-gather.2.cloned.1.call-update
  42.2 0.0 all-reduce.2.cloned.1.call-start
  42.9 3.8 slice_bitcast_fusion
  46.7 63.7 %all-gather.2.cloned.1.call-done = bf16[1,512,3072]{2,1,0:T(8,128)(2,1)} async-done(((bf16[1,512,768]{2,1,0:T(8,128)(2,1)}), bf16[1,512,3072]{2,1,0:T(8,128)(2,1)}) %all-gather.2.cloned.1.call-update) | async-done | bytes 3145744 | tf_op jit(solution)/shard_map/all_gather | solution.py:27
  110.4 2.4 convert_reduce_fusion
  112.8 2.8 fusion.12
  115.6 65.4 %all-to-all-done = bf16[8,384,4,512]{3,2,1,0:T(4,128)(2,1)} async-done(((bf16[8,384,4,512]{3,2,1,0:T(4,128)(2,1)}), bf16[8,384,4,512]{3,2,1,0:T(4,128)(2,1)}, u32[]{:S(2)}, u32[]{:S(2)}) %all-to-all-start) | async-done | bytes 12582944 | tf_op jit(solution)/shard_map/all_to_all | solution.py:21
  181.1 10.2 %slice.46 = bf16[3072,1,512]{2,1,0:T(2,128)(2,1)} slice(bf16[3072,4,512]{2,1,0:T(4,128)(2,1)} %bitcast.8), slice={[0:3072], [3:4], [0:512]} | slice | bytes 6291456 | tf_op jit(solution)/shard_map/slice | solution.py:58
  191.3 18.9 %copy.30 = bf16[3072,3,512]{0,2,1:T(8,128)(2,1)} copy(bf16[3072,3,512]{2,1,0:T(4,128)(2,1)} %bitcast.55) | data formatting | bytes 18874368
  210.2 10.5 %fusion.20 = bf16[512,1536]{1,0:T(8,128)(2,1)} fusion(bf16[3072,1536]{0,1:T(8,128)(2,1)} %bitcast.56, bf16[1,512,3072]{2,1,0:T(8,128)(2,1)} %all-gather.2.cloned.1.call-done, f32[3072]{0:T(1024)S(1)} %bitcast.60, f32[3072]{0:T(1024)S(1)} %bitcast.61, f32[512]{0:T(512)S(1)} %add_rsqrt_fusion, f32[512]{0:T(512)S(1)} %broadcast_multiply_fusion), kind=kOutput, calls=%fused_computation.27 | convolution fusion | flops 4842061824 | bytes 14184448 | tf_op jit(solution)/shard_map/dot_general | solution.py:32
  220.8 2.6 copy.20
  223.4 2.5 slice_bitcast_fusion.2
  225.9 1.3 copy.22
  227.1 2.0 copy.21
  229.2 1.9 constant_dynamic-update-slice_fusion
  231.1 3.9 copy.29
  235.0 8.1 %fusion.23 = f32[4,512,2048]{2,1,0:T(8,128)} fusion(bf16[512,4,128]{0,2,1:T(8,128)(2,1)S(1)} %bitcast.58, bf16[2048,512]{1,0:T(8,128)(2,1)S(1)} %get-tuple-element.13), kind=kOutput, calls=%fused_computation.28 | convolution fusion | flops 1073741824 | bytes 19398656 | tf_op jit(solution)/shard_map/phd,shd->hps/dot_general | solution.py:41
  243.1 14.2 %fusion.39 = f32[4,512]{1,0:T(4,128)S(1)} fusion(f32[4,512,2048]{2,1,0:T(8,128)} %fusion.23), kind=kOutput, calls=%fused_computation.56 | output fusion | flops 16779264 | bytes 16785408 | tf_op jit(solution)/shard_map/sub | solution.py:49
  257.3 15.5 %fusion.27 = bf16[4,128,512]{2,1,0:T(8,128)(2,1)S(1)} fusion(bf16[2048,4,128]{0,2,1:T(8,128)(2,1)S(1)} %bitcast.59, f32[4,512]{1,0:T(4,128)S(1)} %fusion.39, f32[4,512,2048]{2,1,0:T(8,128)} %fusion.23), kind=kOutput, calls=%fused_computation.35 | convolution fusion | flops 1094979584 | bytes 19406848 | tf_op jit(solution)/shard_map/hps,shd->phd/dot_general | solution.py:51
  272.8 6.4 %convolution_convert_fusion = bf16[512,3072]{1,0:T(8,128)(2,1)} fusion(bf16[512,512]{0,1:T(8,128)(2,1)S(1)} %bitcast.62, bf16[3072,1,512]{2,1,0:T(2,128)(2,1)} %slice.46), kind=kOutput, calls=%fused_computation.19 | convolution fusion | flops 1612185600 | bytes 6815744 | tf_op jit(solution)/shard_map/dot_general | solution.py:58
  279.2 0.0 all-reduce.2.cloned.1.call-update
  279.3 121.4 %all-reduce.2.cloned.1.call-done = bf16[512,3072]{1,0:T(8,128)(2,1)} async-done(((bf16[512,3072]{1,0:T(8,128)(2,1)}), bf16[512,3072]{1,0:T(8,128)(2,1)}) %all-reduce.2.cloned.1.call-update) | async-done | bytes 3145744 | tf_op jit(solution)/shard_map/psum | solution.py:61
  400.7 1.4 fusion.28
  402.1 0.1 collective-permute-start
  402.1 12.3 %collective-permute-done = bf16[1,512,768]{2,1,0:T(8,128)(2,1)S(1)} collective-permute-done((bf16[1,512,768]{2,1,0:T(8,128)(2,1)S(1)}, bf16[1,512,768]{2,1,0:T(8,128)(2,1)S(1)}, u32[]{:S(2)}, u32[]{:S(2)}) %collective-permute-start) | collective-permute-done | bytes 786464 | tf_op jit(solution)/shard_map/ppermute | solution.py:12
  414.4 0.9 copy.45
  (12 shorter events, 0.1 us)
Async XLA Ops:
  36.1 145.0 %all-to-all-start = ((bf16[8,384,4,512]{3,2,1,0:T(4,128)(2,1)}), bf16[8,384,4,512]{3,2,1,0:T(4,128)(2,1)}, u32[]{:S(2)}, u32[]{:S(2)}) async-start(bf16[8,384,4,512]{3,2,1,0:T(4,128)(2,1)} %broadcast_select_fusion), calls=%async_computation | async-start | bytes 25165824 | tf_op jit(solution)/shard_map/all_to_all | solution.py:21
  41.4 5.3 %copy-start.2 = (f32[1,3,3072]{2,0,1:T(1,128)S(1)}, f32[1,3,3072]{2,0,1:T(1,128)}, u32[]{:S(2)}) copy-start(f32[1,3,3072]{2,0,1:T(1,128)} %param.7) | copy-start | bytes 110596
  41.5 69.0 %all-gather.2.cloned.1.call-start = ((), (), s32[]{:S(2)}) async-start(), calls=%async_computation.1 | async-start | bytes 3932160 | tf_op jit(solution)/shard_map/all_gather | solution.py:27
  42.2 358.5 %all-reduce.2.cloned.1.call-start = ((), (), s32[]{:S(2)}) async-start(), calls=%async_computation.2 | async-start | bytes 6291456 | tf_op jit(solution)/shard_map/psum | solution.py:61
  243.1 14.2 %copy-start.1 = (bf16[2048,512]{0,1:T(8,128)(2,1)S(1)}, bf16[2048,512]{0,1:T(8,128)(2,1)}, u32[]{:S(2)}) copy-start(bf16[2048,512]{0,1:T(8,128)(2,1)} %copy.29) | copy-start | bytes 6291460
  272.8 127.9 %copy-start = (bf16[1,512,768]{2,1,0:T(8,128)(2,1)S(1)}, bf16[1,512,768]{2,1,0:T(8,128)(2,1)}, u32[]{:S(2)}) copy-start(bf16[1,512,768]{2,1,0:T(8,128)(2,1)} %param.8) | copy-start | bytes 2359300
  402.1 12.4 %collective-permute-start = (bf16[1,512,768]{2,1,0:T(8,128)(2,1)S(1)}, bf16[1,512,768]{2,1,0:T(8,128)(2,1)S(1)}, u32[]{:S(2)}, u32[]{:S(2)}) collective-permute-start(bf16[1,512,768]{2,1,0:T(8,128)(2,1)S(1)} %fusion.28), channel_id=1, source_target_pairs={{28,0},{0,4},{4,8},{8,12},{12,16},{16,20},{20,24},{24,28},{29,1},{... | collective-permute-start | bytes 2359304 | tf_op jit(solution)/shard_map/ppermute | solution.py:12
Sparse Core Ops, SparseCore 0:
  43.9 66.5 all-gather.1
  279.3 121.3 all-reduce.1
where the time goes:
time: 423 us; the launch traced here: 422 us
  waiting for transfers between devices  264 us (62%)
  local copies, waits for them, and re-layouts  65.3 us (15%)
  matrix products  40.5 us (10%)
  other arithmetic  33.2 us (8%)
  between operations  14.2 us (3%)
  starting transfers between devices  5.48 us (1%)
    psum x1, waiting for transfers between devices, local(): lax.psum(partial_value.astype(jnp.bfloat16), 'tp').astype(jnp.float32)  121 us
    all_to_all x1, waiting for transfers between devices, local(): lax.all_to_all(ordered, 'section', split_axis=0, concat_axis=1, tiled=True)  65.4 us
    all_gather x1, waiting for transfers between devices, local(): lax.all_gather(inflow, 'tp', axis=2, tiled=True)[0].astype(jnp.float32)  63.7 us
    unnamed x8, local copies, waits for them, and re-layouts  19.8 us
    gather x1, local copies, waits for them, and re-layouts, local(): ordered = jnp.take(block_weights, inverse, axis=0)  17.1 us
    dot_general x1, matrix products, local(): jnp.einsum('hps,shd->phd', probabilities, values_all.reshape(seq_len, hea...  15.5 us
    sub x1, other arithmetic, local(): expo = jnp.exp(scores - highest)  14.2 us
    ppermute x1, waiting for transfers between devices, passed_along(): return lax.ppermute(block, axis, route)  12.3 us
  transfers between devices with their start and end apart: 4, of which 4 were waited for; matrix products, arithmetic and copies ran while one was open for 2% of the time, Pallas kernels for 0%

commit v1 on v0

v1 whole, which is shorter than its diff:
```python
import functools

import jax
import jax.numpy as jnp
from jax import lax
from jax.experimental import pallas as pl
from jax.experimental.pallas import tpu as pltpu
from jax.sharding import PartitionSpec as P

HD = 128
VMEM_LIMIT = 48 * 1024 * 1024


def split_kernel(lanes, order_ref, rows_ref, *rest):
    outs, wide = rest[:4], rest[4]
    depth = outs[0].shape[1]
    period = 4 * lanes
    wide[...] = rows_ref[0].astype(jnp.float32)
    for kind in range(4):
        for lane in range(lanes):
            part = wide[pl.ds(lane * 4 + kind, depth, stride=period), :]
            outs[kind][0, :, lane * HD : (lane + 1) * HD] = part.astype(jnp.bfloat16)


def split_blocks(block_weights, order):
    blocks, depth, kinds, inner = block_weights.shape
    lanes = inner // HD
    rows = block_weights.reshape(blocks, depth, kinds, lanes, HD)
    rows = rows.transpose(0, 1, 3, 2, 4).reshape(blocks, depth * lanes * kinds, HD)
    steps = 2 if depth % 32 == 0 else 1
    step_rows = depth // steps
    out = jax.ShapeDtypeStruct((blocks, depth, inner), jnp.bfloat16)
    return pl.pallas_call(
        functools.partial(split_kernel, lanes),
        grid_spec=pltpu.PrefetchScalarGridSpec(
            num_scalar_prefetch=1,
            grid=(blocks, steps),
            in_specs=[
                pl.BlockSpec(
                    (1, step_rows * lanes * kinds, HD), lambda i, j, order: (order[i], j, 0)
                )
            ],
            out_specs=[pl.BlockSpec((1, step_rows, inner), lambda i, j, order: (i, j, 0))] * 4,
            scratch_shapes=[pltpu.VMEM((step_rows * lanes * kinds, HD), jnp.float32)],
        ),
        out_shape=[out] * 4,
        compiler_params=pltpu.CompilerParams(vmem_limit_bytes=VMEM_LIMIT),
        cost_estimate=pl.CostEstimate(
            flops=0, bytes_accessed=4 * block_weights.size, transcendentals=0
        ),
        name="split_blocks",
    )(order, rows)


def norm_kernel(tokens_ref, modulation_ref, out_ref):
    tokens = tokens_ref[...].astype(jnp.float32)
    center = jnp.mean(tokens, axis=1, keepdims=True)
    tokens = tokens - center
    spread = jnp.mean(tokens * tokens, axis=1, keepdims=True)
    normed = tokens * lax.rsqrt(spread + 1e-06)
    out_ref[...] = (normed * (1.0 + modulation_ref[0:1]) + modulation_ref[1:2]).astype(jnp.bfloat16)


def norm(tokens, modulation):
    patch, width = tokens.shape
    rows = 128
    return pl.pallas_call(
        norm_kernel,
        grid=(patch // rows,),
        in_specs=[
            pl.BlockSpec((rows, width), lambda i: (i, 0)),
            pl.BlockSpec((3, width), lambda i: (0, 0)),
        ],
        out_specs=pl.BlockSpec((rows, width), lambda i: (i, 0)),
        out_shape=jax.ShapeDtypeStruct((patch, width), jnp.bfloat16),
        compiler_params=pltpu.CompilerParams(vmem_limit_bytes=VMEM_LIMIT),
        cost_estimate=pl.CostEstimate(
            flops=10 * patch * width, bytes_accessed=4 * patch * width, transcendentals=0
        ),
        name="norm",
    )(tokens, modulation)


def attention_kernel(where_ref, q_ref, k_ref, v_ref, stale_ref, out_ref):
    patch = q_ref.shape[0]
    pieces = stale_ref.shape[1] // patch
    query = q_ref[...]
    scale = 1.0 / jnp.sqrt(jnp.float32(HD))

    def scores_of(keys):
        return lax.dot_general(
            query, keys, (((1,), (1,)), ((), ())), preferred_element_type=jnp.float32
        ) * scale

    highest, total, summed = None, None, None
    for piece in range(pieces):
        if piece < pieces - 1:
            start = pl.multiple_of(lax.rem(where_ref[0] + 1 + piece, pieces) * patch, patch)
            keys = stale_ref[0, pl.ds(start, patch), :]
            values = stale_ref[1, pl.ds(start, patch), :]
        else:
            keys, values = k_ref[...], v_ref[...]
        scores = scores_of(keys)
        top = jnp.max(scores, axis=1, keepdims=True)
        if piece > 0:
            top = jnp.maximum(highest, top)
        expo = jnp.exp(scores - top)
        row = jnp.sum(expo, axis=1, keepdims=True)
        part = jnp.dot(expo.astype(jnp.bfloat16), values, preferred_element_type=jnp.float32)
        if piece > 0:
            shrink = jnp.exp(highest - top)
            row = total * shrink + row
            part = summed * shrink + part
        highest, total, summed = top, row, part
    out_ref[...] = (summed / total).astype(jnp.bfloat16)


def attention(where, query, key, value, stale):
    patch, inner = query.shape
    seq_len = stale.shape[1]
    own = pl.BlockSpec((patch, HD), lambda h, where: (0, h))
    return pl.pallas_call(
        attention_kernel,
        grid_spec=pltpu.PrefetchScalarGridSpec(
            num_scalar_prefetch=1,
            grid=(inner // HD,),
            in_specs=[own, own, own, pl.BlockSpec((2, seq_len, HD), lambda h, where: (0, 0, h))],
            out_specs=own,
        ),
        out_shape=jax.ShapeDtypeStruct((patch, inner), jnp.bfloat16),
        compiler_params=pltpu.CompilerParams(vmem_limit_bytes=VMEM_LIMIT),
        cost_estimate=pl.CostEstimate(
            flops=4 * patch * inner * seq_len,
            bytes_accessed=4 * inner * (seq_len + 2 * patch),
            transcendentals=patch * seq_len * (inner // HD),
        ),
        name="attention",
    )(where, query, key, value, stale)


def local(block_weights, modulation, inflow, stale_cache, patch_index, assignment):
    sections = lax.axis_size("section")
    section_ids = jnp.arange(sections, dtype=jnp.int32)
    owner_table = (assignment[None, :] == section_ids[:, None]).astype(jnp.int32)
    inverse = jnp.sum(owner_table * section_ids[None, :], axis=1)
    parts = split_blocks(block_weights, inverse)
    width = modulation.shape[2]
    inner = block_weights.shape[3]

    def relay(part):
        moved = lax.all_to_all(part, "section", split_axis=0, concat_axis=0, tiled=True)
        return moved.reshape(width, inner)

    to_query, to_key, to_value, to_out = [relay(part) for part in parts]
    tokens = lax.all_gather(inflow[0], "tp", axis=1, tiled=True)
    normed = norm(tokens, modulation[0])

    def project(matrix):
        return jnp.dot(normed, matrix, preferred_element_type=jnp.float32).astype(jnp.bfloat16)

    query, key, value = project(to_query), project(to_key), project(to_value)
    attended = attention(patch_index, query, key, value, stale_cache[0])
    partial = lax.dot_general(
        attended, to_out, (((1,), (1,)), ((), ())), preferred_element_type=jnp.float32
    ).astype(jnp.bfloat16)
    mixed = lax.psum_scatter(partial, "tp", scatter_dimension=1, tiled=True).astype(jnp.float32)
    share = inflow.shape[2]
    gate = lax.dynamic_slice_in_dim(modulation[0, 2], lax.axis_index("tp") * share, share, 0)
    result = (inflow[0].astype(jnp.float32) + gate * mixed).astype(jnp.bfloat16)
    route = [((i - 1) % sections, i) for i in range(sections)]
    return lax.ppermute(result, "section", route)[None]


def solution(mesh):
    placed = (
        P(None, "section", None, "tp"),
        P("section", None, None),
        P("section", None, "tp"),
        P("section", None, None, "tp"),
        P("section"),
        P(),
    )
    return jax.shard_map(
        local, mesh=mesh, in_specs=placed, out_specs=P("section", None, "tp"), check_vma=False
    )
```

time: 423 us -> 283 us (0.67)
  waiting for transfers between devices: 264 us -> 126 us
  blocking collectives: 0 us -> 85.1 us
  local copies, waits for them, and re-layouts: 65.3 us -> 1.61 us
  Pallas kernels: 0 us -> 31.1 us
  other arithmetic: 33.2 us -> 2.14 us
  matrix products: 40.5 us -> 12.8 us
    psum x1 -> x0, waiting for transfers between devices: 121 us -> none  [local(): lax.psum(partial_value.astype(jnp.bfloat16), 'tp').astype(jnp.float32)]
    all_to_all x0 -> x2, blocking collectives: none -> 85.1 us  [relay(): lax.all_to_all(part, 'section', split_axis=0, concat_axis=0, tiled=True)]
    all_gather x1, waiting for transfers between devices: 63.7 us -> 0.02 us  [local(): tokens = lax.all_gather(inflow[0], 'tp', axis=1, tiled=True)]
    reduce_scatter x0 -> x1, waiting for transfers between devices: none -> 59.1 us  [local(): lax.psum_scatter(partial, 'tp', scatter_dimension=1, tiled=True)]
    pallas_call x0 -> x3, Pallas kernels: none -> 31.1 us  [the longest x1 17.8 us: split_blocks(): pl.pallas_call(functools.partial(split_kernel, lanes), grid_spec=pltpu.Pr...]
    dot_general x4, matrix products: 40.5 us -> 12.8 us  [the longest x3 7.42 us: project(): jnp.dot(normed, matrix, preferred_element_type=jnp.float32)]
    unnamed x8, local copies, waits for them, and re-layouts: 19.8 us -> 0.91 us
    gather x1 -> x0, local copies, waits for them, and re-layouts: 17.1 us -> none  [local(): ordered = jnp.take(block_weights, inverse, axis=0)]
  transfers between devices with their start and end apart: 4 -> 5, of which waited for: 4 -> 4; matrix products, arithmetic and copies ran while one was open for 2% -> 3% of each run, Pallas kernels for 0% -> 5%
where the time goes in v1:
time: 283 us; the launch traced here: 282 us
  waiting for transfers between devices  126 us (45%)
  blocking collectives  85.1 us (30%)
  Pallas kernels  31.1 us (11%)
  between operations  14.2 us (5%)
  matrix products  12.8 us (5%)
  starting transfers between devices  9.16 us (3%)
    all_to_all x2, blocking collectives, relay(): lax.all_to_all(part, 'section', split_axis=0, concat_axis=0, tiled=True)  85.1 us
    reduce_scatter x1, waiting for transfers between devices, local(): lax.psum_scatter(partial, 'tp', scatter_dimension=1, tiled=True)  59.1 us
    all_to_all x2, waiting for transfers between devices, relay(): lax.all_to_all(part, 'section', split_axis=0, concat_axis=0, tiled=True)  53.6 us
    pallas_call x1, Pallas kernels, split_blocks(): pl.pallas_call(functools.partial(split_kernel, lanes), grid_spec=pltpu.Pr...  17.8 us
    ppermute x1, waiting for transfers between devices, local(): return lax.ppermute(result, 'section', route)[None]  12.3 us
    pallas_call x1, Pallas kernels, attention(): pl.pallas_call(attention_kernel, grid_spec=pltpu.PrefetchScalarGridSpec(n...  9.11 us
    all_to_all x2, starting transfers between devices, relay(): lax.all_to_all(part, 'section', split_axis=0, concat_axis=0, tiled=True)  9.02 us
    dot_general x3, matrix products, project(): jnp.dot(normed, matrix, preferred_element_type=jnp.float32)  7.42 us
  transfers between devices with their start and end apart: 5, of which 4 were waited for; matrix products, arithmetic and copies ran while one was open for 3% of the time, Pallas kernels for 5%

profile of v1, /device:TPU:0, one launch (start us, length us, event | category | flops | bytes accessed | tf_op | source)
XLA Modules:
  0.0 281.7 jit_solution(2196858969095677150)
XLA Ops:
  6.5 0.8 select_reduce_fusion.order_ref
  7.3 17.8 %split_blocks.1 = (bf16[8,384,512]{2,1,0:T(8,128)(2,1)S(1)}, bf16[8,384,512]{2,1,0:T(8,128)(2,1)}, bf16[8,384,512]{2,1,0:T(8,128)(2,1)}, bf16[8,384,512]{2,1,0:T(8,128)(2,1)}) custom-call(s32[8]{0:T(128)S(1)} %select_reduce_fusion.order_ref, bf16[8,6144,128]{2,1,0:T(8,128)(2,1)} %bitcast.27), custom_call_target="tpu_custom_call" | custom-call | bytes 25165824 | tf_op jit(solution)/shard_map/split_blocks/pallas_call | solution.py:33
  25.1 42.8 %all_to_all.20 = bf16[8,384,512]{2,1,0:T(8,128)(2,1)S(1)} all-to-all(bf16[8,384,512]{2,1,0:T(8,128)(2,1)S(1)} %get-tuple-element.9), channel_id=1, replica_groups=mesh['section'=8,'tp'=4] {'section'}, dimensions={0} | all-to-all | bytes 6291456 | tf_op jit(solution)/shard_map/all_to_all | solution.py:151
  67.9 4.4 %all-to-all-start.1 = ((bf16[8,384,512]{2,1,0:T(8,128)(2,1)}), bf16[8,384,512]{2,1,0:T(8,128)(2,1)}, u32[]{:S(2)}, u32[]{:S(2)}) async-start(bf16[8,384,512]{2,1,0:T(8,128)(2,1)} %get-tuple-element.10), calls=%async_computation.1 | async-start | bytes 6291456 | tf_op jit(solution)/shard_map/all_to_all | solution.py:151
  72.4 0.0 all-gather.3.cloned.1.call-start
  72.4 0.7 all-gather.3.cloned.1.call-update
  73.1 37.2 %all-to-all-done.1 = bf16[8,384,512]{2,1,0:T(8,128)(2,1)} async-done(((bf16[8,384,512]{2,1,0:T(8,128)(2,1)}), bf16[8,384,512]{2,1,0:T(8,128)(2,1)}, u32[]{:S(2)}, u32[]{:S(2)}) %all-to-all-start.1) | async-done | bytes 3145760 | tf_op jit(solution)/shard_map/all_to_all | solution.py:151
  110.3 42.3 %all_to_all.21 = bf16[8,384,512]{2,1,0:T(8,128)(2,1)} all-to-all(bf16[8,384,512]{2,1,0:T(8,128)(2,1)} %get-tuple-element.11), channel_id=1, replica_groups=mesh['section'=8,'tp'=4] {'section'}, dimensions={0} | all-to-all | bytes 6291456 | tf_op jit(solution)/shard_map/all_to_all | solution.py:151
  152.6 0.0 copy-start.2
  152.6 4.6 %all-to-all-start.3 = ((bf16[8,384,512]{2,1,0:T(8,128)(2,1)}), bf16[8,384,512]{2,1,0:T(8,128)(2,1)}, u32[]{:S(2)}, u32[]{:S(2)}) async-start(bf16[8,384,512]{2,1,0:T(8,128)(2,1)} %get-tuple-element.12), calls=%async_computation.3 | async-start | bytes 6291456 | tf_op jit(solution)/shard_map/all_to_all | solution.py:151
  157.1 0.0 reduce-scatter.2.cloned.1.call-start
  157.8 0.0 copy-done.2
  157.9 0.0 all-gather.3.cloned.1.call-done
  157.9 4.1 %norm.1 = bf16[512,3072]{1,0:T(8,128)(2,1)S(1)} custom-call(bf16[512,3072]{1,0:T(8,128)(2,1)} %bitcast.29, f32[3,3072]{1,0:T(4,128)S(1)} %bitcast.26), custom_call_target="tpu_custom_call" | custom-call | flops 15728640 | bytes 6291456 | tf_op jit(solution)/shard_map/norm/pallas_call | solution.py:67
  162.0 1.8 convolution_convert_fusion.3.q_ref
  163.8 0.0 copy-start
  163.8 3.8 %convolution_convert_fusion.2.k_ref = bf16[512,512]{1,0:T(8,128)(2,1)S(1)} fusion(bf16[512,3072]{1,0:T(8,128)(2,1)S(1)} %norm.1, bf16[3072,512]{1,0:T(8,128)(2,1)} %bitcast.6), kind=kOutput, calls=%fused_computation.4 | convolution fusion | flops 1610874880 | bytes 6815744 | tf_op jit(solution)/shard_map/dot_general | solution.py:159
  167.7 0.0 copy-done
  167.7 1.8 convolution_convert_fusion.1.v_ref
  169.5 9.1 %attention.1 = bf16[512,512]{1,0:T(8,128)(2,1)S(1)} custom-call(s32[1]{0:T(128)S(6)} %copy.13.where_ref, bf16[512,512]{1,0:T(8,128)(2,1)S(1)} %convolution_convert_fusion.3.q_ref, bf16[512,512]{1,0:T(8,128)(2,1)S(1)} %convolution_convert_fusion.2.k_ref, bf16[512,512]{1,0:T(8,128)(2,1)S(1)} %convolution_convert_fusion.1.v_ref, bf16[2,2048,512]{2,1,0:T(8,128)(2,1)} %bitcast.32), custom_call_target="tpu_custom_call" | custom-call | flops 2147483648 | bytes 6291456 | tf_op jit(solution)/shard_map/attention/pallas_call | solution.py:122
  178.6 16.4 %all-to-all-done.3 = bf16[8,384,512]{2,1,0:T(8,128)(2,1)} async-done(((bf16[8,384,512]{2,1,0:T(8,128)(2,1)}), bf16[8,384,512]{2,1,0:T(8,128)(2,1)}, u32[]{:S(2)}, u32[]{:S(2)}) %all-to-all-start.3) | async-done | bytes 3145760 | tf_op jit(solution)/shard_map/all_to_all | solution.py:151
  195.0 5.4 %convolution_convert_fusion = bf16[512,3072]{1,0:T(8,128)(2,1)} fusion(bf16[512,512]{1,0:T(8,128)(2,1)S(1)} %attention.1, bf16[3072,512]{1,0:T(8,128)(2,1)} %bitcast.9), kind=kOutput, calls=%fused_computation | convolution fusion | flops 1612185600 | bytes 6815744 | tf_op jit(solution)/shard_map/dot_general | solution.py:163
  200.4 0.0 slice-start
  200.4 0.0 copy-start.1
  200.4 0.0 reduce-scatter.2.cloned.1.call-update
  200.4 0.7 slice-done
  201.1 59.1 %reduce-scatter.2.cloned.1.call-done = bf16[512,768]{1,0:T(8,128)(2,1)} async-done(((bf16[512,3072]{1,0:T(8,128)(2,1)}), bf16[512,768]{1,0:T(8,128)(2,1)}) %reduce-scatter.2.cloned.1.call-update) | async-done | bytes 786448 | tf_op jit(solution)/shard_map/reduce_scatter | solution.py:166
  260.2 0.0 copy-done.1
  260.2 1.4 fusion
  261.6 0.1 collective-permute-start
  261.7 12.3 %collective-permute-done = bf16[512,768]{1,0:T(8,128)(2,1)S(1)} collective-permute-done((bf16[512,768]{1,0:T(8,128)(2,1)S(1)}, bf16[512,768]{1,0:T(8,128)(2,1)S(1)}, u32[]{:S(2)}, u32[]{:S(2)}) %collective-permute-start) | collective-permute-done | bytes 786464 | tf_op jit(solution)/shard_map/ppermute | solution.py:171
  274.0 0.9 copy.14
  (2 shorter events, 0.0 us)
Async XLA Ops:
  67.9 42.3 %all-to-all-start.1 = ((bf16[8,384,512]{2,1,0:T(8,128)(2,1)}), bf16[8,384,512]{2,1,0:T(8,128)(2,1)}, u32[]{:S(2)}, u32[]{:S(2)}) async-start(bf16[8,384,512]{2,1,0:T(8,128)(2,1)} %get-tuple-element.10), calls=%async_computation.1 | async-start | bytes 6291456 | tf_op jit(solution)/shard_map/all_to_all | solution.py:151
  72.4 85.5 %all-gather.3.cloned.1.call-start = ((), (), s32[]{:S(2)}) async-start(), calls=%async_computation.6 | async-start | bytes 3932160 | tf_op jit(solution)/shard_map/all_gather | solution.py:155
  152.6 5.3 %copy-start.2 = (f32[1,3,3072]{2,0,1:T(1,128)S(1)}, f32[1,3,3072]{2,0,1:T(1,128)}, u32[]{:S(2)}) copy-start(f32[1,3,3072]{2,0,1:T(1,128)} %param.7) | copy-start | bytes 110596
  152.6 42.5 %all-to-all-start.3 = ((bf16[8,384,512]{2,1,0:T(8,128)(2,1)}), bf16[8,384,512]{2,1,0:T(8,128)(2,1)}, u32[]{:S(2)}, u32[]{:S(2)}) async-start(bf16[8,384,512]{2,1,0:T(8,128)(2,1)} %get-tuple-element.12), calls=%async_computation.3 | async-start | bytes 6291456 | tf_op jit(solution)/shard_map/all_to_all | solution.py:151
  157.1 103.1 %reduce-scatter.2.cloned.1.call-start = ((), (), s32[]{:S(2)}) async-start(), calls=%async_computation.5 | async-start | bytes 3932160 | tf_op jit(solution)/shard_map/reduce_scatter | solution.py:166
  163.8 3.8 %copy-start = (bf16[8,384,512]{2,1,0:T(8,128)(2,1)S(1)}, bf16[8,384,512]{2,1,0:T(8,128)(2,1)}, u32[]{:S(2)}) copy-start(bf16[8,384,512]{2,1,0:T(8,128)(2,1)} %all_to_all.21) | copy-start | bytes 9437188
  200.4 0.7 slice-start
  200.4 59.8 %copy-start.1 = (bf16[1,512,768]{2,1,0:T(8,128)(2,1)S(1)}, bf16[1,512,768]{2,1,0:T(8,128)(2,1)}, u32[]{:S(2)}) copy-start(bf16[1,512,768]{2,1,0:T(8,128)(2,1)} %param.8) | copy-start | bytes 2359300
  261.6 12.4 %collective-permute-start = (bf16[512,768]{1,0:T(8,128)(2,1)S(1)}, bf16[512,768]{1,0:T(8,128)(2,1)S(1)}, u32[]{:S(2)}, u32[]{:S(2)}) collective-permute-start(bf16[512,768]{1,0:T(8,128)(2,1)S(1)} %fusion), channel_id=1, source_target_pairs={{28,0},{0,4},{4,8},{8,12},{12,16},{16,20},{20,24},{24,28},{29,1},{... | collective-permute-start | bytes 2359304 | tf_op jit(solution)/shard_map/ppermute | solution.py:171
Sparse Core Ops, SparseCore 0:
  74.8 65.0 all-gather.2
  200.5 59.6 reduce-scatter.1

commit v2 on v0

v2 whole, which is shorter than its diff:
```python
import functools

import jax
import jax.numpy as jnp
import ml_dtypes
import numpy as np
from jax import lax
from jax.experimental import pallas as pl
from jax.experimental.pallas import tpu as pltpu
from jax.sharding import PartitionSpec as P

HD = 128
VMEM_LIMIT = 48 * 1024 * 1024
F32 = jnp.float32
BF16 = jnp.bfloat16
WHOLE = pl.BlockSpec(memory_space=pltpu.VMEM)
ANYWHERE = pl.BlockSpec(memory_space=pl.ANY)
SCALAR = pl.BlockSpec(memory_space=pltpu.SMEM)
PARAMS = pltpu.CompilerParams(vmem_limit_bytes=VMEM_LIMIT)


def cost(flops, size, exps=0):
    return pl.CostEstimate(flops=flops, bytes_accessed=size, transcendentals=exps)


def turned(left, right):
    return lax.dot_general(left, right, (((1,), (1,)), ((), ())), preferred_element_type=F32)


def pick_matrix(kinds, lanes, depth_step):
    period = 4 * lanes
    row = np.arange(len(kinds) * lanes * depth_step)
    kind = np.asarray(kinds)[row // (lanes * depth_step)]
    source = (row % depth_step) * period + (row // depth_step) % lanes * 4 + kind
    return np.equal.outer(source, np.arange(period * depth_step)).astype(ml_dtypes.bfloat16)


def split_kernel(lanes, plan, kinds, depth_step, order_ref, pick_ref, rows_ref, *outs):
    depth = rows_ref.shape[1] // (4 * lanes)
    chunk = depth_step * 4 * lanes

    def fill(own):
        for first in range(0, depth, depth_step):
            begin = first * 4 * lanes
            sorted_rows = jnp.dot(
                pick_ref[...], rows_ref[0, begin : begin + chunk, :], preferred_element_type=F32
            ).astype(BF16)
            for out, columns in zip(own, plan):
                for column, (kind, lane) in enumerate(columns):
                    at = (kinds.index(kind) * lanes + lane) * depth_step
                    out[first : first + depth_step, column * HD : (column + 1) * HD] = sorted_rows[
                        at : at + depth_step
                    ]

    for block in range(len(outs) // len(plan)):
        own = outs[block * len(plan) : (block + 1) * len(plan)]
        pl.when(pl.program_id(0) == block)(functools.partial(fill, own))


def split_blocks(rows, order, plan, lanes):
    depth = rows.shape[1] // (4 * lanes)
    depth_step = max(n for n in (16, 32, 64) if depth % n == 0 and n * 4 * lanes <= 256)
    kinds = sorted({kind for columns in plan for kind, _ in columns})
    pick = pick_matrix(kinds, lanes, depth_step)
    blocks = order.shape[0]
    shapes = [(depth, len(columns) * HD) for columns in plan]
    flat = pl.pallas_call(
        functools.partial(split_kernel, lanes, plan, kinds, depth_step),
        grid_spec=pltpu.PrefetchScalarGridSpec(
            num_scalar_prefetch=1,
            grid=(blocks,),
            in_specs=[
                pl.BlockSpec(pick.shape, lambda i, order: (0, 0)),
                pl.BlockSpec((1,) + rows.shape[1:], lambda i, order: (order[i], 0, 0)),
            ],
            out_specs=[pl.BlockSpec(shape, lambda i, order: (0, 0)) for shape in shapes] * blocks,
        ),
        out_shape=[jax.ShapeDtypeStruct(shape, BF16) for shape in shapes] * blocks,
        compiler_params=PARAMS,
        cost_estimate=cost(0, 3 * blocks * rows.shape[1] * HD),
        name="split_blocks",
    )(order, jnp.asarray(pick), rows)
    return [list(flat[i :: len(shapes)]) for i in range(len(shapes))]


def norm_kernel(tokens_ref, modulation_ref, out_ref):
    tokens = tokens_ref[...].astype(F32)
    center = jnp.mean(tokens, axis=1, keepdims=True)
    tokens = tokens - center
    spread = jnp.mean(tokens * tokens, axis=1, keepdims=True)
    normed = tokens * lax.rsqrt(spread + 1e-06)
    out_ref[...] = (normed * (1.0 + modulation_ref[0:1]) + modulation_ref[1:2]).astype(BF16)


def norm(tokens, modulation):
    patch, width = tokens.shape
    rows = 128
    return pl.pallas_call(
        norm_kernel,
        grid=(patch // rows,),
        in_specs=[
            pl.BlockSpec((rows, width), lambda i: (i, 0)),
            pl.BlockSpec((3, width), lambda i: (0, 0)),
        ],
        out_specs=pl.BlockSpec((rows, width), lambda i: (i, 0)),
        out_shape=jax.ShapeDtypeStruct((patch, width), BF16),
        compiler_params=PARAMS,
        cost_estimate=cost(10 * patch * width, 4 * patch * width),
        name="norm",
    )(tokens, modulation)


def gathered(pieces, sources_ref, matrix, sems):
    depth = pieces[0].shape[0]
    copies = []
    for index, piece in enumerate(pieces):
        start = pl.multiple_of(sources_ref[index] * depth, 16)
        copies.append(
            pltpu.make_async_copy(piece, matrix.at[pl.ds(start, depth), :], sems.at[index])
        )
        copies[-1].start()
    for copy in copies:
        copy.wait()


def score_kernel(count, sources_ref, where_ref, normed_ref, stale_ref, *rest):
    pieces, (expo_ref, base_ref, share_ref, both, matrix, sems) = rest[:count], rest[count:]
    heads, patch, _ = expo_ref.shape
    parts = stale_ref.shape[1] // patch
    gathered(pieces, sources_ref, matrix, sems)
    both[...] = jnp.dot(normed_ref[...], matrix[...], preferred_element_type=F32).astype(BF16)
    starts = [
        pl.multiple_of(lax.rem(where_ref[0] + 1 + part, parts) * patch, patch)
        for part in range(parts - 1)
    ]
    for head in range(heads):
        cols = slice(head * HD, (head + 1) * HD)
        query = both[:, cols]
        keys = [stale_ref[0, pl.ds(start, patch), cols] for start in starts]
        keys.append(both[:, (heads + head) * HD : (heads + head + 1) * HD])
        scores = [turned(query, key) / jnp.sqrt(F32(HD)) for key in keys]
        top = functools.reduce(jnp.maximum, scores)
        top = jnp.max(top, axis=1, keepdims=True)
        total, summed = 0.0, 0.0
        for part, score in enumerate(scores):
            expo = jnp.exp(score - top)
            total += jnp.sum(expo, axis=1, keepdims=True)
            expo = expo.astype(BF16)
            if part == parts - 1:
                expo_ref[head] = expo
                continue
            values = stale_ref[1, pl.ds(starts[part], patch), cols]
            summed += jnp.dot(expo, values, preferred_element_type=F32)
        share = 1.0 / total
        base_ref[head] = summed * share
        share_ref[head] = jnp.broadcast_to(share, (patch, HD))


def attend_kernel(count, sources_ref, normed_ref, expo_ref, base_ref, share_ref, *rest):
    pieces, (out_ref, values, matrix, sems) = rest[:count], rest[count:]
    gathered(pieces, sources_ref, matrix, sems)
    values[...] = jnp.dot(normed_ref[...], matrix[...], preferred_element_type=F32).astype(BF16)
    for spot in range(expo_ref.shape[0]):
        cols = slice(spot * HD, (spot + 1) * HD)
        new = jnp.dot(expo_ref[spot], values[:, cols], preferred_element_type=F32)
        out_ref[:, cols] = (base_ref[spot] + new * share_ref[spot]).astype(BF16)


def score(normed, pieces, sources, where, stale, group):
    patch, width = normed.shape
    heads, keys = len(group), stale.shape[1]
    columns = heads * HD
    stat = jax.ShapeDtypeStruct((heads, patch, HD), F32)
    at = lambda i: (0, 0, group[0] // heads)
    return pl.pallas_call(
        functools.partial(score_kernel, len(pieces)),
        grid=(1,),
        in_specs=[SCALAR, SCALAR, WHOLE, pl.BlockSpec((2, keys, columns), at)]
        + [ANYWHERE] * len(pieces),
        out_specs=[WHOLE] * 3,
        out_shape=[jax.ShapeDtypeStruct((heads, patch, patch), BF16), stat, stat],
        scratch_shapes=[
            pltpu.VMEM((patch, 2 * columns), BF16),
            pltpu.VMEM((width, 2 * columns), BF16),
            pltpu.SemaphoreType.DMA((len(pieces),)),
        ],
        compiler_params=PARAMS,
        cost_estimate=cost(
            4 * patch * columns * (width + keys), 4 * columns * (width + keys), patch * heads * keys
        ),
        name="score",
    )(sources, where, normed, stale, *pieces)


def attend(normed, pieces, sources, first, expo, base, share):
    patch, width = normed.shape
    columns = pieces[0].shape[1]
    count = columns // HD
    picked = lambda last: pl.BlockSpec((count, patch, last), lambda i: (first // count, 0, 0))
    return pl.pallas_call(
        functools.partial(attend_kernel, len(pieces)),
        grid=(1,),
        in_specs=[SCALAR, WHOLE, picked(patch), picked(HD), picked(HD)]
        + [ANYWHERE] * len(pieces),
        out_specs=WHOLE,
        out_shape=jax.ShapeDtypeStruct((patch, columns), BF16),
        scratch_shapes=[
            pltpu.VMEM((patch, columns), BF16),
            pltpu.VMEM((width, columns), BF16),
            pltpu.SemaphoreType.DMA((len(pieces),)),
        ],
        compiler_params=PARAMS,
        cost_estimate=cost(2 * patch * columns * (width + patch), 2 * columns * width),
        name="attend",
    )(sources, normed, expo, base, share, *pieces)


def output_kernel(tp, chunks, inflow_ref, gate_ref, *rest):
    attended, matrices, out_ref = rest[: tp * chunks], rest[tp * chunks : -1], rest[-1]
    mixed = 0.0
    for index in range(tp):
        own = attended[index * chunks : (index + 1) * chunks]
        left = jnp.concatenate([piece[...] for piece in own], axis=1)
        mixed += turned(left, matrices[index][...])
    out_ref[...] = (inflow_ref[...].astype(F32) + gate_ref[...] * mixed).astype(BF16)


def output(inflow, gate, attended, matrices):
    tp, chunks = len(attended), len(attended[0])
    patch, share = inflow.shape
    inner = matrices[0].shape[1]
    flat = [piece for own in attended for piece in own]
    return pl.pallas_call(
        functools.partial(output_kernel, tp, chunks),
        in_specs=[WHOLE] * (2 + len(flat) + tp),
        out_specs=WHOLE,
        out_shape=jax.ShapeDtypeStruct(inflow.shape, BF16),
        compiler_params=PARAMS,
        cost_estimate=cost(2 * patch * share * inner * tp, 2 * inner * tp * (share + patch)),
        name="output",
    )(inflow, gate, *flat, *matrices)


def after(block, earlier):
    return lax.optimization_barrier((block, earlier))[0]


def swapped(block, axis, distance):
    return lax.ppermute(block, axis, [(i, i ^ distance) for i in range(lax.axis_size(axis))])


def handed_on(block):
    sections = lax.axis_size("section")
    return lax.ppermute(block, "section", [(i, (i + 1) % sections) for i in range(sections)])


def relay(stages, window):
    sections = len(stages[0])
    distances = sorted(range(1, sections), key=lambda d: (d == 1, d % 2, d))
    sent, arrived = [], []
    for pieces in stages:
        received = {0: pieces[0]}
        for distance in distances:
            piece = pieces[distance]
            if len(sent) >= window:
                piece = after(piece, sent[-window])
            received[distance] = swapped(piece, "section", distance)
            sent.append(received[distance])
        arrived.append([received[d] for d in range(sections)])
    return arrived


def place_kernel(count, slots_ref, *rest):
    pieces, (out_ref, sems) = rest[:count], rest[count:]
    copies = [
        pltpu.make_async_copy(piece, out_ref.at[slots_ref[index]], sems.at[index])
        for index, piece in enumerate(pieces)
    ]
    for copy in copies:
        copy.start()
    for copy in copies:
        copy.wait()


def placed(pieces, slots):
    return pl.pallas_call(
        functools.partial(place_kernel, len(pieces)),
        in_specs=[SCALAR] + [ANYWHERE] * len(pieces),
        out_specs=ANYWHERE,
        out_shape=jax.ShapeDtypeStruct((len(pieces),) + pieces[0].shape, BF16),
        scratch_shapes=[pltpu.SemaphoreType.DMA((len(pieces),))],
        compiler_params=PARAMS,
        cost_estimate=cost(0, 4 * len(pieces) * pieces[0].size),
        name="placed",
    )(slots, *pieces)


def local(block_weights, modulation, inflow, stale_cache, patch_index, assignment):
    sections, tp = lax.axis_size("section"), lax.axis_size("tp")
    here, rank = lax.axis_index("section"), lax.axis_index("tp")
    blocks, depth, kinds, inner = block_weights.shape
    lanes = inner // HD
    share = inflow.shape[2]

    section_ids = jnp.arange(sections, dtype=jnp.int32)
    sources = here ^ section_ids

    def block_of(section):
        return jnp.sum((assignment[None] == section[:, None]) * section_ids[None], axis=1)

    rows = block_weights.reshape(blocks, depth, kinds, lanes, HD)
    rows = rows.transpose(0, 1, 3, 2, 4).reshape(blocks, depth * lanes * kinds, HD)
    tokens = lax.all_gather(inflow[0], "tp", axis=1, tiled=True)

    size = 2 if lanes % 2 == 0 else 1
    groups = [tuple(range(first, first + size)) for first in range(0, lanes, size)]
    plan, chunks = [], []
    for group in groups:
        plan.append([(kind, head) for kind in (0, 1) for head in group])
        parts = [group] if group != groups[-1] else [(head,) for head in group]
        plan += [[(2, head) for head in part] for part in parts]
        chunks.append(parts)
    to_out = split_blocks(
        rows, block_of((sources + sections - 1) % sections), [[(3, head) for head in range(lanes)]], lanes
    )
    arrived = iter(relay(to_out + split_blocks(rows, block_of(sources), plan, lanes), 4))

    per = sections // tp
    slots = ((sources // per) ^ rank) * per + sources % per
    held = placed(next(arrived), slots).reshape(tp, per * depth, inner)
    matrices = [held[0]]
    for distance in range(1, tp):
        matrices.append(swapped(after(held[distance], matrices[-1]), "tp", distance))

    normed = norm(tokens, modulation[0])
    attended = [[] for _ in range(tp)]
    for group, parts in zip(groups, chunks):
        stats = score(normed, next(arrived), sources, patch_index, stale_cache[0], group)
        for part in parts:
            own = attend(normed, next(arrived), sources, part[0] - group[0], *stats)
            moved = handed_on(own)
            for distance in range(tp):
                attended[distance].append(swapped(moved, "tp", distance) if distance else moved)
    carried = handed_on(after(inflow[0], own))
    gate = handed_on(modulation[0, 2])
    gate = lax.dynamic_slice_in_dim(gate, rank * share, share, 0)[None]
    return output(carried, gate, attended, matrices)[None]


def solution(mesh):
    spread = (
        P(None, "section", None, "tp"),
        P("section", None, None),
        P("section", None, "tp"),
        P("section", None, None, "tp"),
        P("section"),
        P(),
    )
    return jax.shard_map(
        local, mesh=mesh, in_specs=spread, out_specs=P("section", None, "tp"), check_vma=False
    )
```

time: 423 us -> 304 us (0.72)
  waiting for transfers between devices: 264 us -> 98.3 us
  Pallas kernels: 0 us -> 65.5 us
  starting transfers between devices: 5.48 us -> 59.4 us
  matrix products: 40.5 us -> 0 us
  other arithmetic: 33.2 us -> 0.9 us
  local copies, waits for them, and re-layouts: 65.3 us -> 61 us
    psum x1 -> x0, waiting for transfers between devices: 121 us -> none  [local(): lax.psum(partial_value.astype(jnp.bfloat16), 'tp').astype(jnp.float32)]
    ppermute x1 -> x59, waiting for transfers between devices: 12.3 us -> 97.5 us  [the longest x54 91.7 us: swapped(): lax.ppermute(block, axis, [(i, i ^ distance) for i in range(lax.axis_size...]
    pallas_call x0 -> x10, Pallas kernels: none -> 65.5 us  [the longest x2 22.2 us: split_blocks(): pl.pallas_call(functools.partial(split_kernel, lanes, plan, kinds, depth_...]
    all_to_all x1 -> x0, waiting for transfers between devices: 65.4 us -> none  [local(): lax.all_to_all(ordered, 'section', split_axis=0, concat_axis=1, tiled=True)]
    all_gather x1, waiting for transfers between devices: 63.7 us -> 0.01 us  [local(): tokens = lax.all_gather(inflow[0], 'tp', axis=1, tiled=True)]
    ppermute x1 -> x59, starting transfers between devices: 0.06 us -> 59.4 us  [the longest x54 56.5 us: swapped(): lax.ppermute(block, axis, [(i, i ^ distance) for i in range(lax.axis_size...]
    dot_general x4 -> x0, matrix products: 40.5 us -> none  [the longest x1 15.5 us: local(): jnp.einsum('hps,shd->phd', probabilities, values_all.reshape(seq_len, hea...]
    unnamed x8 -> x287, local copies, waits for them, and re-layouts: 19.8 us -> 57.1 us
  transfers between devices with their start and end apart: 4 -> 60, of which waited for: 4 -> 19; matrix products, arithmetic and copies ran while one was open for 2% -> 2% of each run, Pallas kernels for 0% -> 20%
where the time goes in v2:
time: 304 us; the launch traced here: 300 us
  waiting for transfers between devices  98.3 us (32%)
  Pallas kernels  65.5 us (22%)
  local copies, waits for them, and re-layouts  61 us (20%)
  starting transfers between devices  59.4 us (20%)
  between operations  15.1 us (5%)
    ppermute x54, waiting for transfers between devices, swapped(): lax.ppermute(block, axis, [(i, i ^ distance) for i in range(lax.axis_size...  91.7 us
    unnamed x287, local copies, waits for them, and re-layouts  57.1 us
    ppermute x54, starting transfers between devices, swapped(): lax.ppermute(block, axis, [(i, i ^ distance) for i in range(lax.axis_size...  56.5 us
    pallas_call x2, Pallas kernels, split_blocks(): pl.pallas_call(functools.partial(split_kernel, lanes, plan, kinds, depth_...  22.2 us
    pallas_call x2, Pallas kernels, score(): pl.pallas_call(functools.partial(score_kernel, len(pieces)), grid=(1,), i...  19.7 us
    pallas_call x3, Pallas kernels, attend(): pl.pallas_call(functools.partial(attend_kernel, len(pieces)), grid=(1,),...  12.8 us
  transfers between devices with their start and end apart: 60, of which 19 were waited for; matrix products, arithmetic and copies ran while one was open for 2% of the time, Pallas kernels for 20%

profile of v2, /device:TPU:0, one launch (start us, length us, event | category | flops | bytes accessed | tf_op | source)
XLA Modules:
  0.0 300.1 jit_solution(6677742185844852701)
XLA Ops:
  8.9 9.5 %split_blocks.3 = (bf16[384,512]{1,0:T(8,128)(2,1)S(1)}, bf16[384,512]{1,0:T(8,128)(2,1)}, bf16[384,512]{1,0:T(8,128)(2,1)S(1)}, bf16[384,512]{1,0:T(8,128)(2,1)...) custom-call(s32[8]{0:T(128)S(1)} %get-tuple-element.197.order_ref, ...), custom_call_target="tpu_custom_call" | custom-call | bytes 18874368 | tf_op jit(solution)/shard_map/split_blocks/pallas_call | solution.py:67
  18.4 3.0 %collective-permute-start.7 = (bf16[384,512]{1,0:T(8,128)(2,1)S(1)}, bf16[384,512]{1,0:T(8,128)(2,1)S(1)}, u32[]{:S(2)}, u32[]{:S(2)}) collective-permute-start(bf16[384,512]{1,0:T(8,128)(2,1)S(1)} %get-tuple-element.120), channel_id=1, source_target_pairs={{0,16},{4,20},{8,24},{12,28},{16,0},{20,4},{24,8},{28,12},{1,17},{... | collective-permute-start | bytes 1179656 | tf_op jit(solution)/shard_map/ppermute | solution.py:249
  24.0 6.5 %collective-permute-done.7.rest_4_ = bf16[384,512]{1,0:T(8,128)(2,1)S(1)} collective-permute-done((bf16[384,512]{1,0:T(8,128)(2,1)S(1)}, bf16[384,512]{1,0:T(8,128)(2,1)S(1)}, u32[]{:S(2)}, u32[]{:S(2)}) %collective-permute-start.7) | collective-permute-done | bytes 393248 | tf_op jit(solution)/shard_map/ppermute | solution.py:249
  31.8 12.7 %split_blocks.2 = (bf16[384,512]{1,0:T(8,128)(2,1)S(1)}, bf16[384,256]{1,0:T(8,128)(2,1)S(1)}, bf16[384,512]{1,0:T(8,128)(2,1)S(1)}, bf16[384,128]{1,0:T(8,128)(...) custom-call(s32[8]{0:T(128)S(1)} %get-tuple-element.198.order_ref, ...), custom_call_target="tpu_custom_call" | custom-call | bytes 18874368 | tf_op jit(solution)/shard_map/split_blocks/pallas_call | solution.py:67
  65.0 2.3 collective-permute-start.9
  67.3 5.0 %collective-permute-done.1.rest_2_ = bf16[384,512]{1,0:T(8,128)(2,1)S(1)} collective-permute-done((bf16[384,512]{1,0:T(8,128)(2,1)}, bf16[384,512]{1,0:T(8,128)(2,1)S(1)}, u32[]{:S(2)}, u32[]{:S(2)}) %collective-permute-start.1) | collective-permute-done | bytes 393248 | tf_op jit(solution)/shard_map/ppermute | solution.py:249
  73.6 7.6 %collective-permute-done.14.rest_5_ = bf16[384,512]{1,0:T(8,128)(2,1)S(1)} collective-permute-done((bf16[384,512]{1,0:T(8,128)(2,1)}, bf16[384,512]{1,0:T(8,128)(2,1)S(1)}, u32[]{:S(2)}, u32[]{:S(2)}) %collective-permute-start.14) | collective-permute-done | bytes 393248 | tf_op jit(solution)/shard_map/ppermute | solution.py:249
  91.3 2.3 placed.1
  94.7 3.1 %fusion.2 = (bf16[2,384,512]{2,1,0:T(8,128)(2,1)}, bf16[2,384,512]{2,1,0:T(8,128)(2,1)S(1)}, bf16[2,384,512]{2,1,0:T(8,128)(2,1)S(1)}, bf16[2,384,512]{2,1,0:T(8,128)(2,1)S(1)}) fusion(bf16[8,384,512]{2,1,0:T(8,128)(2,1)} %placed.1), kind=kLoop, calls=%fused_computation.14 | loop fusion | bytes 6291456 | tf_op jit(solution)/shard_map/slice | solution.py:333
  106.1 10.6 %collective-permute-done.23.rest_2_ = bf16[384,256]{1,0:T(8,128)(2,1)S(1)} collective-permute-done((bf16[384,256]{1,0:T(8,128)(2,1)S(1)}, bf16[384,256]{1,0:T(8,128)(2,1)S(1)}, u32[]{:S(2)}, u32[]{:S(2)}) %collective-permute-start.23) | collective-permute-done | bytes 196640 | tf_op jit(solution)/shard_map/ppermute | solution.py:249
  120.1 2.5 collective-permute-start.17
  124.0 8.8 %collective-permute-done.24.rest_5_ = bf16[384,256]{1,0:T(8,128)(2,1)S(1)} collective-permute-done((bf16[384,256]{1,0:T(8,128)(2,1)S(1)}, bf16[384,256]{1,0:T(8,128)(2,1)S(1)}, u32[]{:S(2)}, u32[]{:S(2)}) %collective-permute-start.24) | collective-permute-done | bytes 196640 | tf_op jit(solution)/shard_map/ppermute | solution.py:249
  136.1 2.9 collective-permute-start.57
  143.0 10.9 %collective-permute-done.25.rest_4_ = bf16[384,512]{1,0:T(8,128)(2,1)S(1)} collective-permute-done((bf16[384,512]{1,0:T(8,128)(2,1)S(1)}, bf16[384,512]{1,0:T(8,128)(2,1)S(1)}, u32[]{:S(2)}, u32[]{:S(2)}) %collective-permute-start.25) | collective-permute-done | bytes 393248 | tf_op jit(solution)/shard_map/ppermute | solution.py:249
  158.5 10.0 %collective-permute-done.26.rest_5_ = bf16[384,512]{1,0:T(8,128)(2,1)S(1)} collective-permute-done((bf16[384,512]{1,0:T(8,128)(2,1)S(1)}, bf16[384,512]{1,0:T(8,128)(2,1)S(1)}, u32[]{:S(2)}, u32[]{:S(2)}) %collective-permute-start.26) | collective-permute-done | bytes 393248 | tf_op jit(solution)/shard_map/ppermute | solution.py:249
  170.7 2.2 collective-permute-start.34
  180.0 2.3 collective-permute-done.38.rest_5_
  185.9 2.9 collective-permute-start.58
  195.6 4.3 %norm.1.normed_ref = bf16[512,3072]{1,0:T(8,128)(2,1)S(1)} custom-call(bf16[512,3072]{1,0:T(8,128)(2,1)} %bitcast.23, f32[3,3072]{1,0:T(4,128)S(1)} %bitcast.18), custom_call_target="tpu_custom_call" | custom-call | flops 15728640 | bytes 6291456 | tf_op jit(solution)/shard_map/norm/pallas_call | solution.py:98
  201.7 9.7 %score.2 = (bf16[2,512,512]{2,1,0:T(8,128)(2,1)S(1)}, f32[2,512,128]{2,1,0:T(8,128)S(1)}, f32[2,512,128]{2,1,0:T(8,128)S(1)}) custom-call(s32[8]{0:T(128)S(1)} %iota_xor_fusion.sources_ref, s32[1]{0:T(128)S(6)} %copy.14.where_ref, bf16[512,3072]{1,0:T(8,128)(2,1)} %copy-done, bf16[2,2048,512]{2,1,0:T(8,128)(2,1)} %bitcast.21, ...), custom_call_target="tpu_custom_call" | custom-call | flops 2684354560 | bytes 5242880 | tf_op jit(solution)/shard_map/score/pallas_call | solution.py:175
  211.6 3.6 %attend.3 = bf16[512,128]{1,0:T(8,128)(2,1)S(1)} custom-call(s32[8]{0:T(128)S(1)} %iota_xor_fusion.sources_ref, bf16[512,3072]{1,0:T(8,128)(2,1)S(1)} %copy-done.1, bf16[2,512,512]{2,1,0:T(8,128)(2,1)S(1)} %get-tuple-element.154.expo_ref, f32[2,512,128]{2,1,0:T(8,128)S(1)} %get-tuple-element.155.base_ref, f32[2,512,128]{2,1,0:T(8,128)S(1)} %get-tuple-element.156.share_ref, ...), custom_call_target="tpu_custom_call" | custom-call | flops 469762048 | bytes 786432 | tf_op jit(solution)/shard_map/attend/pallas_call | solution.py:200
  215.8 9.9 %score.3 = (bf16[2,512,512]{2,1,0:T(8,128)(2,1)S(1)}, f32[2,512,128]{2,1,0:T(8,128)S(1)}, f32[2,512,128]{2,1,0:T(8,128)S(1)}) custom-call(s32[8]{0:T(128)S(1)} %iota_xor_fusion.sources_ref, s32[1]{0:T(128)S(6)} %copy.14.where_ref, bf16[512,3072]{1,0:T(8,128)(2,1)} %copy-done, bf16[2,2048,512]{2,1,0:T(8,128)(2,1)} %bitcast.22, ...), custom_call_target="tpu_custom_call" | custom-call | flops 2684354560 | bytes 5242880 | tf_op jit(solution)/shard_map/score/pallas_call | solution.py:175
  226.0 6.1 %attend.4 = bf16[512,256]{1,0:T(8,128)(2,1)S(1)} custom-call(s32[8]{0:T(128)S(1)} %iota_xor_fusion.sources_ref, bf16[512,3072]{1,0:T(8,128)(2,1)} %copy-done, bf16[2,512,512]{2,1,0:T(8,128)(2,1)S(1)} %get-tuple-element.188.expo_ref, f32[2,512,128]{2,1,0:T(8,128)S(1)} %get-tuple-element.189.base_ref, f32[2,512,128]{2,1,0:T(8,128)S(1)} %get-tuple-element.190.share_ref, ...), custom_call_target="tpu_custom_call" | custom-call | flops 939524096 | bytes 1572864 | tf_op jit(solution)/shard_map/attend/pallas_call | solution.py:200
  234.5 3.2 %attend.5 = bf16[512,128]{1,0:T(8,128)(2,1)S(1)} custom-call(s32[8]{0:T(128)S(1)} %iota_xor_fusion.sources_ref, bf16[512,3072]{1,0:T(8,128)(2,1)S(1)} %copy-done.2, bf16[2,512,512]{2,1,0:T(8,128)(2,1)S(1)} %get-tuple-element.154.expo_ref, f32[2,512,128]{2,1,0:T(8,128)S(1)} %get-tuple-element.155.base_ref, f32[2,512,128]{2,1,0:T(8,128)S(1)} %get-tuple-element.156.share_ref, ...), custom_call_target="tpu_custom_call" | custom-call | flops 469762048 | bytes 786432 | tf_op jit(solution)/shard_map/attend/pallas_call | solution.py:200
  238.9 4.1 %collective-permute-done.45.rest_1_ = bf16[512,128]{1,0:T(8,128)(2,1)S(1)} collective-permute-done((bf16[512,128]{1,0:T(8,128)(2,1)S(1)}, bf16[512,128]{1,0:T(8,128)(2,1)S(1)}, u32[]{:S(2)}, u32[]{:S(2)}) %collective-permute-start.45) | collective-permute-done | bytes 131104 | tf_op jit(solution)/shard_map/ppermute | solution.py:254
  247.9 2.3 collective-permute-done.48.rest_4_
  253.2 5.5 %collective-permute-done.51.rest_7_ = bf16[512,128]{1,0:T(8,128)(2,1)S(1)} collective-permute-done((bf16[512,128]{1,0:T(8,128)(2,1)S(1)}, bf16[512,128]{1,0:T(8,128)(2,1)S(1)}, u32[]{:S(2)}, u32[]{:S(2)}) %collective-permute-start.51) | collective-permute-done | bytes 131104 | tf_op jit(solution)/shard_map/ppermute | solution.py:249
  259.3 4.3 %collective-permute-done.52.rest_8_ = bf16[512,128]{1,0:T(8,128)(2,1)S(1)} collective-permute-done((bf16[512,128]{1,0:T(8,128)(2,1)}, bf16[512,128]{1,0:T(8,128)(2,1)S(1)}, u32[]{:S(2)}, u32[]{:S(2)}) %collective-permute-start.52) | collective-permute-done | bytes 131104 | tf_op jit(solution)/shard_map/ppermute | solution.py:249
  266.4 2.4 collective-permute-start.55
  268.8 8.2 %collective-permute-done.55.rest_11_ = bf16[512,128]{1,0:T(8,128)(2,1)} collective-permute-done((bf16[512,128]{1,0:T(8,128)(2,1)}, bf16[512,128]{1,0:T(8,128)(2,1)}, u32[]{:S(2)}, u32[]{:S(2)}) %collective-permute-start.55) | collective-permute-done | bytes 131104 | tf_op jit(solution)/shard_map/ppermute | solution.py:249
  277.1 7.5 %collective-permute-done.50.rest_6_ = bf16[512,256]{1,0:T(8,128)(2,1)} collective-permute-done((bf16[512,256]{1,0:T(8,128)(2,1)S(1)}, bf16[512,256]{1,0:T(8,128)(2,1)}, u32[]{:S(2)}, u32[]{:S(2)}) %collective-permute-start.50) | collective-permute-done | bytes 262176 | tf_op jit(solution)/shard_map/ppermute | solution.py:249
  289.1 4.2 %output.1 = bf16[512,768]{1,0:T(8,128)(2,1)} custom-call(bf16[512,768]{1,0:T(8,128)(2,1)} %collective-permute-done.42.inflow_ref, f32[1,768]{1,0:T(1,128)S(1)} %broadcast_in_dim.4.gate_ref, bf16[512,256]{1,0:T(8,128)(2,1)S(1)} %collective-permute-done.44.rest_0_, bf16[512,128]{1,0:T(8,128)(2,1)S(1)} %collective-permute-done.45.rest_1_, ...), custom_call_target="tpu_custom_call" | custom-call | flops 1610612736 | bytes 5242880 | tf_op jit(solution)/shard_map/output/pallas_call | solution.py:233
  (394 shorter events, 104.8 us)
Async XLA Ops:
  6.5 188.2 %all-gather.3.cloned.1.call-start = ((), (), s32[]{:S(2)}) async-start(), calls=%async_computation | async-start | bytes 3932160 | tf_op jit(solution)/shard_map/all_gather | solution.py:313
  21.4 39.1 %collective-permute-start = (bf16[384,512]{1,0:T(8,128)(2,1)S(1)}, bf16[384,512]{1,0:T(8,128)(2,1)S(1)}, u32[]{:S(2)}, u32[]{:S(2)}) collective-permute-start(bf16[384,512]{1,0:T(8,128)(2,1)S(1)} %get-tuple-element.108), channel_id=1, source_target_pairs={{0,12},{4,8},{8,4},{12,0},{16,28},{20,24},{24,20},{28,16},{1,13},{... | collective-permute-start | bytes 1179656 | tf_op jit(solution)/shard_map/ppermute | solution.py:249
  22.0 39.1 %collective-permute-start.13 = (bf16[384,512]{1,0:T(8,128)(2,1)S(1)}, bf16[384,512]{1,0:T(8,128)(2,1)S(1)}, u32[]{:S(2)}, u32[]{:S(2)}) collective-permute-start(bf16[384,512]{1,0:T(8,128)(2,1)S(1)} %get-tuple-element.132), channel_id=1, source_target_pairs={{0,8},{4,12},{8,0},{12,4},{16,24},{20,28},{24,16},{28,20},{1,9},{5... | collective-permute-start | bytes 1179656 | tf_op jit(solution)/shard_map/ppermute | solution.py:249
  23.0 40.0 %collective-permute-start.20 = (bf16[384,512]{1,0:T(8,128)(2,1)S(1)}, bf16[384,512]{1,0:T(8,128)(2,1)S(1)}, u32[]{:S(2)}, u32[]{:S(2)}) collective-permute-start(bf16[384,512]{1,0:T(8,128)(2,1)S(1)} %get-tuple-element.144), channel_id=1, source_target_pairs={{0,24},{4,28},{8,16},{12,20},{16,8},{20,12},{24,0},{28,4},{1,25},{... | collective-permute-start | bytes 1179656 | tf_op jit(solution)/shard_map/ppermute | solution.py:249
  30.5 33.7 %collective-permute-start.8 = (bf16[384,512]{1,0:T(8,128)(2,1)S(1)}, bf16[384,512]{1,0:T(8,128)(2,1)S(1)}, u32[]{:S(2)}, u32[]{:S(2)}) collective-permute-start(bf16[384,512]{1,0:T(8,128)(2,1)S(1)} %get-tuple-element.121), channel_id=1, source_target_pairs={{0,28},{4,24},{8,20},{12,16},{16,12},{20,8},{24,4},{28,0},{1,29},{... | collective-permute-start | bytes 1179656 | tf_op jit(solution)/shard_map/ppermute | solution.py:249
  61.9 19.4 %collective-permute-start.14 = (bf16[384,512]{1,0:T(8,128)(2,1)}, bf16[384,512]{1,0:T(8,128)(2,1)S(1)}, u32[]{:S(2)}, u32[]{:S(2)}) collective-permute-start(bf16[384,512]{1,0:T(8,128)(2,1)} %get-tuple-element.133), channel_id=1, source_target_pairs={{0,20},{4,16},{8,28},{12,24},{16,4},{20,0},{24,12},{28,8},{1,21},{... | collective-permute-start | bytes 1179656 | tf_op jit(solution)/shard_map/ppermute | solution.py:249
  63.7 20.1 %collective-permute-start.21 = (bf16[384,512]{1,0:T(8,128)(2,1)}, bf16[384,512]{1,0:T(8,128)(2,1)S(1)}, u32[]{:S(2)}, u32[]{:S(2)}) collective-permute-start(bf16[384,512]{1,0:T(8,128)(2,1)} %get-tuple-element.145), channel_id=1, source_target_pairs={{0,4},{4,0},{8,12},{12,8},{16,20},{20,16},{24,28},{28,24},{1,5},{5... | collective-permute-start | bytes 1179656 | tf_op jit(solution)/shard_map/ppermute | solution.py:249
  65.0 28.6 %collective-permute-start.9 = (bf16[384,512]{1,0:T(8,128)(2,1)}, bf16[384,512]{1,0:T(8,128)(2,1)S(1)}, u32[]{:S(2)}, u32[]{:S(2)}) collective-permute-start(bf16[384,512]{1,0:T(8,128)(2,1)} %get-tuple-element.122), channel_id=1, source_target_pairs={{0,24},{4,28},{8,16},{12,20},{16,8},{20,12},{24,0},{28,4},{1,25},{... | collective-permute-start | bytes 1179656 | tf_op jit(solution)/shard_map/ppermute | solution.py:249
  72.3 30.9 %collective-permute-start.2 = (bf16[384,512]{1,0:T(8,128)(2,1)}, bf16[384,512]{1,0:T(8,128)(2,1)S(1)}, u32[]{:S(2)}, u32[]{:S(2)}) collective-permute-start(bf16[384,512]{1,0:T(8,128)(2,1)} %get-tuple-element.110), channel_id=1, source_target_pairs={{0,20},{4,16},{8,28},{12,24},{16,4},{20,0},{24,12},{28,8},{1,21},{... | collective-permute-start | bytes 1179656 | tf_op jit(solution)/shard_map/ppermute | solution.py:249
  82.0 17.4 %collective-permute-start.15 = (bf16[384,512]{1,0:T(8,128)(2,1)}, bf16[384,512]{1,0:T(8,128)(2,1)S(1)}, u32[]{:S(2)}, u32[]{:S(2)}) collective-permute-start(bf16[384,512]{1,0:T(8,128)(2,1)} %get-tuple-element.134), channel_id=1, source_target_pairs={{0,16},{4,20},{8,24},{12,28},{16,0},{20,4},{24,8},{28,12},{1,17},{... | collective-permute-start | bytes 1179656 | tf_op jit(solution)/shard_map/ppermute | solution.py:249
  97.8 38.3 %collective-permute-start.56 = (bf16[768,512]{1,0:T(8,128)(2,1)S(1)}, bf16[768,512]{1,0:T(8,128)(2,1)S(1)}, u32[]{:S(2)}, u32[]{:S(2)}) collective-permute-start(bf16[768,512]{1,0:T(8,128)(2,1)S(1)} %bitcast.25), channel_id=1, source_target_pairs={{0,1},{1,0},{2,3},{3,2},{4,5},{5,4},{6,7},{7,6},{8,9},{9,8},{10,11... | collective-permute-start | bytes 2359304 | tf_op jit(solution)/shard_map/ppermute | solution.py:249
  100.2 19.1 %collective-permute-start.16 = (bf16[384,512]{1,0:T(8,128)(2,1)S(1)}, bf16[384,512]{1,0:T(8,128)(2,1)S(1)}, u32[]{:S(2)}, u32[]{:S(2)}) collective-permute-start(bf16[384,512]{1,0:T(8,128)(2,1)S(1)} %copy-done.142), channel_id=1, source_target_pairs={{0,28},{4,24},{8,20},{12,16},{16,12},{20,8},{24,4},{28,0},{1,29},{... | collective-permute-start | bytes 1179656 | tf_op jit(solution)/shard_map/ppermute | solution.py:249
  106.0 16.6 %collective-permute-start.11 = (bf16[384,256]{1,0:T(8,128)(2,1)S(1)}, bf16[384,256]{1,0:T(8,128)(2,1)S(1)}, u32[]{:S(2)}, u32[]{:S(2)}) collective-permute-start(bf16[384,256]{1,0:T(8,128)(2,1)S(1)} %copy-done.111), channel_id=1, source_target_pairs={{0,12},{4,8},{8,4},{12,0},{16,28},{20,24},{24,20},{28,16},{1,13},{... | collective-permute-start | bytes 589832 | tf_op jit(solution)/shard_map/ppermute | solution.py:249
  118.0 16.2 %collective-permute-start.4 = (bf16[384,256]{1,0:T(8,128)(2,1)S(1)}, bf16[384,256]{1,0:T(8,128)(2,1)S(1)}, u32[]{:S(2)}, u32[]{:S(2)}) collective-permute-start(bf16[384,256]{1,0:T(8,128)(2,1)S(1)} %copy-done.107), channel_id=1, source_target_pairs={{0,28},{4,24},{8,20},{12,16},{16,12},{20,8},{24,4},{28,0},{1,29},{... | collective-permute-start | bytes 589832 | tf_op jit(solution)/shard_map/ppermute | solution.py:249
  123.2 18.2 %collective-permute-start.12 = (bf16[384,512]{1,0:T(8,128)(2,1)S(1)}, bf16[384,512]{1,0:T(8,128)(2,1)S(1)}, u32[]{:S(2)}, u32[]{:S(2)}) collective-permute-start(bf16[384,512]{1,0:T(8,128)(2,1)S(1)} %copy-done.99), channel_id=1, source_target_pairs={{0,8},{4,12},{8,0},{12,4},{16,24},{20,28},{24,16},{28,20},{1,9},{5... | collective-permute-start | bytes 1179656 | tf_op jit(solution)/shard_map/ppermute | solution.py:249
  133.4 20.4 %collective-permute-start.25 = (bf16[384,512]{1,0:T(8,128)(2,1)S(1)}, bf16[384,512]{1,0:T(8,128)(2,1)S(1)}, u32[]{:S(2)}, u32[]{:S(2)}) collective-permute-start(bf16[384,512]{1,0:T(8,128)(2,1)S(1)} %copy-done.141), channel_id=1, source_target_pairs={{0,16},{4,20},{8,24},{12,28},{16,0},{20,4},{24,8},{28,12},{1,17},{... | collective-permute-start | bytes 1179656 | tf_op jit(solution)/shard_map/ppermute | solution.py:249
  134.9 19.7 %collective-permute-start.5 = (bf16[384,512]{1,0:T(8,128)(2,1)S(1)}, bf16[384,512]{1,0:T(8,128)(2,1)S(1)}, u32[]{:S(2)}, u32[]{:S(2)}) collective-permute-start(bf16[384,512]{1,0:T(8,128)(2,1)S(1)} %copy-done.140), channel_id=1, source_target_pairs={{0,24},{4,28},{8,16},{12,20},{16,8},{20,12},{24,0},{28,4},{1,25},{... | collective-permute-start | bytes 1179656 | tf_op jit(solution)/shard_map/ppermute | solution.py:249
  136.1 49.7 %collective-permute-start.57 = (bf16[768,512]{1,0:T(8,128)(2,1)S(1)}, bf16[768,512]{1,0:T(8,128)(2,1)S(1)}, u32[]{:S(2)}, u32[]{:S(2)}) collective-permute-start(bf16[768,512]{1,0:T(8,128)(2,1)S(1)} %bitcast.24), channel_id=1, source_target_pairs={{0,2},{1,3},{2,0},{3,1},{4,6},{5,7},{6,4},{7,5},{8,10},{9,11},{10,... | collective-permute-start | bytes 2359304 | tf_op jit(solution)/shard_map/ppermute | solution.py:249
  139.7 17.0 %collective-permute-start.19 = (bf16[384,512]{1,0:T(8,128)(2,1)S(1)}, bf16[384,512]{1,0:T(8,128)(2,1)S(1)}, u32[]{:S(2)}, u32[]{:S(2)}) collective-permute-start(bf16[384,512]{1,0:T(8,128)(2,1)S(1)} %copy-done.139), channel_id=1, source_target_pairs={{0,12},{4,8},{8,4},{12,0},{16,28},{20,24},{24,20},{28,16},{1,13},{... | collective-permute-start | bytes 1179656 | tf_op jit(solution)/shard_map/ppermute | solution.py:249
  142.2 26.3 %collective-permute-start.26 = (bf16[384,512]{1,0:T(8,128)(2,1)S(1)}, bf16[384,512]{1,0:T(8,128)(2,1)S(1)}, u32[]{:S(2)}, u32[]{:S(2)}) collective-permute-start(bf16[384,512]{1,0:T(8,128)(2,1)S(1)} %copy-done.138), channel_id=1, source_target_pairs={{0,20},{4,16},{8,28},{12,24},{16,4},{20,0},{24,12},{28,8},{1,21},{... | collective-permute-start | bytes 1179656 | tf_op jit(solution)/shard_map/ppermute | solution.py:249
  155.4 17.5 %collective-permute-start.6 = (bf16[384,512]{1,0:T(8,128)(2,1)S(1)}, bf16[384,512]{1,0:T(8,128)(2,1)S(1)}, u32[]{:S(2)}, u32[]{:S(2)}) collective-permute-start(bf16[384,512]{1,0:T(8,128)(2,1)S(1)} %copy-done.97), channel_id=1, source_target_pairs={{0,4},{4,0},{8,12},{12,8},{16,20},{20,16},{24,28},{28,24},{1,5},{5... | collective-permute-start | bytes 1179656 | tf_op jit(solution)/shard_map/ppermute | solution.py:249
  157.4 17.1 %collective-permute-start.37 = (bf16[384,128]{1,0:T(8,128)(2,1)S(1)}, bf16[384,128]{1,0:T(8,128)(2,1)S(1)}, u32[]{:S(2)}, u32[]{:S(2)}) collective-permute-start(bf16[384,128]{1,0:T(8,128)(2,1)S(1)} %copy-done.135), channel_id=1, source_target_pairs={{0,8},{4,12},{8,0},{12,4},{16,24},{20,28},{24,16},{28,20},{1,9},{5... | collective-permute-start | bytes 294920 | tf_op jit(solution)/shard_map/ppermute | solution.py:249
  185.9 59.1 %collective-permute-start.58 = (bf16[768,512]{1,0:T(8,128)(2,1)}, bf16[768,512]{1,0:T(8,128)(2,1)S(1)}, u32[]{:S(2)}, u32[]{:S(2)}) collective-permute-start(bf16[768,512]{1,0:T(8,128)(2,1)} %bitcast.12), channel_id=1, source_target_pairs={{0,3},{1,2},{2,1},{3,0},{4,7},{5,6},{6,5},{7,4},{8,11},{9,10},{10,... | collective-permute-start | bytes 2359304 | tf_op jit(solution)/shard_map/ppermute | solution.py:249
  189.4 22.1 %collective-permute-start.36 = (bf16[384,128]{1,0:T(8,128)(2,1)}, bf16[384,128]{1,0:T(8,128)(2,1)}, u32[]{:S(2)}, u32[]{:S(2)}) collective-permute-start(bf16[384,128]{1,0:T(8,128)(2,1)} %get-tuple-element.175), channel_id=1, source_target_pairs={{0,12},{4,8},{8,4},{12,0},{16,28},{20,24},{24,20},{28,16},{1,13},{... | collective-permute-start | bytes 294920 | tf_op jit(solution)/shard_map/ppermute | solution.py:249
  191.7 19.7 %collective-permute-start.40 = (bf16[384,128]{1,0:T(8,128)(2,1)}, bf16[384,128]{1,0:T(8,128)(2,1)}, u32[]{:S(2)}, u32[]{:S(2)}) collective-permute-start(bf16[384,128]{1,0:T(8,128)(2,1)} %get-tuple-element.183), channel_id=1, source_target_pairs={{0,20},{4,16},{8,28},{12,24},{16,4},{20,0},{24,12},{28,8},{1,21},{... | collective-permute-start | bytes 294920 | tf_op jit(solution)/shard_map/ppermute | solution.py:249
  192.8 18.7 %collective-permute-start.41 = (bf16[384,128]{1,0:T(8,128)(2,1)}, bf16[384,128]{1,0:T(8,128)(2,1)}, u32[]{:S(2)}, u32[]{:S(2)}) collective-permute-start(bf16[384,128]{1,0:T(8,128)(2,1)} %get-tuple-element.185), channel_id=1, source_target_pairs={{0,28},{4,24},{8,20},{12,16},{16,12},{20,8},{24,4},{28,0},{1,29},{... | collective-permute-start | bytes 294920 | tf_op jit(solution)/shard_map/ppermute | solution.py:249
  194.8 16.8 %collective-permute-start.31 = (bf16[384,128]{1,0:T(8,128)(2,1)}, bf16[384,128]{1,0:T(8,128)(2,1)}, u32[]{:S(2)}, u32[]{:S(2)}) collective-permute-start(bf16[384,128]{1,0:T(8,128)(2,1)} %get-tuple-element.165), channel_id=1, source_target_pairs={{0,4},{4,0},{8,12},{12,8},{16,20},{20,16},{24,28},{28,24},{1,5},{5... | collective-permute-start | bytes 294920 | tf_op jit(solution)/shard_map/ppermute | solution.py:249
  215.2 69.4 %collective-permute-start.42 = (bf16[512,768]{1,0:T(8,128)(2,1)}, bf16[512,768]{1,0:T(8,128)(2,1)}, u32[]{:S(2)}, u32[]{:S(2)}) collective-permute-start(bf16[512,768]{1,0:T(8,128)(2,1)} %bitcast), channel_id=1, source_target_pairs={{0,4},{4,8},{8,12},{12,16},{16,20},{20,24},{24,28},{28,0},{1,5},{5... | collective-permute-start | bytes 2359304 | tf_op jit(solution)/shard_map/ppermute | solution.py:254
  246.5 17.1 %collective-permute-start.52 = (bf16[512,128]{1,0:T(8,128)(2,1)}, bf16[512,128]{1,0:T(8,128)(2,1)S(1)}, u32[]{:S(2)}, u32[]{:S(2)}) collective-permute-start(bf16[512,128]{1,0:T(8,128)(2,1)} %collective-permute-done.46.rest_2_), channel_id=1, source_target_pairs={{0,2},{1,3},{2,0},{3,1},{4,6},{5,7},{6,4},{7,5},{8,10},{9,11},{10,... | collective-permute-start | bytes 393224 | tf_op jit(solution)/shard_map/ppermute | solution.py:249
  253.0 24.0 %collective-permute-start.47 = (bf16[512,256]{1,0:T(8,128)(2,1)S(1)}, bf16[512,256]{1,0:T(8,128)(2,1)}, u32[]{:S(2)}, u32[]{:S(2)}) collective-permute-start(bf16[512,256]{1,0:T(8,128)(2,1)S(1)} %collective-permute-done.44.rest_0_), channel_id=1, source_target_pairs={{0,1},{1,0},{2,3},{3,2},{4,5},{5,4},{6,7},{7,6},{8,9},{9,8},{10,11... | collective-permute-start | bytes 786440 | tf_op jit(solution)/shard_map/ppermute | solution.py:249
  259.3 25.2 %collective-permute-start.50 = (bf16[512,256]{1,0:T(8,128)(2,1)S(1)}, bf16[512,256]{1,0:T(8,128)(2,1)}, u32[]{:S(2)}, u32[]{:S(2)}) collective-permute-start(bf16[512,256]{1,0:T(8,128)(2,1)S(1)} %collective-permute-done.44.rest_0_), channel_id=1, source_target_pairs={{0,2},{1,3},{2,0},{3,1},{4,6},{5,7},{6,4},{7,5},{8,10},{9,11},{10,... | collective-permute-start | bytes 786440 | tf_op jit(solution)/shard_map/ppermute | solution.py:249
  264.3 20.3 %collective-permute-start.53 = (bf16[512,256]{1,0:T(8,128)(2,1)S(1)}, bf16[512,256]{1,0:T(8,128)(2,1)}, u32[]{:S(2)}, u32[]{:S(2)}) collective-permute-start(bf16[512,256]{1,0:T(8,128)(2,1)S(1)} %collective-permute-done.44.rest_0_), channel_id=1, source_target_pairs={{0,3},{1,2},{2,1},{3,0},{4,7},{5,6},{6,5},{7,4},{8,11},{9,10},{10,... | collective-permute-start | bytes 786440 | tf_op jit(solution)/shard_map/ppermute | solution.py:249
  (171 other events, 2045.9 us)
Sparse Core Ops, SparseCore 0:
  8.9 66.1 all-gather.2

commit v3 on v2

--- a/solution.py
+++ b/solution.py
@@ -10,13 +10,19 @@
 from jax.sharding import PartitionSpec as P
 
 HD = 128
-VMEM_LIMIT = 48 * 1024 * 1024
 F32 = jnp.float32
 BF16 = jnp.bfloat16
 WHOLE = pl.BlockSpec(memory_space=pltpu.VMEM)
 ANYWHERE = pl.BlockSpec(memory_space=pl.ANY)
 SCALAR = pl.BlockSpec(memory_space=pltpu.SMEM)
-PARAMS = pltpu.CompilerParams(vmem_limit_bytes=VMEM_LIMIT)
+
+
+def params(mebibytes):
+    return pltpu.CompilerParams(vmem_limit_bytes=mebibytes * 1024 * 1024)
+
+
+def in_hbm(array):
+    return pltpu.with_memory_space_constraint(array, pltpu.HBM)
 
 
 def cost(flops, size, exps=0):
@@ -73,13 +79,13 @@
                 pl.BlockSpec(pick.shape, lambda i, order: (0, 0)),
                 pl.BlockSpec((1,) + rows.shape[1:], lambda i, order: (order[i], 0, 0)),
             ],
-            out_specs=[pl.BlockSpec(shape, lambda i, order: (0, 0)) for shape in shapes] * blocks,
+            out_specs=[WHOLE] * (len(shapes) * blocks),
         ),
         out_shape=[jax.ShapeDtypeStruct(shape, BF16) for shape in shapes] * blocks,
-        compiler_params=PARAMS,
+        compiler_params=params(10),
         cost_estimate=cost(0, 3 * blocks * rows.shape[1] * HD),
         name="split_blocks",
-    )(order, jnp.asarray(pick), rows)
+    )(order, jnp.asarray(pick), in_hbm(rows))
     return [list(flat[i :: len(shapes)]) for i in range(len(shapes))]
 
 
@@ -104,66 +110,71 @@
         ],
         out_specs=pl.BlockSpec((rows, width), lambda i: (i, 0)),
         out_shape=jax.ShapeDtypeStruct((patch, width), BF16),
-        compiler_params=PARAMS,
+        compiler_params=params(14),
         cost_estimate=cost(10 * patch * width, 4 * patch * width),
         name="norm",
-    )(tokens, modulation)
-
-
-def gathered(pieces, sources_ref, matrix, sems):
-    depth = pieces[0].shape[0]
-    copies = []
+    )(in_hbm(tokens), modulation)
+
+
+def fetched(pairs, pieces, first, sources_ref, matrix, sems):
+    depth, columns = pieces[0].shape[0], pl.ds(first, matrix.shape[1])
     for index, piece in enumerate(pieces):
         start = pl.multiple_of(sources_ref[index] * depth, 16)
-        copies.append(
-            pltpu.make_async_copy(piece, matrix.at[pl.ds(start, depth), :], sems.at[index])
-        )
-        copies[-1].start()
+        pairs = pairs + [(piece.at[:, columns], matrix.at[pl.ds(start, depth), :])]
+    copies = [
+        pltpu.make_async_copy(source, target, sems.at[index])
+        for index, (source, target) in enumerate(pairs)
+    ]
+    for copy in copies:
+        copy.start()
     for copy in copies:
         copy.wait()
 
 
-def score_kernel(count, sources_ref, where_ref, normed_ref, stale_ref, *rest):
-    pieces, (expo_ref, base_ref, share_ref, both, matrix, sems) = rest[:count], rest[count:]
+def score_kernel(count, cols, sources_ref, where_ref, normed, stale_hbm, *rest):
+    pieces, (expo_ref, base_ref, share_ref, both, matrix, stale, sems) = (
+        rest[:count], rest[count:]
+    )
     heads, patch, _ = expo_ref.shape
-    parts = stale_ref.shape[1] // patch
-    gathered(pieces, sources_ref, matrix, sems)
-    both[...] = jnp.dot(normed_ref[...], matrix[...], preferred_element_type=F32).astype(BF16)
+    parts = stale.shape[1] // patch
+    fetched([(stale_hbm.at[:, :, cols], stale)], pieces, 0, sources_ref, matrix, sems)
+    both[...] = jnp.dot(normed[...], matrix[...], preferred_element_type=F32).astype(BF16)
     starts = [
         pl.multiple_of(lax.rem(where_ref[0] + 1 + part, parts) * patch, patch)
         for part in range(parts - 1)
     ]
+    scale = F32(np.log2(np.e) / np.sqrt(HD))
     for head in range(heads):
-        cols = slice(head * HD, (head + 1) * HD)
-        query = both[:, cols]
-        keys = [stale_ref[0, pl.ds(start, patch), cols] for start in starts]
+        own = slice(head * HD, (head + 1) * HD)
+        query = both[:, own]
+        keys = [stale[0, pl.ds(start, patch), own] for start in starts]
         keys.append(both[:, (heads + head) * HD : (heads + head + 1) * HD])
-        scores = [turned(query, key) / jnp.sqrt(F32(HD)) for key in keys]
+        scores = [turned(query, key) for key in keys]
         top = functools.reduce(jnp.maximum, scores)
         top = jnp.max(top, axis=1, keepdims=True)
         total, summed = 0.0, 0.0
         for part, score in enumerate(scores):
-            expo = jnp.exp(score - top)
-            total += jnp.sum(expo, axis=1, keepdims=True)
+            expo = jnp.exp2((score - top) * scale)
+            total += expo
             expo = expo.astype(BF16)
             if part == parts - 1:
                 expo_ref[head] = expo
                 continue
-            values = stale_ref[1, pl.ds(starts[part], patch), cols]
+            values = stale[1, pl.ds(starts[part], patch), own]
             summed += jnp.dot(expo, values, preferred_element_type=F32)
-        share = 1.0 / total
+        share = 1.0 / jnp.sum(total, axis=1, keepdims=True)
         base_ref[head] = summed * share
         share_ref[head] = jnp.broadcast_to(share, (patch, HD))
 
 
-def attend_kernel(count, sources_ref, normed_ref, expo_ref, base_ref, share_ref, *rest):
+def attend_kernel(count, first, sources_ref, normed, expo_ref, base_ref, share_ref, *rest):
     pieces, (out_ref, values, matrix, sems) = rest[:count], rest[count:]
-    gathered(pieces, sources_ref, matrix, sems)
-    values[...] = jnp.dot(normed_ref[...], matrix[...], preferred_element_type=F32).astype(BF16)
+    fetched([], pieces, first, sources_ref, matrix, sems)
+    values[...] = jnp.dot(normed[...], matrix[...], preferred_element_type=F32).astype(BF16)
     for spot in range(expo_ref.shape[0]):
-        cols = slice(spot * HD, (spot + 1) * HD)
-        new = jnp.dot(expo_ref[spot], values[:, cols], preferred_element_type=F32)
-        out_ref[:, cols] = (base_ref[spot] + new * share_ref[spot]).astype(BF16)
+        own = slice(spot * HD, (spot + 1) * HD)
+        new = jnp.dot(expo_ref[spot], values[:, own], preferred_element_type=F32)
+        out_ref[:, own] = (base_ref[spot] + new * share_ref[spot]).astype(BF16)
 
 
 def score(normed, pieces, sources, where, stale, group):
@@ -171,37 +182,32 @@
     heads, keys = len(group), stale.shape[1]
     columns = heads * HD
     stat = jax.ShapeDtypeStruct((heads, patch, HD), F32)
-    at = lambda i: (0, 0, group[0] // heads)
+    cols = slice(group[0] * HD, group[0] * HD + columns)
     return pl.pallas_call(
-        functools.partial(score_kernel, len(pieces)),
-        grid=(1,),
-        in_specs=[SCALAR, SCALAR, WHOLE, pl.BlockSpec((2, keys, columns), at)]
-        + [ANYWHERE] * len(pieces),
+        functools.partial(score_kernel, len(pieces), cols),
+        in_specs=[SCALAR, SCALAR, WHOLE] + [ANYWHERE] * (1 + len(pieces)),
         out_specs=[WHOLE] * 3,
         out_shape=[jax.ShapeDtypeStruct((heads, patch, patch), BF16), stat, stat],
         scratch_shapes=[
             pltpu.VMEM((patch, 2 * columns), BF16),
             pltpu.VMEM((width, 2 * columns), BF16),
-            pltpu.SemaphoreType.DMA((len(pieces),)),
+            pltpu.VMEM((2, keys, columns), BF16),
+            pltpu.SemaphoreType.DMA((len(pieces) + 1,)),
         ],
-        compiler_params=PARAMS,
+        compiler_params=params(20),
         cost_estimate=cost(
             4 * patch * columns * (width + keys), 4 * columns * (width + keys), patch * heads * keys
         ),
         name="score",
-    )(sources, where, normed, stale, *pieces)
+    )(sources, where, normed, in_hbm(stale), *pieces)
 
 
 def attend(normed, pieces, sources, first, expo, base, share):
     patch, width = normed.shape
-    columns = pieces[0].shape[1]
-    count = columns // HD
-    picked = lambda last: pl.BlockSpec((count, patch, last), lambda i: (first // count, 0, 0))
+    columns = expo.shape[0] * HD
     return pl.pallas_call(
-        functools.partial(attend_kernel, len(pieces)),
-        grid=(1,),
-        in_specs=[SCALAR, WHOLE, picked(patch), picked(HD), picked(HD)]
-        + [ANYWHERE] * len(pieces),
+        functools.partial(attend_kernel, len(pieces), first),
+        in_specs=[SCALAR, WHOLE, WHOLE, WHOLE, WHOLE] + [ANYWHERE] * len(pieces),
         out_specs=WHOLE,
         out_shape=jax.ShapeDtypeStruct((patch, columns), BF16),
         scratch_shapes=[
@@ -209,7 +215,7 @@
             pltpu.VMEM((width, columns), BF16),
             pltpu.SemaphoreType.DMA((len(pieces),)),
         ],
-        compiler_params=PARAMS,
+        compiler_params=params(10),
         cost_estimate=cost(2 * patch * columns * (width + patch), 2 * columns * width),
         name="attend",
     )(sources, normed, expo, base, share, *pieces)
@@ -229,16 +235,17 @@
     tp, chunks = len(attended), len(attended[0])
     patch, share = inflow.shape
     inner = matrices[0].shape[1]
-    flat = [piece for own in attended for piece in own]
+    arrays = [inflow, gate] + [piece for own in attended for piece in own] + matrices
     return pl.pallas_call(
         functools.partial(output_kernel, tp, chunks),
-        in_specs=[WHOLE] * (2 + len(flat) + tp),
-        out_specs=WHOLE,
+        grid=(1,),
+        in_specs=[pl.BlockSpec(array.shape, lambda i: (0, 0)) for array in arrays],
+        out_specs=pl.BlockSpec(inflow.shape, lambda i: (0, 0)),
         out_shape=jax.ShapeDtypeStruct(inflow.shape, BF16),
-        compiler_params=PARAMS,
+        compiler_params=params(20),
         cost_estimate=cost(2 * patch * share * inner * tp, 2 * inner * tp * (share + patch)),
         name="output",
-    )(inflow, gate, *flat, *matrices)
+    )(*arrays)
 
 
 def after(block, earlier):
@@ -254,20 +261,21 @@
     return lax.ppermute(block, "section", [(i, (i + 1) % sections) for i in range(sections)])
 
 
-def relay(stages, window):
-    sections = len(stages[0])
-    distances = sorted(range(1, sections), key=lambda d: (d == 1, d % 2, d))
-    sent, arrived = [], []
-    for pieces in stages:
-        received = {0: pieces[0]}
-        for distance in distances:
-            piece = pieces[distance]
-            if len(sent) >= window:
-                piece = after(piece, sent[-window])
-            received[distance] = swapped(piece, "section", distance)
-            sent.append(received[distance])
-        arrived.append([received[d] for d in range(sections)])
-    return arrived
+class Relay:
+    def __init__(self, window):
+        self.window, self.sent = window, []
+
+    def swap(self, piece, distance, *earlier):
+        size = piece.size
+        for other in reversed(self.sent):
+            size += other.size
+            if size > self.window:
+                earlier += (other,)
+                break
+        for other in earlier:
+            piece = after(piece, other)
+        self.sent.append(swapped(piece, "section", distance))
+        return self.sent[-1]
 
 
 def place_kernel(count, slots_ref, *rest):
@@ -289,7 +297,7 @@
         out_specs=ANYWHERE,
         out_shape=jax.ShapeDtypeStruct((len(pieces),) + pieces[0].shape, BF16),
         scratch_shapes=[pltpu.SemaphoreType.DMA((len(pieces),))],
-        compiler_params=PARAMS,
+        compiler_params=params(4),
         cost_estimate=cost(0, 4 * len(pieces) * pieces[0].size),
         name="placed",
     )(slots, *pieces)
@@ -312,35 +320,66 @@
     rows = rows.transpose(0, 1, 3, 2, 4).reshape(blocks, depth * lanes * kinds, HD)
     tokens = lax.all_gather(inflow[0], "tp", axis=1, tiled=True)
 
-    size = 2 if lanes % 2 == 0 else 1
+    order = sorted(range(1, sections), key=lambda d: (d == 1, d % 2, d))
+    own_blocks = block_of(sources)
+    before = block_of((sources + sections - 1) % sections)
+
+    ahead = [order[:3], order[3:] + [0]]
+    to_out = {}
+    for some in ahead:
+        blocks_now = jnp.stack([before[d] for d in some])
+        (made,) = split_blocks(rows, blocks_now, [[(3, head) for head in range(lanes)]], lanes)
+        to_out.update(zip(some, made))
+    size = max(1, lanes // 2)
     groups = [tuple(range(first, first + size)) for first in range(0, lanes, size)]
-    plan, chunks = [], []
+    plan = []
     for group in groups:
         plan.append([(kind, head) for kind in (0, 1) for head in group])
-        parts = [group] if group != groups[-1] else [(head,) for head in group]
-        plan += [[(2, head) for head in part] for part in parts]
-        chunks.append(parts)
-    to_out = split_blocks(
-        rows, block_of((sources + sections - 1) % sections), [[(3, head) for head in range(lanes)]], lanes
-    )
-    arrived = iter(relay(to_out + split_blocks(rows, block_of(sources), plan, lanes), 4))
-
+        values = [(2, head) for head in group]
+        if group == groups[-1]:
+            plan.append(values)
+        else:
+            plan[-1] += values
+    split = split_blocks(rows, own_blocks, plan, lanes)
+
+    relay = Relay(4 * depth * inner)
+    for distance in order:
+        to_out[distance] = relay.swap(to_out[distance], distance)
     per = sections // tp
     slots = ((sources // per) ^ rank) * per + sources % per
-    held = placed(next(arrived), slots).reshape(tp, per * depth, inner)
+    held = placed([to_out[d] for d in range(sections)], slots).reshape(tp, per * depth, inner)
     matrices = [held[0]]
     for distance in range(1, tp):
         matrices.append(swapped(after(held[distance], matrices[-1]), "tp", distance))
-
     normed = norm(tokens, modulation[0])
+
+    def relayed(stage, *earlier, at=0):
+        pieces = [split[stage][0]] * sections
+        for index, distance in enumerate(order):
+            wait = earlier if index == at else ()
+            pieces[distance] = relay.swap(split[stage][distance], distance, *wait)
+        return pieces
+
     attended = [[] for _ in range(tp)]
-    for group, parts in zip(groups, chunks):
-        stats = score(normed, next(arrived), sources, patch_index, stale_cache[0], group)
-        for part in parts:
-            own = attend(normed, next(arrived), sources, part[0] - group[0], *stats)
-            moved = handed_on(own)
-            for distance in range(tp):
-                attended[distance].append(swapped(moved, "tp", distance) if distance else moved)
+
+    def share_out(part):
+        moved = handed_on(part)
+        for distance in range(tp):
+            attended[distance].append(swapped(moved, "tp", distance) if distance else moved)
+        return moved
+
+    done = (normed,)
+    for stage, group in enumerate(groups[:-1]):
+        pieces = relayed(stage, *done, at=sections - 2)
+        stats = score(normed, pieces, sources, patch_index, stale_cache[0], group)
+        own = attend(normed, pieces, sources, 2 * len(group) * HD, *stats)
+        done = (own,)
+        share_out(own)
+    pieces = relayed(len(plan) - 2, *done, at=min(4, sections - 2))
+    value_pieces = relayed(len(plan) - 1)
+    stats = score(normed, pieces, sources, patch_index, stale_cache[0], groups[-1])
+    own = attend(normed, value_pieces, sources, 0, *stats)
+    share_out(own)
     carried = handed_on(after(inflow[0], own))
     gate = handed_on(modulation[0, 2])
     gate = lax.dynamic_slice_in_dim(gate, rank * share, share, 0)[None]

time: 304 us -> 273 us (0.90)
  local copies, waits for them, and re-layouts: 61 us -> 30.3 us
  waiting for transfers between devices: 98.3 us -> 118 us
  starting transfers between devices: 59.4 us -> 45.5 us
  Pallas kernels: 65.5 us -> 58.6 us
    unnamed x287 -> x107, local copies, waits for them, and re-layouts: 57.1 us -> 24.1 us
    ppermute x54 -> x37, waiting for transfers between devices: 91.7 us -> 109 us  [swapped(): lax.ppermute(block, axis, [(i, i ^ distance) for i in range(lax.axis_size...]
    ppermute x54 -> x37, starting transfers between devices: 56.5 us -> 42.7 us  [swapped(): lax.ppermute(block, axis, [(i, i ^ distance) for i in range(lax.axis_size...]
    pallas_call x6 -> x5, Pallas kernels: 36.7 us -> 28.5 us  [the longest x2 15.5 us: score(): pl.pallas_call(functools.partial(score_kernel, len(pieces), cols), in_spe...]
    another operation x0 -> x1, local copies, waits for them, and re-layouts: none -> 3.2 us  [local(): blocks_now = jnp.stack([before[d] for d in some])]
    ppermute x5 -> x4, waiting for transfers between devices: 5.88 us -> 8.13 us  [handed_on(): lax.ppermute(block, 'section', [(i, (i + 1) % sections) for i in range(se...]
    pallas_call x2 -> x3, Pallas kernels: 22.2 us -> 23.8 us  [split_blocks(): pl.pallas_call(functools.partial(split_kernel, lanes, plan, kinds, depth_...]
  transfers between devices with their start and end apart: 60 -> 42, of which waited for: 19 -> 14; matrix products, arithmetic and copies ran while one was open for 2% -> 4% of each run, Pallas kernels for 20% -> 20%
where the time goes in v3:
time: 273 us; the launch traced here: 270 us
  waiting for transfers between devices  118 us (43%)
  Pallas kernels  58.6 us (21%)
  starting transfers between devices  45.5 us (17%)
  local copies, waits for them, and re-layouts  30.3 us (11%)
  between operations  14.4 us (5%)
  other arithmetic  2.97 us (1%)
    ppermute x37, waiting for transfers between devices, swapped(): lax.ppermute(block, axis, [(i, i ^ distance) for i in range(lax.axis_size...  109 us
    ppermute x37, starting transfers between devices, swapped(): lax.ppermute(block, axis, [(i, i ^ distance) for i in range(lax.axis_size...  42.7 us
    unnamed x107, local copies, waits for them, and re-layouts  24.1 us
    pallas_call x3, Pallas kernels, split_blocks(): pl.pallas_call(functools.partial(split_kernel, lanes, plan, kinds, depth_...  23.8 us
    pallas_call x2, Pallas kernels, score(): pl.pallas_call(functools.partial(score_kernel, len(pieces), cols), in_spe...  15.5 us
    pallas_call x2, Pallas kernels, attend(): pl.pallas_call(functools.partial(attend_kernel, len(pieces), first), in_s...  8.73 us
    ppermute x4, waiting for transfers between devices, handed_on(): lax.ppermute(block, 'section', [(i, (i + 1) % sections) for i in range(se...  8.13 us
  transfers between devices with their start and end apart: 42, of which 14 were waited for; matrix products, arithmetic and copies ran while one was open for 4% of the time, Pallas kernels for 20%

profile of v3, /device:TPU:0, one launch (start us, length us, event | category | flops | bytes accessed | tf_op | source)
XLA Modules:
  0.0 269.7 jit_solution(15383882147406042622)
XLA Ops:
  8.9 2.1 pad_add_fusion.order_ref
  11.7 4.9 %split_blocks.5 = (bf16[384,512]{1,0:T(8,128)(2,1)S(1)}, bf16[384,512]{1,0:T(8,128)(2,1)S(1)}, bf16[384,512]{1,0:T(8,128)(2,1)}) custom-call(s32[3]{0:T(128)S(1)} %pad_add_fusion.order_ref, bf16[64,256]{1,0:T(8,128)(2,1)S(1)} %copy-done.17, bf16[8,6144,128]{2,1,0:T(8,128)(2,1)} %bitcast.19), custom_call_target="tpu_custom_call" | custom-call | bytes 7077888 | tf_op jit(solution)/shard_map/split_blocks/pallas_call | solution.py:73
  16.6 2.9 %collective-permute-start = (bf16[384,512]{1,0:T(8,128)(2,1)S(1)}, bf16[384,512]{1,0:T(8,128)(2,1)S(1)}, u32[]{:S(2)}, u32[]{:S(2)}) collective-permute-start(bf16[384,512]{1,0:T(8,128)(2,1)S(1)} %get-tuple-element.82), channel_id=1, source_target_pairs={{0,8},{4,12},{8,0},{12,4},{16,24},{20,28},{24,16},{28,20},{1,9},{5... | collective-permute-start | bytes 1179656 | tf_op jit(solution)/shard_map/ppermute | solution.py:256
  21.1 3.2 %stack.6.order_ref = s32[5]{0:T(128)S(1)} concatenate(s32[1]{0:T(128)} %get-tuple-element.154, s32[1]{0:T(128)} %get-tuple-element.153, s32[1]{0:T(128)} %get-tuple-element.152, s32[1]{0:T(128)} %get-tuple-element.151, s32[1]{0:T(128)} %get-tuple-element.150), dimensions={0} | concatenate | bytes 40 | tf_op jit(solution)/shard_map/stack | solution.py:330
  24.3 6.9 %split_blocks.4 = (bf16[384,512]{1,0:T(8,128)(2,1)}, bf16[384,512]{1,0:T(8,128)(2,1)S(1)}, bf16[384,512]{1,0:T(8,128)(2,1)S(1)}, bf16[384,512]{1,0:T(8,128)(2,1)}, bf16[384,512]{1,0:T(8,128)(2,1)S(1)}) custom-call(s32[5]{0:T(128)S(1)} %stack.6.order_ref, bf16[64,256]{1,0:T(8,128)(2,1)S(1)} %copy-done.18, bf16[8,6144,128]{2,1,0:T(8,128)(2,1)} %bitcast.20), custom_call_target="tpu_custom_call" | custom-call | bytes 11796480 | tf_op jit(solution)/shard_map/split_blocks/pallas_call | solution.py:73
  33.7 12.0 %split_blocks.3 = (bf16[384,768]{1,0:T(8,128)(2,1)S(1)}, bf16[384,512]{1,0:T(8,128)(2,1)S(1)}, bf16[384,256]{1,0:T(8,128)(2,1)S(1)}, bf16[384,768]{1,0:T(8,128)(...) custom-call(s32[8]{0:T(128)S(1)} %get-tuple-element.142.order_ref, ...), custom_call_target="tpu_custom_call" | custom-call | bytes 18874368 | tf_op jit(solution)/shard_map/split_blocks/pallas_call | solution.py:73
  62.2 12.0 %collective-permute-done.2.rest_2_ = bf16[384,768]{1,0:T(8,128)(2,1)S(1)} collective-permute-done((bf16[384,768]{1,0:T(8,128)(2,1)S(1)}, bf16[384,768]{1,0:T(8,128)(2,1)S(1)}, u32[]{:S(2)}, u32[]{:S(2)}) %collective-permute-start.2) | collective-permute-done | bytes 589856 | tf_op jit(solution)/shard_map/ppermute | solution.py:256
  75.6 6.5 %collective-permute-done.35.rest_6_ = bf16[384,512]{1,0:T(8,128)(2,1)S(1)} collective-permute-done((bf16[384,512]{1,0:T(8,128)(2,1)}, bf16[384,512]{1,0:T(8,128)(2,1)S(1)}, u32[]{:S(2)}, u32[]{:S(2)}) %collective-permute-start.35) | collective-permute-done | bytes 393248 | tf_op jit(solution)/shard_map/ppermute | solution.py:256
  82.8 12.6 %collective-permute-done.12.rest_4_ = bf16[384,768]{1,0:T(8,128)(2,1)S(1)} collective-permute-done((bf16[384,768]{1,0:T(8,128)(2,1)S(1)}, bf16[384,768]{1,0:T(8,128)(2,1)S(1)}, u32[]{:S(2)}, u32[]{:S(2)}) %collective-permute-start.12) | collective-permute-done | bytes 589856 | tf_op jit(solution)/shard_map/ppermute | solution.py:256
  95.5 7.4 %collective-permute-done.37.rest_3_ = bf16[384,512]{1,0:T(8,128)(2,1)} collective-permute-done((bf16[384,512]{1,0:T(8,128)(2,1)}, bf16[384,512]{1,0:T(8,128)(2,1)}, u32[]{:S(2)}, u32[]{:S(2)}) %collective-permute-start.37) | collective-permute-done | bytes 393248 | tf_op jit(solution)/shard_map/ppermute | solution.py:256
  106.9 2.0 placed.1
  111.0 2.2 collective-permute-start.38
  113.7 2.8 %collective-permute-start.14 = (bf16[384,768]{1,0:T(8,128)(2,1)}, bf16[384,768]{1,0:T(8,128)(2,1)}, u32[]{:S(2)}, u32[]{:S(2)}) collective-permute-start(bf16[384,768]{1,0:T(8,128)(2,1)} %get-tuple-element.103), channel_id=1, source_target_pairs={{0,28},{4,24},{8,20},{12,16},{16,12},{20,8},{24,4},{28,0},{1,29},{... | collective-permute-start | bytes 1769480 | tf_op jit(solution)/shard_map/ppermute | solution.py:256
  118.0 4.3 %norm.1.normed = bf16[512,3072]{1,0:T(8,128)(2,1)S(1)} custom-call(bf16[512,3072]{1,0:T(8,128)(2,1)} %bitcast.24, f32[3,3072]{1,0:T(4,128)S(1)} %bitcast.18), custom_call_target="tpu_custom_call" | custom-call | flops 15728640 | bytes 6291456 | tf_op jit(solution)/shard_map/norm/pallas_call | solution.py:104
  122.3 13.9 %collective-permute-done.4.rest_5_ = bf16[384,768]{1,0:T(8,128)(2,1)} collective-permute-done((bf16[384,768]{1,0:T(8,128)(2,1)}, bf16[384,768]{1,0:T(8,128)(2,1)}, u32[]{:S(2)}, u32[]{:S(2)}) %collective-permute-start.4) | collective-permute-done | bytes 589856 | tf_op jit(solution)/shard_map/ppermute | solution.py:256
  138.6 2.4 collective-permute-start.39
  144.1 4.3 %collective-permute-done.15.rest_4_ = bf16[384,512]{1,0:T(8,128)(2,1)S(1)} collective-permute-done((bf16[384,512]{1,0:T(8,128)(2,1)S(1)}, bf16[384,512]{1,0:T(8,128)(2,1)S(1)}, u32[]{:S(2)}, u32[]{:S(2)}) %collective-permute-start.15) | collective-permute-done | bytes 393248 | tf_op jit(solution)/shard_map/ppermute | solution.py:256
  149.3 1.9 collective-permute-start.9
  151.2 7.9 %score.2 = (bf16[2,512,512]{2,1,0:T(8,128)(2,1)S(1)}, f32[2,512,128]{2,1,0:T(8,128)S(1)}, f32[2,512,128]{2,1,0:T(8,128)S(1)}) custom-call(s32[8]{0:T(128)S(1)} %iota_xor_fusion.sources_ref, s32[1]{0:T(128)S(6)} %copy.15.where_ref, bf16[512,3072]{1,0:T(8,128)(2,1)S(1)} %norm.1.normed, bf16[2,2048,512]{2,1,0:T(8,128)(2,1)} %bitcast.22, ...), custom_call_target="tpu_custom_call" | custom-call | flops 2684354560 | bytes 5242880 | tf_op jit(solution)/shard_map/score/pallas_call | solution.py:186
  159.1 3.9 %attend.2 = bf16[512,256]{1,0:T(8,128)(2,1)S(1)} custom-call(s32[8]{0:T(128)S(1)} %iota_xor_fusion.sources_ref, bf16[512,3072]{1,0:T(8,128)(2,1)S(1)} %norm.1.normed, bf16[2,512,512]{2,1,0:T(8,128)(2,1)S(1)} %get-tuple-element.107.expo_ref, f32[2,512,128]{2,1,0:T(8,128)S(1)} %get-tuple-element.108.base_ref, f32[2,512,128]{2,1,0:T(8,128)S(1)} %get-tuple-element.109.share_ref, ...), custom_call_target="tpu_custom_call" | custom-call | flops 939524096 | bytes 1572864 | tf_op jit(solution)/shard_map/attend/pallas_call | solution.py:208
  163.8 5.2 %collective-permute-done.17.rest_7_ = bf16[384,512]{1,0:T(8,128)(2,1)S(1)} collective-permute-done((bf16[384,512]{1,0:T(8,128)(2,1)S(1)}, bf16[384,512]{1,0:T(8,128)(2,1)S(1)}, u32[]{:S(2)}, u32[]{:S(2)}) %collective-permute-start.17) | collective-permute-done | bytes 393248 | tf_op jit(solution)/shard_map/ppermute | solution.py:256
  168.9 2.2 collective-permute-start.22
  171.1 4.8 %collective-permute-done.9.rest_3_ = bf16[384,512]{1,0:T(8,128)(2,1)S(1)} collective-permute-done((bf16[384,512]{1,0:T(8,128)(2,1)S(1)}, bf16[384,512]{1,0:T(8,128)(2,1)S(1)}, u32[]{:S(2)}, u32[]{:S(2)}) %collective-permute-start.9) | collective-permute-done | bytes 393248 | tf_op jit(solution)/shard_map/ppermute | solution.py:256
  175.9 2.1 collective-permute-start.24
  180.5 5.2 %collective-permute-done.22.rest_5_ = bf16[384,256]{1,0:T(8,128)(2,1)S(1)} collective-permute-done((bf16[384,256]{1,0:T(8,128)(2,1)S(1)}, bf16[384,256]{1,0:T(8,128)(2,1)S(1)}, u32[]{:S(2)}, u32[]{:S(2)}) %collective-permute-start.22) | collective-permute-done | bytes 196640 | tf_op jit(solution)/shard_map/ppermute | solution.py:256
  189.0 7.6 %score.3 = (bf16[2,512,512]{2,1,0:T(8,128)(2,1)S(1)}, f32[2,512,128]{2,1,0:T(8,128)S(1)}, f32[2,512,128]{2,1,0:T(8,128)S(1)}) custom-call(s32[8]{0:T(128)S(1)} %iota_xor_fusion.sources_ref, s32[1]{0:T(128)S(6)} %copy.15.where_ref, bf16[512,3072]{1,0:T(8,128)(2,1)S(1)} %norm.1.normed, bf16[2,2048,512]{2,1,0:T(8,128)(2,1)} %bitcast.23, ...), custom_call_target="tpu_custom_call" | custom-call | flops 2684354560 | bytes 5242880 | tf_op jit(solution)/shard_map/score/pallas_call | solution.py:186
  197.2 4.9 %attend.3 = bf16[512,256]{1,0:T(8,128)(2,1)S(1)} custom-call(s32[8]{0:T(128)S(1)} %iota_xor_fusion.sources_ref, bf16[512,3072]{1,0:T(8,128)(2,1)S(1)} %norm.1.normed, bf16[2,512,512]{2,1,0:T(8,128)(2,1)S(1)} %get-tuple-element.114.expo_ref, f32[2,512,128]{2,1,0:T(8,128)S(1)} %get-tuple-element.115.base_ref, f32[2,512,128]{2,1,0:T(8,128)S(1)} %get-tuple-element.116.share_ref, ...), custom_call_target="tpu_custom_call" | custom-call | flops 939524096 | bytes 1572864 | tf_op jit(solution)/shard_map/attend/pallas_call | solution.py:208
  206.7 8.1 %collective-permute-done.26 = f32[3072]{0:T(1024)S(1)} collective-permute-done((f32[3072]{0:T(1024)S(1)}, f32[3072]{0:T(1024)S(1)}, u32[]{:S(2)}, u32[]{:S(2)}) %collective-permute-start.26) | collective-permute-done | bytes 12320 | tf_op jit(solution)/shard_map/ppermute | solution.py:261
  215.2 3.6 %collective-permute-start.33 = (bf16[512,256]{1,0:T(8,128)(2,1)S(1)}, bf16[512,256]{1,0:T(8,128)(2,1)}, u32[]{:S(2)}, u32[]{:S(2)}) collective-permute-start(bf16[512,256]{1,0:T(8,128)(2,1)S(1)} %collective-permute-done.27.rest_0_), channel_id=1, source_target_pairs={{0,3},{1,2},{2,1},{3,0},{4,7},{5,6},{6,5},{7,4},{8,11},{9,10},{10,... | collective-permute-start | bytes 786440 | tf_op jit(solution)/shard_map/ppermute | solution.py:256
  220.4 22.1 %collective-permute-done.31.rest_4_ = bf16[512,256]{1,0:T(8,128)(2,1)S(1)} collective-permute-done((bf16[512,256]{1,0:T(8,128)(2,1)S(1)}, bf16[512,256]{1,0:T(8,128)(2,1)S(1)}, u32[]{:S(2)}, u32[]{:S(2)}) %collective-permute-start.31) | collective-permute-done | bytes 262176 | tf_op jit(solution)/shard_map/ppermute | solution.py:256
  243.3 13.3 %collective-permute-done.32.rest_5_ = bf16[512,256]{1,0:T(8,128)(2,1)} collective-permute-done((bf16[512,256]{1,0:T(8,128)(2,1)}, bf16[512,256]{1,0:T(8,128)(2,1)}, u32[]{:S(2)}, u32[]{:S(2)}) %collective-permute-start.32) | collective-permute-done | bytes 262176 | tf_op jit(solution)/shard_map/ppermute | solution.py:256
  258.6 4.3 %output.1 = bf16[512,768]{1,0:T(8,128)(2,1)} custom-call(bf16[512,768]{1,0:T(8,128)(2,1)S(1)} %collective-permute-done.25.inflow_ref, f32[1,768]{1,0:T(1,128)S(1)} %broadcast_in_dim.4.gate_ref, bf16[512,256]{1,0:T(8,128)(2,1)S(1)} %collective-permute-done.27.rest_0_, bf16[512,256]{1,0:T(8,128)(2,1)} %collective-permute-done.28.rest_1_, ...), custom_call_target="tpu_custom_call" | custom-call | flops 1610612736 | bytes 5242880 | tf_op jit(solution)/shard_map/output/pallas_call | solution.py:239
  (181 shorter events, 55.8 us)
Async XLA Ops:
  6.5 110.7 %all-gather.3.cloned.1.call-start = ((), (), s32[]{:S(2)}) async-start(), calls=%async_computation | async-start | bytes 3932160 | tf_op jit(solution)/shard_map/all_gather | solution.py:321
  16.6 15.3 %collective-permute-start = (bf16[384,512]{1,0:T(8,128)(2,1)S(1)}, bf16[384,512]{1,0:T(8,128)(2,1)S(1)}, u32[]{:S(2)}, u32[]{:S(2)}) collective-permute-start(bf16[384,512]{1,0:T(8,128)(2,1)S(1)} %get-tuple-element.82), channel_id=1, source_target_pairs={{0,8},{4,12},{8,0},{12,4},{16,24},{20,28},{24,16},{28,20},{1,9},{5... | collective-permute-start | bytes 1179656 | tf_op jit(solution)/shard_map/ppermute | solution.py:256
  31.9 25.3 %collective-permute-start.1 = (bf16[384,512]{1,0:T(8,128)(2,1)S(1)}, bf16[384,512]{1,0:T(8,128)(2,1)S(1)}, u32[]{:S(2)}, u32[]{:S(2)}) collective-permute-start(bf16[384,512]{1,0:T(8,128)(2,1)S(1)} %get-tuple-element.83), channel_id=1, source_target_pairs={{0,20},{4,16},{8,28},{12,24},{16,4},{20,0},{24,12},{28,8},{1,21},{... | collective-permute-start | bytes 1179656 | tf_op jit(solution)/shard_map/ppermute | solution.py:256
  31.9 27.5 %collective-permute-start.11 = (bf16[384,512]{1,0:T(8,128)(2,1)S(1)}, bf16[384,512]{1,0:T(8,128)(2,1)S(1)}, u32[]{:S(2)}, u32[]{:S(2)}) collective-permute-start(bf16[384,512]{1,0:T(8,128)(2,1)S(1)} %get-tuple-element.100), channel_id=1, source_target_pairs={{0,28},{4,24},{8,20},{12,16},{16,12},{20,8},{24,4},{28,0},{1,29},{... | collective-permute-start | bytes 1179656 | tf_op jit(solution)/shard_map/ppermute | solution.py:256
  58.0 16.3 %collective-permute-start.2 = (bf16[384,768]{1,0:T(8,128)(2,1)S(1)}, bf16[384,768]{1,0:T(8,128)(2,1)S(1)}, u32[]{:S(2)}, u32[]{:S(2)}) collective-permute-start(bf16[384,768]{1,0:T(8,128)(2,1)S(1)} %get-tuple-element.84), channel_id=1, source_target_pairs={{0,8},{4,12},{8,0},{12,4},{16,24},{20,28},{24,16},{28,20},{1,9},{5... | collective-permute-start | bytes 1769480 | tf_op jit(solution)/shard_map/ppermute | solution.py:256
  60.2 35.3 %collective-permute-start.12 = (bf16[384,768]{1,0:T(8,128)(2,1)S(1)}, bf16[384,768]{1,0:T(8,128)(2,1)S(1)}, u32[]{:S(2)}, u32[]{:S(2)}) collective-permute-start(bf16[384,768]{1,0:T(8,128)(2,1)S(1)} %get-tuple-element.101), channel_id=1, source_target_pairs={{0,16},{4,20},{8,24},{12,28},{16,0},{20,4},{24,8},{28,12},{1,17},{... | collective-permute-start | bytes 1769480 | tf_op jit(solution)/shard_map/ppermute | solution.py:256
  60.7 21.4 %collective-permute-start.35 = (bf16[384,512]{1,0:T(8,128)(2,1)}, bf16[384,512]{1,0:T(8,128)(2,1)S(1)}, u32[]{:S(2)}, u32[]{:S(2)}) collective-permute-start(bf16[384,512]{1,0:T(8,128)(2,1)} %get-tuple-element.135), channel_id=1, source_target_pairs={{0,24},{4,28},{8,16},{12,20},{16,8},{20,12},{24,0},{28,4},{1,25},{... | collective-permute-start | bytes 1179656 | tf_op jit(solution)/shard_map/ppermute | solution.py:256
  74.2 34.7 %collective-permute-start.3 = (bf16[384,768]{1,0:T(8,128)(2,1)}, bf16[384,768]{1,0:T(8,128)(2,1)S(1)}, u32[]{:S(2)}, u32[]{:S(2)}) collective-permute-start(bf16[384,768]{1,0:T(8,128)(2,1)} %get-tuple-element.85), channel_id=1, source_target_pairs={{0,24},{4,28},{8,16},{12,20},{16,8},{20,12},{24,0},{28,4},{1,25},{... | collective-permute-start | bytes 1769480 | tf_op jit(solution)/shard_map/ppermute | solution.py:256
  75.6 27.3 %collective-permute-start.37 = (bf16[384,512]{1,0:T(8,128)(2,1)}, bf16[384,512]{1,0:T(8,128)(2,1)}, u32[]{:S(2)}, u32[]{:S(2)}) collective-permute-start(bf16[384,512]{1,0:T(8,128)(2,1)} %get-tuple-element.137), channel_id=1, source_target_pairs={{0,12},{4,8},{8,4},{12,0},{16,28},{20,24},{24,20},{28,16},{1,13},{... | collective-permute-start | bytes 1179656 | tf_op jit(solution)/shard_map/ppermute | solution.py:256
  82.8 20.1 %collective-permute-start.36 = (bf16[384,512]{1,0:T(8,128)(2,1)}, bf16[384,512]{1,0:T(8,128)(2,1)}, u32[]{:S(2)}, u32[]{:S(2)}) collective-permute-start(bf16[384,512]{1,0:T(8,128)(2,1)} %get-tuple-element.136), channel_id=1, source_target_pairs={{0,4},{4,0},{8,12},{12,8},{16,20},{20,16},{24,28},{28,24},{1,5},{5... | collective-permute-start | bytes 1179656 | tf_op jit(solution)/shard_map/ppermute | solution.py:256
  95.5 18.3 %collective-permute-start.13 = (bf16[384,768]{1,0:T(8,128)(2,1)}, bf16[384,768]{1,0:T(8,128)(2,1)}, u32[]{:S(2)}, u32[]{:S(2)}) collective-permute-start(bf16[384,768]{1,0:T(8,128)(2,1)} %get-tuple-element.102), channel_id=1, source_target_pairs={{0,12},{4,8},{8,4},{12,0},{16,28},{20,24},{24,20},{28,16},{1,13},{... | collective-permute-start | bytes 1769480 | tf_op jit(solution)/shard_map/ppermute | solution.py:256
  108.9 27.3 %collective-permute-start.4 = (bf16[384,768]{1,0:T(8,128)(2,1)}, bf16[384,768]{1,0:T(8,128)(2,1)}, u32[]{:S(2)}, u32[]{:S(2)}) collective-permute-start(bf16[384,768]{1,0:T(8,128)(2,1)} %get-tuple-element.86), channel_id=1, source_target_pairs={{0,20},{4,16},{8,28},{12,24},{16,4},{20,0},{24,12},{28,8},{1,21},{... | collective-permute-start | bytes 1769480 | tf_op jit(solution)/shard_map/ppermute | solution.py:256
  111.0 27.6 %collective-permute-start.38 = (bf16[768,512]{1,0:T(8,128)(2,1)}, bf16[768,512]{1,0:T(8,128)(2,1)}, u32[]{:S(2)}, u32[]{:S(2)}) collective-permute-start(bf16[768,512]{1,0:T(8,128)(2,1)} %bitcast.10), channel_id=1, source_target_pairs={{0,1},{1,0},{2,3},{3,2},{4,5},{5,4},{6,7},{7,6},{8,9},{9,8},{10,11... | collective-permute-start | bytes 2359304 | tf_op jit(solution)/shard_map/ppermute | solution.py:256
  113.7 23.7 %collective-permute-start.14 = (bf16[384,768]{1,0:T(8,128)(2,1)}, bf16[384,768]{1,0:T(8,128)(2,1)}, u32[]{:S(2)}, u32[]{:S(2)}) collective-permute-start(bf16[384,768]{1,0:T(8,128)(2,1)} %get-tuple-element.103), channel_id=1, source_target_pairs={{0,28},{4,24},{8,20},{12,16},{16,12},{20,8},{24,4},{28,0},{1,29},{... | collective-permute-start | bytes 1769480 | tf_op jit(solution)/shard_map/ppermute | solution.py:256
  138.6 39.4 %collective-permute-start.39 = (bf16[768,512]{1,0:T(8,128)(2,1)S(1)}, bf16[768,512]{1,0:T(8,128)(2,1)S(1)}, u32[]{:S(2)}, u32[]{:S(2)}) collective-permute-start(bf16[768,512]{1,0:T(8,128)(2,1)S(1)} %bitcast.26), channel_id=1, source_target_pairs={{0,2},{1,3},{2,0},{3,1},{4,6},{5,7},{6,4},{7,5},{8,10},{9,11},{10,... | collective-permute-start | bytes 2359304 | tf_op jit(solution)/shard_map/ppermute | solution.py:256
  141.0 22.0 %collective-permute-start.8 = (bf16[384,512]{1,0:T(8,128)(2,1)S(1)}, bf16[384,512]{1,0:T(8,128)(2,1)S(1)}, u32[]{:S(2)}, u32[]{:S(2)}) collective-permute-start(bf16[384,512]{1,0:T(8,128)(2,1)S(1)} %copy-done.33), channel_id=1, source_target_pairs={{0,8},{4,12},{8,0},{12,4},{16,24},{20,28},{24,16},{28,20},{1,9},{5... | collective-permute-start | bytes 1179656 | tf_op jit(solution)/shard_map/ppermute | solution.py:256
  142.5 20.6 %collective-permute-start.6 = (bf16[384,512]{1,0:T(8,128)(2,1)S(1)}, bf16[384,512]{1,0:T(8,128)(2,1)S(1)}, u32[]{:S(2)}, u32[]{:S(2)}) collective-permute-start(bf16[384,512]{1,0:T(8,128)(2,1)S(1)} %copy-done.31), channel_id=1, source_target_pairs={{0,24},{4,28},{8,16},{12,20},{16,8},{20,12},{24,0},{28,4},{1,25},{... | collective-permute-start | bytes 1179656 | tf_op jit(solution)/shard_map/ppermute | solution.py:256
  148.5 20.5 %collective-permute-start.17 = (bf16[384,512]{1,0:T(8,128)(2,1)S(1)}, bf16[384,512]{1,0:T(8,128)(2,1)S(1)}, u32[]{:S(2)}, u32[]{:S(2)}) collective-permute-start(bf16[384,512]{1,0:T(8,128)(2,1)S(1)} %copy-done.29), channel_id=1, source_target_pairs={{0,28},{4,24},{8,20},{12,16},{16,12},{20,8},{24,4},{28,0},{1,29},{... | collective-permute-start | bytes 1179656 | tf_op jit(solution)/shard_map/ppermute | solution.py:256
  149.3 26.6 %collective-permute-start.9 = (bf16[384,512]{1,0:T(8,128)(2,1)S(1)}, bf16[384,512]{1,0:T(8,128)(2,1)S(1)}, u32[]{:S(2)}, u32[]{:S(2)}) collective-permute-start(bf16[384,512]{1,0:T(8,128)(2,1)S(1)} %copy-done.27), channel_id=1, source_target_pairs={{0,12},{4,8},{8,4},{12,0},{16,28},{20,24},{24,20},{28,16},{1,13},{... | collective-permute-start | bytes 1179656 | tf_op jit(solution)/shard_map/ppermute | solution.py:256
  163.0 16.1 %collective-permute-start.16 = (bf16[384,512]{1,0:T(8,128)(2,1)S(1)}, bf16[384,512]{1,0:T(8,128)(2,1)S(1)}, u32[]{:S(2)}, u32[]{:S(2)}) collective-permute-start(bf16[384,512]{1,0:T(8,128)(2,1)S(1)} %copy-done.25), channel_id=1, source_target_pairs={{0,20},{4,16},{8,28},{12,24},{16,4},{20,0},{24,12},{28,8},{1,21},{... | collective-permute-start | bytes 1179656 | tf_op jit(solution)/shard_map/ppermute | solution.py:256
  163.1 17.4 %collective-permute-start.7 = (bf16[384,512]{1,0:T(8,128)(2,1)S(1)}, bf16[384,512]{1,0:T(8,128)(2,1)S(1)}, u32[]{:S(2)}, u32[]{:S(2)}) collective-permute-start(bf16[384,512]{1,0:T(8,128)(2,1)S(1)} %copy-done.23), channel_id=1, source_target_pairs={{0,4},{4,0},{8,12},{12,8},{16,20},{20,16},{24,28},{28,24},{1,5},{5... | collective-permute-start | bytes 1179656 | tf_op jit(solution)/shard_map/ppermute | solution.py:256
  168.9 16.8 %collective-permute-start.22 = (bf16[384,256]{1,0:T(8,128)(2,1)S(1)}, bf16[384,256]{1,0:T(8,128)(2,1)S(1)}, u32[]{:S(2)}, u32[]{:S(2)}) collective-permute-start(bf16[384,256]{1,0:T(8,128)(2,1)S(1)} %copy-done.49), channel_id=1, source_target_pairs={{0,20},{4,16},{8,28},{12,24},{16,4},{20,0},{24,12},{28,8},{1,21},{... | collective-permute-start | bytes 589832 | tf_op jit(solution)/shard_map/ppermute | solution.py:256
  179.1 36.1 %collective-permute-start.40 = (bf16[768,512]{1,0:T(8,128)(2,1)S(1)}, bf16[768,512]{1,0:T(8,128)(2,1)S(1)}, u32[]{:S(2)}, u32[]{:S(2)}) collective-permute-start(bf16[768,512]{1,0:T(8,128)(2,1)S(1)} %bitcast.25), channel_id=1, source_target_pairs={{0,3},{1,2},{2,1},{3,0},{4,7},{5,6},{6,5},{7,4},{8,11},{9,10},{10,... | collective-permute-start | bytes 2359304 | tf_op jit(solution)/shard_map/ppermute | solution.py:256
  180.5 16.2 %collective-permute-start.20 = (bf16[384,256]{1,0:T(8,128)(2,1)S(1)}, bf16[384,256]{1,0:T(8,128)(2,1)S(1)}, u32[]{:S(2)}, u32[]{:S(2)}) collective-permute-start(bf16[384,256]{1,0:T(8,128)(2,1)S(1)} %copy-done.43), channel_id=1, source_target_pairs={{0,12},{4,8},{8,4},{12,0},{16,28},{20,24},{24,20},{28,16},{1,13},{... | collective-permute-start | bytes 589832 | tf_op jit(solution)/shard_map/ppermute | solution.py:256
  202.1 54.5 %collective-permute-start.25 = (bf16[512,768]{1,0:T(8,128)(2,1)}, bf16[512,768]{1,0:T(8,128)(2,1)S(1)}, u32[]{:S(2)}, u32[]{:S(2)}) collective-permute-start(bf16[512,768]{1,0:T(8,128)(2,1)} %bitcast), channel_id=1, source_target_pairs={{0,4},{4,8},{8,12},{12,16},{16,20},{20,24},{24,28},{28,0},{1,5},{5... | collective-permute-start | bytes 2359304 | tf_op jit(solution)/shard_map/ppermute | solution.py:261
  204.0 14.8 %collective-permute-start.28 = (bf16[512,256]{1,0:T(8,128)(2,1)S(1)}, bf16[512,256]{1,0:T(8,128)(2,1)}, u32[]{:S(2)}, u32[]{:S(2)}) collective-permute-start(bf16[512,256]{1,0:T(8,128)(2,1)S(1)} %attend.3), channel_id=1, source_target_pairs={{0,4},{4,8},{8,12},{12,16},{16,20},{20,24},{24,28},{28,0},{1,5},{5... | collective-permute-start | bytes 786440 | tf_op jit(solution)/shard_map/ppermute | solution.py:261
  205.1 14.2 %collective-permute-start.29 = (bf16[512,256]{1,0:T(8,128)(2,1)S(1)}, bf16[512,256]{1,0:T(8,128)(2,1)S(1)}, u32[]{:S(2)}, u32[]{:S(2)}) collective-permute-start(bf16[512,256]{1,0:T(8,128)(2,1)S(1)} %collective-permute-done.27.rest_0_), channel_id=1, source_target_pairs={{0,1},{1,0},{2,3},{3,2},{4,5},{5,4},{6,7},{7,6},{8,9},{9,8},{10,11... | collective-permute-start | bytes 786440 | tf_op jit(solution)/shard_map/ppermute | solution.py:256
  214.8 27.7 %collective-permute-start.31 = (bf16[512,256]{1,0:T(8,128)(2,1)S(1)}, bf16[512,256]{1,0:T(8,128)(2,1)S(1)}, u32[]{:S(2)}, u32[]{:S(2)}) collective-permute-start(bf16[512,256]{1,0:T(8,128)(2,1)S(1)} %collective-permute-done.27.rest_0_), channel_id=1, source_target_pairs={{0,2},{1,3},{2,0},{3,1},{4,6},{5,7},{6,4},{7,5},{8,10},{9,11},{10,... | collective-permute-start | bytes 786440 | tf_op jit(solution)/shard_map/ppermute | solution.py:256
  215.2 28.1 %collective-permute-start.33 = (bf16[512,256]{1,0:T(8,128)(2,1)S(1)}, bf16[512,256]{1,0:T(8,128)(2,1)}, u32[]{:S(2)}, u32[]{:S(2)}) collective-permute-start(bf16[512,256]{1,0:T(8,128)(2,1)S(1)} %collective-permute-done.27.rest_0_), channel_id=1, source_target_pairs={{0,3},{1,2},{2,1},{3,0},{4,7},{5,6},{6,5},{7,4},{8,11},{9,10},{10,... | collective-permute-start | bytes 786440 | tf_op jit(solution)/shard_map/ppermute | solution.py:256
  218.8 24.5 %collective-permute-start.30 = (bf16[512,256]{1,0:T(8,128)(2,1)}, bf16[512,256]{1,0:T(8,128)(2,1)}, u32[]{:S(2)}, u32[]{:S(2)}) collective-permute-start(bf16[512,256]{1,0:T(8,128)(2,1)} %collective-permute-done.28.rest_1_), channel_id=1, source_target_pairs={{0,1},{1,0},{2,3},{3,2},{4,5},{5,4},{6,7},{7,6},{8,9},{9,8},{10,11... | collective-permute-start | bytes 786440 | tf_op jit(solution)/shard_map/ppermute | solution.py:256
  220.1 36.6 %collective-permute-start.32 = (bf16[512,256]{1,0:T(8,128)(2,1)}, bf16[512,256]{1,0:T(8,128)(2,1)}, u32[]{:S(2)}, u32[]{:S(2)}) collective-permute-start(bf16[512,256]{1,0:T(8,128)(2,1)} %collective-permute-done.28.rest_1_), channel_id=1, source_target_pairs={{0,2},{1,3},{2,0},{3,1},{4,6},{5,7},{6,4},{7,5},{8,10},{9,11},{10,... | collective-permute-start | bytes 786440 | tf_op jit(solution)/shard_map/ppermute | solution.py:256
  243.2 13.4 %collective-permute-start.34 = (bf16[512,256]{1,0:T(8,128)(2,1)}, bf16[512,256]{1,0:T(8,128)(2,1)}, u32[]{:S(2)}, u32[]{:S(2)}) collective-permute-start(bf16[512,256]{1,0:T(8,128)(2,1)} %collective-permute-done.28.rest_1_), channel_id=1, source_target_pairs={{0,3},{1,2},{2,1},{3,0},{4,7},{5,6},{6,5},{7,4},{8,11},{9,10},{10,... | collective-permute-start | bytes 786440 | tf_op jit(solution)/shard_map/ppermute | solution.py:256
  (63 other events, 587.5 us)
Sparse Core Ops, SparseCore 0:
  8.9 66.1 all-gather.2

commit v4 on v3

--- a/solution.py
+++ b/solution.py
@@ -2,7 +2,6 @@
 
 import jax
 import jax.numpy as jnp
-import ml_dtypes
 import numpy as np
 from jax import lax
 from jax.experimental import pallas as pl
@@ -35,21 +34,28 @@
 
 def pick_matrix(kinds, lanes, depth_step):
     period = 4 * lanes
-    row = np.arange(len(kinds) * lanes * depth_step)
-    kind = np.asarray(kinds)[row // (lanes * depth_step)]
-    source = (row % depth_step) * period + (row // depth_step) % lanes * 4 + kind
-    return np.equal.outer(source, np.arange(period * depth_step)).astype(ml_dtypes.bfloat16)
-
-
-def split_kernel(lanes, plan, kinds, depth_step, order_ref, pick_ref, rows_ref, *outs):
+    shape = (len(kinds) * lanes * depth_step, period * depth_step)
+    row = lax.broadcasted_iota(jnp.int32, shape, 0)
+    column = lax.broadcasted_iota(jnp.int32, shape, 1)
+    source = row % depth_step * period + row // depth_step % lanes * 4 + kinds[0]
+    source += row // (lanes * depth_step)
+    return jnp.where(source == column, 1.0, 0.0).astype(BF16)
+
+
+def split_kernel(lanes, plan, kinds, depth_step, order_ref, rows_ref, *rest):
+    outs, pick = rest[:-1], rest[-1]
     depth = rows_ref.shape[1] // (4 * lanes)
     chunk = depth_step * 4 * lanes
+
+    @pl.when(pl.program_id(0) == 0)
+    def _():
+        pick[...] = pick_matrix(kinds, lanes, depth_step)
 
     def fill(own):
         for first in range(0, depth, depth_step):
             begin = first * 4 * lanes
             sorted_rows = jnp.dot(
-                pick_ref[...], rows_ref[0, begin : begin + chunk, :], preferred_element_type=F32
+                pick[...], rows_ref[0, begin : begin + chunk, :], preferred_element_type=F32
             ).astype(BF16)
             for out, columns in zip(own, plan):
                 for column, (kind, lane) in enumerate(columns):
@@ -63,30 +69,34 @@
         pl.when(pl.program_id(0) == block)(functools.partial(fill, own))
 
 
-def split_blocks(rows, order, plan, lanes):
+def split_blocks(rows, order, first, count, plan, lanes, early):
     depth = rows.shape[1] // (4 * lanes)
     depth_step = max(n for n in (16, 32, 64) if depth % n == 0 and n * 4 * lanes <= 256)
     kinds = sorted({kind for columns in plan for kind, _ in columns})
-    pick = pick_matrix(kinds, lanes, depth_step)
-    blocks = order.shape[0]
-    shapes = [(depth, len(columns) * HD) for columns in plan]
+    shapes = [(depth, len(columns) * HD) for columns in plan] * count
+    if early:
+        out_specs = [WHOLE] * len(shapes)
+        out_shape = [jax.ShapeDtypeStruct(shape, BF16) for shape in shapes]
+    else:
+        out_specs = [pl.BlockSpec(shape, lambda i, order: (0, 0)) for shape in shapes]
+        out_shape = [pltpu.HBM(shape, BF16) for shape in shapes]
     flat = pl.pallas_call(
         functools.partial(split_kernel, lanes, plan, kinds, depth_step),
         grid_spec=pltpu.PrefetchScalarGridSpec(
             num_scalar_prefetch=1,
-            grid=(blocks,),
-            in_specs=[
-                pl.BlockSpec(pick.shape, lambda i, order: (0, 0)),
-                pl.BlockSpec((1,) + rows.shape[1:], lambda i, order: (order[i], 0, 0)),
+            grid=(count,),
+            in_specs=[pl.BlockSpec((1,) + rows.shape[1:], lambda i, order: (order[first + i], 0, 0))],
+            out_specs=out_specs,
+            scratch_shapes=[
+                pltpu.VMEM((len(kinds) * lanes * depth_step, depth_step * 4 * lanes), BF16)
             ],
-            out_specs=[WHOLE] * (len(shapes) * blocks),
         ),
-        out_shape=[jax.ShapeDtypeStruct(shape, BF16) for shape in shapes] * blocks,
-        compiler_params=params(10),
-        cost_estimate=cost(0, 3 * blocks * rows.shape[1] * HD),
+        out_shape=out_shape,
+        compiler_params=params(10 if early else 32),
+        cost_estimate=cost(0, 3 * count * rows.shape[1] * HD),
         name="split_blocks",
-    )(order, jnp.asarray(pick), in_hbm(rows))
-    return [list(flat[i :: len(shapes)]) for i in range(len(shapes))]
+    )(order, in_hbm(rows))
+    return [list(flat[i :: len(plan)]) for i in range(len(plan))]
 
 
 def norm_kernel(tokens_ref, modulation_ref, out_ref):
@@ -266,13 +276,7 @@
         self.window, self.sent = window, []
 
     def swap(self, piece, distance, *earlier):
-        size = piece.size
-        for other in reversed(self.sent):
-            size += other.size
-            if size > self.window:
-                earlier += (other,)
-                break
-        for other in earlier:
+        for other in (*earlier, *self.sent[-self.window :][:1]):
             piece = after(piece, other)
         self.sent.append(swapped(piece, "section", distance))
         return self.sent[-1]
@@ -300,7 +304,7 @@
         compiler_params=params(4),
         cost_estimate=cost(0, 4 * len(pieces) * pieces[0].size),
         name="placed",
-    )(slots, *pieces)
+    )(slots, *[in_hbm(piece) for piece in pieces])
 
 
 def local(block_weights, modulation, inflow, stale_cache, patch_index, assignment):
@@ -312,6 +316,8 @@
 
     section_ids = jnp.arange(sections, dtype=jnp.int32)
     sources = here ^ section_ids
+    order = sorted(range(1, sections), key=lambda d: (d == 1, d % 2, d))
+    turn = here ^ jnp.asarray(order + [0], jnp.int32)
 
     def block_of(section):
         return jnp.sum((assignment[None] == section[:, None]) * section_ids[None], axis=1)
@@ -320,16 +326,11 @@
     rows = rows.transpose(0, 1, 3, 2, 4).reshape(blocks, depth * lanes * kinds, HD)
     tokens = lax.all_gather(inflow[0], "tp", axis=1, tiled=True)
 
-    order = sorted(range(1, sections), key=lambda d: (d == 1, d % 2, d))
-    own_blocks = block_of(sources)
-    before = block_of((sources + sections - 1) % sections)
-
-    ahead = [order[:3], order[3:] + [0]]
-    to_out = {}
-    for some in ahead:
-        blocks_now = jnp.stack([before[d] for d in some])
-        (made,) = split_blocks(rows, blocks_now, [[(3, head) for head in range(lanes)]], lanes)
-        to_out.update(zip(some, made))
+    before = block_of((turn + sections - 1) % sections)
+    out_plan = [[(3, head) for head in range(lanes)]]
+    soon = split_blocks(rows, before, 0, 3, out_plan, lanes, True)[0]
+    soon += split_blocks(rows, before, 3, sections - 3, out_plan, lanes, True)[0]
+    to_out = dict(zip(order + [0], soon))
     size = max(1, lanes // 2)
     groups = [tuple(range(first, first + size)) for first in range(0, lanes, size)]
     plan = []
@@ -340,9 +341,10 @@
             plan.append(values)
         else:
             plan[-1] += values
-    split = split_blocks(rows, own_blocks, plan, lanes)
-
-    relay = Relay(4 * depth * inner)
+    split = split_blocks(rows, block_of(turn), 0, sections, plan, lanes, False)
+    split = [dict(zip(order + [0], made)) for made in split]
+
+    relay = Relay(4)
     for distance in order:
         to_out[distance] = relay.swap(to_out[distance], distance)
     per = sections // tp
@@ -352,11 +354,12 @@
     for distance in range(1, tp):
         matrices.append(swapped(after(held[distance], matrices[-1]), "tp", distance))
     normed = norm(tokens, modulation[0])
-
-    def relayed(stage, *earlier, at=0):
+    gate = handed_on(modulation[0, 2])
+
+    def relayed(stage, waits):
         pieces = [split[stage][0]] * sections
         for index, distance in enumerate(order):
-            wait = earlier if index == at else ()
+            wait = waits.get(index, ())
             pieces[distance] = relay.swap(split[stage][distance], distance, *wait)
         return pieces
 
@@ -368,20 +371,21 @@
             attended[distance].append(swapped(moved, "tp", distance) if distance else moved)
         return moved
 
-    done = (normed,)
+    last = sections - 2
+    waits = {0: (gate,), last - 1: (matrices[1],), last: (normed,)}
     for stage, group in enumerate(groups[:-1]):
-        pieces = relayed(stage, *done, at=sections - 2)
+        pieces = relayed(stage, waits)
         stats = score(normed, pieces, sources, patch_index, stale_cache[0], group)
         own = attend(normed, pieces, sources, 2 * len(group) * HD, *stats)
-        done = (own,)
-        share_out(own)
-    pieces = relayed(len(plan) - 2, *done, at=min(4, sections - 2))
-    value_pieces = relayed(len(plan) - 1)
+        moved = share_out(own)
+        waits = {2: (matrices[2],), min(4, last): (own,), last: (moved,)}
+    pieces = relayed(len(plan) - 2, waits)
     stats = score(normed, pieces, sources, patch_index, stale_cache[0], groups[-1])
-    own = attend(normed, value_pieces, sources, 0, *stats)
-    share_out(own)
-    carried = handed_on(after(inflow[0], own))
-    gate = handed_on(modulation[0, 2])
+    value_pieces = relayed(len(plan) - 1, {last: (stats[0], matrices[-1])})
+    ready = functools.reduce(after, [part for own in attended for part in own], stats[0])
+    own = attend(normed, value_pieces, sources, 0, ready, *stats[1:])
+    moved = share_out(own)
+    carried = handed_on(after(inflow[0], moved))
     gate = lax.dynamic_slice_in_dim(gate, rank * share, share, 0)[None]
     return output(carried, gate, attended, matrices)[None]
 

time: 273 us -> 269 us (0.985)
  local copies, waits for them, and re-layouts: 30.3 us -> 7.04 us
  waiting for transfers between devices: 118 us -> 140 us
    ppermute x37, waiting for transfers between devices: 109 us -> 133 us  [swapped(): lax.ppermute(block, axis, [(i, i ^ distance) for i in range(lax.axis_size...]
    unnamed x107 -> x71, local copies, waits for them, and re-layouts: 24.1 us -> 5.57 us
    another operation x1 -> x0, local copies, waits for them, and re-layouts: 3.2 us -> none  [local(): blocks_now = jnp.stack([before[d] for d in some])]
  transfers between devices with their start and end apart: 42 -> 42, of which waited for: 14 -> 17; matrix products, arithmetic and copies ran while one was open for 4% -> 1% of each run, Pallas kernels for 20% -> 19%
where the time goes in v4:
time: 269 us; the launch traced here: 268 us
  waiting for transfers between devices  140 us (52%)
  Pallas kernels  59.5 us (22%)
  starting transfers between devices  45.3 us (17%)
  between operations  14.6 us (5%)
  local copies, waits for them, and re-layouts  7.04 us (3%)
    ppermute x37, waiting for transfers between devices, swapped(): lax.ppermute(block, axis, [(i, i ^ distance) for i in range(lax.axis_size...  133 us
    ppermute x37, starting transfers between devices, swapped(): lax.ppermute(block, axis, [(i, i ^ distance) for i in range(lax.axis_size...  44.6 us
    pallas_call x3, Pallas kernels, split_blocks(): pl.pallas_call(functools.partial(split_kernel, lanes, plan, kinds, depth_...  24.5 us
    pallas_call x2, Pallas kernels, score(): pl.pallas_call(functools.partial(score_kernel, len(pieces), cols), in_spe...  15.6 us
    pallas_call x2, Pallas kernels, attend(): pl.pallas_call(functools.partial(attend_kernel, len(pieces), first), in_s...  8.54 us
    ppermute x4, waiting for transfers between devices, handed_on(): lax.ppermute(block, 'section', [(i, (i + 1) % sections) for i in range(se...  6.79 us
    unnamed x71, local copies, waits for them, and re-layouts  5.57 us
  transfers between devices with their start and end apart: 42, of which 17 were waited for; matrix products, arithmetic and copies ran while one was open for 1% of the time, Pallas kernels for 19%

profile of v4, /device:TPU:0, one launch (start us, length us, event | category | flops | bytes accessed | tf_op | source)
XLA Modules:
  0.0 268.4 jit_solution(16346375407328226996)
XLA Ops:
  8.8 4.2 %split_blocks.5 = (bf16[384,512]{1,0:T(8,128)(2,1)S(1)}, bf16[384,512]{1,0:T(8,128)(2,1)S(1)}, bf16[384,512]{1,0:T(8,128)(2,1)S(1)}) custom-call(s32[8]{0:T(128)S(1)} %get-tuple-element.167.order_ref, bf16[8,6144,128]{2,1,0:T(8,128)(2,1)} %bitcast.19), custom_call_target="tpu_custom_call" | custom-call | bytes 7077888 | tf_op jit(solution)/shard_map/split_blocks/pallas_call | solution.py:83
  13.0 3.0 %collective-permute-start = (bf16[384,512]{1,0:T(8,128)(2,1)S(1)}, bf16[384,512]{1,0:T(8,128)(2,1)S(1)}, u32[]{:S(2)}, u32[]{:S(2)}) collective-permute-start(bf16[384,512]{1,0:T(8,128)(2,1)S(1)} %get-tuple-element.94), channel_id=1, source_target_pairs={{0,8},{4,12},{8,0},{12,4},{16,24},{20,28},{24,16},{28,20},{1,9},{5... | collective-permute-start | bytes 1179656 | tf_op jit(solution)/shard_map/ppermute | solution.py:266
  16.0 9.1 %collective-permute-done.rest_2_ = bf16[384,512]{1,0:T(8,128)(2,1)S(1)} collective-permute-done((bf16[384,512]{1,0:T(8,128)(2,1)S(1)}, bf16[384,512]{1,0:T(8,128)(2,1)S(1)}, u32[]{:S(2)}, u32[]{:S(2)}) %collective-permute-start) | collective-permute-done | bytes 393248 | tf_op jit(solution)/shard_map/ppermute | solution.py:266
  28.3 6.0 %split_blocks.4 = (bf16[384,512]{1,0:T(8,128)(2,1)S(1)}, bf16[384,512]{1,0:T(8,128)(2,1)S(1)}, bf16[384,512]{1,0:T(8,128)(2,1)S(1)}, bf16[384,512]{1,0:T(8,128)(2,1)S(1)}, bf16[384,512]{1,0:T(8,128)(2,1)S(1)}) custom-call(s32[8]{0:T(128)S(1)} %get-tuple-element.167.order_ref, bf16[8,6144,128]{2,1,0:T(8,128)(2,1)} %bitcast.20), custom_call_target="tpu_custom_call" | custom-call | bytes 11796480 | tf_op jit(solution)/shard_map/split_blocks/pallas_call | solution.py:83
  36.8 8.7 %collective-permute-done.1.rest_4_ = bf16[384,512]{1,0:T(8,128)(2,1)S(1)} collective-permute-done((bf16[384,512]{1,0:T(8,128)(2,1)S(1)}, bf16[384,512]{1,0:T(8,128)(2,1)S(1)}, u32[]{:S(2)}, u32[]{:S(2)}) %collective-permute-start.1) | collective-permute-done | bytes 393248 | tf_op jit(solution)/shard_map/ppermute | solution.py:266
  47.8 11.9 %collective-permute-done.11.rest_5_ = bf16[384,512]{1,0:T(8,128)(2,1)S(1)} collective-permute-done((bf16[384,512]{1,0:T(8,128)(2,1)S(1)}, bf16[384,512]{1,0:T(8,128)(2,1)S(1)}, u32[]{:S(2)}, u32[]{:S(2)}) %collective-permute-start.11) | collective-permute-done | bytes 393248 | tf_op jit(solution)/shard_map/ppermute | solution.py:266
  66.7 14.3 %split_blocks.3 = (bf16[384,768]{1,0:T(8,128)(2,1)}, bf16[384,512]{1,0:T(8,128)(2,1)}, bf16[384,256]{1,0:T(8,128)(2,1)}, bf16[384,768]{1,0:T(8,128)(2,1)}, bf16[...) custom-call(s32[8]{0:T(128)S(1)} %get-tuple-element.168.order_ref, ...), custom_call_target="tpu_custom_call" | custom-call | bytes 18874368 | tf_op jit(solution)/shard_map/split_blocks/pallas_call | solution.py:83
  84.5 5.1 %collective-permute-done.14.rest_9_ = bf16[768,512]{1,0:T(8,128)(2,1)S(1)} collective-permute-done((bf16[768,512]{1,0:T(8,128)(2,1)S(1)}, bf16[768,512]{1,0:T(8,128)(2,1)S(1)}, u32[]{:S(2)}, u32[]{:S(2)}) %collective-permute-start.14) | collective-permute-done | bytes 786464 | tf_op jit(solution)/shard_map/ppermute | solution.py:266
  90.6 2.9 %collective-permute-start.17 = (bf16[768,512]{1,0:T(8,128)(2,1)}, bf16[768,512]{1,0:T(8,128)(2,1)}, u32[]{:S(2)}, u32[]{:S(2)}) collective-permute-start(bf16[768,512]{1,0:T(8,128)(2,1)} %bitcast.11), channel_id=1, source_target_pairs={{0,2},{1,3},{2,0},{3,1},{4,6},{5,7},{6,4},{7,5},{8,10},{9,11},{10,... | collective-permute-start | bytes 2359304 | tf_op jit(solution)/shard_map/ppermute | solution.py:266
  94.6 2.8 %collective-permute-done.7.rest_2_ = bf16[384,768]{1,0:T(8,128)(2,1)S(1)} collective-permute-done((bf16[384,768]{1,0:T(8,128)(2,1)}, bf16[384,768]{1,0:T(8,128)(2,1)S(1)}, u32[]{:S(2)}, u32[]{:S(2)}) %collective-permute-start.7) | collective-permute-done | bytes 589856 | tf_op jit(solution)/shard_map/ppermute | solution.py:266
  98.3 13.0 %collective-permute-done.12.rest_4_ = bf16[384,768]{1,0:T(8,128)(2,1)S(1)} collective-permute-done((bf16[384,768]{1,0:T(8,128)(2,1)}, bf16[384,768]{1,0:T(8,128)(2,1)S(1)}, u32[]{:S(2)}, u32[]{:S(2)}) %collective-permute-start.12) | collective-permute-done | bytes 589856 | tf_op jit(solution)/shard_map/ppermute | solution.py:266
  111.3 4.3 %norm.1.normed = bf16[512,3072]{1,0:T(8,128)(2,1)S(1)} custom-call(bf16[512,3072]{1,0:T(8,128)(2,1)} %bitcast.24, f32[3,3072]{1,0:T(4,128)S(1)} %bitcast.18), custom_call_target="tpu_custom_call" | custom-call | flops 15728640 | bytes 6291456 | tf_op jit(solution)/shard_map/norm/pallas_call | solution.py:114
  117.9 5.0 %collective-permute-done.10.rest_3_ = bf16[384,768]{1,0:T(8,128)(2,1)S(1)} collective-permute-done((bf16[384,768]{1,0:T(8,128)(2,1)}, bf16[384,768]{1,0:T(8,128)(2,1)S(1)}, u32[]{:S(2)}, u32[]{:S(2)}) %collective-permute-start.10) | collective-permute-done | bytes 589856 | tf_op jit(solution)/shard_map/ppermute | solution.py:266
  123.9 12.4 %collective-permute-done.13.rest_5_ = bf16[384,768]{1,0:T(8,128)(2,1)} collective-permute-done((bf16[384,768]{1,0:T(8,128)(2,1)}, bf16[384,768]{1,0:T(8,128)(2,1)}, u32[]{:S(2)}, u32[]{:S(2)}) %collective-permute-start.13) | collective-permute-done | bytes 589856 | tf_op jit(solution)/shard_map/ppermute | solution.py:266
  137.8 7.8 %score.2 = (bf16[2,512,512]{2,1,0:T(8,128)(2,1)S(1)}, f32[2,512,128]{2,1,0:T(8,128)S(1)}, f32[2,512,128]{2,1,0:T(8,128)S(1)}) custom-call(s32[8]{0:T(128)S(1)} %iota_xor_fusion.sources_ref, s32[1]{0:T(128)S(6)} %copy.13.where_ref, bf16[512,3072]{1,0:T(8,128)(2,1)S(1)} %norm.1.normed, bf16[2,2048,512]{2,1,0:T(8,128)(2,1)} %bitcast.22, ...), custom_call_target="tpu_custom_call" | custom-call | flops 2684354560 | bytes 5242880 | tf_op jit(solution)/shard_map/score/pallas_call | solution.py:196
  145.7 3.9 %attend.2 = bf16[512,256]{1,0:T(8,128)(2,1)S(1)} custom-call(s32[8]{0:T(128)S(1)} %iota_xor_fusion.sources_ref, bf16[512,3072]{1,0:T(8,128)(2,1)S(1)} %norm.1.normed, bf16[2,512,512]{2,1,0:T(8,128)(2,1)S(1)} %get-tuple-element.121.expo_ref, f32[2,512,128]{2,1,0:T(8,128)S(1)} %get-tuple-element.122.base_ref, f32[2,512,128]{2,1,0:T(8,128)S(1)} %get-tuple-element.123.share_ref, ...), custom_call_target="tpu_custom_call" | custom-call | flops 939524096 | bytes 1572864 | tf_op jit(solution)/shard_map/attend/pallas_call | solution.py:218
  149.6 3.2 %collective-permute-start.21 = (bf16[384,512]{1,0:T(8,128)(2,1)S(1)}, bf16[384,512]{1,0:T(8,128)(2,1)S(1)}, u32[]{:S(2)}, u32[]{:S(2)}) collective-permute-start(bf16[384,512]{1,0:T(8,128)(2,1)S(1)} %copy-done.24), channel_id=1, source_target_pairs={{0,12},{4,8},{8,4},{12,0},{16,28},{20,24},{24,20},{28,16},{1,13},{... | collective-permute-start | bytes 1179656 | tf_op jit(solution)/shard_map/ppermute | solution.py:266
  152.8 6.6 %collective-permute-done.22.rest_4_ = bf16[384,512]{1,0:T(8,128)(2,1)S(1)} collective-permute-done((bf16[384,512]{1,0:T(8,128)(2,1)S(1)}, bf16[384,512]{1,0:T(8,128)(2,1)S(1)}, u32[]{:S(2)}, u32[]{:S(2)}) %collective-permute-start.22) | collective-permute-done | bytes 393248 | tf_op jit(solution)/shard_map/ppermute | solution.py:266
  161.5 4.9 %collective-permute-done.21.rest_3_ = bf16[384,512]{1,0:T(8,128)(2,1)S(1)} collective-permute-done((bf16[384,512]{1,0:T(8,128)(2,1)S(1)}, bf16[384,512]{1,0:T(8,128)(2,1)S(1)}, u32[]{:S(2)}, u32[]{:S(2)}) %collective-permute-start.21) | collective-permute-done | bytes 393248 | tf_op jit(solution)/shard_map/ppermute | solution.py:266
  166.6 8.3 %collective-permute-done.23.rest_5_ = bf16[384,512]{1,0:T(8,128)(2,1)S(1)} collective-permute-done((bf16[384,512]{1,0:T(8,128)(2,1)S(1)}, bf16[384,512]{1,0:T(8,128)(2,1)S(1)}, u32[]{:S(2)}, u32[]{:S(2)}) %collective-permute-start.23) | collective-permute-done | bytes 393248 | tf_op jit(solution)/shard_map/ppermute | solution.py:266
  175.3 3.4 %collective-permute-start.26 = (bf16[512,256]{1,0:T(8,128)(2,1)S(1)}, bf16[512,256]{1,0:T(8,128)(2,1)S(1)}, u32[]{:S(2)}, u32[]{:S(2)}) collective-permute-start(bf16[512,256]{1,0:T(8,128)(2,1)S(1)} %collective-permute-done.16.rest_0_), channel_id=1, source_target_pairs={{0,2},{1,3},{2,0},{3,1},{4,6},{5,7},{6,4},{7,5},{8,10},{9,11},{10,... | collective-permute-start | bytes 786440 | tf_op jit(solution)/shard_map/ppermute | solution.py:266
  179.0 3.5 %collective-permute-done.33.rest_4_ = bf16[384,256]{1,0:T(8,128)(2,1)S(1)} collective-permute-done((bf16[384,256]{1,0:T(8,128)(2,1)S(1)}, bf16[384,256]{1,0:T(8,128)(2,1)S(1)}, u32[]{:S(2)}, u32[]{:S(2)}) %collective-permute-start.33) | collective-permute-done | bytes 196640 | tf_op jit(solution)/shard_map/ppermute | solution.py:266
  184.6 7.8 %score.3 = (bf16[2,512,512]{2,1,0:T(8,128)(2,1)S(1)}, f32[2,512,128]{2,1,0:T(8,128)S(1)}, f32[2,512,128]{2,1,0:T(8,128)S(1)}) custom-call(s32[8]{0:T(128)S(1)} %iota_xor_fusion.sources_ref, s32[1]{0:T(128)S(6)} %copy.13.where_ref, bf16[512,3072]{1,0:T(8,128)(2,1)S(1)} %norm.1.normed, bf16[2,2048,512]{2,1,0:T(8,128)(2,1)} %bitcast.23, ...), custom_call_target="tpu_custom_call" | custom-call | flops 2684354560 | bytes 5242880 | tf_op jit(solution)/shard_map/score/pallas_call | solution.py:196
  193.3 3.3 %collective-permute-start.35 = (bf16[384,256]{1,0:T(8,128)(2,1)S(1)}, bf16[384,256]{1,0:T(8,128)(2,1)S(1)}, u32[]{:S(2)}, u32[]{:S(2)}) collective-permute-start(bf16[384,256]{1,0:T(8,128)(2,1)S(1)} %copy-done.30), channel_id=1, source_target_pairs={{0,28},{4,24},{8,20},{12,16},{16,12},{20,8},{24,4},{28,0},{1,29},{... | collective-permute-start | bytes 589832 | tf_op jit(solution)/shard_map/ppermute | solution.py:266
  196.6 16.6 %collective-permute-done.26.rest_4_ = bf16[512,256]{1,0:T(8,128)(2,1)S(1)} collective-permute-done((bf16[512,256]{1,0:T(8,128)(2,1)S(1)}, bf16[512,256]{1,0:T(8,128)(2,1)S(1)}, u32[]{:S(2)}, u32[]{:S(2)}) %collective-permute-start.26) | collective-permute-done | bytes 262176 | tf_op jit(solution)/shard_map/ppermute | solution.py:266
  213.4 4.9 %collective-permute-done.32.rest_3_ = bf16[384,256]{1,0:T(8,128)(2,1)S(1)} collective-permute-done((bf16[384,256]{1,0:T(8,128)(2,1)S(1)}, bf16[384,256]{1,0:T(8,128)(2,1)S(1)}, u32[]{:S(2)}, u32[]{:S(2)}) %collective-permute-start.32) | collective-permute-done | bytes 196640 | tf_op jit(solution)/shard_map/ppermute | solution.py:266
  218.4 4.6 %attend.3 = bf16[512,256]{1,0:T(8,128)(2,1)S(1)} custom-call(s32[8]{0:T(128)S(1)} %iota_xor_fusion.sources_ref, bf16[512,3072]{1,0:T(8,128)(2,1)S(1)} %norm.1.normed, bf16[2,512,512]{2,1,0:T(8,128)(2,1)S(1)} %get-tuple-element.145.expo_ref, f32[2,512,128]{2,1,0:T(8,128)S(1)} %get-tuple-element.146.base_ref, f32[2,512,128]{2,1,0:T(8,128)S(1)} %get-tuple-element.147.share_ref, ...), custom_call_target="tpu_custom_call" | custom-call | flops 939524096 | bytes 1572864 | tf_op jit(solution)/shard_map/attend/pallas_call | solution.py:218
  223.1 6.8 %collective-permute-done.36.rest_1_ = bf16[512,256]{1,0:T(8,128)(2,1)} collective-permute-done((bf16[512,256]{1,0:T(8,128)(2,1)S(1)}, bf16[512,256]{1,0:T(8,128)(2,1)}, u32[]{:S(2)}, u32[]{:S(2)}) %collective-permute-start.36) | collective-permute-done | bytes 262176 | tf_op jit(solution)/shard_map/ppermute | solution.py:271
  229.9 2.7 %collective-permute-start.40 = (bf16[512,256]{1,0:T(8,128)(2,1)}, bf16[512,256]{1,0:T(8,128)(2,1)}, u32[]{:S(2)}, u32[]{:S(2)}) collective-permute-start(bf16[512,256]{1,0:T(8,128)(2,1)} %collective-permute-done.36.rest_1_), channel_id=1, source_target_pairs={{0,3},{1,2},{2,1},{3,0},{4,7},{5,6},{6,5},{7,4},{8,11},{9,10},{10,... | collective-permute-start | bytes 786440 | tf_op jit(solution)/shard_map/ppermute | solution.py:266
  234.4 6.8 %collective-permute-done.40.rest_7_ = bf16[512,256]{1,0:T(8,128)(2,1)} collective-permute-done((bf16[512,256]{1,0:T(8,128)(2,1)}, bf16[512,256]{1,0:T(8,128)(2,1)}, u32[]{:S(2)}, u32[]{:S(2)}) %collective-permute-start.40) | collective-permute-done | bytes 262176 | tf_op jit(solution)/shard_map/ppermute | solution.py:266
  241.2 13.3 %collective-permute-done.39.rest_5_ = bf16[512,256]{1,0:T(8,128)(2,1)} collective-permute-done((bf16[512,256]{1,0:T(8,128)(2,1)}, bf16[512,256]{1,0:T(8,128)(2,1)}, u32[]{:S(2)}, u32[]{:S(2)}) %collective-permute-start.39) | collective-permute-done | bytes 262176 | tf_op jit(solution)/shard_map/ppermute | solution.py:266
  257.3 4.2 %output.1 = bf16[512,768]{1,0:T(8,128)(2,1)} custom-call(bf16[512,768]{1,0:T(8,128)(2,1)S(1)} %collective-permute-done.37.inflow_ref, f32[1,768]{1,0:T(1,128)S(1)} %broadcast_in_dim.4.gate_ref, bf16[512,256]{1,0:T(8,128)(2,1)S(1)} %collective-permute-done.16.rest_0_, bf16[512,256]{1,0:T(8,128)(2,1)} %collective-permute-done.36.rest_1_, ...), custom_call_target="tpu_custom_call" | custom-call | flops 1610612736 | bytes 5242880 | tf_op jit(solution)/shard_map/output/pallas_call | solution.py:249
  (142 shorter events, 38.6 us)
Async XLA Ops:
  6.5 104.7 %all-gather.3.cloned.1.call-start = ((), (), s32[]{:S(2)}) async-start(), calls=%async_computation | async-start | bytes 3932160 | tf_op jit(solution)/shard_map/all_gather | solution.py:327
  25.1 20.5 %collective-permute-start.1 = (bf16[384,512]{1,0:T(8,128)(2,1)S(1)}, bf16[384,512]{1,0:T(8,128)(2,1)S(1)}, u32[]{:S(2)}, u32[]{:S(2)}) collective-permute-start(bf16[384,512]{1,0:T(8,128)(2,1)S(1)} %get-tuple-element.95), channel_id=1, source_target_pairs={{0,16},{4,20},{8,24},{12,28},{16,0},{20,4},{24,8},{28,12},{1,17},{... | collective-permute-start | bytes 1179656 | tf_op jit(solution)/shard_map/ppermute | solution.py:266
  26.9 18.7 %collective-permute-start.8 = (bf16[384,512]{1,0:T(8,128)(2,1)S(1)}, bf16[384,512]{1,0:T(8,128)(2,1)S(1)}, u32[]{:S(2)}, u32[]{:S(2)}) collective-permute-start(bf16[384,512]{1,0:T(8,128)(2,1)S(1)} %get-tuple-element.107), channel_id=1, source_target_pairs={{0,24},{4,28},{8,16},{12,20},{16,8},{20,12},{24,0},{28,4},{1,25},{... | collective-permute-start | bytes 1179656 | tf_op jit(solution)/shard_map/ppermute | solution.py:266
  35.1 24.7 %collective-permute-start.11 = (bf16[384,512]{1,0:T(8,128)(2,1)S(1)}, bf16[384,512]{1,0:T(8,128)(2,1)S(1)}, u32[]{:S(2)}, u32[]{:S(2)}) collective-permute-start(bf16[384,512]{1,0:T(8,128)(2,1)S(1)} %get-tuple-element.112), channel_id=1, source_target_pairs={{0,20},{4,16},{8,28},{12,24},{16,4},{20,0},{24,12},{28,8},{1,21},{... | collective-permute-start | bytes 1179656 | tf_op jit(solution)/shard_map/ppermute | solution.py:266
  35.1 24.7 %collective-permute-start.6 = (bf16[384,512]{1,0:T(8,128)(2,1)S(1)}, bf16[384,512]{1,0:T(8,128)(2,1)S(1)}, u32[]{:S(2)}, u32[]{:S(2)}) collective-permute-start(bf16[384,512]{1,0:T(8,128)(2,1)S(1)} %get-tuple-element.102), channel_id=1, source_target_pairs={{0,12},{4,8},{8,4},{12,0},{16,28},{20,24},{24,20},{28,16},{1,13},{... | collective-permute-start | bytes 1179656 | tf_op jit(solution)/shard_map/ppermute | solution.py:266
  45.6 14.2 %collective-permute-start.9 = (bf16[384,512]{1,0:T(8,128)(2,1)S(1)}, bf16[384,512]{1,0:T(8,128)(2,1)S(1)}, u32[]{:S(2)}, u32[]{:S(2)}) collective-permute-start(bf16[384,512]{1,0:T(8,128)(2,1)S(1)} %get-tuple-element.108), channel_id=1, source_target_pairs={{0,4},{4,0},{8,12},{12,8},{16,20},{20,16},{24,28},{28,24},{1,5},{5... | collective-permute-start | bytes 1179656 | tf_op jit(solution)/shard_map/ppermute | solution.py:266
  45.6 14.1 %collective-permute-start.2 = (bf16[384,512]{1,0:T(8,128)(2,1)S(1)}, bf16[384,512]{1,0:T(8,128)(2,1)}, u32[]{:S(2)}, u32[]{:S(2)}) collective-permute-start(bf16[384,512]{1,0:T(8,128)(2,1)S(1)} %get-tuple-element.96), channel_id=1, source_target_pairs={{0,28},{4,24},{8,20},{12,16},{16,12},{20,8},{24,4},{28,0},{1,29},{... | collective-permute-start | bytes 1179656 | tf_op jit(solution)/shard_map/ppermute | solution.py:266
  64.6 25.1 %collective-permute-start.14 = (bf16[768,512]{1,0:T(8,128)(2,1)S(1)}, bf16[768,512]{1,0:T(8,128)(2,1)S(1)}, u32[]{:S(2)}, u32[]{:S(2)}) collective-permute-start(bf16[768,512]{1,0:T(8,128)(2,1)S(1)} %bitcast.26), channel_id=1, source_target_pairs={{0,1},{1,0},{2,3},{3,2},{4,5},{5,4},{6,7},{7,6},{8,9},{9,8},{10,11... | collective-permute-start | bytes 2359304 | tf_op jit(solution)/shard_map/ppermute | solution.py:266
  66.2 14.8 %collective-permute-start.5 = (f32[3072]{0:T(1024)S(1)}, f32[3072]{0:T(1024)S(1)}, u32[]{:S(2)}, u32[]{:S(2)}) collective-permute-start(f32[3072]{0:T(1024)S(1)} %bitcast.27), channel_id=1, source_target_pairs={{0,4},{4,8},{8,12},{12,16},{16,20},{20,24},{24,28},{28,0},{1,5},{5... | collective-permute-start | bytes 36872 | tf_op jit(solution)/shard_map/ppermute | solution.py:271
  81.0 16.4 %collective-permute-start.7 = (bf16[384,768]{1,0:T(8,128)(2,1)}, bf16[384,768]{1,0:T(8,128)(2,1)S(1)}, u32[]{:S(2)}, u32[]{:S(2)}) collective-permute-start(bf16[384,768]{1,0:T(8,128)(2,1)} %get-tuple-element.103), channel_id=1, source_target_pairs={{0,8},{4,12},{8,0},{12,4},{16,24},{20,28},{24,16},{28,20},{1,9},{5... | collective-permute-start | bytes 1769480 | tf_op jit(solution)/shard_map/ppermute | solution.py:266
  82.5 28.7 %collective-permute-start.12 = (bf16[384,768]{1,0:T(8,128)(2,1)}, bf16[384,768]{1,0:T(8,128)(2,1)S(1)}, u32[]{:S(2)}, u32[]{:S(2)}) collective-permute-start(bf16[384,768]{1,0:T(8,128)(2,1)} %get-tuple-element.113), channel_id=1, source_target_pairs={{0,16},{4,20},{8,24},{12,28},{16,0},{20,4},{24,8},{28,12},{1,17},{... | collective-permute-start | bytes 1769480 | tf_op jit(solution)/shard_map/ppermute | solution.py:266
  84.0 31.5 %collective-permute-start.3 = (bf16[384,768]{1,0:T(8,128)(2,1)}, bf16[384,768]{1,0:T(8,128)(2,1)S(1)}, u32[]{:S(2)}, u32[]{:S(2)}) collective-permute-start(bf16[384,768]{1,0:T(8,128)(2,1)} %get-tuple-element.97), channel_id=1, source_target_pairs={{0,24},{4,28},{8,16},{12,20},{16,8},{20,12},{24,0},{28,4},{1,25},{... | collective-permute-start | bytes 1769480 | tf_op jit(solution)/shard_map/ppermute | solution.py:266
  90.6 46.5 %collective-permute-start.17 = (bf16[768,512]{1,0:T(8,128)(2,1)}, bf16[768,512]{1,0:T(8,128)(2,1)}, u32[]{:S(2)}, u32[]{:S(2)}) collective-permute-start(bf16[768,512]{1,0:T(8,128)(2,1)} %bitcast.11), channel_id=1, source_target_pairs={{0,2},{1,3},{2,0},{3,1},{4,6},{5,7},{6,4},{7,5},{8,10},{9,11},{10,... | collective-permute-start | bytes 2359304 | tf_op jit(solution)/shard_map/ppermute | solution.py:266
  93.5 29.4 %collective-permute-start.10 = (bf16[384,768]{1,0:T(8,128)(2,1)}, bf16[384,768]{1,0:T(8,128)(2,1)S(1)}, u32[]{:S(2)}, u32[]{:S(2)}) collective-permute-start(bf16[384,768]{1,0:T(8,128)(2,1)} %get-tuple-element.109), channel_id=1, source_target_pairs={{0,12},{4,8},{8,4},{12,0},{16,28},{20,24},{24,20},{28,16},{1,13},{... | collective-permute-start | bytes 1769480 | tf_op jit(solution)/shard_map/ppermute | solution.py:266
  97.3 38.9 %collective-permute-start.13 = (bf16[384,768]{1,0:T(8,128)(2,1)}, bf16[384,768]{1,0:T(8,128)(2,1)}, u32[]{:S(2)}, u32[]{:S(2)}) collective-permute-start(bf16[384,768]{1,0:T(8,128)(2,1)} %get-tuple-element.115), channel_id=1, source_target_pairs={{0,20},{4,16},{8,28},{12,24},{16,4},{20,0},{24,12},{28,8},{1,21},{... | collective-permute-start | bytes 1769480 | tf_op jit(solution)/shard_map/ppermute | solution.py:266
  111.2 25.8 %collective-permute-start.15 = (bf16[384,768]{1,0:T(8,128)(2,1)}, bf16[384,768]{1,0:T(8,128)(2,1)}, u32[]{:S(2)}, u32[]{:S(2)}) collective-permute-start(bf16[384,768]{1,0:T(8,128)(2,1)} %get-tuple-element.120), channel_id=1, source_target_pairs={{0,28},{4,24},{8,20},{12,16},{16,12},{20,8},{24,4},{28,0},{1,29},{... | collective-permute-start | bytes 1769480 | tf_op jit(solution)/shard_map/ppermute | solution.py:266
  115.5 22.3 %collective-permute-start.4 = (bf16[384,768]{1,0:T(8,128)(2,1)S(1)}, bf16[384,768]{1,0:T(8,128)(2,1)S(1)}, u32[]{:S(2)}, u32[]{:S(2)}) collective-permute-start(bf16[384,768]{1,0:T(8,128)(2,1)S(1)} %copy-done.20), channel_id=1, source_target_pairs={{0,4},{4,0},{8,12},{12,8},{16,20},{20,16},{24,28},{28,24},{1,5},{5... | collective-permute-start | bytes 1769480 | tf_op jit(solution)/shard_map/ppermute | solution.py:266
  122.9 29.9 %collective-permute-start.20 = (bf16[384,512]{1,0:T(8,128)(2,1)S(1)}, bf16[384,512]{1,0:T(8,128)(2,1)S(1)}, u32[]{:S(2)}, u32[]{:S(2)}) collective-permute-start(bf16[384,512]{1,0:T(8,128)(2,1)S(1)} %copy-done.27), channel_id=1, source_target_pairs={{0,8},{4,12},{8,0},{12,4},{16,24},{20,28},{24,16},{28,20},{1,9},{5... | collective-permute-start | bytes 1179656 | tf_op jit(solution)/shard_map/ppermute | solution.py:266
  136.2 23.2 %collective-permute-start.22 = (bf16[384,512]{1,0:T(8,128)(2,1)S(1)}, bf16[384,512]{1,0:T(8,128)(2,1)S(1)}, u32[]{:S(2)}, u32[]{:S(2)}) collective-permute-start(bf16[384,512]{1,0:T(8,128)(2,1)S(1)} %copy-done.26), channel_id=1, source_target_pairs={{0,16},{4,20},{8,24},{12,28},{16,0},{20,4},{24,8},{28,12},{1,17},{... | collective-permute-start | bytes 1179656 | tf_op jit(solution)/shard_map/ppermute | solution.py:266
  137.1 24.4 %collective-permute-start.18 = (bf16[384,512]{1,0:T(8,128)(2,1)S(1)}, bf16[384,512]{1,0:T(8,128)(2,1)S(1)}, u32[]{:S(2)}, u32[]{:S(2)}) collective-permute-start(bf16[384,512]{1,0:T(8,128)(2,1)S(1)} %copy-done.25), channel_id=1, source_target_pairs={{0,24},{4,28},{8,16},{12,20},{16,8},{20,12},{24,0},{28,4},{1,25},{... | collective-permute-start | bytes 1179656 | tf_op jit(solution)/shard_map/ppermute | solution.py:266
  149.6 16.8 %collective-permute-start.21 = (bf16[384,512]{1,0:T(8,128)(2,1)S(1)}, bf16[384,512]{1,0:T(8,128)(2,1)S(1)}, u32[]{:S(2)}, u32[]{:S(2)}) collective-permute-start(bf16[384,512]{1,0:T(8,128)(2,1)S(1)} %copy-done.24), channel_id=1, source_target_pairs={{0,12},{4,8},{8,4},{12,0},{16,28},{20,24},{24,20},{28,16},{1,13},{... | collective-permute-start | bytes 1179656 | tf_op jit(solution)/shard_map/ppermute | solution.py:266
  152.8 22.0 %collective-permute-start.23 = (bf16[384,512]{1,0:T(8,128)(2,1)S(1)}, bf16[384,512]{1,0:T(8,128)(2,1)S(1)}, u32[]{:S(2)}, u32[]{:S(2)}) collective-permute-start(bf16[384,512]{1,0:T(8,128)(2,1)S(1)} %copy-done.23), channel_id=1, source_target_pairs={{0,20},{4,16},{8,28},{12,24},{16,4},{20,0},{24,12},{28,8},{1,21},{... | collective-permute-start | bytes 1179656 | tf_op jit(solution)/shard_map/ppermute | solution.py:266
  159.4 33.0 %collective-permute-start.28 = (bf16[768,512]{1,0:T(8,128)(2,1)S(1)}, bf16[768,512]{1,0:T(8,128)(2,1)S(1)}, u32[]{:S(2)}, u32[]{:S(2)}) collective-permute-start(bf16[768,512]{1,0:T(8,128)(2,1)S(1)} %bitcast.25), channel_id=1, source_target_pairs={{0,3},{1,2},{2,1},{3,0},{4,7},{5,6},{6,5},{7,4},{8,11},{9,10},{10,... | collective-permute-start | bytes 2359304 | tf_op jit(solution)/shard_map/ppermute | solution.py:266
  161.5 21.0 %collective-permute-start.19 = (bf16[384,512]{1,0:T(8,128)(2,1)S(1)}, bf16[384,512]{1,0:T(8,128)(2,1)S(1)}, u32[]{:S(2)}, u32[]{:S(2)}) collective-permute-start(bf16[384,512]{1,0:T(8,128)(2,1)S(1)} %copy-done.21), channel_id=1, source_target_pairs={{0,4},{4,0},{8,12},{12,8},{16,20},{20,16},{24,28},{28,24},{1,5},{5... | collective-permute-start | bytes 1179656 | tf_op jit(solution)/shard_map/ppermute | solution.py:266
  175.3 38.0 %collective-permute-start.26 = (bf16[512,256]{1,0:T(8,128)(2,1)S(1)}, bf16[512,256]{1,0:T(8,128)(2,1)S(1)}, u32[]{:S(2)}, u32[]{:S(2)}) collective-permute-start(bf16[512,256]{1,0:T(8,128)(2,1)S(1)} %collective-permute-done.16.rest_0_), channel_id=1, source_target_pairs={{0,2},{1,3},{2,0},{3,1},{4,6},{5,7},{6,4},{7,5},{8,10},{9,11},{10,... | collective-permute-start | bytes 786440 | tf_op jit(solution)/shard_map/ppermute | solution.py:266
  178.7 34.6 %collective-permute-start.25 = (bf16[512,256]{1,0:T(8,128)(2,1)S(1)}, bf16[512,256]{1,0:T(8,128)(2,1)S(1)}, u32[]{:S(2)}, u32[]{:S(2)}) collective-permute-start(bf16[512,256]{1,0:T(8,128)(2,1)S(1)} %collective-permute-done.16.rest_0_), channel_id=1, source_target_pairs={{0,1},{1,0},{2,3},{3,2},{4,5},{5,4},{6,7},{7,6},{8,9},{9,8},{10,11... | collective-permute-start | bytes 786440 | tf_op jit(solution)/shard_map/ppermute | solution.py:266
  182.5 30.9 %collective-permute-start.27 = (bf16[512,256]{1,0:T(8,128)(2,1)S(1)}, bf16[512,256]{1,0:T(8,128)(2,1)S(1)}, u32[]{:S(2)}, u32[]{:S(2)}) collective-permute-start(bf16[512,256]{1,0:T(8,128)(2,1)S(1)} %collective-permute-done.16.rest_0_), channel_id=1, source_target_pairs={{0,3},{1,2},{2,1},{3,0},{4,7},{5,6},{6,5},{7,4},{8,11},{9,10},{10,... | collective-permute-start | bytes 786440 | tf_op jit(solution)/shard_map/ppermute | solution.py:266
  192.5 20.9 %collective-permute-start.34 = (bf16[384,256]{1,0:T(8,128)(2,1)S(1)}, bf16[384,256]{1,0:T(8,128)(2,1)S(1)}, u32[]{:S(2)}, u32[]{:S(2)}) collective-permute-start(bf16[384,256]{1,0:T(8,128)(2,1)S(1)} %copy-done.31), channel_id=1, source_target_pairs={{0,20},{4,16},{8,28},{12,24},{16,4},{20,0},{24,12},{28,8},{1,21},{... | collective-permute-start | bytes 589832 | tf_op jit(solution)/shard_map/ppermute | solution.py:266
  193.3 20.1 %collective-permute-start.35 = (bf16[384,256]{1,0:T(8,128)(2,1)S(1)}, bf16[384,256]{1,0:T(8,128)(2,1)S(1)}, u32[]{:S(2)}, u32[]{:S(2)}) collective-permute-start(bf16[384,256]{1,0:T(8,128)(2,1)S(1)} %copy-done.30), channel_id=1, source_target_pairs={{0,28},{4,24},{8,20},{12,16},{16,12},{20,8},{24,4},{28,0},{1,29},{... | collective-permute-start | bytes 589832 | tf_op jit(solution)/shard_map/ppermute | solution.py:266
  229.9 24.6 %collective-permute-start.37 = (bf16[512,768]{1,0:T(8,128)(2,1)}, bf16[512,768]{1,0:T(8,128)(2,1)S(1)}, u32[]{:S(2)}, u32[]{:S(2)}) collective-permute-start(bf16[512,768]{1,0:T(8,128)(2,1)} %bitcast), channel_id=1, source_target_pairs={{0,4},{4,8},{8,12},{12,16},{16,20},{20,24},{24,28},{28,0},{1,5},{5... | collective-permute-start | bytes 2359304 | tf_op jit(solution)/shard_map/ppermute | solution.py:271
  232.6 21.9 %collective-permute-start.39 = (bf16[512,256]{1,0:T(8,128)(2,1)}, bf16[512,256]{1,0:T(8,128)(2,1)}, u32[]{:S(2)}, u32[]{:S(2)}) collective-permute-start(bf16[512,256]{1,0:T(8,128)(2,1)} %collective-permute-done.36.rest_1_), channel_id=1, source_target_pairs={{0,2},{1,3},{2,0},{3,1},{4,6},{5,7},{6,4},{7,5},{8,10},{9,11},{10,... | collective-permute-start | bytes 786440 | tf_op jit(solution)/shard_map/ppermute | solution.py:266
  232.6 21.9 %collective-permute-start.38 = (bf16[512,256]{1,0:T(8,128)(2,1)}, bf16[512,256]{1,0:T(8,128)(2,1)}, u32[]{:S(2)}, u32[]{:S(2)}) collective-permute-start(bf16[512,256]{1,0:T(8,128)(2,1)} %collective-permute-done.36.rest_1_), channel_id=1, source_target_pairs={{0,1},{1,0},{2,3},{3,2},{4,5},{5,4},{6,7},{7,6},{8,9},{9,8},{10,11... | collective-permute-start | bytes 786440 | tf_op jit(solution)/shard_map/ppermute | solution.py:266
  (45 other events, 593.5 us)
Sparse Core Ops, SparseCore 0:
  8.9 66.4 all-gather.2

commit v5 on v0

v5 whole, which is shorter than its diff:
```python
import functools

import jax
import jax.numpy as jnp
import numpy as np
from jax import lax
from jax.experimental import pallas as pl
from jax.experimental.pallas import tpu as pltpu
from jax.sharding import PartitionSpec as P

HD = 128
F32 = jnp.float32
BF16 = jnp.bfloat16
WHOLE = pl.BlockSpec(memory_space=pltpu.VMEM)
ANYWHERE = pl.BlockSpec(memory_space=pl.ANY)
SCALAR = pl.BlockSpec(memory_space=pltpu.SMEM)


def params(mebibytes):
    return pltpu.CompilerParams(vmem_limit_bytes=mebibytes * 1024 * 1024)


def in_hbm(array):
    return pltpu.with_memory_space_constraint(array, pltpu.HBM)


def cost(flops, size, exps=0):
    return pl.CostEstimate(flops=flops, bytes_accessed=size, transcendentals=exps)


def turned(left, right):
    return lax.dot_general(left, right, (((1,), (1,)), ((), ())), preferred_element_type=F32)


def pick_matrix(kinds, lanes, depth_step):
    period = 4 * lanes
    shape = (len(kinds) * lanes * depth_step, period * depth_step)
    row = lax.broadcasted_iota(jnp.int32, shape, 0)
    column = lax.broadcasted_iota(jnp.int32, shape, 1)
    source = row % depth_step * period + row // depth_step % lanes * 4 + kinds[0]
    source += row // (lanes * depth_step)
    return jnp.where(source == column, 1.0, 0.0).astype(BF16)


def split_kernel(lanes, plan, kinds, depth_step, order_ref, rows_ref, *rest):
    outs, pick = rest[:-1], rest[-1]
    depth = rows_ref.shape[1] // (4 * lanes)
    chunk = depth_step * 4 * lanes
    beside = 2 if depth % (2 * depth_step) == 0 else 1

    @pl.when(pl.program_id(0) == 0)
    def _():
        pick[...] = pick_matrix(kinds, lanes, depth_step)

    for first in range(0, depth, beside * depth_step):
        begin = first * 4 * lanes
        chunks = [
            rows_ref[0, begin + i * chunk : begin + (i + 1) * chunk, :] for i in range(beside)
        ]
        sorted_rows = jnp.dot(
            pick[...], jnp.concatenate(chunks, axis=1), preferred_element_type=F32
        ).astype(BF16)
        for i in range(beside):
            to = slice(first + i * depth_step, first + (i + 1) * depth_step)
            for out, columns in zip(outs, plan):
                for column, (kind, lane) in enumerate(columns):
                    at = (kinds.index(kind) * lanes + lane) * depth_step
                    out[0, to, column * HD : (column + 1) * HD] = sorted_rows[
                        at : at + depth_step, i * HD : (i + 1) * HD
                    ]


def split_blocks(rows, order, plan, lanes):
    depth = rows.shape[1] // (4 * lanes)
    depth_step = max(n for n in (16, 32, 64) if depth % n == 0 and n * 4 * lanes <= 256)
    kinds = sorted({kind for columns in plan for kind, _ in columns})
    blocks = order.shape[0]
    shapes = [(blocks, depth, len(columns) * HD) for columns in plan]
    return pl.pallas_call(
        functools.partial(split_kernel, lanes, plan, kinds, depth_step),
        grid_spec=pltpu.PrefetchScalarGridSpec(
            num_scalar_prefetch=1,
            grid=(blocks,),
            in_specs=[pl.BlockSpec((1,) + rows.shape[1:], lambda i, order: (order[i], 0, 0))],
            out_specs=[pl.BlockSpec((1,) + shape[1:], lambda i, order: (i, 0, 0)) for shape in shapes],
            scratch_shapes=[
                pltpu.VMEM((len(kinds) * lanes * depth_step, depth_step * 4 * lanes), BF16)
            ],
        ),
        out_shape=[jax.ShapeDtypeStruct(shape, BF16) for shape in shapes],
        compiler_params=params(16),
        cost_estimate=cost(0, 3 * blocks * rows.shape[1] * HD),
        name="split_blocks",
    )(order, in_hbm(rows))


def norm_kernel(tokens_ref, modulation_ref, out_ref):
    tokens = tokens_ref[...].astype(F32)
    center = jnp.mean(tokens, axis=1, keepdims=True)
    tokens = tokens - center
    spread = jnp.mean(tokens * tokens, axis=1, keepdims=True)
    normed = tokens * lax.rsqrt(spread + 1e-06)
    out_ref[...] = (normed * (1.0 + modulation_ref[0:1]) + modulation_ref[1:2]).astype(BF16)


def norm(tokens, modulation):
    patch, width = tokens.shape
    rows = 128
    return pl.pallas_call(
        norm_kernel,
        grid=(patch // rows,),
        in_specs=[
            pl.BlockSpec((rows, width), lambda i: (i, 0)),
            pl.BlockSpec((3, width), lambda i: (0, 0)),
        ],
        out_specs=pl.BlockSpec((rows, width), lambda i: (i, 0)),
        out_shape=jax.ShapeDtypeStruct((patch, width), BF16),
        compiler_params=params(14),
        cost_estimate=cost(10 * patch * width, 4 * patch * width),
        name="norm",
    )(in_hbm(tokens), modulation)


def attend_kernel(where_ref, normed_ref, matrix_ref, stale_ref, out_ref, own):
    patch = normed_ref.shape[0]
    parts = stale_ref.shape[1] // patch
    own[...] = jnp.dot(normed_ref[...], matrix_ref[...], preferred_element_type=F32).astype(BF16)
    starts = [
        pl.multiple_of(lax.rem(where_ref[0] + 1 + part, parts) * patch, patch)
        for part in range(parts - 1)
    ]
    scale = F32(np.log2(np.e) / np.sqrt(HD))
    keys = [stale_ref[0, pl.ds(start, patch), :] for start in starts] + [own[:, HD : 2 * HD]]
    values = [stale_ref[1, pl.ds(start, patch), :] for start in starts] + [own[:, 2 * HD :]]
    scores = [turned(own[:, :HD], key) for key in keys]
    top = jnp.max(functools.reduce(jnp.maximum, scores), axis=1, keepdims=True)
    total, summed = 0.0, 0.0
    for score, value in zip(scores, values):
        expo = jnp.exp2((score - top) * scale)
        total += expo
        summed += jnp.dot(expo.astype(BF16), value, preferred_element_type=F32)
    out_ref[...] = (summed / jnp.sum(total, axis=1, keepdims=True)).astype(BF16)


def attend(normed, matrix, where, stale, group):
    patch, width = normed.shape
    heads, keys = len(group), stale.shape[1]
    first = group[0]
    return pl.pallas_call(
        attend_kernel,
        grid_spec=pltpu.PrefetchScalarGridSpec(
            num_scalar_prefetch=1,
            grid=(heads,),
            in_specs=[
                pl.BlockSpec((patch, width), lambda h, where: (0, 0)),
                pl.BlockSpec((width, 3 * HD), lambda h, where: (0, h)),
                pl.BlockSpec((2, keys, HD), lambda h, where: (0, 0, first + h)),
            ],
            out_specs=pl.BlockSpec((patch, HD), lambda h, where: (0, h)),
            scratch_shapes=[pltpu.VMEM((patch, 3 * HD), BF16)],
        ),
        out_shape=jax.ShapeDtypeStruct((patch, heads * HD), BF16),
        compiler_params=params(32),
        cost_estimate=cost(
            2 * patch * heads * HD * (3 * width + 2 * keys), 2 * heads * HD * (3 * width + 2 * keys),
            patch * heads * keys,
        ),
        name="attend",
    )(where, normed, matrix, stale)


def output_kernel(tp, chunks, inflow_ref, gate_ref, *rest):
    attended, matrices, out_ref = rest[: tp * chunks], rest[tp * chunks : -1], rest[-1]
    mixed = 0.0
    for index in range(tp):
        own = attended[index * chunks : (index + 1) * chunks]
        left = jnp.concatenate([piece[...] for piece in own], axis=1)
        mixed += turned(left, matrices[index][...])
    out_ref[...] = (inflow_ref[...].astype(F32) + gate_ref[...] * mixed).astype(BF16)


def output(inflow, gate, attended, matrices):
    tp, chunks = len(attended), len(attended[0])
    patch, share = inflow.shape
    inner = matrices[0].shape[1]
    arrays = [inflow, gate] + [piece for own in attended for piece in own] + matrices
    return pl.pallas_call(
        functools.partial(output_kernel, tp, chunks),
        grid=(1,),
        in_specs=[pl.BlockSpec(array.shape, lambda i: (0, 0)) for array in arrays],
        out_specs=pl.BlockSpec(inflow.shape, lambda i: (0, 0)),
        out_shape=jax.ShapeDtypeStruct(inflow.shape, BF16),
        compiler_params=params(20),
        cost_estimate=cost(2 * patch * share * inner * tp, 2 * inner * tp * (share + patch)),
        name="output",
    )(*arrays)


def after(block, earlier):
    return lax.optimization_barrier((block, earlier))[0]


def swapped(block, axis, distance):
    return lax.ppermute(block, axis, [(i, i ^ distance) for i in range(lax.axis_size(axis))])


def handed_on(block):
    sections = lax.axis_size("section")
    return lax.ppermute(block, "section", [(i, (i + 1) % sections) for i in range(sections)])


def relayed(pieces):
    moved = lax.all_to_all(pieces, "section", split_axis=0, concat_axis=0, tiled=True)
    return moved.reshape(-1, moved.shape[2])


def local(block_weights, modulation, inflow, stale_cache, patch_index, assignment):
    sections, tp = lax.axis_size("section"), lax.axis_size("tp")
    rank = lax.axis_index("tp")
    blocks, depth, kinds, inner = block_weights.shape
    lanes = inner // HD
    share = inflow.shape[2]

    section_ids = jnp.arange(sections, dtype=jnp.int32)

    def block_of(section):
        return jnp.sum((assignment[None] == section[:, None]) * section_ids[None], axis=1)

    rows = block_weights.reshape(blocks, depth, kinds, lanes, HD)
    rows = rows.transpose(0, 1, 3, 2, 4).reshape(blocks, depth * lanes * kinds, HD)
    tokens = lax.all_gather(inflow[0], "tp", axis=1, tiled=True)

    out_plan = [[(3, head) for head in range(lanes)]]
    (to_out,) = split_blocks(rows, block_of((section_ids + sections - 1) % sections), out_plan, lanes)
    half = max(1, lanes // 2)
    groups = [tuple(range(half))] + [(head,) for head in range(half, lanes)]
    plan = [[(kind, head) for head in group for kind in range(3)] for group in groups]
    split = split_blocks(rows, block_of(section_ids), plan, lanes)

    to_out = relayed(to_out)
    normed = norm(tokens, modulation[0])
    matrices = []
    for distance in range(tp):
        held = lax.dynamic_slice_in_dim(to_out, (rank ^ distance) * share, share, 0)
        if distance > 2:
            held = after(held, matrices[distance - 2])
        matrices.append(swapped(held, "tp", distance) if distance else held)
    gate = handed_on(modulation[0, 2])

    waits = [[], [normed, gate, *matrices[1:3]], matrices[3:]]
    attended = [[] for _ in range(tp)]
    ready = normed
    for index, group in enumerate(groups):
        pieces = split[index]
        for earlier in waits[index] if index < len(waits) else []:
            pieces = after(pieces, earlier)
        matrix = relayed(pieces)
        own = attend(ready, matrix, patch_index, stale_cache[0], group)
        moved = handed_on(own)
        for distance in range(tp):
            attended[distance].append(swapped(moved, "tp", distance) if distance else moved)
        if index + 2 < len(groups):
            waits[index + 2] = [*waits[index + 2], *[own[-1] for own in attended]]
        elif index + 1 < len(groups):
            ready = functools.reduce(after, [own[-1] for own in attended], ready)
    carried = handed_on(after(inflow[0], moved))
    gate = lax.dynamic_slice_in_dim(gate, rank * share, share, 0)[None]
    return output(carried, gate, attended, matrices)[None]


def solution(mesh):
    spread = (
        P(None, "section", None, "tp"),
        P("section", None, None),
        P("section", None, "tp"),
        P("section", None, None, "tp"),
        P("section"),
        P(),
    )
    return jax.shard_map(
        local, mesh=mesh, in_specs=spread, out_specs=P("section", None, "tp"), check_vma=False
    )
```

time: 423 us -> 277 us (0.65)
  waiting for transfers between devices: 264 us -> 149 us
  Pallas kernels: 0 us -> 50.3 us
  local copies, waits for them, and re-layouts: 65.3 us -> 18.3 us
  matrix products: 40.5 us -> 0 us
  starting transfers between devices: 5.48 us -> 43.3 us
  other arithmetic: 33.2 us -> 0.87 us
    psum x1 -> x0, waiting for transfers between devices: 121 us -> none  [local(): lax.psum(partial_value.astype(jnp.bfloat16), 'tp').astype(jnp.float32)]
    ppermute x1 -> x17, waiting for transfers between devices: 12.3 us -> 83.2 us  [the longest x5 45.4 us: handed_on(): lax.ppermute(block, 'section', [(i, (i + 1) % sections) for i in range(se...]
    pallas_call x0 -> x7, Pallas kernels: none -> 50.3 us  [the longest x3 23 us: attend(): pl.pallas_call(attend_kernel, grid_spec=pltpu.PrefetchScalarGridSpec(num_...]
    all_to_all x1 -> x4, waiting for transfers between devices: 65.4 us -> 23.2 us  [relayed(): lax.all_to_all(pieces, 'section', split_axis=0, concat_axis=0, tiled=True)]
    dot_general x4 -> x0, matrix products: 40.5 us -> none  [the longest x1 15.5 us: local(): jnp.einsum('hps,shd->phd', probabilities, values_all.reshape(seq_len, hea...]
    ppermute x1 -> x17, starting transfers between devices: 0.06 us -> 24.7 us  [the longest x12 23.9 us: swapped(): lax.ppermute(block, axis, [(i, i ^ distance) for i in range(lax.axis_size...]
    all_gather x1, waiting for transfers between devices: 63.7 us -> 42.1 us  [local(): tokens = lax.all_gather(inflow[0], 'tp', axis=1, tiled=True)]
    gather x1 -> x0, local copies, waits for them, and re-layouts: 17.1 us -> none  [local(): ordered = jnp.take(block_weights, inverse, axis=0)]
  transfers between devices with their start and end apart: 4 -> 22, of which waited for: 4 -> 13; matrix products, arithmetic and copies ran while one was open for 2% -> 1% of each run, Pallas kernels for 0% -> 11%
where the time goes in v5:
time: 277 us; the launch traced here: 276 us
  waiting for transfers between devices  149 us (54%)
  Pallas kernels  50.3 us (18%)
  starting transfers between devices  43.3 us (16%)
  local copies, waits for them, and re-layouts  18.3 us (7%)
  between operations  14.3 us (5%)
    ppermute x5, waiting for transfers between devices, handed_on(): lax.ppermute(block, 'section', [(i, (i + 1) % sections) for i in range(se...  45.4 us
    all_gather x1, waiting for transfers between devices, local(): tokens = lax.all_gather(inflow[0], 'tp', axis=1, tiled=True)  42.1 us
    ppermute x12, waiting for transfers between devices, swapped(): lax.ppermute(block, axis, [(i, i ^ distance) for i in range(lax.axis_size...  37.7 us
    ppermute x12, starting transfers between devices, swapped(): lax.ppermute(block, axis, [(i, i ^ distance) for i in range(lax.axis_size...  23.9 us
    all_to_all x4, waiting for transfers between devices, relayed(): lax.all_to_all(pieces, 'section', split_axis=0, concat_axis=0, tiled=True)  23.2 us
    pallas_call x3, Pallas kernels, attend(): pl.pallas_call(attend_kernel, grid_spec=pltpu.PrefetchScalarGridSpec(num_...  23 us
    pallas_call x2, Pallas kernels, split_blocks(): pl.pallas_call(functools.partial(split_kernel, lanes, plan, kinds, depth_...  19.1 us
    all_to_all x4, starting transfers between devices, relayed(): lax.all_to_all(pieces, 'section', split_axis=0, concat_axis=0, tiled=True)  18.5 us
  transfers between devices with their start and end apart: 22, of which 13 were waited for; matrix products, arithmetic and copies ran while one was open for 1% of the time, Pallas kernels for 11%

profile of v5, /device:TPU:0, one launch (start us, length us, event | category | flops | bytes accessed | tf_op | source)
XLA Modules:
  0.0 276.3 jit_solution(4155644859732446393)
XLA Ops:
  7.4 10.1 %split_blocks.3 = bf16[8,384,512]{2,1,0:T(8,128)(2,1)} custom-call(s32[8]{0:T(128)S(1)} %get-tuple-element.41.order_ref, bf16[8,6144,128]{2,1,0:T(8,128)(2,1)} %bitcast.21), custom_call_target="tpu_custom_call" | custom-call | bytes 18874368 | tf_op jit(solution)/shard_map/split_blocks/pallas_call | solution.py:79
  17.5 5.2 %all-to-all-start = ((bf16[8,384,512]{2,1,0:T(8,128)(2,1)}), bf16[8,384,512]{2,1,0:T(8,128)(2,1)S(1)}, u32[]{:S(2)}, u32[]{:S(2)}) async-start(bf16[8,384,512]{2,1,0:T(8,128)(2,1)} %split_blocks.3), calls=%async_computation | async-start | bytes 6291456 | tf_op jit(solution)/shard_map/all_to_all | solution.py:213
  23.4 9.1 %split_blocks.2 = (bf16[8,384,768]{2,1,0:T(8,128)(2,1)S(1)}, bf16[8,384,384]{2,1,0:T(8,128)(2,1)S(1)}, bf16[8,384,384]{2,1,0:T(8,128)(2,1)S(1)}) custom-call(s32[8]{0:T(128)S(1)} %get-tuple-element.42.order_ref, bf16[8,6144,128]{2,1,0:T(8,128)(2,1)} %bitcast.22), custom_call_target="tpu_custom_call" | custom-call | bytes 18874368 | tf_op jit(solution)/shard_map/split_blocks/pallas_call | solution.py:79
  37.4 23.2 %all-to-all-done = bf16[8,384,512]{2,1,0:T(8,128)(2,1)S(1)} async-done(((bf16[8,384,512]{2,1,0:T(8,128)(2,1)}), bf16[8,384,512]{2,1,0:T(8,128)(2,1)S(1)}, u32[]{:S(2)}, u32[]{:S(2)}) %all-to-all-start) | async-done | bytes 3145760 | tf_op jit(solution)/shard_map/all_to_all | solution.py:213
  60.5 4.6 %all-to-all-start.2 = ((bf16[8,384,768]{2,1,0:T(8,128)(2,1)}), bf16[8,384,768]{2,1,0:T(8,128)(2,1)}, u32[]{:S(2)}, u32[]{:S(2)}) async-start(bf16[8,384,768]{2,1,0:T(8,128)(2,1)} %copy-done.3), calls=%async_computation.2 | async-start | bytes 9437184 | tf_op jit(solution)/shard_map/all_to_all | solution.py:213
  68.5 2.6 collective-permute-start.2
  71.1 42.1 %all-gather.3.cloned.1.call-done = bf16[1,512,3072]{2,1,0:T(8,128)(2,1)} async-done(((bf16[1,512,768]{2,1,0:T(8,128)(2,1)}), bf16[1,512,3072]{2,1,0:T(8,128)(2,1)}) %all-gather.3.cloned.1.call-update) | async-done | bytes 3145744 | tf_op jit(solution)/shard_map/all_gather | solution.py:231
  113.3 4.1 %norm.1.normed_ref = bf16[512,3072]{1,0:T(8,128)(2,1)S(1)} custom-call(bf16[512,3072]{1,0:T(8,128)(2,1)} %bitcast.24, f32[3,3072]{1,0:T(4,128)S(1)} %bitcast.20), custom_call_target="tpu_custom_call" | custom-call | flops 15728640 | bytes 6291456 | tf_op jit(solution)/shard_map/norm/pallas_call | solution.py:109
  117.4 2.2 collective-permute-done
  119.6 2.3 collective-permute-done.1.rest_13_
  121.9 4.4 %all-to-all-start.1 = ((bf16[8,384,384]{2,1,0:T(8,128)(2,1)}), bf16[8,384,384]{2,1,0:T(8,128)(2,1)}, u32[]{:S(2)}, u32[]{:S(2)}) async-start(bf16[8,384,384]{2,1,0:T(8,128)(2,1)} %copy-done.6), calls=%async_computation.1 | async-start | bytes 4718592 | tf_op jit(solution)/shard_map/all_to_all | solution.py:213
  126.9 2.5 collective-permute-start.7
  129.4 2.2 copy-done
  131.5 10.6 %attend.4 = bf16[512,256]{1,0:T(8,128)(2,1)S(1)} custom-call(s32[1]{0:T(128)S(6)} %copy.12.where_ref, bf16[512,3072]{1,0:T(8,128)(2,1)S(1)} %norm.1.normed_ref, bf16[3072,768]{1,0:T(8,128)(2,1)} %bitcast.11.matrix_ref, bf16[2,2048,512]{2,1,0:T(8,128)(2,1)S(1)} %bitcast.17), custom_call_target="tpu_custom_call" | custom-call | flops 3489660928 | bytes 6815744 | tf_op jit(solution)/shard_map/attend/pallas_call | solution.py:149
  142.3 16.1 %collective-permute-done.8.rest_0_ = bf16[512,256]{1,0:T(8,128)(2,1)S(1)} collective-permute-done((bf16[512,256]{1,0:T(8,128)(2,1)S(1)}, bf16[512,256]{1,0:T(8,128)(2,1)S(1)}, u32[]{:S(2)}, u32[]{:S(2)}) %collective-permute-start.8) | collective-permute-done | bytes 262176 | tf_op jit(solution)/shard_map/ppermute | solution.py:209
  158.4 2.8 collective-permute-start.9
  164.5 3.5 %collective-permute-done.9.rest_3_ = bf16[512,256]{1,0:T(8,128)(2,1)S(1)} collective-permute-done((bf16[512,256]{1,0:T(8,128)(2,1)S(1)}, bf16[512,256]{1,0:T(8,128)(2,1)S(1)}, u32[]{:S(2)}, u32[]{:S(2)}) %collective-permute-start.9) | collective-permute-done | bytes 262176 | tf_op jit(solution)/shard_map/ppermute | solution.py:204
  168.6 13.9 %collective-permute-done.10.rest_6_ = bf16[512,256]{1,0:T(8,128)(2,1)S(1)} collective-permute-done((bf16[512,256]{1,0:T(8,128)(2,1)S(1)}, bf16[512,256]{1,0:T(8,128)(2,1)S(1)}, u32[]{:S(2)}, u32[]{:S(2)}) %collective-permute-start.10) | collective-permute-done | bytes 262176 | tf_op jit(solution)/shard_map/ppermute | solution.py:204
  184.0 4.4 %all-to-all-start.3 = ((bf16[8,384,384]{2,1,0:T(8,128)(2,1)}), bf16[8,384,384]{2,1,0:T(8,128)(2,1)}, u32[]{:S(2)}, u32[]{:S(2)}) async-start(bf16[8,384,384]{2,1,0:T(8,128)(2,1)} %copy-done.5), calls=%async_computation.3 | async-start | bytes 4718592 | tf_op jit(solution)/shard_map/all_to_all | solution.py:213
  188.3 2.2 copy-done.1
  190.5 6.1 %attend.3 = bf16[512,128]{1,0:T(8,128)(2,1)S(1)} custom-call(s32[1]{0:T(128)S(6)} %copy.12.where_ref, bf16[512,3072]{1,0:T(8,128)(2,1)S(1)} %norm.1.normed_ref, bf16[3072,384]{1,0:T(8,128)(2,1)} %bitcast.9.matrix_ref, bf16[2,2048,512]{2,1,0:T(8,128)(2,1)S(1)} %bitcast.18), custom_call_target="tpu_custom_call" | custom-call | flops 1744830464 | bytes 3407872 | tf_op jit(solution)/shard_map/attend/pallas_call | solution.py:149
  197.2 21.8 %collective-permute-done.3.rest_1_ = bf16[512,128]{1,0:T(8,128)(2,1)S(1)} collective-permute-done((bf16[512,128]{1,0:T(8,128)(2,1)S(1)}, bf16[512,128]{1,0:T(8,128)(2,1)S(1)}, u32[]{:S(2)}, u32[]{:S(2)}) %collective-permute-start.3) | collective-permute-done | bytes 131104 | tf_op jit(solution)/shard_map/ppermute | solution.py:209
  219.1 5.4 %collective-permute-start.4 = (bf16[512,128]{1,0:T(8,128)(2,1)S(1)}, bf16[512,128]{1,0:T(8,128)(2,1)S(1)}, u32[]{:S(2)}, u32[]{:S(2)}) collective-permute-start(bf16[512,128]{1,0:T(8,128)(2,1)S(1)} %collective-permute-done.3.rest_1_), channel_id=1, source_target_pairs={{0,1},{1,0},{2,3},{3,2},{4,5},{5,4},{6,7},{7,6},{8,9},{9,8},{10,11... | collective-permute-start | bytes 393224 | tf_op jit(solution)/shard_map/ppermute | solution.py:204
  224.6 2.2 collective-permute-start.6
  226.9 3.2 %collective-permute-done.4.rest_4_ = bf16[512,128]{1,0:T(8,128)(2,1)S(1)} collective-permute-done((bf16[512,128]{1,0:T(8,128)(2,1)S(1)}, bf16[512,128]{1,0:T(8,128)(2,1)S(1)}, u32[]{:S(2)}, u32[]{:S(2)}) %collective-permute-start.4) | collective-permute-done | bytes 131104 | tf_op jit(solution)/shard_map/ppermute | solution.py:204
  230.7 3.9 %collective-permute-done.5.rest_7_ = bf16[512,128]{1,0:T(8,128)(2,1)S(1)} collective-permute-done((bf16[512,128]{1,0:T(8,128)(2,1)S(1)}, bf16[512,128]{1,0:T(8,128)(2,1)S(1)}, u32[]{:S(2)}, u32[]{:S(2)}) %collective-permute-start.5) | collective-permute-done | bytes 131104 | tf_op jit(solution)/shard_map/ppermute | solution.py:204
  236.0 2.2 copy-done.2
  238.2 6.3 %attend.5 = bf16[512,128]{1,0:T(8,128)(2,1)S(1)} custom-call(s32[1]{0:T(128)S(6)} %copy.12.where_ref, bf16[512,3072]{1,0:T(8,128)(2,1)S(1)} %norm.1.normed_ref, bf16[3072,384]{1,0:T(8,128)(2,1)} %bitcast.12.matrix_ref, bf16[2,2048,512]{2,1,0:T(8,128)(2,1)S(1)} %bitcast.19), custom_call_target="tpu_custom_call" | custom-call | flops 1744830464 | bytes 3407872 | tf_op jit(solution)/shard_map/attend/pallas_call | solution.py:149
  244.6 5.3 %collective-permute-done.12.rest_2_ = bf16[512,128]{1,0:T(8,128)(2,1)S(1)} collective-permute-done((bf16[512,128]{1,0:T(8,128)(2,1)S(1)}, bf16[512,128]{1,0:T(8,128)(2,1)S(1)}, u32[]{:S(2)}, u32[]{:S(2)}) %collective-permute-start.12) | collective-permute-done | bytes 131104 | tf_op jit(solution)/shard_map/ppermute | solution.py:209
  254.3 3.7 %collective-permute-done.16.rest_11_ = bf16[512,128]{1,0:T(8,128)(2,1)S(1)} collective-permute-done((bf16[512,128]{1,0:T(8,128)(2,1)S(1)}, bf16[512,128]{1,0:T(8,128)(2,1)S(1)}, u32[]{:S(2)}, u32[]{:S(2)}) %collective-permute-start.16) | collective-permute-done | bytes 131104 | tf_op jit(solution)/shard_map/ppermute | solution.py:204
  258.1 7.2 %collective-permute-done.15.rest_8_ = bf16[512,128]{1,0:T(8,128)(2,1)S(1)} collective-permute-done((bf16[512,128]{1,0:T(8,128)(2,1)S(1)}, bf16[512,128]{1,0:T(8,128)(2,1)S(1)}, u32[]{:S(2)}, u32[]{:S(2)}) %collective-permute-start.15) | collective-permute-done | bytes 131104 | tf_op jit(solution)/shard_map/ppermute | solution.py:204
  265.4 4.1 %output.1 = bf16[512,768]{1,0:T(8,128)(2,1)} custom-call(bf16[512,768]{1,0:T(8,128)(2,1)S(1)} %collective-permute-done.13.inflow_ref, f32[1,768]{1,0:T(1,128)S(1)} %broadcast_in_dim.4.gate_ref, bf16[512,256]{1,0:T(8,128)(2,1)S(1)} %collective-permute-done.8.rest_0_, bf16[512,128]{1,0:T(8,128)(2,1)S(1)} %collective-permute-done.3.rest_1_, ...), custom_call_target="tpu_custom_call" | custom-call | flops 1610612736 | bytes 5242880 | tf_op jit(solution)/shard_map/output/pallas_call | solution.py:187
  (73 shorter events, 22.7 us)
Async XLA Ops:
  17.5 43.1 %all-to-all-start = ((bf16[8,384,512]{2,1,0:T(8,128)(2,1)}), bf16[8,384,512]{2,1,0:T(8,128)(2,1)S(1)}, u32[]{:S(2)}, u32[]{:S(2)}) async-start(bf16[8,384,512]{2,1,0:T(8,128)(2,1)} %split_blocks.3), calls=%async_computation | async-start | bytes 6291456 | tf_op jit(solution)/shard_map/all_to_all | solution.py:213
  22.6 90.6 %all-gather.3.cloned.1.call-start = ((), (), s32[]{:S(2)}) async-start(), calls=%async_computation.4 | async-start | bytes 3932160 | tf_op jit(solution)/shard_map/all_gather | solution.py:231
  60.5 61.3 %all-to-all-start.2 = ((bf16[8,384,768]{2,1,0:T(8,128)(2,1)}), bf16[8,384,768]{2,1,0:T(8,128)(2,1)}, u32[]{:S(2)}, u32[]{:S(2)}) async-start(bf16[8,384,768]{2,1,0:T(8,128)(2,1)} %copy-done.3), calls=%async_computation.2 | async-start | bytes 9437184 | tf_op jit(solution)/shard_map/all_to_all | solution.py:213
  65.2 5.9 %copy-start.22 = (f32[1,3,3072]{2,0,1:T(1,128)S(1)}, f32[1,3,3072]{2,0,1:T(1,128)}, u32[]{:S(2)}) copy-start(f32[1,3,3072]{2,0,1:T(1,128)} %param.7) | copy-start | bytes 110596
  66.9 54.9 %collective-permute-start.1 = (bf16[768,512]{1,0:T(8,128)(2,1)}, bf16[768,512]{1,0:T(8,128)(2,1)}, u32[]{:S(2)}, u32[]{:S(2)}) collective-permute-start(bf16[768,512]{1,0:T(8,128)(2,1)} %get-tuple-element.46), channel_id=1, source_target_pairs={{0,1},{1,0},{2,3},{3,2},{4,5},{5,4},{6,7},{7,6},{8,9},{9,8},{10,11... | collective-permute-start | bytes 2359304 | tf_op jit(solution)/shard_map/ppermute | solution.py:204
  68.5 53.3 %collective-permute-start.2 = (bf16[768,512]{1,0:T(8,128)(2,1)}, bf16[768,512]{1,0:T(8,128)(2,1)}, u32[]{:S(2)}, u32[]{:S(2)}) collective-permute-start(bf16[768,512]{1,0:T(8,128)(2,1)} %get-tuple-element.45), channel_id=1, source_target_pairs={{0,2},{1,3},{2,0},{3,1},{4,6},{5,7},{6,4},{7,5},{8,10},{9,11},{10,... | collective-permute-start | bytes 2359304 | tf_op jit(solution)/shard_map/ppermute | solution.py:204
  71.1 48.5 %collective-permute-start = (f32[3072]{0:T(1024)S(1)}, f32[3072]{0:T(1024)S(1)}, u32[]{:S(2)}, u32[]{:S(2)}) collective-permute-start(f32[3072]{0:T(1024)S(1)} %bitcast.26), channel_id=1, source_target_pairs={{0,4},{4,8},{8,12},{12,16},{16,20},{20,24},{24,28},{28,0},{1,5},{5... | collective-permute-start | bytes 36872 | tf_op jit(solution)/shard_map/ppermute | solution.py:209
  121.9 62.1 %all-to-all-start.1 = ((bf16[8,384,384]{2,1,0:T(8,128)(2,1)}), bf16[8,384,384]{2,1,0:T(8,128)(2,1)}, u32[]{:S(2)}, u32[]{:S(2)}) async-start(bf16[8,384,384]{2,1,0:T(8,128)(2,1)} %copy-done.6), calls=%async_computation.1 | async-start | bytes 4718592 | tf_op jit(solution)/shard_map/all_to_all | solution.py:213
  126.9 36.6 %collective-permute-start.7 = (bf16[768,512]{1,0:T(8,128)(2,1)}, bf16[768,512]{1,0:T(8,128)(2,1)S(1)}, u32[]{:S(2)}, u32[]{:S(2)}) collective-permute-start(bf16[768,512]{1,0:T(8,128)(2,1)} %get-tuple-element.33), channel_id=1, source_target_pairs={{0,3},{1,2},{2,1},{3,0},{4,7},{5,6},{6,5},{7,4},{8,11},{9,10},{10,... | collective-permute-start | bytes 2359304 | tf_op jit(solution)/shard_map/ppermute | solution.py:204
  142.1 16.3 %collective-permute-start.8 = (bf16[512,256]{1,0:T(8,128)(2,1)S(1)}, bf16[512,256]{1,0:T(8,128)(2,1)S(1)}, u32[]{:S(2)}, u32[]{:S(2)}) collective-permute-start(bf16[512,256]{1,0:T(8,128)(2,1)S(1)} %attend.4), channel_id=1, source_target_pairs={{0,4},{4,8},{8,12},{12,16},{16,20},{20,24},{24,28},{28,0},{1,5},{5... | collective-permute-start | bytes 786440 | tf_op jit(solution)/shard_map/ppermute | solution.py:209
  158.4 9.5 %collective-permute-start.9 = (bf16[512,256]{1,0:T(8,128)(2,1)S(1)}, bf16[512,256]{1,0:T(8,128)(2,1)S(1)}, u32[]{:S(2)}, u32[]{:S(2)}) collective-permute-start(bf16[512,256]{1,0:T(8,128)(2,1)S(1)} %collective-permute-done.8.rest_0_), channel_id=1, source_target_pairs={{0,1},{1,0},{2,3},{3,2},{4,5},{5,4},{6,7},{7,6},{8,9},{9,8},{10,11... | collective-permute-start | bytes 786440 | tf_op jit(solution)/shard_map/ppermute | solution.py:204
  161.2 21.4 %collective-permute-start.10 = (bf16[512,256]{1,0:T(8,128)(2,1)S(1)}, bf16[512,256]{1,0:T(8,128)(2,1)S(1)}, u32[]{:S(2)}, u32[]{:S(2)}) collective-permute-start(bf16[512,256]{1,0:T(8,128)(2,1)S(1)} %collective-permute-done.8.rest_0_), channel_id=1, source_target_pairs={{0,2},{1,3},{2,0},{3,1},{4,6},{5,7},{6,4},{7,5},{8,10},{9,11},{10,... | collective-permute-start | bytes 786440 | tf_op jit(solution)/shard_map/ppermute | solution.py:204
  161.4 21.9 %collective-permute-start.11 = (bf16[512,256]{1,0:T(8,128)(2,1)S(1)}, bf16[512,256]{1,0:T(8,128)(2,1)S(1)}, u32[]{:S(2)}, u32[]{:S(2)}) collective-permute-start(bf16[512,256]{1,0:T(8,128)(2,1)S(1)} %collective-permute-done.8.rest_0_), channel_id=1, source_target_pairs={{0,3},{1,2},{2,1},{3,0},{4,7},{5,6},{6,5},{7,4},{8,11},{9,10},{10,... | collective-permute-start | bytes 786440 | tf_op jit(solution)/shard_map/ppermute | solution.py:204
  184.0 52.0 %all-to-all-start.3 = ((bf16[8,384,384]{2,1,0:T(8,128)(2,1)}), bf16[8,384,384]{2,1,0:T(8,128)(2,1)}, u32[]{:S(2)}, u32[]{:S(2)}) async-start(bf16[8,384,384]{2,1,0:T(8,128)(2,1)} %copy-done.5), calls=%async_computation.3 | async-start | bytes 4718592 | tf_op jit(solution)/shard_map/all_to_all | solution.py:213
  196.6 22.5 %collective-permute-start.3 = (bf16[512,128]{1,0:T(8,128)(2,1)S(1)}, bf16[512,128]{1,0:T(8,128)(2,1)S(1)}, u32[]{:S(2)}, u32[]{:S(2)}) collective-permute-start(bf16[512,128]{1,0:T(8,128)(2,1)S(1)} %attend.3), channel_id=1, source_target_pairs={{0,4},{4,8},{8,12},{12,16},{16,20},{20,24},{24,28},{28,0},{1,5},{5... | collective-permute-start | bytes 393224 | tf_op jit(solution)/shard_map/ppermute | solution.py:209
  219.1 11.0 %collective-permute-start.4 = (bf16[512,128]{1,0:T(8,128)(2,1)S(1)}, bf16[512,128]{1,0:T(8,128)(2,1)S(1)}, u32[]{:S(2)}, u32[]{:S(2)}) collective-permute-start(bf16[512,128]{1,0:T(8,128)(2,1)S(1)} %collective-permute-done.3.rest_1_), channel_id=1, source_target_pairs={{0,1},{1,0},{2,3},{3,2},{4,5},{5,4},{6,7},{7,6},{8,9},{9,8},{10,11... | collective-permute-start | bytes 393224 | tf_op jit(solution)/shard_map/ppermute | solution.py:204
  224.5 10.1 %collective-permute-start.5 = (bf16[512,128]{1,0:T(8,128)(2,1)S(1)}, bf16[512,128]{1,0:T(8,128)(2,1)S(1)}, u32[]{:S(2)}, u32[]{:S(2)}) collective-permute-start(bf16[512,128]{1,0:T(8,128)(2,1)S(1)} %collective-permute-done.3.rest_1_), channel_id=1, source_target_pairs={{0,2},{1,3},{2,0},{3,1},{4,6},{5,7},{6,4},{7,5},{8,10},{9,11},{10,... | collective-permute-start | bytes 393224 | tf_op jit(solution)/shard_map/ppermute | solution.py:204
  224.6 10.7 %collective-permute-start.6 = (bf16[512,128]{1,0:T(8,128)(2,1)S(1)}, bf16[512,128]{1,0:T(8,128)(2,1)S(1)}, u32[]{:S(2)}, u32[]{:S(2)}) collective-permute-start(bf16[512,128]{1,0:T(8,128)(2,1)S(1)} %collective-permute-done.3.rest_1_), channel_id=1, source_target_pairs={{0,3},{1,2},{2,1},{3,0},{4,7},{5,6},{6,5},{7,4},{8,11},{9,10},{10,... | collective-permute-start | bytes 393224 | tf_op jit(solution)/shard_map/ppermute | solution.py:204
  238.2 11.7 %copy-start.21 = (bf16[1,512,768]{2,1,0:T(8,128)(2,1)S(1)}, bf16[1,512,768]{2,1,0:T(8,128)(2,1)}, u32[]{:S(2)}) copy-start(bf16[1,512,768]{2,1,0:T(8,128)(2,1)} %param.8) | copy-start | bytes 2359300
  238.2 27.1 %copy-start.4 = (bf16[768,512]{1,0:T(8,128)(2,1)S(1)}, bf16[768,512]{1,0:T(8,128)(2,1)}, u32[]{:S(2)}) copy-start(bf16[768,512]{1,0:T(8,128)(2,1)} %get-tuple-element.43.rest_12_) | copy-start | bytes 2359300
  238.2 27.1 %copy-start.8 = (bf16[768,512]{1,0:T(8,128)(2,1)S(1)}, bf16[768,512]{1,0:T(8,128)(2,1)}, u32[]{:S(2)}) copy-start(bf16[768,512]{1,0:T(8,128)(2,1)} %copy-done.7) | copy-start | bytes 2359300
  238.2 27.1 %copy-start.10 = (bf16[512,256]{1,0:T(8,128)(2,1)S(1)}, bf16[512,256]{1,0:T(8,128)(2,1)}, u32[]{:S(2)}) copy-start(bf16[512,256]{1,0:T(8,128)(2,1)} %copy-done.9) | copy-start | bytes 786436
  238.2 27.1 %copy-start.12 = (bf16[512,256]{1,0:T(8,128)(2,1)S(1)}, bf16[512,256]{1,0:T(8,128)(2,1)}, u32[]{:S(2)}) copy-start(bf16[512,256]{1,0:T(8,128)(2,1)} %copy-done.11) | copy-start | bytes 786436
  238.2 27.1 %copy-start.14 = (bf16[512,256]{1,0:T(8,128)(2,1)S(1)}, bf16[512,256]{1,0:T(8,128)(2,1)}, u32[]{:S(2)}) copy-start(bf16[512,256]{1,0:T(8,128)(2,1)} %copy-done.13) | copy-start | bytes 786436
  238.2 27.1 %copy-start.16 = (bf16[512,128]{1,0:T(8,128)(2,1)S(1)}, bf16[512,128]{1,0:T(8,128)(2,1)}, u32[]{:S(2)}) copy-start(bf16[512,128]{1,0:T(8,128)(2,1)} %copy-done.15) | copy-start | bytes 393220
  238.2 27.1 %copy-start.18 = (bf16[512,128]{1,0:T(8,128)(2,1)S(1)}, bf16[512,128]{1,0:T(8,128)(2,1)}, u32[]{:S(2)}) copy-start(bf16[512,128]{1,0:T(8,128)(2,1)} %copy-done.17) | copy-start | bytes 393220
  238.2 27.1 %copy-start.20 = (bf16[512,128]{1,0:T(8,128)(2,1)S(1)}, bf16[512,128]{1,0:T(8,128)(2,1)}, u32[]{:S(2)}) copy-start(bf16[512,128]{1,0:T(8,128)(2,1)} %copy-done.19) | copy-start | bytes 393220
  244.5 5.3 %collective-permute-start.12 = (bf16[512,128]{1,0:T(8,128)(2,1)S(1)}, bf16[512,128]{1,0:T(8,128)(2,1)S(1)}, u32[]{:S(2)}, u32[]{:S(2)}) collective-permute-start(bf16[512,128]{1,0:T(8,128)(2,1)S(1)} %attend.5), channel_id=1, source_target_pairs={{0,4},{4,8},{8,12},{12,16},{16,20},{20,24},{24,28},{28,0},{1,5},{5... | collective-permute-start | bytes 393224 | tf_op jit(solution)/shard_map/ppermute | solution.py:209
  249.8 15.4 %collective-permute-start.13 = (bf16[512,768]{1,0:T(8,128)(2,1)S(1)}, bf16[512,768]{1,0:T(8,128)(2,1)S(1)}, u32[]{:S(2)}, u32[]{:S(2)}) collective-permute-start(bf16[512,768]{1,0:T(8,128)(2,1)S(1)} %bitcast.25), channel_id=1, source_target_pairs={{0,4},{4,8},{8,12},{12,16},{16,20},{20,24},{24,28},{28,0},{1,5},{5... | collective-permute-start | bytes 2359304 | tf_op jit(solution)/shard_map/ppermute | solution.py:209
  249.8 8.2 %collective-permute-start.16 = (bf16[512,128]{1,0:T(8,128)(2,1)S(1)}, bf16[512,128]{1,0:T(8,128)(2,1)S(1)}, u32[]{:S(2)}, u32[]{:S(2)}) collective-permute-start(bf16[512,128]{1,0:T(8,128)(2,1)S(1)} %collective-permute-done.12.rest_2_), channel_id=1, source_target_pairs={{0,3},{1,2},{2,1},{3,0},{4,7},{5,6},{6,5},{7,4},{8,11},{9,10},{10,... | collective-permute-start | bytes 393224 | tf_op jit(solution)/shard_map/ppermute | solution.py:204
  251.4 13.8 %collective-permute-start.15 = (bf16[512,128]{1,0:T(8,128)(2,1)S(1)}, bf16[512,128]{1,0:T(8,128)(2,1)S(1)}, u32[]{:S(2)}, u32[]{:S(2)}) collective-permute-start(bf16[512,128]{1,0:T(8,128)(2,1)S(1)} %collective-permute-done.12.rest_2_), channel_id=1, source_target_pairs={{0,2},{1,3},{2,0},{3,1},{4,6},{5,7},{6,4},{7,5},{8,10},{9,11},{10,... | collective-permute-start | bytes 393224 | tf_op jit(solution)/shard_map/ppermute | solution.py:204
  252.7 12.6 %collective-permute-start.14 = (bf16[512,128]{1,0:T(8,128)(2,1)S(1)}, bf16[512,128]{1,0:T(8,128)(2,1)S(1)}, u32[]{:S(2)}, u32[]{:S(2)}) collective-permute-start(bf16[512,128]{1,0:T(8,128)(2,1)S(1)} %collective-permute-done.12.rest_2_), channel_id=1, source_target_pairs={{0,1},{1,0},{2,3},{3,2},{4,5},{5,4},{6,7},{7,6},{8,9},{9,8},{10,11... | collective-permute-start | bytes 393224 | tf_op jit(solution)/shard_map/ppermute | solution.py:204
  (13 other events, 16.5 us)
Sparse Core Ops, SparseCore 0:
  25.0 88.2 all-gather.2

commit v6 on v5

--- a/solution.py
+++ b/solution.py
@@ -42,7 +42,7 @@
     return jnp.where(source == column, 1.0, 0.0).astype(BF16)
 
 
-def split_kernel(lanes, plan, kinds, depth_step, order_ref, rows_ref, *rest):
+def split_kernel(lanes, plan, single, kinds, depth_step, order_ref, to_ref, rows_ref, *rest):
     outs, pick = rest[:-1], rest[-1]
     depth = rows_ref.shape[1] // (4 * lanes)
     chunk = depth_step * 4 * lanes
@@ -51,6 +51,9 @@
     @pl.when(pl.program_id(0) == 0)
     def _():
         pick[...] = pick_matrix(kinds, lanes, depth_step)
+
+    def store(out, to, columns, values):
+        out[to, columns] = values
 
     for first in range(0, depth, beside * depth_step):
         begin = first * 4 * lanes
@@ -65,33 +68,46 @@
             for out, columns in zip(outs, plan):
                 for column, (kind, lane) in enumerate(columns):
                     at = (kinds.index(kind) * lanes + lane) * depth_step
-                    out[0, to, column * HD : (column + 1) * HD] = sorted_rows[
-                        at : at + depth_step, i * HD : (i + 1) * HD
-                    ]
-
-
-def split_blocks(rows, order, plan, lanes):
+                    values = sorted_rows[at : at + depth_step, i * HD : (i + 1) * HD]
+                    spot = slice(column * HD, (column + 1) * HD)
+                    if columns is not plan[-1] or not single:
+                        out[0, to, spot] = values
+                        continue
+                    for block, own in enumerate(outs[len(plan) - 1 :]):
+                        pl.when(pl.program_id(0) == block)(
+                            functools.partial(store, own, to, spot, values)
+                        )
+
+
+def split_blocks(rows, order, to, plan, lanes, single=False):
     depth = rows.shape[1] // (4 * lanes)
     depth_step = max(n for n in (16, 32, 64) if depth % n == 0 and n * 4 * lanes <= 256)
     kinds = sorted({kind for columns in plan for kind, _ in columns})
     blocks = order.shape[0]
     shapes = [(blocks, depth, len(columns) * HD) for columns in plan]
-    return pl.pallas_call(
-        functools.partial(split_kernel, lanes, plan, kinds, depth_step),
+    out_specs = [
+        pl.BlockSpec((1,) + shape[1:], lambda i, order, to: (to[i], 0, 0)) for shape in shapes
+    ]
+    if single:
+        alone = shapes.pop()[1:]
+        shapes += [alone] * blocks
+        out_specs[-1:] = [pl.BlockSpec(alone, lambda i, order, to: (0, 0))] * blocks
+    return pl.pallas_call(
+        functools.partial(split_kernel, lanes, plan, single, kinds, depth_step),
         grid_spec=pltpu.PrefetchScalarGridSpec(
-            num_scalar_prefetch=1,
+            num_scalar_prefetch=2,
             grid=(blocks,),
-            in_specs=[pl.BlockSpec((1,) + rows.shape[1:], lambda i, order: (order[i], 0, 0))],
-            out_specs=[pl.BlockSpec((1,) + shape[1:], lambda i, order: (i, 0, 0)) for shape in shapes],
+            in_specs=[pl.BlockSpec((1,) + rows.shape[1:], lambda i, order, to: (order[i], 0, 0))],
+            out_specs=out_specs,
             scratch_shapes=[
                 pltpu.VMEM((len(kinds) * lanes * depth_step, depth_step * 4 * lanes), BF16)
             ],
         ),
         out_shape=[jax.ShapeDtypeStruct(shape, BF16) for shape in shapes],
-        compiler_params=params(16),
+        compiler_params=params(24),
         cost_estimate=cost(0, 3 * blocks * rows.shape[1] * HD),
         name="split_blocks",
-    )(order, in_hbm(rows))
+    )(order, to, in_hbm(rows))
 
 
 def norm_kernel(tokens_ref, modulation_ref, out_ref):
@@ -214,14 +230,40 @@
     return moved.reshape(-1, moved.shape[2])
 
 
+def place_kernel(count, slots_ref, *rest):
+    pieces, (out_ref, sems) = rest[:count], rest[count:]
+    copies = [
+        pltpu.make_async_copy(piece, out_ref.at[slots_ref[index]], sems.at[index])
+        for index, piece in enumerate(pieces)
+    ]
+    for copy in copies:
+        copy.start()
+    for copy in copies:
+        copy.wait()
+
+
+def placed(pieces, slots):
+    return pl.pallas_call(
+        functools.partial(place_kernel, len(pieces)),
+        in_specs=[SCALAR] + [ANYWHERE] * len(pieces),
+        out_specs=ANYWHERE,
+        out_shape=jax.ShapeDtypeStruct((len(pieces),) + pieces[0].shape, BF16),
+        scratch_shapes=[pltpu.SemaphoreType.DMA((len(pieces),))],
+        compiler_params=params(4),
+        cost_estimate=cost(0, 4 * len(pieces) * pieces[0].size),
+        name="placed",
+    )(slots, *[in_hbm(piece) for piece in pieces])
+
+
 def local(block_weights, modulation, inflow, stale_cache, patch_index, assignment):
     sections, tp = lax.axis_size("section"), lax.axis_size("tp")
-    rank = lax.axis_index("tp")
+    here, rank = lax.axis_index("section"), lax.axis_index("tp")
     blocks, depth, kinds, inner = block_weights.shape
     lanes = inner // HD
     share = inflow.shape[2]
 
     section_ids = jnp.arange(sections, dtype=jnp.int32)
+    sources = here ^ section_ids
 
     def block_of(section):
         return jnp.sum((assignment[None] == section[:, None]) * section_ids[None], axis=1)
@@ -229,43 +271,59 @@
     rows = block_weights.reshape(blocks, depth, kinds, lanes, HD)
     rows = rows.transpose(0, 1, 3, 2, 4).reshape(blocks, depth * lanes * kinds, HD)
     tokens = lax.all_gather(inflow[0], "tp", axis=1, tiled=True)
+    normed = norm(tokens, modulation[0])
+    gate = handed_on(modulation[0, 2])
 
     out_plan = [[(3, head) for head in range(lanes)]]
-    (to_out,) = split_blocks(rows, block_of((section_ids + sections - 1) % sections), out_plan, lanes)
+    before = block_of((section_ids + sections - 1) % sections)
+    (to_out,) = split_blocks(rows, before, section_ids, out_plan, lanes)
     half = max(1, lanes // 2)
     groups = [tuple(range(half))] + [(head,) for head in range(half, lanes)]
     plan = [[(kind, head) for head in group for kind in range(3)] for group in groups]
-    split = split_blocks(rows, block_of(section_ids), plan, lanes)
+    alone = len(groups) > 1
+    split = split_blocks(rows, after(block_of(sources), to_out), sources, plan, lanes, alone)
+
+    pieces = list(split[len(groups) - 1 :]) if alone else []
+    chain = []
+    for distance in sorted(range(1, len(pieces)), key=lambda d: (d == 1, d % 2, d)):
+        piece = pieces[distance]
+        if len(chain) >= 3:
+            piece = after(piece, chain[-3])
+        chain.append(swapped(piece, "section", distance))
+        pieces[distance] = chain[-1]
 
     to_out = relayed(to_out)
-    normed = norm(tokens, modulation[0])
     matrices = []
     for distance in range(tp):
         held = lax.dynamic_slice_in_dim(to_out, (rank ^ distance) * share, share, 0)
-        if distance > 2:
-            held = after(held, matrices[distance - 2])
         matrices.append(swapped(held, "tp", distance) if distance else held)
-    gate = handed_on(modulation[0, 2])
-
-    waits = [[], [normed, gate, *matrices[1:3]], matrices[3:]]
+
     attended = [[] for _ in range(tp)]
-    ready = normed
-    for index, group in enumerate(groups):
-        pieces = split[index]
-        for earlier in waits[index] if index < len(waits) else []:
-            pieces = after(pieces, earlier)
-        matrix = relayed(pieces)
-        own = attend(ready, matrix, patch_index, stale_cache[0], group)
+
+    def share_out(group, matrix, tokens):
+        own = attend(tokens, matrix, patch_index, stale_cache[0], group)
         moved = handed_on(own)
         for distance in range(tp):
             attended[distance].append(swapped(moved, "tp", distance) if distance else moved)
-        if index + 2 < len(groups):
-            waits[index + 2] = [*waits[index + 2], *[own[-1] for own in attended]]
-        elif index + 1 < len(groups):
-            ready = functools.reduce(after, [own[-1] for own in attended], ready)
+        return moved
+
+    def waiting(block, *earlier):
+        return functools.reduce(after, earlier, block)
+
+    first = relayed(waiting(split[0], normed, gate, *chain))
+    if alone:
+        last = relayed(waiting(split[1], *matrices[1:3]))
+        matrix = placed(pieces, sources)
+        share_out(groups[2], matrix.reshape(-1, matrix.shape[2]), normed)
+        share_out(groups[0], first, normed)
+        ready = waiting(normed, *matrices[3:], *[part for own in attended for part in own])
+        moved = share_out(groups[1], last, ready)
+    else:
+        moved = share_out(groups[0], first, normed)
+    heads_first = [own[1:2] + own[2:] + own[:1] if alone else own for own in attended]
     carried = handed_on(after(inflow[0], moved))
     gate = lax.dynamic_slice_in_dim(gate, rank * share, share, 0)[None]
-    return output(carried, gate, attended, matrices)[None]
+    return output(carried, gate, heads_first, matrices)[None]
 
 
 def solution(mesh):

time: 277 us -> 272 us (0.982)
  waiting for transfers between devices: 149 us -> 112 us
  Pallas kernels: 50.3 us -> 77.6 us
  starting transfers between devices: 43.3 us -> 49.6 us
    ppermute x12 -> x19, waiting for transfers between devices: 37.7 us -> 86.6 us  [swapped(): lax.ppermute(block, axis, [(i, i ^ distance) for i in range(lax.axis_size...]
    all_gather x1, waiting for transfers between devices: 42.1 us -> 0.02 us  [local(): tokens = lax.all_gather(inflow[0], 'tp', axis=1, tiled=True)]
    ppermute x5, waiting for transfers between devices: 45.4 us -> 14.1 us  [handed_on(): lax.ppermute(block, 'section', [(i, (i + 1) % sections) for i in range(se...]
    pallas_call x2 -> x3, Pallas kernels: 19.1 us -> 49.2 us  [the longest x2 47 us: split_blocks(): pl.pallas_call(functools.partial(split_kernel, lanes, plan, single, kinds...]
    all_to_all x4 -> x3, waiting for transfers between devices: 23.2 us -> 10.7 us  [relayed(): lax.all_to_all(pieces, 'section', split_axis=0, concat_axis=0, tiled=True)]
    ppermute x12 -> x19, starting transfers between devices: 23.9 us -> 33.1 us  [swapped(): lax.ppermute(block, axis, [(i, i ^ distance) for i in range(lax.axis_size...]
    all_to_all x4 -> x3, starting transfers between devices: 18.5 us -> 14.2 us  [relayed(): lax.all_to_all(pieces, 'section', split_axis=0, concat_axis=0, tiled=True)]
    unnamed x47 -> x61, local copies, waits for them, and re-layouts: 16.5 us -> 13.3 us
  transfers between devices with their start and end apart: 22 -> 28, of which waited for: 13 -> 15; matrix products, arithmetic and copies ran while one was open for 1% -> 2% of each run, Pallas kernels for 11% -> 25%
where the time goes in v6:
time: 272 us; the launch traced here: 271 us
  waiting for transfers between devices  112 us (41%)
  Pallas kernels  77.6 us (29%)
  starting transfers between devices  49.6 us (18%)
  local copies, waits for them, and re-layouts  16.6 us (6%)
  between operations  14.4 us (5%)
    ppermute x19, waiting for transfers between devices, swapped(): lax.ppermute(block, axis, [(i, i ^ distance) for i in range(lax.axis_size...  86.6 us
    pallas_call x2, Pallas kernels, split_blocks(): pl.pallas_call(functools.partial(split_kernel, lanes, plan, single, kinds...  47 us
    ppermute x19, starting transfers between devices, swapped(): lax.ppermute(block, axis, [(i, i ^ distance) for i in range(lax.axis_size...  33.1 us
    pallas_call x3, Pallas kernels, attend(): pl.pallas_call(attend_kernel, grid_spec=pltpu.PrefetchScalarGridSpec(num_...  21.5 us
    all_to_all x3, starting transfers between devices, relayed(): lax.all_to_all(pieces, 'section', split_axis=0, concat_axis=0, tiled=True)  14.2 us
    ppermute x5, waiting for transfers between devices, handed_on(): lax.ppermute(block, 'section', [(i, (i + 1) % sections) for i in range(se...  14.1 us
    unnamed x61, local copies, waits for them, and re-layouts  13.3 us
    all_to_all x3, waiting for transfers between devices, relayed(): lax.all_to_all(pieces, 'section', split_axis=0, concat_axis=0, tiled=True)  10.7 us
  transfers between devices with their start and end apart: 28, of which 15 were waited for; matrix products, arithmetic and copies ran while one was open for 2% of the time, Pallas kernels for 25%

profile of v6, /device:TPU:0, one launch (start us, length us, event | category | flops | bytes accessed | tf_op | source)
XLA Modules:
  0.0 271.2 jit_solution(16065632567759720398)
XLA Ops:
  8.2 10.1 %split_blocks.2 = bf16[8,384,512]{2,1,0:T(8,128)(2,1)} custom-call(s32[8]{0:T(128)S(1)} %get-tuple-element.78.order_ref, s32[8]{0:T(128)S(1)} %iota.15.to_ref, bf16[8,6144,128]{2,1,0:T(8,128)(2,1)} %bitcast.22), custom_call_target="tpu_custom_call" | custom-call | bytes 18874368 | tf_op jit(solution)/shard_map/split_blocks/pallas_call | solution.py:95
  18.2 5.2 %all-to-all-start = ((bf16[8,384,512]{2,1,0:T(8,128)(2,1)}), bf16[8,384,512]{2,1,0:T(8,128)(2,1)}, u32[]{:S(2)}, u32[]{:S(2)}) async-start(bf16[8,384,512]{2,1,0:T(8,128)(2,1)} %split_blocks.2), calls=%async_computation | async-start | bytes 6291456 | tf_op jit(solution)/shard_map/all_to_all | solution.py:229
  23.4 36.9 %split_blocks.3 = (bf16[8,384,768]{2,1,0:T(8,128)(2,1)S(1)}, bf16[8,384,384]{2,1,0:T(8,128)(2,1)S(1)}, bf16[384,384]{1,0:T(8,128)(2,1)S(1)}, bf16[384,384]{1,0:T...) custom-call(s32[8]{0:T(128)S(1)} %get-tuple-element.42.order_ref, ...), custom_call_target="tpu_custom_call" | custom-call | bytes 18874368 | tf_op jit(solution)/shard_map/split_blocks/pallas_call | solution.py:95
  68.3 6.2 %collective-permute-done.1.rest_2_ = bf16[384,384]{1,0:T(8,128)(2,1)S(1)} collective-permute-done((bf16[384,384]{1,0:T(8,128)(2,1)S(1)}, bf16[384,384]{1,0:T(8,128)(2,1)S(1)}, u32[]{:S(2)}, u32[]{:S(2)}) %collective-permute-start.1) | collective-permute-done | bytes 294944 | tf_op jit(solution)/shard_map/ppermute | solution.py:220
  74.6 6.4 %collective-permute-done.4.rest_4_ = bf16[384,384]{1,0:T(8,128)(2,1)S(1)} collective-permute-done((bf16[384,384]{1,0:T(8,128)(2,1)S(1)}, bf16[384,384]{1,0:T(8,128)(2,1)S(1)}, u32[]{:S(2)}, u32[]{:S(2)}) %collective-permute-start.4) | collective-permute-done | bytes 294944 | tf_op jit(solution)/shard_map/ppermute | solution.py:220
  82.5 4.4 %collective-permute-done.2.rest_3_ = bf16[384,384]{1,0:T(8,128)(2,1)S(1)} collective-permute-done((bf16[384,384]{1,0:T(8,128)(2,1)S(1)}, bf16[384,384]{1,0:T(8,128)(2,1)S(1)}, u32[]{:S(2)}, u32[]{:S(2)}) %collective-permute-start.2) | collective-permute-done | bytes 294944 | tf_op jit(solution)/shard_map/ppermute | solution.py:220
  87.6 4.1 %norm.1.normed_ref = bf16[512,3072]{1,0:T(8,128)(2,1)S(1)} custom-call(bf16[512,3072]{1,0:T(8,128)(2,1)} %bitcast.24, f32[3,3072]{1,0:T(4,128)S(1)} %bitcast.21), custom_call_target="tpu_custom_call" | custom-call | flops 15728640 | bytes 6291456 | tf_op jit(solution)/shard_map/norm/pallas_call | solution.py:125
  93.5 2.8 %collective-permute-done.5.rest_5_ = bf16[384,384]{1,0:T(8,128)(2,1)} collective-permute-done((bf16[384,384]{1,0:T(8,128)(2,1)}, bf16[384,384]{1,0:T(8,128)(2,1)}, u32[]{:S(2)}, u32[]{:S(2)}) %collective-permute-start.5) | collective-permute-done | bytes 294944 | tf_op jit(solution)/shard_map/ppermute | solution.py:220
  96.3 4.6 %all-to-all-start.1 = ((bf16[8,384,768]{2,1,0:T(8,128)(2,1)}), bf16[8,384,768]{2,1,0:T(8,128)(2,1)}, u32[]{:S(2)}, u32[]{:S(2)}) async-start(bf16[8,384,768]{2,1,0:T(8,128)(2,1)} %copy-done.2), calls=%async_computation.1 | async-start | bytes 9437184 | tf_op jit(solution)/shard_map/all_to_all | solution.py:229
  100.9 3.2 %constant_dynamic-slice_fusion.3 = (bf16[768,512]{1,0:T(8,128)(2,1)}, bf16[768,512]{1,0:T(8,128)(2,1)S(1)}, bf16[768,512]{1,0:T(8,128)(2,1)S(1)}, bf16[768,512]{1,0:T(8,128)(2,1)}) fusion(bf16[3072,512]{1,0:T(8,128)(2,1)} %bitcast.5, s32[]{:T(128)S(6)} %select_n.28, s32[]{:T(128)S(6)} %select_n.27, s32[]{:T(128)S(6)} %select_n.26, s32[]{:T(128)S(6)} %select_n.25), kind=kLoop, calls=%fused_computation.9 | loop fusion | bytes 6291472 | tf_op jit(solution)/shard_map/dynamic_slice | solution.py:298
  104.1 2.6 collective-permute-start.17
  106.8 2.6 collective-permute-start.18
  109.4 32.2 %collective-permute-done.17.rest_13_ = bf16[768,512]{1,0:T(8,128)(2,1)S(1)} collective-permute-done((bf16[768,512]{1,0:T(8,128)(2,1)S(1)}, bf16[768,512]{1,0:T(8,128)(2,1)S(1)}, u32[]{:S(2)}, u32[]{:S(2)}) %collective-permute-start.17) | collective-permute-done | bytes 786464 | tf_op jit(solution)/shard_map/ppermute | solution.py:220
  144.9 10.7 %all-to-all-done.1 = bf16[8,384,768]{2,1,0:T(8,128)(2,1)} async-done(((bf16[8,384,768]{2,1,0:T(8,128)(2,1)}), bf16[8,384,768]{2,1,0:T(8,128)(2,1)}, u32[]{:S(2)}, u32[]{:S(2)}) %all-to-all-start.1) | async-done | bytes 4718624 | tf_op jit(solution)/shard_map/all_to_all | solution.py:229
  155.7 4.4 %all-to-all-start.2 = ((bf16[8,384,384]{2,1,0:T(8,128)(2,1)}), bf16[8,384,384]{2,1,0:T(8,128)(2,1)}, u32[]{:S(2)}, u32[]{:S(2)}) async-start(bf16[8,384,384]{2,1,0:T(8,128)(2,1)} %copy-done.4), calls=%async_computation.2 | async-start | bytes 4718592 | tf_op jit(solution)/shard_map/all_to_all | solution.py:229
  160.1 4.7 %collective-permute-start = (bf16[768,512]{1,0:T(8,128)(2,1)}, bf16[768,512]{1,0:T(8,128)(2,1)S(1)}, u32[]{:S(2)}, u32[]{:S(2)}) collective-permute-start(bf16[768,512]{1,0:T(8,128)(2,1)} %get-tuple-element.82), channel_id=1, source_target_pairs={{0,3},{1,2},{2,1},{3,0},{4,7},{5,6},{6,5},{7,4},{8,11},{9,10},{10,... | collective-permute-start | bytes 2359304 | tf_op jit(solution)/shard_map/ppermute | solution.py:220
  165.5 2.2 placed.1
  167.7 10.7 %attend.4 = bf16[512,256]{1,0:T(8,128)(2,1)S(1)} custom-call(s32[1]{0:T(128)S(6)} %copy.12.where_ref, bf16[512,3072]{1,0:T(8,128)(2,1)S(1)} %norm.1.normed_ref, bf16[3072,768]{1,0:T(8,128)(2,1)} %bitcast.11.matrix_ref, bf16[2,2048,512]{2,1,0:T(8,128)(2,1)S(1)} %bitcast.17), custom_call_target="tpu_custom_call" | custom-call | flops 3489660928 | bytes 6815744 | tf_op jit(solution)/shard_map/attend/pallas_call | solution.py:165
  178.6 4.6 %attend.3 = bf16[512,128]{1,0:T(8,128)(2,1)S(1)} custom-call(s32[1]{0:T(128)S(6)} %copy.12.where_ref, bf16[512,3072]{1,0:T(8,128)(2,1)S(1)} %norm.1.normed_ref, bf16[3072,384]{1,0:T(8,128)(2,1)S(1)} %bitcast.20, bf16[2,2048,512]{2,1,0:T(8,128)(2,1)S(1)} %bitcast.18), custom_call_target="tpu_custom_call" | custom-call | flops 1744830464 | bytes 3407872 | tf_op jit(solution)/shard_map/attend/pallas_call | solution.py:165
  185.1 7.1 %collective-permute-done.10.rest_0_ = bf16[512,256]{1,0:T(8,128)(2,1)S(1)} collective-permute-done((bf16[512,256]{1,0:T(8,128)(2,1)S(1)}, bf16[512,256]{1,0:T(8,128)(2,1)S(1)}, u32[]{:S(2)}, u32[]{:S(2)}) %collective-permute-start.10) | collective-permute-done | bytes 262176 | tf_op jit(solution)/shard_map/ppermute | solution.py:225
  192.2 2.6 collective-permute-start.12
  194.8 2.6 collective-permute-start.14
  200.2 4.8 %collective-permute-start.13 = (bf16[512,128]{1,0:T(8,128)(2,1)S(1)}, bf16[512,128]{1,0:T(8,128)(2,1)S(1)}, u32[]{:S(2)}, u32[]{:S(2)}) collective-permute-start(bf16[512,128]{1,0:T(8,128)(2,1)S(1)} %collective-permute-done.8.rest_2_), channel_id=1, source_target_pairs={{0,2},{1,3},{2,0},{3,1},{4,6},{5,7},{6,4},{7,5},{8,10},{9,11},{10,... | collective-permute-start | bytes 393224 | tf_op jit(solution)/shard_map/ppermute | solution.py:220
  204.9 5.1 %collective-permute-done.11.rest_5_ = bf16[512,128]{1,0:T(8,128)(2,1)S(1)} collective-permute-done((bf16[512,128]{1,0:T(8,128)(2,1)S(1)}, bf16[512,128]{1,0:T(8,128)(2,1)S(1)}, u32[]{:S(2)}, u32[]{:S(2)}) %collective-permute-start.11) | collective-permute-done | bytes 131104 | tf_op jit(solution)/shard_map/ppermute | solution.py:220
  210.7 2.5 collective-permute-start.15
  213.9 16.6 %collective-permute-done.13.rest_8_ = bf16[512,128]{1,0:T(8,128)(2,1)S(1)} collective-permute-done((bf16[512,128]{1,0:T(8,128)(2,1)S(1)}, bf16[512,128]{1,0:T(8,128)(2,1)S(1)}, u32[]{:S(2)}, u32[]{:S(2)}) %collective-permute-start.13) | collective-permute-done | bytes 131104 | tf_op jit(solution)/shard_map/ppermute | solution.py:220
  233.3 2.2 copy-done.1
  235.6 6.3 %attend.5 = bf16[512,128]{1,0:T(8,128)(2,1)S(1)} custom-call(s32[1]{0:T(128)S(6)} %copy.12.where_ref, bf16[512,3072]{1,0:T(8,128)(2,1)S(1)} %norm.1.normed_ref, bf16[3072,384]{1,0:T(8,128)(2,1)} %bitcast.12.matrix_ref, bf16[2,2048,512]{2,1,0:T(8,128)(2,1)S(1)} %bitcast.19), custom_call_target="tpu_custom_call" | custom-call | flops 1744830464 | bytes 3407872 | tf_op jit(solution)/shard_map/attend/pallas_call | solution.py:165
  241.9 5.3 %collective-permute-done.19.rest_1_ = bf16[512,128]{1,0:T(8,128)(2,1)S(1)} collective-permute-done((bf16[512,128]{1,0:T(8,128)(2,1)S(1)}, bf16[512,128]{1,0:T(8,128)(2,1)S(1)}, u32[]{:S(2)}, u32[]{:S(2)}) %collective-permute-start.19) | collective-permute-done | bytes 131104 | tf_op jit(solution)/shard_map/ppermute | solution.py:225
  251.7 4.4 %collective-permute-done.21.rest_4_ = bf16[512,128]{1,0:T(8,128)(2,1)S(1)} collective-permute-done((bf16[512,128]{1,0:T(8,128)(2,1)S(1)}, bf16[512,128]{1,0:T(8,128)(2,1)S(1)}, u32[]{:S(2)}, u32[]{:S(2)}) %collective-permute-start.21) | collective-permute-done | bytes 131104 | tf_op jit(solution)/shard_map/ppermute | solution.py:220
  256.1 5.3 %collective-permute-done.22.rest_7_ = bf16[512,128]{1,0:T(8,128)(2,1)S(1)} collective-permute-done((bf16[512,128]{1,0:T(8,128)(2,1)S(1)}, bf16[512,128]{1,0:T(8,128)(2,1)S(1)}, u32[]{:S(2)}, u32[]{:S(2)}) %collective-permute-start.22) | collective-permute-done | bytes 131104 | tf_op jit(solution)/shard_map/ppermute | solution.py:220
  261.6 2.8 %output.1 = bf16[512,768]{1,0:T(8,128)(2,1)} custom-call(bf16[512,768]{1,0:T(8,128)(2,1)S(1)} %collective-permute-done.20.inflow_ref, f32[1,768]{1,0:T(1,128)S(1)} %broadcast_in_dim.4.gate_ref, bf16[512,256]{1,0:T(8,128)(2,1)S(1)} %collective-permute-done.10.rest_0_, bf16[512,128]{1,0:T(8,128)(2,1)S(1)} %collective-permute-done.19.rest_1_, ...), custom_call_target="tpu_custom_call" | custom-call | flops 1610612736 | bytes 5242880 | tf_op jit(solution)/shard_map/output/pallas_call | solution.py:203
  (101 shorter events, 30.5 us)
Async XLA Ops:
  6.5 81.1 %all-gather.3.cloned.1.call-start = ((), (), s32[]{:S(2)}) async-start(), calls=%async_computation.3 | async-start | bytes 3932160 | tf_op jit(solution)/shard_map/all_gather | solution.py:273
  18.2 78.1 %all-to-all-start = ((bf16[8,384,512]{2,1,0:T(8,128)(2,1)}), bf16[8,384,512]{2,1,0:T(8,128)(2,1)}, u32[]{:S(2)}, u32[]{:S(2)}) async-start(bf16[8,384,512]{2,1,0:T(8,128)(2,1)} %split_blocks.2), calls=%async_computation | async-start | bytes 6291456 | tf_op jit(solution)/shard_map/all_to_all | solution.py:229
  23.4 64.0 %copy-start.29 = (f32[1,3,3072]{2,0,1:T(1,128)S(1)}, f32[1,3,3072]{2,0,1:T(1,128)}, u32[]{:S(2)}) copy-start(f32[1,3,3072]{2,0,1:T(1,128)} %param.7) | copy-start | bytes 110596
  64.6 10.0 %collective-permute-start.1 = (bf16[384,384]{1,0:T(8,128)(2,1)S(1)}, bf16[384,384]{1,0:T(8,128)(2,1)S(1)}, u32[]{:S(2)}, u32[]{:S(2)}) collective-permute-start(bf16[384,384]{1,0:T(8,128)(2,1)S(1)} %get-tuple-element.46), channel_id=1, source_target_pairs={{0,8},{4,12},{8,0},{12,4},{16,24},{20,28},{24,16},{28,20},{1,9},{5... | collective-permute-start | bytes 884744 | tf_op jit(solution)/shard_map/ppermute | solution.py:220
  66.8 14.2 %collective-permute-start.4 = (bf16[384,384]{1,0:T(8,128)(2,1)S(1)}, bf16[384,384]{1,0:T(8,128)(2,1)S(1)}, u32[]{:S(2)}, u32[]{:S(2)}) collective-permute-start(bf16[384,384]{1,0:T(8,128)(2,1)S(1)} %get-tuple-element.49), channel_id=1, source_target_pairs={{0,16},{4,20},{8,24},{12,28},{16,0},{20,4},{24,8},{28,12},{1,17},{... | collective-permute-start | bytes 884744 | tf_op jit(solution)/shard_map/ppermute | solution.py:220
  68.3 14.1 %collective-permute-start.6 = (bf16[384,384]{1,0:T(8,128)(2,1)S(1)}, bf16[384,384]{1,0:T(8,128)(2,1)S(1)}, u32[]{:S(2)}, u32[]{:S(2)}) collective-permute-start(bf16[384,384]{1,0:T(8,128)(2,1)S(1)} %get-tuple-element.52), channel_id=1, source_target_pairs={{0,24},{4,28},{8,16},{12,20},{16,8},{20,12},{24,0},{28,4},{1,25},{... | collective-permute-start | bytes 884744 | tf_op jit(solution)/shard_map/ppermute | solution.py:220
  74.6 12.3 %collective-permute-start.2 = (bf16[384,384]{1,0:T(8,128)(2,1)S(1)}, bf16[384,384]{1,0:T(8,128)(2,1)S(1)}, u32[]{:S(2)}, u32[]{:S(2)}) collective-permute-start(bf16[384,384]{1,0:T(8,128)(2,1)S(1)} %get-tuple-element.47), channel_id=1, source_target_pairs={{0,12},{4,8},{8,4},{12,0},{16,28},{20,24},{24,20},{28,16},{1,13},{... | collective-permute-start | bytes 884744 | tf_op jit(solution)/shard_map/ppermute | solution.py:220
  81.0 15.3 %collective-permute-start.5 = (bf16[384,384]{1,0:T(8,128)(2,1)}, bf16[384,384]{1,0:T(8,128)(2,1)}, u32[]{:S(2)}, u32[]{:S(2)}) collective-permute-start(bf16[384,384]{1,0:T(8,128)(2,1)} %get-tuple-element.51), channel_id=1, source_target_pairs={{0,20},{4,16},{8,28},{12,24},{16,4},{20,0},{24,12},{28,8},{1,21},{... | collective-permute-start | bytes 884744 | tf_op jit(solution)/shard_map/ppermute | solution.py:220
  82.5 13.8 %collective-permute-start.7 = (bf16[384,384]{1,0:T(8,128)(2,1)}, bf16[384,384]{1,0:T(8,128)(2,1)}, u32[]{:S(2)}, u32[]{:S(2)}) collective-permute-start(bf16[384,384]{1,0:T(8,128)(2,1)} %get-tuple-element.54), channel_id=1, source_target_pairs={{0,28},{4,24},{8,20},{12,16},{16,12},{20,8},{24,4},{28,0},{1,29},{... | collective-permute-start | bytes 884744 | tf_op jit(solution)/shard_map/ppermute | solution.py:220
  86.9 9.4 %collective-permute-start.3 = (bf16[384,384]{1,0:T(8,128)(2,1)S(1)}, bf16[384,384]{1,0:T(8,128)(2,1)}, u32[]{:S(2)}, u32[]{:S(2)}) collective-permute-start(bf16[384,384]{1,0:T(8,128)(2,1)S(1)} %get-tuple-element.48), channel_id=1, source_target_pairs={{0,4},{4,0},{8,12},{12,8},{16,20},{20,16},{24,28},{28,24},{1,5},{5... | collective-permute-start | bytes 884744 | tf_op jit(solution)/shard_map/ppermute | solution.py:220
  87.5 6.0 %collective-permute-start.9 = (f32[3072]{0:T(1024)S(1)}, f32[3072]{0:T(1024)S(1)}, u32[]{:S(2)}, u32[]{:S(2)}) collective-permute-start(f32[3072]{0:T(1024)S(1)} %bitcast.26), channel_id=1, source_target_pairs={{0,4},{4,8},{8,12},{12,16},{16,20},{20,24},{24,28},{28,0},{1,5},{5... | collective-permute-start | bytes 36872 | tf_op jit(solution)/shard_map/ppermute | solution.py:225
  96.3 59.4 %all-to-all-start.1 = ((bf16[8,384,768]{2,1,0:T(8,128)(2,1)}), bf16[8,384,768]{2,1,0:T(8,128)(2,1)}, u32[]{:S(2)}, u32[]{:S(2)}) async-start(bf16[8,384,768]{2,1,0:T(8,128)(2,1)} %copy-done.2), calls=%async_computation.1 | async-start | bytes 9437184 | tf_op jit(solution)/shard_map/all_to_all | solution.py:229
  104.1 37.4 %collective-permute-start.17 = (bf16[768,512]{1,0:T(8,128)(2,1)S(1)}, bf16[768,512]{1,0:T(8,128)(2,1)S(1)}, u32[]{:S(2)}, u32[]{:S(2)}) collective-permute-start(bf16[768,512]{1,0:T(8,128)(2,1)S(1)} %get-tuple-element.81), channel_id=1, source_target_pairs={{0,1},{1,0},{2,3},{3,2},{4,5},{5,4},{6,7},{7,6},{8,9},{9,8},{10,11... | collective-permute-start | bytes 2359304 | tf_op jit(solution)/shard_map/ppermute | solution.py:220
  106.8 37.3 %collective-permute-start.18 = (bf16[768,512]{1,0:T(8,128)(2,1)S(1)}, bf16[768,512]{1,0:T(8,128)(2,1)S(1)}, u32[]{:S(2)}, u32[]{:S(2)}) collective-permute-start(bf16[768,512]{1,0:T(8,128)(2,1)S(1)} %get-tuple-element.80), channel_id=1, source_target_pairs={{0,2},{1,3},{2,0},{3,1},{4,6},{5,7},{6,4},{7,5},{8,10},{9,11},{10,... | collective-permute-start | bytes 2359304 | tf_op jit(solution)/shard_map/ppermute | solution.py:220
  155.7 77.6 %all-to-all-start.2 = ((bf16[8,384,384]{2,1,0:T(8,128)(2,1)}), bf16[8,384,384]{2,1,0:T(8,128)(2,1)}, u32[]{:S(2)}, u32[]{:S(2)}) async-start(bf16[8,384,384]{2,1,0:T(8,128)(2,1)} %copy-done.4), calls=%async_computation.2 | async-start | bytes 4718592 | tf_op jit(solution)/shard_map/all_to_all | solution.py:229
  160.1 39.2 %collective-permute-start = (bf16[768,512]{1,0:T(8,128)(2,1)}, bf16[768,512]{1,0:T(8,128)(2,1)S(1)}, u32[]{:S(2)}, u32[]{:S(2)}) collective-permute-start(bf16[768,512]{1,0:T(8,128)(2,1)} %get-tuple-element.82), channel_id=1, source_target_pairs={{0,3},{1,2},{2,1},{3,0},{4,7},{5,6},{6,5},{7,4},{8,11},{9,10},{10,... | collective-permute-start | bytes 2359304 | tf_op jit(solution)/shard_map/ppermute | solution.py:220
  178.4 13.9 %collective-permute-start.10 = (bf16[512,256]{1,0:T(8,128)(2,1)S(1)}, bf16[512,256]{1,0:T(8,128)(2,1)S(1)}, u32[]{:S(2)}, u32[]{:S(2)}) collective-permute-start(bf16[512,256]{1,0:T(8,128)(2,1)S(1)} %attend.4), channel_id=1, source_target_pairs={{0,4},{4,8},{8,12},{12,16},{16,20},{20,24},{24,28},{28,0},{1,5},{5... | collective-permute-start | bytes 786440 | tf_op jit(solution)/shard_map/ppermute | solution.py:225
  183.2 14.3 %collective-permute-start.8 = (bf16[512,128]{1,0:T(8,128)(2,1)S(1)}, bf16[512,128]{1,0:T(8,128)(2,1)S(1)}, u32[]{:S(2)}, u32[]{:S(2)}) collective-permute-start(bf16[512,128]{1,0:T(8,128)(2,1)S(1)} %attend.3), channel_id=1, source_target_pairs={{0,4},{4,8},{8,12},{12,16},{16,20},{20,24},{24,28},{28,0},{1,5},{5... | collective-permute-start | bytes 393224 | tf_op jit(solution)/shard_map/ppermute | solution.py:225
  192.2 21.0 %collective-permute-start.12 = (bf16[512,256]{1,0:T(8,128)(2,1)S(1)}, bf16[512,256]{1,0:T(8,128)(2,1)S(1)}, u32[]{:S(2)}, u32[]{:S(2)}) collective-permute-start(bf16[512,256]{1,0:T(8,128)(2,1)S(1)} %collective-permute-done.10.rest_0_), channel_id=1, source_target_pairs={{0,1},{1,0},{2,3},{3,2},{4,5},{5,4},{6,7},{7,6},{8,9},{9,8},{10,11... | collective-permute-start | bytes 786440 | tf_op jit(solution)/shard_map/ppermute | solution.py:220
  194.8 36.4 %collective-permute-start.14 = (bf16[512,256]{1,0:T(8,128)(2,1)S(1)}, bf16[512,256]{1,0:T(8,128)(2,1)S(1)}, u32[]{:S(2)}, u32[]{:S(2)}) collective-permute-start(bf16[512,256]{1,0:T(8,128)(2,1)S(1)} %collective-permute-done.10.rest_0_), channel_id=1, source_target_pairs={{0,2},{1,3},{2,0},{3,1},{4,6},{5,7},{6,4},{7,5},{8,10},{9,11},{10,... | collective-permute-start | bytes 786440 | tf_op jit(solution)/shard_map/ppermute | solution.py:220
  197.5 12.6 %collective-permute-start.11 = (bf16[512,128]{1,0:T(8,128)(2,1)S(1)}, bf16[512,128]{1,0:T(8,128)(2,1)S(1)}, u32[]{:S(2)}, u32[]{:S(2)}) collective-permute-start(bf16[512,128]{1,0:T(8,128)(2,1)S(1)} %collective-permute-done.8.rest_2_), channel_id=1, source_target_pairs={{0,1},{1,0},{2,3},{3,2},{4,5},{5,4},{6,7},{7,6},{8,9},{9,8},{10,11... | collective-permute-start | bytes 393224 | tf_op jit(solution)/shard_map/ppermute | solution.py:220
  197.9 34.7 %collective-permute-start.16 = (bf16[512,256]{1,0:T(8,128)(2,1)S(1)}, bf16[512,256]{1,0:T(8,128)(2,1)S(1)}, u32[]{:S(2)}, u32[]{:S(2)}) collective-permute-start(bf16[512,256]{1,0:T(8,128)(2,1)S(1)} %collective-permute-done.10.rest_0_), channel_id=1, source_target_pairs={{0,3},{1,2},{2,1},{3,0},{4,7},{5,6},{6,5},{7,4},{8,11},{9,10},{10,... | collective-permute-start | bytes 786440 | tf_op jit(solution)/shard_map/ppermute | solution.py:220
  200.2 30.4 %collective-permute-start.13 = (bf16[512,128]{1,0:T(8,128)(2,1)S(1)}, bf16[512,128]{1,0:T(8,128)(2,1)S(1)}, u32[]{:S(2)}, u32[]{:S(2)}) collective-permute-start(bf16[512,128]{1,0:T(8,128)(2,1)S(1)} %collective-permute-done.8.rest_2_), channel_id=1, source_target_pairs={{0,2},{1,3},{2,0},{3,1},{4,6},{5,7},{6,4},{7,5},{8,10},{9,11},{10,... | collective-permute-start | bytes 393224 | tf_op jit(solution)/shard_map/ppermute | solution.py:220
  210.7 21.3 %collective-permute-start.15 = (bf16[512,128]{1,0:T(8,128)(2,1)S(1)}, bf16[512,128]{1,0:T(8,128)(2,1)S(1)}, u32[]{:S(2)}, u32[]{:S(2)}) collective-permute-start(bf16[512,128]{1,0:T(8,128)(2,1)S(1)} %collective-permute-done.8.rest_2_), channel_id=1, source_target_pairs={{0,3},{1,2},{2,1},{3,0},{4,7},{5,6},{6,5},{7,4},{8,11},{9,10},{10,... | collective-permute-start | bytes 393224 | tf_op jit(solution)/shard_map/ppermute | solution.py:220
  235.5 26.0 %copy-start.10 = (bf16[768,512]{1,0:T(8,128)(2,1)S(1)}, bf16[768,512]{1,0:T(8,128)(2,1)}, u32[]{:S(2)}) copy-start(bf16[768,512]{1,0:T(8,128)(2,1)} %copy-done.9) | copy-start | bytes 2359300
  235.5 26.0 %copy-start.13 = (bf16[512,256]{1,0:T(8,128)(2,1)S(1)}, bf16[512,256]{1,0:T(8,128)(2,1)}, u32[]{:S(2)}) copy-start(bf16[512,256]{1,0:T(8,128)(2,1)} %copy-done.12) | copy-start | bytes 786436
  235.5 26.0 %copy-start.15 = (bf16[512,256]{1,0:T(8,128)(2,1)S(1)}, bf16[512,256]{1,0:T(8,128)(2,1)}, u32[]{:S(2)}) copy-start(bf16[512,256]{1,0:T(8,128)(2,1)} %copy-done.14) | copy-start | bytes 786436
  241.9 5.3 %collective-permute-start.19 = (bf16[512,128]{1,0:T(8,128)(2,1)S(1)}, bf16[512,128]{1,0:T(8,128)(2,1)S(1)}, u32[]{:S(2)}, u32[]{:S(2)}) collective-permute-start(bf16[512,128]{1,0:T(8,128)(2,1)S(1)} %attend.5), channel_id=1, source_target_pairs={{0,4},{4,8},{8,12},{12,16},{16,20},{20,24},{24,28},{28,0},{1,5},{5... | collective-permute-start | bytes 393224 | tf_op jit(solution)/shard_map/ppermute | solution.py:225
  247.2 14.2 %collective-permute-start.20 = (bf16[512,768]{1,0:T(8,128)(2,1)S(1)}, bf16[512,768]{1,0:T(8,128)(2,1)S(1)}, u32[]{:S(2)}, u32[]{:S(2)}) collective-permute-start(bf16[512,768]{1,0:T(8,128)(2,1)S(1)} %bitcast.25), channel_id=1, source_target_pairs={{0,4},{4,8},{8,12},{12,16},{16,20},{20,24},{24,28},{28,0},{1,5},{5... | collective-permute-start | bytes 2359304 | tf_op jit(solution)/shard_map/ppermute | solution.py:225
  247.2 8.9 %collective-permute-start.21 = (bf16[512,128]{1,0:T(8,128)(2,1)S(1)}, bf16[512,128]{1,0:T(8,128)(2,1)S(1)}, u32[]{:S(2)}, u32[]{:S(2)}) collective-permute-start(bf16[512,128]{1,0:T(8,128)(2,1)S(1)} %collective-permute-done.19.rest_1_), channel_id=1, source_target_pairs={{0,1},{1,0},{2,3},{3,2},{4,5},{5,4},{6,7},{7,6},{8,9},{9,8},{10,11... | collective-permute-start | bytes 393224 | tf_op jit(solution)/shard_map/ppermute | solution.py:220
  248.6 12.8 %collective-permute-start.22 = (bf16[512,128]{1,0:T(8,128)(2,1)S(1)}, bf16[512,128]{1,0:T(8,128)(2,1)S(1)}, u32[]{:S(2)}, u32[]{:S(2)}) collective-permute-start(bf16[512,128]{1,0:T(8,128)(2,1)S(1)} %collective-permute-done.19.rest_1_), channel_id=1, source_target_pairs={{0,2},{1,3},{2,0},{3,1},{4,6},{5,7},{6,4},{7,5},{8,10},{9,11},{10,... | collective-permute-start | bytes 393224 | tf_op jit(solution)/shard_map/ppermute | solution.py:220
  250.3 11.2 %collective-permute-start.23 = (bf16[512,128]{1,0:T(8,128)(2,1)S(1)}, bf16[512,128]{1,0:T(8,128)(2,1)S(1)}, u32[]{:S(2)}, u32[]{:S(2)}) collective-permute-start(bf16[512,128]{1,0:T(8,128)(2,1)S(1)} %collective-permute-done.19.rest_1_), channel_id=1, source_target_pairs={{0,3},{1,2},{2,1},{3,0},{4,7},{5,6},{6,5},{7,4},{8,11},{9,10},{10,... | collective-permute-start | bytes 393224 | tf_op jit(solution)/shard_map/ppermute | solution.py:220
  (26 other events, 240.0 us)
Sparse Core Ops, SparseCore 0:
  8.9 66.1 all-gather.2

commit v7 on v6

--- a/solution.py
+++ b/solution.py
@@ -43,7 +43,8 @@
 
 
 def split_kernel(lanes, plan, single, kinds, depth_step, order_ref, to_ref, rows_ref, *rest):
-    outs, pick = rest[:-1], rest[-1]
+    outs, pick, alone = rest[: len(plan) - single], rest[-2], rest[-1]
+    singles = rest[len(outs) : -2]
     depth = rows_ref.shape[1] // (4 * lanes)
     chunk = depth_step * 4 * lanes
     beside = 2 if depth % (2 * depth_step) == 0 else 1
@@ -52,9 +53,7 @@
     def _():
         pick[...] = pick_matrix(kinds, lanes, depth_step)
 
-    def store(out, to, columns, values):
-        out[to, columns] = values
-
+    targets = [out.at[0] for out in outs] + [alone] * single
     for first in range(0, depth, beside * depth_step):
         begin = first * 4 * lanes
         chunks = [
@@ -65,18 +64,18 @@
         ).astype(BF16)
         for i in range(beside):
             to = slice(first + i * depth_step, first + (i + 1) * depth_step)
-            for out, columns in zip(outs, plan):
+            for out, columns in zip(targets, plan):
                 for column, (kind, lane) in enumerate(columns):
                     at = (kinds.index(kind) * lanes + lane) * depth_step
-                    values = sorted_rows[at : at + depth_step, i * HD : (i + 1) * HD]
-                    spot = slice(column * HD, (column + 1) * HD)
-                    if columns is not plan[-1] or not single:
-                        out[0, to, spot] = values
-                        continue
-                    for block, own in enumerate(outs[len(plan) - 1 :]):
-                        pl.when(pl.program_id(0) == block)(
-                            functools.partial(store, own, to, spot, values)
-                        )
+                    out[to, column * HD : (column + 1) * HD] = sorted_rows[
+                        at : at + depth_step, i * HD : (i + 1) * HD
+                    ]
+
+    def keep(own):
+        own[...] = alone[...]
+
+    for block, own in enumerate(singles):
+        pl.when(pl.program_id(0) == block)(functools.partial(keep, own))
 
 
 def split_blocks(rows, order, to, plan, lanes, single=False):
@@ -100,11 +99,12 @@
             in_specs=[pl.BlockSpec((1,) + rows.shape[1:], lambda i, order, to: (order[i], 0, 0))],
             out_specs=out_specs,
             scratch_shapes=[
-                pltpu.VMEM((len(kinds) * lanes * depth_step, depth_step * 4 * lanes), BF16)
+                pltpu.VMEM((len(kinds) * lanes * depth_step, depth_step * 4 * lanes), BF16),
+                pltpu.VMEM((depth, len(plan[-1]) * HD), BF16),
             ],
         ),
         out_shape=[jax.ShapeDtypeStruct(shape, BF16) for shape in shapes],
-        compiler_params=params(24),
+        compiler_params=params(32),
         cost_estimate=cost(0, 3 * blocks * rows.shape[1] * HD),
         name="split_blocks",
     )(order, to, in_hbm(rows))
@@ -278,10 +278,11 @@
     before = block_of((section_ids + sections - 1) % sections)
     (to_out,) = split_blocks(rows, before, section_ids, out_plan, lanes)
     half = max(1, lanes // 2)
-    groups = [tuple(range(half))] + [(head,) for head in range(half, lanes)]
+    groups = [(head,) for head in range(half, lanes)] + [tuple(range(half))]
     plan = [[(kind, head) for head in group for kind in range(3)] for group in groups]
-    alone = len(groups) > 1
-    split = split_blocks(rows, after(block_of(sources), to_out), sources, plan, lanes, alone)
+    alone = len(groups) == 3
+    order = after(block_of(sources), to_out)
+    split = split_blocks(rows, order, sources, plan, lanes, alone)
 
     pieces = list(split[len(groups) - 1 :]) if alone else []
     chain = []
@@ -300,30 +301,30 @@
 
     attended = [[] for _ in range(tp)]
 
-    def share_out(group, matrix, tokens):
-        own = attend(tokens, matrix, patch_index, stale_cache[0], group)
-        moved = handed_on(own)
-        for distance in range(tp):
-            attended[distance].append(swapped(moved, "tp", distance) if distance else moved)
-        return moved
+    def share_out(group, matrix, ready, *earlier):
+        own = attend(waiting(normed, *ready), matrix, patch_index, stale_cache[0], group)
+        moved = waiting(handed_on(own), *earlier)
+        parts = [swapped(moved, "tp", distance) if distance else moved for distance in range(tp)]
+        for kept, part in zip(attended, parts):
+            kept.append(part)
+        return parts
 
     def waiting(block, *earlier):
         return functools.reduce(after, earlier, block)
 
-    first = relayed(waiting(split[0], normed, gate, *chain))
     if alone:
+        matrix = relayed(waiting(split[0], tokens, gate, *chain))
         last = relayed(waiting(split[1], *matrices[1:3]))
-        matrix = placed(pieces, sources)
-        share_out(groups[2], matrix.reshape(-1, matrix.shape[2]), normed)
-        share_out(groups[0], first, normed)
-        ready = waiting(normed, *matrices[3:], *[part for own in attended for part in own])
-        moved = share_out(groups[1], last, ready)
+        placed_rows = placed(pieces, sources)
+        parts = share_out(groups[2], placed_rows.reshape(-1, placed_rows.shape[2]), ())
+        parts = share_out(groups[0], matrix, (*matrices[3:], *parts))
+        parts = share_out(groups[1], last, (), *parts)
     else:
-        moved = share_out(groups[0], first, normed)
-    heads_first = [own[1:2] + own[2:] + own[:1] if alone else own for own in attended]
-    carried = handed_on(after(inflow[0], moved))
+        for group, own in zip(groups, split):
+            parts = share_out(group, relayed(own), ())
+    carried = handed_on(after(inflow[0], parts[0]))
     gate = lax.dynamic_slice_in_dim(gate, rank * share, share, 0)[None]
-    return output(carried, gate, heads_first, matrices)[None]
+    return output(carried, gate, attended, matrices)[None]
 
 
 def solution(mesh):

time: 272 us -> 283 us (1.040)
  waiting for transfers between devices: 112 us -> 157 us
  Pallas kernels: 77.6 us -> 50.9 us
  local copies, waits for them, and re-layouts: 16.6 us -> 12.5 us
    ppermute x19, waiting for transfers between devices: 86.6 us -> 133 us  [swapped(): lax.ppermute(block, axis, [(i, i ^ distance) for i in range(lax.axis_size...]
    pallas_call x2, Pallas kernels: 47 us -> 19.5 us  [split_blocks(): pl.pallas_call(functools.partial(split_kernel, lanes, plan, single, kinds...]
    all_to_all x3, waiting for transfers between devices: 10.7 us -> 0.01 us  [relayed(): lax.all_to_all(pieces, 'section', split_axis=0, concat_axis=0, tiled=True)]
    ppermute x5, waiting for transfers between devices: 14.1 us -> 23.3 us  [handed_on(): lax.ppermute(block, 'section', [(i, (i + 1) % sections) for i in range(se...]
    unnamed x61 -> x53, local copies, waits for them, and re-layouts: 13.3 us -> 8.48 us
  transfers between devices with their start and end apart: 28 -> 28, of which waited for: 15 -> 13; matrix products, arithmetic and copies ran while one was open for 2% -> 2% of each run, Pallas kernels for 25% -> 17%
where the time goes in v7:
time: 283 us; the launch traced here: 282 us
  waiting for transfers between devices  157 us (55%)
  Pallas kernels  50.9 us (18%)
  starting transfers between devices  46.8 us (17%)
  between operations  14.4 us (5%)
  local copies, waits for them, and re-layouts  12.5 us (4%)
    ppermute x19, waiting for transfers between devices, swapped(): lax.ppermute(block, axis, [(i, i ^ distance) for i in range(lax.axis_size...  133 us
    ppermute x19, starting transfers between devices, swapped(): lax.ppermute(block, axis, [(i, i ^ distance) for i in range(lax.axis_size...  31 us
    ppermute x5, waiting for transfers between devices, handed_on(): lax.ppermute(block, 'section', [(i, (i + 1) % sections) for i in range(se...  23.3 us
    pallas_call x3, Pallas kernels, attend(): pl.pallas_call(attend_kernel, grid_spec=pltpu.PrefetchScalarGridSpec(num_...  20.6 us
    pallas_call x2, Pallas kernels, split_blocks(): pl.pallas_call(functools.partial(split_kernel, lanes, plan, single, kinds...  19.5 us
    all_to_all x3, starting transfers between devices, relayed(): lax.all_to_all(pieces, 'section', split_axis=0, concat_axis=0, tiled=True)  13.2 us
    unnamed x53, local copies, waits for them, and re-layouts  8.48 us
  transfers between devices with their start and end apart: 28, of which 13 were waited for; matrix products, arithmetic and copies ran while one was open for 2% of the time, Pallas kernels for 17%

profile of v7, /device:TPU:0, one launch (start us, length us, event | category | flops | bytes accessed | tf_op | source)
XLA Modules:
  0.0 282.2 jit_solution(9274655492354667659)
XLA Ops:
  8.2 10.0 %split_blocks.2 = bf16[8,384,512]{2,1,0:T(8,128)(2,1)} custom-call(s32[8]{0:T(128)S(1)} %get-tuple-element.77.order_ref, s32[8]{0:T(128)S(1)} %iota.16.to_ref, bf16[8,6144,128]{2,1,0:T(8,128)(2,1)} %bitcast.23), custom_call_target="tpu_custom_call" | custom-call | bytes 18874368 | tf_op jit(solution)/shard_map/split_blocks/pallas_call | solution.py:94
  18.2 5.2 %all-to-all-start = ((bf16[8,384,512]{2,1,0:T(8,128)(2,1)}), bf16[8,384,512]{2,1,0:T(8,128)(2,1)}, u32[]{:S(2)}, u32[]{:S(2)}) async-start(bf16[8,384,512]{2,1,0:T(8,128)(2,1)} %split_blocks.2), calls=%async_computation | async-start | bytes 6291456 | tf_op jit(solution)/shard_map/all_to_all | solution.py:229
  23.4 9.4 %split_blocks.3 = (bf16[8,384,384]{2,1,0:T(8,128)(2,1)S(1)}, bf16[8,384,384]{2,1,0:T(8,128)(2,1)S(1)}, bf16[384,768]{1,0:T(8,128)(2,1)S(1)}, bf16[384,768]{1,0:T...) custom-call(s32[8]{0:T(128)S(1)} %get-tuple-element.41.order_ref, ...), custom_call_target="tpu_custom_call" | custom-call | bytes 18874368 | tf_op jit(solution)/shard_map/split_blocks/pallas_call | solution.py:94
  40.2 33.4 %collective-permute-done.4.rest_2_ = bf16[384,768]{1,0:T(8,128)(2,1)S(1)} collective-permute-done((bf16[384,768]{1,0:T(8,128)(2,1)S(1)}, bf16[384,768]{1,0:T(8,128)(2,1)S(1)}, u32[]{:S(2)}, u32[]{:S(2)}) %collective-permute-start.4) | collective-permute-done | bytes 589856 | tf_op jit(solution)/shard_map/ppermute | solution.py:220
  75.4 11.9 %collective-permute-done.9.rest_6_ = bf16[384,768]{1,0:T(8,128)(2,1)S(1)} collective-permute-done((bf16[384,768]{1,0:T(8,128)(2,1)S(1)}, bf16[384,768]{1,0:T(8,128)(2,1)S(1)}, u32[]{:S(2)}, u32[]{:S(2)}) %collective-permute-start.9) | collective-permute-done | bytes 589856 | tf_op jit(solution)/shard_map/ppermute | solution.py:220
  87.3 10.5 %collective-permute-done.5.rest_3_ = bf16[384,768]{1,0:T(8,128)(2,1)S(1)} collective-permute-done((bf16[384,768]{1,0:T(8,128)(2,1)S(1)}, bf16[384,768]{1,0:T(8,128)(2,1)S(1)}, u32[]{:S(2)}, u32[]{:S(2)}) %collective-permute-start.5) | collective-permute-done | bytes 589856 | tf_op jit(solution)/shard_map/ppermute | solution.py:220
  100.0 11.6 %collective-permute-done.15 = f32[3072]{0:T(1024)S(1)} collective-permute-done((f32[3072]{0:T(1024)S(1)}, f32[3072]{0:T(1024)S(1)}, u32[]{:S(2)}, u32[]{:S(2)}) %collective-permute-start.15) | collective-permute-done | bytes 12320 | tf_op jit(solution)/shard_map/ppermute | solution.py:225
  111.6 3.6 %all-to-all-start.2 = ((bf16[8,384,384]{2,1,0:T(8,128)(2,1)}), bf16[8,384,384]{2,1,0:T(8,128)(2,1)S(1)}, u32[]{:S(2)}, u32[]{:S(2)}) async-start(bf16[8,384,384]{2,1,0:T(8,128)(2,1)} %copy-done.6), calls=%async_computation.2 | async-start | bytes 4718592 | tf_op jit(solution)/shard_map/all_to_all | solution.py:229
  115.3 3.2 %constant_dynamic-slice_fusion.3 = (bf16[768,512]{1,0:T(8,128)(2,1)}, bf16[768,512]{1,0:T(8,128)(2,1)}, bf16[768,512]{1,0:T(8,128)(2,1)S(1)}, bf16[768,512]{1,0:T(8,128)(2,1)S(1)}) fusion(bf16[3072,512]{1,0:T(8,128)(2,1)} %bitcast.5, s32[]{:T(128)S(6)} %select_n.28, s32[]{:T(128)S(6)} %select_n.27, s32[]{:T(128)S(6)} %select_n.26, s32[]{:T(128)S(6)} %select_n.25), kind=kLoop, calls=%fused_computation.9 | loop fusion | bytes 6291472 | tf_op jit(solution)/shard_map/dynamic_slice | solution.py:299
  118.5 2.4 collective-permute-start
  120.9 2.6 collective-permute-start.1
  123.5 32.2 %collective-permute-done.rest_13_ = bf16[768,512]{1,0:T(8,128)(2,1)S(1)} collective-permute-done((bf16[768,512]{1,0:T(8,128)(2,1)S(1)}, bf16[768,512]{1,0:T(8,128)(2,1)S(1)}, u32[]{:S(2)}, u32[]{:S(2)}) %collective-permute-start) | collective-permute-done | bytes 786464 | tf_op jit(solution)/shard_map/ppermute | solution.py:220
  159.1 4.4 %all-to-all-start.1 = ((bf16[8,384,384]{2,1,0:T(8,128)(2,1)}), bf16[8,384,384]{2,1,0:T(8,128)(2,1)}, u32[]{:S(2)}, u32[]{:S(2)}) async-start(bf16[8,384,384]{2,1,0:T(8,128)(2,1)} %copy-done.5), calls=%async_computation.1 | async-start | bytes 4718592 | tf_op jit(solution)/shard_map/all_to_all | solution.py:229
  164.2 2.9 %placed.1 = bf16[8,384,768]{2,1,0:T(8,128)(2,1)S(1)} custom-call(s32[8]{0:T(128)S(1)} %get-tuple-element.84.to_ref.slots_ref, bf16[384,768]{1,0:T(8,128)(2,1)} %copy-done.13, bf16[384,768]{1,0:T(8,128)(2,1)} %collective-permute-done.6.rest_1_, bf16[384,768]{1,0:T(8,128)(2,1)} %copy-done.21, bf16[384,768]{1,0:T(8,128)(2,1)} %copy-done.24, ...), custom_call_target="tpu_custom_call" | custom-call | bytes 9437184 | tf_op jit(solution)/shard_map/placed/pallas_call | solution.py:246
  167.1 2.6 collective-permute-start.3
  169.7 4.3 %norm.1.normed_ref = bf16[512,3072]{1,0:T(8,128)(2,1)S(1)} custom-call(bf16[512,3072]{1,0:T(8,128)(2,1)} %bitcast.25, f32[3,3072]{1,0:T(4,128)S(1)} %bitcast.22), custom_call_target="tpu_custom_call" | custom-call | flops 15728640 | bytes 6291456 | tf_op jit(solution)/shard_map/norm/pallas_call | solution.py:125
  174.0 9.8 %attend.4 = bf16[512,256]{1,0:T(8,128)(2,1)S(1)} custom-call(s32[1]{0:T(128)S(6)} %copy.12.where_ref, bf16[512,3072]{1,0:T(8,128)(2,1)S(1)} %norm.1.normed_ref, bf16[3072,768]{1,0:T(8,128)(2,1)S(1)} %bitcast.21, bf16[2,2048,512]{2,1,0:T(8,128)(2,1)S(1)} %bitcast.17), custom_call_target="tpu_custom_call" | custom-call | flops 3489660928 | bytes 6815744 | tf_op jit(solution)/shard_map/attend/pallas_call | solution.py:165
  183.9 11.7 %collective-permute-done.11.rest_0_ = bf16[512,256]{1,0:T(8,128)(2,1)S(1)} collective-permute-done((bf16[512,256]{1,0:T(8,128)(2,1)S(1)}, bf16[512,256]{1,0:T(8,128)(2,1)S(1)}, u32[]{:S(2)}, u32[]{:S(2)}) %collective-permute-start.11) | collective-permute-done | bytes 262176 | tf_op jit(solution)/shard_map/ppermute | solution.py:225
  196.1 2.6 collective-permute-start.13
  200.0 2.8 %collective-permute-done.12.rest_3_ = bf16[512,256]{1,0:T(8,128)(2,1)S(1)} collective-permute-done((bf16[512,256]{1,0:T(8,128)(2,1)S(1)}, bf16[512,256]{1,0:T(8,128)(2,1)S(1)}, u32[]{:S(2)}, u32[]{:S(2)}) %collective-permute-start.12) | collective-permute-done | bytes 262176 | tf_op jit(solution)/shard_map/ppermute | solution.py:220
  203.6 17.8 %collective-permute-done.13.rest_6_ = bf16[512,256]{1,0:T(8,128)(2,1)S(1)} collective-permute-done((bf16[512,256]{1,0:T(8,128)(2,1)S(1)}, bf16[512,256]{1,0:T(8,128)(2,1)S(1)}, u32[]{:S(2)}, u32[]{:S(2)}) %collective-permute-start.13) | collective-permute-done | bytes 262176 | tf_op jit(solution)/shard_map/ppermute | solution.py:220
  221.4 4.5 %attend.5 = bf16[512,128]{1,0:T(8,128)(2,1)S(1)} custom-call(s32[1]{0:T(128)S(6)} %copy.12.where_ref, bf16[512,3072]{1,0:T(8,128)(2,1)S(1)} %norm.1.normed_ref, bf16[3072,384]{1,0:T(8,128)(2,1)S(1)} %bitcast.20, bf16[2,2048,512]{2,1,0:T(8,128)(2,1)S(1)} %bitcast.18), custom_call_target="tpu_custom_call" | custom-call | flops 1744830464 | bytes 3407872 | tf_op jit(solution)/shard_map/attend/pallas_call | solution.py:165
  226.2 2.2 copy-done.1
  228.4 6.3 %attend.3 = bf16[512,128]{1,0:T(8,128)(2,1)S(1)} custom-call(s32[1]{0:T(128)S(6)} %copy.12.where_ref, bf16[512,3072]{1,0:T(8,128)(2,1)S(1)} %norm.1.normed_ref, bf16[3072,384]{1,0:T(8,128)(2,1)} %bitcast.6.matrix_ref, bf16[2,2048,512]{2,1,0:T(8,128)(2,1)S(1)} %bitcast.19), custom_call_target="tpu_custom_call" | custom-call | flops 1744830464 | bytes 3407872 | tf_op jit(solution)/shard_map/attend/pallas_call | solution.py:165
  236.8 5.4 %collective-permute-start.17 = (bf16[512,128]{1,0:T(8,128)(2,1)}, bf16[512,128]{1,0:T(8,128)(2,1)S(1)}, u32[]{:S(2)}, u32[]{:S(2)}) collective-permute-start(bf16[512,128]{1,0:T(8,128)(2,1)} %collective-permute-done.16.rest_1_), channel_id=1, source_target_pairs={{0,1},{1,0},{2,3},{3,2},{4,5},{5,4},{6,7},{7,6},{8,9},{9,8},{10,11... | collective-permute-start | bytes 393224 | tf_op jit(solution)/shard_map/ppermute | solution.py:220
  242.2 2.4 collective-permute-start.19
  244.5 2.7 collective-permute-done.17.rest_4_
  247.2 7.8 %collective-permute-done.18.rest_7_ = bf16[512,128]{1,0:T(8,128)(2,1)S(1)} collective-permute-done((bf16[512,128]{1,0:T(8,128)(2,1)}, bf16[512,128]{1,0:T(8,128)(2,1)S(1)}, u32[]{:S(2)}, u32[]{:S(2)}) %collective-permute-start.18) | collective-permute-done | bytes 131104 | tf_op jit(solution)/shard_map/ppermute | solution.py:220
  256.7 2.3 collective-permute-start.22
  259.6 3.4 %collective-permute-done.23.rest_11_ = bf16[512,128]{1,0:T(8,128)(2,1)S(1)} collective-permute-done((bf16[512,128]{1,0:T(8,128)(2,1)S(1)}, bf16[512,128]{1,0:T(8,128)(2,1)S(1)}, u32[]{:S(2)}, u32[]{:S(2)}) %collective-permute-start.23) | collective-permute-done | bytes 131104 | tf_op jit(solution)/shard_map/ppermute | solution.py:220
  262.9 8.7 %collective-permute-done.22.rest_8_ = bf16[512,128]{1,0:T(8,128)(2,1)S(1)} collective-permute-done((bf16[512,128]{1,0:T(8,128)(2,1)S(1)}, bf16[512,128]{1,0:T(8,128)(2,1)S(1)}, u32[]{:S(2)}, u32[]{:S(2)}) %collective-permute-start.22) | collective-permute-done | bytes 131104 | tf_op jit(solution)/shard_map/ppermute | solution.py:220
  271.7 3.6 %output.1 = bf16[512,768]{1,0:T(8,128)(2,1)} custom-call(bf16[512,768]{1,0:T(8,128)(2,1)S(1)} %collective-permute-done.20.inflow_ref, f32[1,768]{1,0:T(1,128)S(1)} %broadcast_in_dim.4.gate_ref, bf16[512,256]{1,0:T(8,128)(2,1)S(1)} %collective-permute-done.11.rest_0_, bf16[512,128]{1,0:T(8,128)(2,1)} %collective-permute-done.16.rest_1_, ...), custom_call_target="tpu_custom_call" | custom-call | flops 1610612736 | bytes 5242880 | tf_op jit(solution)/shard_map/output/pallas_call | solution.py:203
  (93 shorter events, 23.6 us)
Async XLA Ops:
  6.5 93.5 %all-gather.3.cloned.1.call-start = ((), (), s32[]{:S(2)}) async-start(), calls=%async_computation.3 | async-start | bytes 3932160 | tf_op jit(solution)/shard_map/all_gather | solution.py:273
  18.2 93.4 %all-to-all-start = ((bf16[8,384,512]{2,1,0:T(8,128)(2,1)}), bf16[8,384,512]{2,1,0:T(8,128)(2,1)}, u32[]{:S(2)}, u32[]{:S(2)}) async-start(bf16[8,384,512]{2,1,0:T(8,128)(2,1)} %split_blocks.2), calls=%async_computation | async-start | bytes 6291456 | tf_op jit(solution)/shard_map/all_to_all | solution.py:229
  36.5 37.1 %collective-permute-start.4 = (bf16[384,768]{1,0:T(8,128)(2,1)S(1)}, bf16[384,768]{1,0:T(8,128)(2,1)S(1)}, u32[]{:S(2)}, u32[]{:S(2)}) collective-permute-start(bf16[384,768]{1,0:T(8,128)(2,1)S(1)} %get-tuple-element.49), channel_id=1, source_target_pairs={{0,8},{4,12},{8,0},{12,4},{16,24},{20,28},{24,16},{28,20},{1,9},{5... | collective-permute-start | bytes 1769480 | tf_op jit(solution)/shard_map/ppermute | solution.py:220
  38.7 34.9 %collective-permute-start.7 = (bf16[384,768]{1,0:T(8,128)(2,1)S(1)}, bf16[384,768]{1,0:T(8,128)(2,1)S(1)}, u32[]{:S(2)}, u32[]{:S(2)}) collective-permute-start(bf16[384,768]{1,0:T(8,128)(2,1)S(1)} %get-tuple-element.52), channel_id=1, source_target_pairs={{0,16},{4,20},{8,24},{12,28},{16,0},{20,4},{24,8},{28,12},{1,17},{... | collective-permute-start | bytes 1769480 | tf_op jit(solution)/shard_map/ppermute | solution.py:220
  40.2 47.1 %collective-permute-start.9 = (bf16[384,768]{1,0:T(8,128)(2,1)S(1)}, bf16[384,768]{1,0:T(8,128)(2,1)S(1)}, u32[]{:S(2)}, u32[]{:S(2)}) collective-permute-start(bf16[384,768]{1,0:T(8,128)(2,1)S(1)} %get-tuple-element.55), channel_id=1, source_target_pairs={{0,24},{4,28},{8,16},{12,20},{16,8},{20,12},{24,0},{28,4},{1,25},{... | collective-permute-start | bytes 1769480 | tf_op jit(solution)/shard_map/ppermute | solution.py:220
  73.6 44.8 %copy-start.21 = (bf16[384,768]{1,0:T(8,128)(2,1)}, bf16[384,768]{1,0:T(8,128)(2,1)S(1)}, u32[]{:S(2)}) copy-start(bf16[384,768]{1,0:T(8,128)(2,1)S(1)} %collective-permute-done.4.rest_2_) | copy-start | bytes 1769476
  73.6 24.2 %collective-permute-start.5 = (bf16[384,768]{1,0:T(8,128)(2,1)S(1)}, bf16[384,768]{1,0:T(8,128)(2,1)S(1)}, u32[]{:S(2)}, u32[]{:S(2)}) collective-permute-start(bf16[384,768]{1,0:T(8,128)(2,1)S(1)} %get-tuple-element.50), channel_id=1, source_target_pairs={{0,12},{4,8},{8,4},{12,0},{16,28},{20,24},{24,20},{28,16},{1,13},{... | collective-permute-start | bytes 1769480 | tf_op jit(solution)/shard_map/ppermute | solution.py:220
  73.6 44.8 %copy-start.22 = (bf16[384,768]{1,0:T(8,128)(2,1)}, bf16[384,768]{1,0:T(8,128)(2,1)S(1)}, u32[]{:S(2)}) copy-start(bf16[384,768]{1,0:T(8,128)(2,1)S(1)} %collective-permute-done.7.rest_4_) | copy-start | bytes 1769476
  73.6 37.9 %collective-permute-start.8 = (bf16[384,768]{1,0:T(8,128)(2,1)S(1)}, bf16[384,768]{1,0:T(8,128)(2,1)}, u32[]{:S(2)}, u32[]{:S(2)}) collective-permute-start(bf16[384,768]{1,0:T(8,128)(2,1)S(1)} %get-tuple-element.54), channel_id=1, source_target_pairs={{0,20},{4,16},{8,28},{12,24},{16,4},{20,0},{24,12},{28,8},{1,21},{... | collective-permute-start | bytes 1769480 | tf_op jit(solution)/shard_map/ppermute | solution.py:220
  87.3 24.3 %collective-permute-start.10 = (bf16[384,768]{1,0:T(8,128)(2,1)S(1)}, bf16[384,768]{1,0:T(8,128)(2,1)}, u32[]{:S(2)}, u32[]{:S(2)}) collective-permute-start(bf16[384,768]{1,0:T(8,128)(2,1)S(1)} %get-tuple-element.57), channel_id=1, source_target_pairs={{0,28},{4,24},{8,20},{12,16},{16,12},{20,8},{24,4},{28,0},{1,29},{... | collective-permute-start | bytes 1769480 | tf_op jit(solution)/shard_map/ppermute | solution.py:220
  97.8 13.8 %collective-permute-start.6 = (bf16[384,768]{1,0:T(8,128)(2,1)S(1)}, bf16[384,768]{1,0:T(8,128)(2,1)}, u32[]{:S(2)}, u32[]{:S(2)}) collective-permute-start(bf16[384,768]{1,0:T(8,128)(2,1)S(1)} %get-tuple-element.51), channel_id=1, source_target_pairs={{0,4},{4,0},{8,12},{12,8},{16,20},{20,16},{24,28},{28,24},{1,5},{5... | collective-permute-start | bytes 1769480 | tf_op jit(solution)/shard_map/ppermute | solution.py:220
  99.9 11.7 %collective-permute-start.15 = (f32[3072]{0:T(1024)S(1)}, f32[3072]{0:T(1024)S(1)}, u32[]{:S(2)}, u32[]{:S(2)}) collective-permute-start(f32[3072]{0:T(1024)S(1)} %bitcast.27), channel_id=1, source_target_pairs={{0,4},{4,8},{8,12},{12,16},{16,20},{20,24},{24,28},{28,0},{1,5},{5... | collective-permute-start | bytes 36872 | tf_op jit(solution)/shard_map/ppermute | solution.py:225
  111.6 47.5 %all-to-all-start.2 = ((bf16[8,384,384]{2,1,0:T(8,128)(2,1)}), bf16[8,384,384]{2,1,0:T(8,128)(2,1)S(1)}, u32[]{:S(2)}, u32[]{:S(2)}) async-start(bf16[8,384,384]{2,1,0:T(8,128)(2,1)} %copy-done.6), calls=%async_computation.2 | async-start | bytes 4718592 | tf_op jit(solution)/shard_map/all_to_all | solution.py:229
  118.5 45.0 %copy-start.25 = (f32[1,3,3072]{2,0,1:T(1,128)S(1)}, f32[1,3,3072]{2,0,1:T(1,128)}, u32[]{:S(2)}) copy-start(f32[1,3,3072]{2,0,1:T(1,128)} %param.7) | copy-start | bytes 110596
  118.5 37.3 %collective-permute-start = (bf16[768,512]{1,0:T(8,128)(2,1)S(1)}, bf16[768,512]{1,0:T(8,128)(2,1)S(1)}, u32[]{:S(2)}, u32[]{:S(2)}) collective-permute-start(bf16[768,512]{1,0:T(8,128)(2,1)S(1)} %get-tuple-element.82), channel_id=1, source_target_pairs={{0,1},{1,0},{2,3},{3,2},{4,5},{5,4},{6,7},{7,6},{8,9},{9,8},{10,11... | collective-permute-start | bytes 2359304 | tf_op jit(solution)/shard_map/ppermute | solution.py:220
  120.9 37.3 %collective-permute-start.1 = (bf16[768,512]{1,0:T(8,128)(2,1)S(1)}, bf16[768,512]{1,0:T(8,128)(2,1)S(1)}, u32[]{:S(2)}, u32[]{:S(2)}) collective-permute-start(bf16[768,512]{1,0:T(8,128)(2,1)S(1)} %get-tuple-element.81), channel_id=1, source_target_pairs={{0,2},{1,3},{2,0},{3,1},{4,6},{5,7},{6,4},{7,5},{8,10},{9,11},{10,... | collective-permute-start | bytes 2359304 | tf_op jit(solution)/shard_map/ppermute | solution.py:220
  159.1 67.1 %all-to-all-start.1 = ((bf16[8,384,384]{2,1,0:T(8,128)(2,1)}), bf16[8,384,384]{2,1,0:T(8,128)(2,1)}, u32[]{:S(2)}, u32[]{:S(2)}) async-start(bf16[8,384,384]{2,1,0:T(8,128)(2,1)} %copy-done.5), calls=%async_computation.1 | async-start | bytes 4718592 | tf_op jit(solution)/shard_map/all_to_all | solution.py:229
  167.1 32.9 %collective-permute-start.3 = (bf16[768,512]{1,0:T(8,128)(2,1)}, bf16[768,512]{1,0:T(8,128)(2,1)S(1)}, u32[]{:S(2)}, u32[]{:S(2)}) collective-permute-start(bf16[768,512]{1,0:T(8,128)(2,1)} %get-tuple-element.80), channel_id=1, source_target_pairs={{0,3},{1,2},{2,1},{3,0},{4,7},{5,6},{6,5},{7,4},{8,11},{9,10},{10,... | collective-permute-start | bytes 2359304 | tf_op jit(solution)/shard_map/ppermute | solution.py:220
  174.0 47.4 %copy-start.3 = (bf16[8,384,384]{2,1,0:T(8,128)(2,1)S(1)}, bf16[8,384,384]{2,1,0:T(8,128)(2,1)}, u32[]{:S(2)}) copy-start(bf16[8,384,384]{2,1,0:T(8,128)(2,1)} %copy-done.2) | copy-start | bytes 7077892
  183.8 11.9 %collective-permute-start.11 = (bf16[512,256]{1,0:T(8,128)(2,1)S(1)}, bf16[512,256]{1,0:T(8,128)(2,1)S(1)}, u32[]{:S(2)}, u32[]{:S(2)}) collective-permute-start(bf16[512,256]{1,0:T(8,128)(2,1)S(1)} %attend.4), channel_id=1, source_target_pairs={{0,4},{4,8},{8,12},{12,16},{16,20},{20,24},{24,28},{28,0},{1,5},{5... | collective-permute-start | bytes 786440 | tf_op jit(solution)/shard_map/ppermute | solution.py:225
  195.7 7.2 %collective-permute-start.12 = (bf16[512,256]{1,0:T(8,128)(2,1)S(1)}, bf16[512,256]{1,0:T(8,128)(2,1)S(1)}, u32[]{:S(2)}, u32[]{:S(2)}) collective-permute-start(bf16[512,256]{1,0:T(8,128)(2,1)S(1)} %collective-permute-done.11.rest_0_), channel_id=1, source_target_pairs={{0,1},{1,0},{2,3},{3,2},{4,5},{5,4},{6,7},{7,6},{8,9},{9,8},{10,11... | collective-permute-start | bytes 786440 | tf_op jit(solution)/shard_map/ppermute | solution.py:220
  196.1 25.2 %collective-permute-start.13 = (bf16[512,256]{1,0:T(8,128)(2,1)S(1)}, bf16[512,256]{1,0:T(8,128)(2,1)S(1)}, u32[]{:S(2)}, u32[]{:S(2)}) collective-permute-start(bf16[512,256]{1,0:T(8,128)(2,1)S(1)} %collective-permute-done.11.rest_0_), channel_id=1, source_target_pairs={{0,2},{1,3},{2,0},{3,1},{4,6},{5,7},{6,4},{7,5},{8,10},{9,11},{10,... | collective-permute-start | bytes 786440 | tf_op jit(solution)/shard_map/ppermute | solution.py:220
  198.7 22.7 %collective-permute-start.14 = (bf16[512,256]{1,0:T(8,128)(2,1)S(1)}, bf16[512,256]{1,0:T(8,128)(2,1)S(1)}, u32[]{:S(2)}, u32[]{:S(2)}) collective-permute-start(bf16[512,256]{1,0:T(8,128)(2,1)S(1)} %collective-permute-done.11.rest_0_), channel_id=1, source_target_pairs={{0,3},{1,2},{2,1},{3,0},{4,7},{5,6},{6,5},{7,4},{8,11},{9,10},{10,... | collective-permute-start | bytes 786440 | tf_op jit(solution)/shard_map/ppermute | solution.py:220
  225.9 10.8 %collective-permute-start.16 = (bf16[512,128]{1,0:T(8,128)(2,1)S(1)}, bf16[512,128]{1,0:T(8,128)(2,1)}, u32[]{:S(2)}, u32[]{:S(2)}) collective-permute-start(bf16[512,128]{1,0:T(8,128)(2,1)S(1)} %attend.5), channel_id=1, source_target_pairs={{0,4},{4,8},{8,12},{12,16},{16,20},{20,24},{24,28},{28,0},{1,5},{5... | collective-permute-start | bytes 393224 | tf_op jit(solution)/shard_map/ppermute | solution.py:225
  234.7 9.8 %collective-permute-start.2 = (bf16[512,128]{1,0:T(8,128)(2,1)S(1)}, bf16[512,128]{1,0:T(8,128)(2,1)S(1)}, u32[]{:S(2)}, u32[]{:S(2)}) collective-permute-start(bf16[512,128]{1,0:T(8,128)(2,1)S(1)} %attend.3), channel_id=1, source_target_pairs={{0,4},{4,8},{8,12},{12,16},{16,20},{20,24},{24,28},{28,0},{1,5},{5... | collective-permute-start | bytes 393224 | tf_op jit(solution)/shard_map/ppermute | solution.py:225
  236.8 10.4 %collective-permute-start.17 = (bf16[512,128]{1,0:T(8,128)(2,1)}, bf16[512,128]{1,0:T(8,128)(2,1)S(1)}, u32[]{:S(2)}, u32[]{:S(2)}) collective-permute-start(bf16[512,128]{1,0:T(8,128)(2,1)} %collective-permute-done.16.rest_1_), channel_id=1, source_target_pairs={{0,1},{1,0},{2,3},{3,2},{4,5},{5,4},{6,7},{7,6},{8,9},{9,8},{10,11... | collective-permute-start | bytes 393224 | tf_op jit(solution)/shard_map/ppermute | solution.py:220
  242.2 12.8 %collective-permute-start.18 = (bf16[512,128]{1,0:T(8,128)(2,1)}, bf16[512,128]{1,0:T(8,128)(2,1)S(1)}, u32[]{:S(2)}, u32[]{:S(2)}) collective-permute-start(bf16[512,128]{1,0:T(8,128)(2,1)} %collective-permute-done.16.rest_1_), channel_id=1, source_target_pairs={{0,2},{1,3},{2,0},{3,1},{4,6},{5,7},{6,4},{7,5},{8,10},{9,11},{10,... | collective-permute-start | bytes 393224 | tf_op jit(solution)/shard_map/ppermute | solution.py:220
  242.2 12.8 %collective-permute-start.19 = (bf16[512,128]{1,0:T(8,128)(2,1)}, bf16[512,128]{1,0:T(8,128)(2,1)S(1)}, u32[]{:S(2)}, u32[]{:S(2)}) collective-permute-start(bf16[512,128]{1,0:T(8,128)(2,1)} %collective-permute-done.16.rest_1_), channel_id=1, source_target_pairs={{0,3},{1,2},{2,1},{3,0},{4,7},{5,6},{6,5},{7,4},{8,11},{9,10},{10,... | collective-permute-start | bytes 393224 | tf_op jit(solution)/shard_map/ppermute | solution.py:220
  255.0 16.6 %collective-permute-start.20 = (bf16[512,768]{1,0:T(8,128)(2,1)S(1)}, bf16[512,768]{1,0:T(8,128)(2,1)S(1)}, u32[]{:S(2)}, u32[]{:S(2)}) collective-permute-start(bf16[512,768]{1,0:T(8,128)(2,1)S(1)} %bitcast.26), channel_id=1, source_target_pairs={{0,4},{4,8},{8,12},{12,16},{16,20},{20,24},{24,28},{28,0},{1,5},{5... | collective-permute-start | bytes 2359304 | tf_op jit(solution)/shard_map/ppermute | solution.py:225
  255.0 7.9 %collective-permute-start.23 = (bf16[512,128]{1,0:T(8,128)(2,1)S(1)}, bf16[512,128]{1,0:T(8,128)(2,1)S(1)}, u32[]{:S(2)}, u32[]{:S(2)}) collective-permute-start(bf16[512,128]{1,0:T(8,128)(2,1)S(1)} %collective-permute-done.2.rest_2_), channel_id=1, source_target_pairs={{0,3},{1,2},{2,1},{3,0},{4,7},{5,6},{6,5},{7,4},{8,11},{9,10},{10,... | collective-permute-start | bytes 393224 | tf_op jit(solution)/shard_map/ppermute | solution.py:220
  256.7 14.9 %collective-permute-start.22 = (bf16[512,128]{1,0:T(8,128)(2,1)S(1)}, bf16[512,128]{1,0:T(8,128)(2,1)S(1)}, u32[]{:S(2)}, u32[]{:S(2)}) collective-permute-start(bf16[512,128]{1,0:T(8,128)(2,1)S(1)} %collective-permute-done.2.rest_2_), channel_id=1, source_target_pairs={{0,2},{1,3},{2,0},{3,1},{4,6},{5,7},{6,4},{7,5},{8,10},{9,11},{10,... | collective-permute-start | bytes 393224 | tf_op jit(solution)/shard_map/ppermute | solution.py:220
  258.9 12.7 %collective-permute-start.21 = (bf16[512,128]{1,0:T(8,128)(2,1)S(1)}, bf16[512,128]{1,0:T(8,128)(2,1)S(1)}, u32[]{:S(2)}, u32[]{:S(2)}) collective-permute-start(bf16[512,128]{1,0:T(8,128)(2,1)S(1)} %collective-permute-done.2.rest_2_), channel_id=1, source_target_pairs={{0,1},{1,0},{2,3},{3,2},{4,5},{5,4},{6,7},{7,6},{8,9},{9,8},{10,11... | collective-permute-start | bytes 393224 | tf_op jit(solution)/shard_map/ppermute | solution.py:220
  (22 other events, 399.0 us)
Sparse Core Ops, SparseCore 0:
  8.9 66.1 all-gather.2

commit v8 on v7

--- a/solution.py
+++ b/solution.py
@@ -277,51 +277,57 @@
     out_plan = [[(3, head) for head in range(lanes)]]
     before = block_of((section_ids + sections - 1) % sections)
     (to_out,) = split_blocks(rows, before, section_ids, out_plan, lanes)
+    def waiting(block, *earlier):
+        return functools.reduce(after, earlier, block)
+
     half = max(1, lanes // 2)
-    groups = [(head,) for head in range(half, lanes)] + [tuple(range(half))]
+    groups = [tuple(range(half))] + [(head,) for head in range(half, lanes)][::-1]
     plan = [[(kind, head) for head in group for kind in range(3)] for group in groups]
     alone = len(groups) == 3
     order = after(block_of(sources), to_out)
     split = split_blocks(rows, order, sources, plan, lanes, alone)
 
-    pieces = list(split[len(groups) - 1 :]) if alone else []
-    chain = []
-    for distance in sorted(range(1, len(pieces)), key=lambda d: (d == 1, d % 2, d)):
-        piece = pieces[distance]
-        if len(chain) >= 3:
-            piece = after(piece, chain[-3])
-        chain.append(swapped(piece, "section", distance))
-        pieces[distance] = chain[-1]
-
     to_out = relayed(to_out)
-    matrices = []
-    for distance in range(tp):
-        held = lax.dynamic_slice_in_dim(to_out, (rank ^ distance) * share, share, 0)
-        matrices.append(swapped(held, "tp", distance) if distance else held)
+    held = [
+        lax.dynamic_slice_in_dim(to_out, (rank ^ distance) * share, share, 0)
+        for distance in range(tp)
+    ]
+    matrices = held[:1] + [swapped(held[distance], "tp", distance) for distance in range(1, tp)]
 
     attended = [[] for _ in range(tp)]
 
-    def share_out(group, matrix, ready, *earlier):
-        own = attend(waiting(normed, *ready), matrix, patch_index, stale_cache[0], group)
+    def share_out(own, *earlier):
         moved = waiting(handed_on(own), *earlier)
         parts = [swapped(moved, "tp", distance) if distance else moved for distance in range(tp)]
         for kept, part in zip(attended, parts):
             kept.append(part)
         return parts
 
-    def waiting(block, *earlier):
-        return functools.reduce(after, earlier, block)
-
+    def attended_by(index, matrix, *earlier):
+        ready = waiting(normed, *earlier)
+        return attend(ready, matrix, patch_index, stale_cache[0], groups[index])
+
+    first = relayed(split[0])
     if alone:
-        matrix = relayed(waiting(split[0], tokens, gate, *chain))
-        last = relayed(waiting(split[1], *matrices[1:3]))
-        placed_rows = placed(pieces, sources)
-        parts = share_out(groups[2], placed_rows.reshape(-1, placed_rows.shape[2]), ())
-        parts = share_out(groups[0], matrix, (*matrices[3:], *parts))
-        parts = share_out(groups[1], last, (), *parts)
+        pieces = list(split[2:])
+        chain = []
+        for distance in sorted(range(1, sections), key=lambda d: (d == 1, d % 2, d)):
+            earlier = [chain[-3]] if len(chain) > 2 else matrices[1:2]
+            if len(chain) == 1:
+                earlier.append(tokens)
+            chain.append(swapped(waiting(pieces[distance], *earlier), "section", distance))
+            pieces[distance] = chain[-1]
+        own = attended_by(0, first, gate)
+        last = relayed(waiting(split[1], own, *chain, *matrices[1:]))
+        done = share_out(own)
+        middle = placed(pieces, sources)
+        middle = middle.reshape(-1, middle.shape[2])
+        parts = share_out(attended_by(2, middle, done[0]))
+        parts = share_out(attended_by(1, last, *done, parts[0]), *parts)
     else:
-        for group, own in zip(groups, split):
-            parts = share_out(group, relayed(own), ())
+        for index, pieces in enumerate(split):
+            moved = first if index == 0 else relayed(pieces)
+            parts = share_out(attended_by(index, moved))
     carried = handed_on(after(inflow[0], parts[0]))
     gate = lax.dynamic_slice_in_dim(gate, rank * share, share, 0)[None]
     return output(carried, gate, attended, matrices)[None]

time: 283 us -> 290 us (1.025)
  starting transfers between devices: 46.8 us -> 58.3 us
  waiting for transfers between devices: 157 us -> 146 us
  local copies, waits for them, and re-layouts: 12.5 us -> 16.5 us
    ppermute x19, waiting for transfers between devices: 133 us -> 91.3 us  [swapped(): lax.ppermute(block, axis, [(i, i ^ distance) for i in range(lax.axis_size...]
    all_to_all x3, waiting for transfers between devices: 0.01 us -> 22.6 us  [relayed(): lax.all_to_all(pieces, 'section', split_axis=0, concat_axis=0, tiled=True)]
    ppermute x19, starting transfers between devices: 31 us -> 42.9 us  [swapped(): lax.ppermute(block, axis, [(i, i ^ distance) for i in range(lax.axis_size...]
    ppermute x5, waiting for transfers between devices: 23.3 us -> 31.8 us  [handed_on(): lax.ppermute(block, 'section', [(i, (i + 1) % sections) for i in range(se...]
    unnamed x53 -> x43, local copies, waits for them, and re-layouts: 8.48 us -> 13.1 us
  transfers between devices with their start and end apart: 28 -> 28, of which waited for: 13 -> 12; matrix products, arithmetic and copies ran while one was open for 2% -> 1% of each run, Pallas kernels for 17% -> 11%
where the time goes in v8:
time: 290 us; the launch traced here: 289 us
  waiting for transfers between devices  146 us (50%)
  starting transfers between devices  58.3 us (20%)
  Pallas kernels  52.4 us (18%)
  local copies, waits for them, and re-layouts  16.5 us (6%)
  between operations  14.4 us (5%)
    ppermute x19, waiting for transfers between devices, swapped(): lax.ppermute(block, axis, [(i, i ^ distance) for i in range(lax.axis_size...  91.3 us
    ppermute x19, starting transfers between devices, swapped(): lax.ppermute(block, axis, [(i, i ^ distance) for i in range(lax.axis_size...  42.9 us
    ppermute x5, waiting for transfers between devices, handed_on(): lax.ppermute(block, 'section', [(i, (i + 1) % sections) for i in range(se...  31.8 us
    all_to_all x3, waiting for transfers between devices, relayed(): lax.all_to_all(pieces, 'section', split_axis=0, concat_axis=0, tiled=True)  22.6 us
    pallas_call x3, Pallas kernels, attend(): pl.pallas_call(attend_kernel, grid_spec=pltpu.PrefetchScalarGridSpec(num_...  21.5 us
    pallas_call x2, Pallas kernels, split_blocks(): pl.pallas_call(functools.partial(split_kernel, lanes, plan, single, kinds...  20.4 us
    all_to_all x3, starting transfers between devices, relayed(): lax.all_to_all(pieces, 'section', split_axis=0, concat_axis=0, tiled=True)  14.2 us
    unnamed x43, local copies, waits for them, and re-layouts  13.1 us
  transfers between devices with their start and end apart: 28, of which 12 were waited for; matrix products, arithmetic and copies ran while one was open for 1% of the time, Pallas kernels for 11%

profile of v8, /device:TPU:0, one launch (start us, length us, event | category | flops | bytes accessed | tf_op | source)
XLA Modules:
  0.0 288.8 jit_solution(12700382496782618723)
XLA Ops:
  7.4 10.0 %split_blocks.2 = bf16[8,384,512]{2,1,0:T(8,128)(2,1)} custom-call(s32[8]{0:T(128)S(1)} %get-tuple-element.87.order_ref, s32[8]{0:T(128)S(1)} %iota.16.to_ref, bf16[8,6144,128]{2,1,0:T(8,128)(2,1)} %bitcast.22), custom_call_target="tpu_custom_call" | custom-call | bytes 18874368 | tf_op jit(solution)/shard_map/split_blocks/pallas_call | solution.py:94
  17.5 5.2 %all-to-all-start.1 = ((bf16[8,384,512]{2,1,0:T(8,128)(2,1)}), bf16[8,384,512]{2,1,0:T(8,128)(2,1)}, u32[]{:S(2)}, u32[]{:S(2)}) async-start(bf16[8,384,512]{2,1,0:T(8,128)(2,1)} %split_blocks.2), calls=%async_computation.1 | async-start | bytes 6291456 | tf_op jit(solution)/shard_map/all_to_all | solution.py:229
  23.4 10.4 %split_blocks.3 = (bf16[8,384,768]{2,1,0:T(8,128)(2,1)S(1)}, bf16[8,384,384]{2,1,0:T(8,128)(2,1)S(1)}, bf16[384,384]{1,0:T(8,128)(2,1)S(1)}, bf16[384,384]{1,0:T...) custom-call(s32[8]{0:T(128)S(1)} %get-tuple-element.47.order_ref, ...), custom_call_target="tpu_custom_call" | custom-call | bytes 18874368 | tf_op jit(solution)/shard_map/split_blocks/pallas_call | solution.py:94
  33.8 2.2 copy-done.3
  38.0 22.6 %all-to-all-done.1 = bf16[8,384,512]{2,1,0:T(8,128)(2,1)} async-done(((bf16[8,384,512]{2,1,0:T(8,128)(2,1)}), bf16[8,384,512]{2,1,0:T(8,128)(2,1)}, u32[]{:S(2)}, u32[]{:S(2)}) %all-to-all-start.1) | async-done | bytes 3145760 | tf_op jit(solution)/shard_map/all_to_all | solution.py:229
  60.6 4.6 %all-to-all-start = ((bf16[8,384,768]{2,1,0:T(8,128)(2,1)}), bf16[8,384,768]{2,1,0:T(8,128)(2,1)}, u32[]{:S(2)}, u32[]{:S(2)}) async-start(bf16[8,384,768]{2,1,0:T(8,128)(2,1)} %copy-done.3), calls=%async_computation | async-start | bytes 9437184 | tf_op jit(solution)/shard_map/all_to_all | solution.py:229
  65.3 3.3 %constant_dynamic-slice_fusion.3 = (bf16[768,512]{1,0:T(8,128)(2,1)}, bf16[768,512]{1,0:T(8,128)(2,1)}, bf16[768,512]{1,0:T(8,128)(2,1)}, bf16[768,512]{1,0:T(8,128)(2,1)S(1)}) fusion(bf16[3072,512]{1,0:T(8,128)(2,1)} %bitcast.8, s32[]{:T(128)S(6)} %select_n.28, s32[]{:T(128)S(6)} %select_n.27, s32[]{:T(128)S(6)} %select_n.26, s32[]{:T(128)S(6)} %select_n.25), kind=kLoop, calls=%fused_computation.9 | loop fusion | bytes 6291472 | tf_op jit(solution)/shard_map/dynamic_slice | solution.py:292
  68.6 2.2 collective-permute-start.5
  70.8 34.7 %collective-permute-done.5.rest_13_ = bf16[768,512]{1,0:T(8,128)(2,1)S(1)} collective-permute-done((bf16[768,512]{1,0:T(8,128)(2,1)S(1)}, bf16[768,512]{1,0:T(8,128)(2,1)S(1)}, u32[]{:S(2)}, u32[]{:S(2)}) %collective-permute-start.5) | collective-permute-done | bytes 786464 | tf_op jit(solution)/shard_map/ppermute | solution.py:220
  107.9 2.8 collective-permute-start.14
  112.6 13.1 %collective-permute-done.6.rest_2_ = bf16[384,384]{1,0:T(8,128)(2,1)S(1)} collective-permute-done((bf16[384,384]{1,0:T(8,128)(2,1)S(1)}, bf16[384,384]{1,0:T(8,128)(2,1)S(1)}, u32[]{:S(2)}, u32[]{:S(2)}) %collective-permute-start.6) | collective-permute-done | bytes 294944 | tf_op jit(solution)/shard_map/ppermute | solution.py:220
  128.0 5.1 %collective-permute-done.11.rest_6_ = bf16[384,384]{1,0:T(8,128)(2,1)S(1)} collective-permute-done((bf16[384,384]{1,0:T(8,128)(2,1)S(1)}, bf16[384,384]{1,0:T(8,128)(2,1)S(1)}, u32[]{:S(2)}, u32[]{:S(2)}) %collective-permute-start.11) | collective-permute-done | bytes 294944 | tf_op jit(solution)/shard_map/ppermute | solution.py:220
  133.8 3.7 %collective-permute-done.7.rest_3_ = bf16[384,384]{1,0:T(8,128)(2,1)S(1)} collective-permute-done((bf16[384,384]{1,0:T(8,128)(2,1)S(1)}, bf16[384,384]{1,0:T(8,128)(2,1)S(1)}, u32[]{:S(2)}, u32[]{:S(2)}) %collective-permute-start.7) | collective-permute-done | bytes 294944 | tf_op jit(solution)/shard_map/ppermute | solution.py:220
  137.5 2.0 collective-permute-start.12
  139.4 4.1 %norm.1.normed_ref = bf16[512,3072]{1,0:T(8,128)(2,1)S(1)} custom-call(bf16[512,3072]{1,0:T(8,128)(2,1)} %bitcast.24, f32[3,3072]{1,0:T(4,128)S(1)} %bitcast.21), custom_call_target="tpu_custom_call" | custom-call | flops 15728640 | bytes 6291456 | tf_op jit(solution)/shard_map/norm/pallas_call | solution.py:125
  144.4 2.2 copy-done
  146.6 10.7 %attend.3 = bf16[512,256]{1,0:T(8,128)(2,1)S(1)} custom-call(s32[1]{0:T(128)S(6)} %copy.12.where_ref, bf16[512,3072]{1,0:T(8,128)(2,1)S(1)} %norm.1.normed_ref, bf16[3072,768]{1,0:T(8,128)(2,1)} %bitcast.6.matrix_ref, bf16[2,2048,512]{2,1,0:T(8,128)(2,1)S(1)} %bitcast.17), custom_call_target="tpu_custom_call" | custom-call | flops 3489660928 | bytes 6815744 | tf_op jit(solution)/shard_map/attend/pallas_call | solution.py:165
  158.0 4.4 %collective-permute-done.14.rest_14_ = bf16[768,512]{1,0:T(8,128)(2,1)} collective-permute-done((bf16[768,512]{1,0:T(8,128)(2,1)}, bf16[768,512]{1,0:T(8,128)(2,1)}, u32[]{:S(2)}, u32[]{:S(2)}) %collective-permute-start.14) | collective-permute-done | bytes 786464 | tf_op jit(solution)/shard_map/ppermute | solution.py:220
  162.4 4.4 %all-to-all-start.2 = ((bf16[8,384,384]{2,1,0:T(8,128)(2,1)}), bf16[8,384,384]{2,1,0:T(8,128)(2,1)}, u32[]{:S(2)}, u32[]{:S(2)}) async-start(bf16[8,384,384]{2,1,0:T(8,128)(2,1)} %copy-done.5), calls=%async_computation.2 | async-start | bytes 4718592 | tf_op jit(solution)/shard_map/all_to_all | solution.py:229
  167.2 31.8 %collective-permute-done.1.rest_0_ = bf16[512,256]{1,0:T(8,128)(2,1)S(1)} collective-permute-done((bf16[512,256]{1,0:T(8,128)(2,1)}, bf16[512,256]{1,0:T(8,128)(2,1)S(1)}, u32[]{:S(2)}, u32[]{:S(2)}) %collective-permute-start.1) | collective-permute-done | bytes 262176 | tf_op jit(solution)/shard_map/ppermute | solution.py:225
  198.9 17.3 %collective-permute-start.2 = (bf16[512,256]{1,0:T(8,128)(2,1)S(1)}, bf16[512,256]{1,0:T(8,128)(2,1)S(1)}, u32[]{:S(2)}, u32[]{:S(2)}) collective-permute-start(bf16[512,256]{1,0:T(8,128)(2,1)S(1)} %collective-permute-done.1.rest_0_), channel_id=1, source_target_pairs={{0,1},{1,0},{2,3},{3,2},{4,5},{5,4},{6,7},{7,6},{8,9},{9,8},{10,11... | collective-permute-start | bytes 786440 | tf_op jit(solution)/shard_map/ppermute | solution.py:220
  216.9 1.6 collective-permute-start.4
  218.6 2.2 placed.1
  220.8 4.6 %attend.4 = bf16[512,128]{1,0:T(8,128)(2,1)S(1)} custom-call(s32[1]{0:T(128)S(6)} %copy.12.where_ref, bf16[512,3072]{1,0:T(8,128)(2,1)S(1)} %norm.1.normed_ref, bf16[3072,384]{1,0:T(8,128)(2,1)S(1)} %bitcast.20, bf16[2,2048,512]{2,1,0:T(8,128)(2,1)S(1)} %bitcast.18), custom_call_target="tpu_custom_call" | custom-call | flops 1744830464 | bytes 3407872 | tf_op jit(solution)/shard_map/attend/pallas_call | solution.py:165
  226.3 10.0 %collective-permute-done.3.rest_6_ = bf16[512,256]{1,0:T(8,128)(2,1)S(1)} collective-permute-done((bf16[512,256]{1,0:T(8,128)(2,1)S(1)}, bf16[512,256]{1,0:T(8,128)(2,1)S(1)}, u32[]{:S(2)}, u32[]{:S(2)}) %collective-permute-start.3) | collective-permute-done | bytes 262176 | tf_op jit(solution)/shard_map/ppermute | solution.py:220
  237.6 2.2 copy-done.2
  239.9 6.3 %attend.5 = bf16[512,128]{1,0:T(8,128)(2,1)S(1)} custom-call(s32[1]{0:T(128)S(6)} %copy.12.where_ref, bf16[512,3072]{1,0:T(8,128)(2,1)S(1)} %norm.1.normed_ref, bf16[3072,384]{1,0:T(8,128)(2,1)} %bitcast.10.matrix_ref, bf16[2,2048,512]{2,1,0:T(8,128)(2,1)S(1)} %bitcast.19), custom_call_target="tpu_custom_call" | custom-call | flops 1744830464 | bytes 3407872 | tf_op jit(solution)/shard_map/attend/pallas_call | solution.py:165
  246.2 2.8 collective-permute-start.17
  252.4 9.2 %collective-permute-done.18.rest_7_ = bf16[512,128]{1,0:T(8,128)(2,1)S(1)} collective-permute-done((bf16[512,128]{1,0:T(8,128)(2,1)S(1)}, bf16[512,128]{1,0:T(8,128)(2,1)S(1)}, u32[]{:S(2)}, u32[]{:S(2)}) %collective-permute-start.18) | collective-permute-done | bytes 131104 | tf_op jit(solution)/shard_map/ppermute | solution.py:220
  262.1 3.0 %collective-permute-start.21 = (bf16[512,128]{1,0:T(8,128)(2,1)S(1)}, bf16[512,128]{1,0:T(8,128)(2,1)S(1)}, u32[]{:S(2)}, u32[]{:S(2)}) collective-permute-start(bf16[512,128]{1,0:T(8,128)(2,1)S(1)} %collective-permute-done.16.rest_2_), channel_id=1, source_target_pairs={{0,1},{1,0},{2,3},{3,2},{4,5},{5,4},{6,7},{7,6},{8,9},{9,8},{10,11... | collective-permute-start | bytes 393224 | tf_op jit(solution)/shard_map/ppermute | solution.py:220
  268.6 9.2 %collective-permute-done.22.rest_8_ = bf16[512,128]{1,0:T(8,128)(2,1)S(1)} collective-permute-done((bf16[512,128]{1,0:T(8,128)(2,1)S(1)}, bf16[512,128]{1,0:T(8,128)(2,1)S(1)}, u32[]{:S(2)}, u32[]{:S(2)}) %collective-permute-start.22) | collective-permute-done | bytes 131104 | tf_op jit(solution)/shard_map/ppermute | solution.py:220
  277.8 4.1 %output.1 = bf16[512,768]{1,0:T(8,128)(2,1)} custom-call(bf16[512,768]{1,0:T(8,128)(2,1)S(1)} %collective-permute-done.20.inflow_ref, f32[1,768]{1,0:T(1,128)S(1)} %broadcast_in_dim.4.gate_ref, bf16[512,256]{1,0:T(8,128)(2,1)S(1)} %collective-permute-done.1.rest_0_, bf16[512,128]{1,0:T(8,128)(2,1)S(1)} %collective-permute-done.13.rest_1_, ...), custom_call_target="tpu_custom_call" | custom-call | flops 1610612736 | bytes 5242880 | tf_op jit(solution)/shard_map/output/pallas_call | solution.py:203
  (83 shorter events, 22.6 us)
Async XLA Ops:
  17.5 43.2 %all-to-all-start.1 = ((bf16[8,384,512]{2,1,0:T(8,128)(2,1)}), bf16[8,384,512]{2,1,0:T(8,128)(2,1)}, u32[]{:S(2)}, u32[]{:S(2)}) async-start(bf16[8,384,512]{2,1,0:T(8,128)(2,1)} %split_blocks.2), calls=%async_computation.1 | async-start | bytes 6291456 | tf_op jit(solution)/shard_map/all_to_all | solution.py:229
  22.6 103.8 %all-gather.3.cloned.1.call-start = ((), (), s32[]{:S(2)}) async-start(), calls=%async_computation.3 | async-start | bytes 3932160 | tf_op jit(solution)/shard_map/all_gather | solution.py:273
  60.6 83.8 %all-to-all-start = ((bf16[8,384,768]{2,1,0:T(8,128)(2,1)}), bf16[8,384,768]{2,1,0:T(8,128)(2,1)}, u32[]{:S(2)}, u32[]{:S(2)}) async-start(bf16[8,384,768]{2,1,0:T(8,128)(2,1)} %copy-done.3), calls=%async_computation | async-start | bytes 9437184 | tf_op jit(solution)/shard_map/all_to_all | solution.py:229
  65.3 62.7 %copy-start.20 = (f32[1,3,3072]{2,0,1:T(1,128)S(1)}, f32[1,3,3072]{2,0,1:T(1,128)}, u32[]{:S(2)}) copy-start(f32[1,3,3072]{2,0,1:T(1,128)} %param.7) | copy-start | bytes 110596
  68.6 36.9 %collective-permute-start.5 = (bf16[768,512]{1,0:T(8,128)(2,1)S(1)}, bf16[768,512]{1,0:T(8,128)(2,1)S(1)}, u32[]{:S(2)}, u32[]{:S(2)}) collective-permute-start(bf16[768,512]{1,0:T(8,128)(2,1)S(1)} %get-tuple-element.92), channel_id=1, source_target_pairs={{0,1},{1,0},{2,3},{3,2},{4,5},{5,4},{6,7},{7,6},{8,9},{9,8},{10,11... | collective-permute-start | bytes 2359304 | tf_op jit(solution)/shard_map/ppermute | solution.py:220
  106.5 19.3 %collective-permute-start.6 = (bf16[384,384]{1,0:T(8,128)(2,1)S(1)}, bf16[384,384]{1,0:T(8,128)(2,1)S(1)}, u32[]{:S(2)}, u32[]{:S(2)}) collective-permute-start(bf16[384,384]{1,0:T(8,128)(2,1)S(1)} %get-tuple-element.57), channel_id=1, source_target_pairs={{0,8},{4,12},{8,0},{12,4},{16,24},{20,28},{24,16},{28,20},{1,9},{5... | collective-permute-start | bytes 884744 | tf_op jit(solution)/shard_map/ppermute | solution.py:220
  107.9 54.5 %collective-permute-start.14 = (bf16[768,512]{1,0:T(8,128)(2,1)}, bf16[768,512]{1,0:T(8,128)(2,1)}, u32[]{:S(2)}, u32[]{:S(2)}) collective-permute-start(bf16[768,512]{1,0:T(8,128)(2,1)} %get-tuple-element.91), channel_id=1, source_target_pairs={{0,2},{1,3},{2,0},{3,1},{4,6},{5,7},{6,4},{7,5},{8,10},{9,11},{10,... | collective-permute-start | bytes 2359304 | tf_op jit(solution)/shard_map/ppermute | solution.py:220
  110.7 51.7 %collective-permute-start.15 = (bf16[768,512]{1,0:T(8,128)(2,1)}, bf16[768,512]{1,0:T(8,128)(2,1)}, u32[]{:S(2)}, u32[]{:S(2)}) collective-permute-start(bf16[768,512]{1,0:T(8,128)(2,1)} %get-tuple-element.90), channel_id=1, source_target_pairs={{0,3},{1,2},{2,1},{3,0},{4,7},{5,6},{6,5},{7,4},{8,11},{9,10},{10,... | collective-permute-start | bytes 2359304 | tf_op jit(solution)/shard_map/ppermute | solution.py:220
  111.2 21.9 %collective-permute-start.11 = (bf16[384,384]{1,0:T(8,128)(2,1)S(1)}, bf16[384,384]{1,0:T(8,128)(2,1)S(1)}, u32[]{:S(2)}, u32[]{:S(2)}) collective-permute-start(bf16[384,384]{1,0:T(8,128)(2,1)S(1)} %get-tuple-element.66), channel_id=1, source_target_pairs={{0,24},{4,28},{8,16},{12,20},{16,8},{20,12},{24,0},{28,4},{1,25},{... | collective-permute-start | bytes 884744 | tf_op jit(solution)/shard_map/ppermute | solution.py:220
  125.8 11.7 %collective-permute-start.7 = (bf16[384,384]{1,0:T(8,128)(2,1)S(1)}, bf16[384,384]{1,0:T(8,128)(2,1)S(1)}, u32[]{:S(2)}, u32[]{:S(2)}) collective-permute-start(bf16[384,384]{1,0:T(8,128)(2,1)S(1)} %get-tuple-element.58), channel_id=1, source_target_pairs={{0,12},{4,8},{8,4},{12,0},{16,28},{20,24},{24,20},{28,16},{1,13},{... | collective-permute-start | bytes 884744 | tf_op jit(solution)/shard_map/ppermute | solution.py:220
  126.5 17.2 %collective-permute-start.9 = (bf16[384,384]{1,0:T(8,128)(2,1)}, bf16[384,384]{1,0:T(8,128)(2,1)}, u32[]{:S(2)}, u32[]{:S(2)}) collective-permute-start(bf16[384,384]{1,0:T(8,128)(2,1)} %get-tuple-element.62), channel_id=1, source_target_pairs={{0,16},{4,20},{8,24},{12,28},{16,0},{20,4},{24,8},{28,12},{1,17},{... | collective-permute-start | bytes 884744 | tf_op jit(solution)/shard_map/ppermute | solution.py:220
  133.0 10.5 %collective-permute-start = (f32[3072]{0:T(1024)S(1)}, f32[3072]{0:T(1024)S(1)}, u32[]{:S(2)}, u32[]{:S(2)}) collective-permute-start(f32[3072]{0:T(1024)S(1)} %bitcast.26), channel_id=1, source_target_pairs={{0,4},{4,8},{8,12},{12,16},{16,20},{20,24},{24,28},{28,0},{1,5},{5... | collective-permute-start | bytes 36872 | tf_op jit(solution)/shard_map/ppermute | solution.py:225
  137.5 20.5 %collective-permute-start.12 = (bf16[384,384]{1,0:T(8,128)(2,1)}, bf16[384,384]{1,0:T(8,128)(2,1)}, u32[]{:S(2)}, u32[]{:S(2)}) collective-permute-start(bf16[384,384]{1,0:T(8,128)(2,1)} %get-tuple-element.68), channel_id=1, source_target_pairs={{0,28},{4,24},{8,20},{12,16},{16,12},{20,8},{24,4},{28,0},{1,29},{... | collective-permute-start | bytes 884744 | tf_op jit(solution)/shard_map/ppermute | solution.py:220
  143.6 14.4 %collective-permute-start.8 = (bf16[384,384]{1,0:T(8,128)(2,1)}, bf16[384,384]{1,0:T(8,128)(2,1)}, u32[]{:S(2)}, u32[]{:S(2)}) collective-permute-start(bf16[384,384]{1,0:T(8,128)(2,1)} %get-tuple-element.59), channel_id=1, source_target_pairs={{0,4},{4,0},{8,12},{12,8},{16,20},{20,16},{24,28},{28,24},{1,5},{5... | collective-permute-start | bytes 884744 | tf_op jit(solution)/shard_map/ppermute | solution.py:220
  143.7 14.3 %collective-permute-start.10 = (bf16[384,384]{1,0:T(8,128)(2,1)}, bf16[384,384]{1,0:T(8,128)(2,1)}, u32[]{:S(2)}, u32[]{:S(2)}) collective-permute-start(bf16[384,384]{1,0:T(8,128)(2,1)} %get-tuple-element.64), channel_id=1, source_target_pairs={{0,20},{4,16},{8,28},{12,24},{16,4},{20,0},{24,12},{28,8},{1,21},{... | collective-permute-start | bytes 884744 | tf_op jit(solution)/shard_map/ppermute | solution.py:220
  162.4 75.2 %all-to-all-start.2 = ((bf16[8,384,384]{2,1,0:T(8,128)(2,1)}), bf16[8,384,384]{2,1,0:T(8,128)(2,1)}, u32[]{:S(2)}, u32[]{:S(2)}) async-start(bf16[8,384,384]{2,1,0:T(8,128)(2,1)} %copy-done.5), calls=%async_computation.2 | async-start | bytes 4718592 | tf_op jit(solution)/shard_map/all_to_all | solution.py:229
  166.8 54.0 %copy-start.1 = (bf16[1,2,2048,512]{3,2,1,0:T(8,128)(2,1)S(1)}, bf16[1,2,2048,512]{3,2,1,0:T(8,128)(2,1)}, u32[]{:S(2)}) copy-start(bf16[1,2,2048,512]{3,2,1,0:T(8,128)(2,1)} %param.9) | copy-start | bytes 12582916
  166.8 32.2 %collective-permute-start.1 = (bf16[512,256]{1,0:T(8,128)(2,1)}, bf16[512,256]{1,0:T(8,128)(2,1)S(1)}, u32[]{:S(2)}, u32[]{:S(2)}) collective-permute-start(bf16[512,256]{1,0:T(8,128)(2,1)} %copy-done.15), channel_id=1, source_target_pairs={{0,4},{4,8},{8,12},{12,16},{16,20},{20,24},{24,28},{28,0},{1,5},{5... | collective-permute-start | bytes 786440 | tf_op jit(solution)/shard_map/ppermute | solution.py:225
  198.9 26.6 %collective-permute-start.2 = (bf16[512,256]{1,0:T(8,128)(2,1)S(1)}, bf16[512,256]{1,0:T(8,128)(2,1)S(1)}, u32[]{:S(2)}, u32[]{:S(2)}) collective-permute-start(bf16[512,256]{1,0:T(8,128)(2,1)S(1)} %collective-permute-done.1.rest_0_), channel_id=1, source_target_pairs={{0,1},{1,0},{2,3},{3,2},{4,5},{5,4},{6,7},{7,6},{8,9},{9,8},{10,11... | collective-permute-start | bytes 786440 | tf_op jit(solution)/shard_map/ppermute | solution.py:220
  216.2 20.1 %collective-permute-start.3 = (bf16[512,256]{1,0:T(8,128)(2,1)S(1)}, bf16[512,256]{1,0:T(8,128)(2,1)S(1)}, u32[]{:S(2)}, u32[]{:S(2)}) collective-permute-start(bf16[512,256]{1,0:T(8,128)(2,1)S(1)} %collective-permute-done.1.rest_0_), channel_id=1, source_target_pairs={{0,2},{1,3},{2,0},{3,1},{4,6},{5,7},{6,4},{7,5},{8,10},{9,11},{10,... | collective-permute-start | bytes 786440 | tf_op jit(solution)/shard_map/ppermute | solution.py:220
  216.9 20.0 %collective-permute-start.4 = (bf16[512,256]{1,0:T(8,128)(2,1)S(1)}, bf16[512,256]{1,0:T(8,128)(2,1)S(1)}, u32[]{:S(2)}, u32[]{:S(2)}) collective-permute-start(bf16[512,256]{1,0:T(8,128)(2,1)S(1)} %collective-permute-done.1.rest_0_), channel_id=1, source_target_pairs={{0,3},{1,2},{2,1},{3,0},{4,7},{5,6},{6,5},{7,4},{8,11},{9,10},{10,... | collective-permute-start | bytes 786440 | tf_op jit(solution)/shard_map/ppermute | solution.py:220
  225.3 12.3 %collective-permute-start.13 = (bf16[512,128]{1,0:T(8,128)(2,1)S(1)}, bf16[512,128]{1,0:T(8,128)(2,1)S(1)}, u32[]{:S(2)}, u32[]{:S(2)}) collective-permute-start(bf16[512,128]{1,0:T(8,128)(2,1)S(1)} %attend.4), channel_id=1, source_target_pairs={{0,4},{4,8},{8,12},{12,16},{16,20},{20,24},{24,28},{28,0},{1,5},{5... | collective-permute-start | bytes 393224 | tf_op jit(solution)/shard_map/ppermute | solution.py:225
  239.8 37.9 %copy-start.12 = (bf16[512,256]{1,0:T(8,128)(2,1)S(1)}, bf16[512,256]{1,0:T(8,128)(2,1)}, u32[]{:S(2)}) copy-start(bf16[512,256]{1,0:T(8,128)(2,1)} %copy-done.11) | copy-start | bytes 786436
  239.8 37.9 %copy-start.14 = (bf16[512,256]{1,0:T(8,128)(2,1)S(1)}, bf16[512,256]{1,0:T(8,128)(2,1)}, u32[]{:S(2)}) copy-start(bf16[512,256]{1,0:T(8,128)(2,1)} %copy-done.13) | copy-start | bytes 786436
  246.2 5.3 %collective-permute-start.16 = (bf16[512,128]{1,0:T(8,128)(2,1)S(1)}, bf16[512,128]{1,0:T(8,128)(2,1)S(1)}, u32[]{:S(2)}, u32[]{:S(2)}) collective-permute-start(bf16[512,128]{1,0:T(8,128)(2,1)S(1)} %attend.5), channel_id=1, source_target_pairs={{0,4},{4,8},{8,12},{12,16},{16,20},{20,24},{24,28},{28,0},{1,5},{5... | collective-permute-start | bytes 393224 | tf_op jit(solution)/shard_map/ppermute | solution.py:225
  246.2 6.2 %collective-permute-start.17 = (bf16[512,128]{1,0:T(8,128)(2,1)S(1)}, bf16[512,128]{1,0:T(8,128)(2,1)S(1)}, u32[]{:S(2)}, u32[]{:S(2)}) collective-permute-start(bf16[512,128]{1,0:T(8,128)(2,1)S(1)} %collective-permute-done.13.rest_1_), channel_id=1, source_target_pairs={{0,1},{1,0},{2,3},{3,2},{4,5},{5,4},{6,7},{7,6},{8,9},{9,8},{10,11... | collective-permute-start | bytes 393224 | tf_op jit(solution)/shard_map/ppermute | solution.py:220
  249.0 12.5 %collective-permute-start.18 = (bf16[512,128]{1,0:T(8,128)(2,1)S(1)}, bf16[512,128]{1,0:T(8,128)(2,1)S(1)}, u32[]{:S(2)}, u32[]{:S(2)}) collective-permute-start(bf16[512,128]{1,0:T(8,128)(2,1)S(1)} %collective-permute-done.13.rest_1_), channel_id=1, source_target_pairs={{0,2},{1,3},{2,0},{3,1},{4,6},{5,7},{6,4},{7,5},{8,10},{9,11},{10,... | collective-permute-start | bytes 393224 | tf_op jit(solution)/shard_map/ppermute | solution.py:220
  249.9 11.7 %collective-permute-start.19 = (bf16[512,128]{1,0:T(8,128)(2,1)S(1)}, bf16[512,128]{1,0:T(8,128)(2,1)S(1)}, u32[]{:S(2)}, u32[]{:S(2)}) collective-permute-start(bf16[512,128]{1,0:T(8,128)(2,1)S(1)} %collective-permute-done.13.rest_1_), channel_id=1, source_target_pairs={{0,3},{1,2},{2,1},{3,0},{4,7},{5,6},{6,5},{7,4},{8,11},{9,10},{10,... | collective-permute-start | bytes 393224 | tf_op jit(solution)/shard_map/ppermute | solution.py:220
  261.6 16.1 %collective-permute-start.20 = (bf16[512,768]{1,0:T(8,128)(2,1)S(1)}, bf16[512,768]{1,0:T(8,128)(2,1)S(1)}, u32[]{:S(2)}, u32[]{:S(2)}) collective-permute-start(bf16[512,768]{1,0:T(8,128)(2,1)S(1)} %bitcast.25), channel_id=1, source_target_pairs={{0,4},{4,8},{8,12},{12,16},{16,20},{20,24},{24,28},{28,0},{1,5},{5... | collective-permute-start | bytes 2359304 | tf_op jit(solution)/shard_map/ppermute | solution.py:225
  262.1 6.5 %collective-permute-start.21 = (bf16[512,128]{1,0:T(8,128)(2,1)S(1)}, bf16[512,128]{1,0:T(8,128)(2,1)S(1)}, u32[]{:S(2)}, u32[]{:S(2)}) collective-permute-start(bf16[512,128]{1,0:T(8,128)(2,1)S(1)} %collective-permute-done.16.rest_2_), channel_id=1, source_target_pairs={{0,1},{1,0},{2,3},{3,2},{4,5},{5,4},{6,7},{7,6},{8,9},{9,8},{10,11... | collective-permute-start | bytes 393224 | tf_op jit(solution)/shard_map/ppermute | solution.py:220
  265.1 12.6 %collective-permute-start.22 = (bf16[512,128]{1,0:T(8,128)(2,1)S(1)}, bf16[512,128]{1,0:T(8,128)(2,1)S(1)}, u32[]{:S(2)}, u32[]{:S(2)}) collective-permute-start(bf16[512,128]{1,0:T(8,128)(2,1)S(1)} %collective-permute-done.16.rest_2_), channel_id=1, source_target_pairs={{0,2},{1,3},{2,0},{3,1},{4,6},{5,7},{6,4},{7,5},{8,10},{9,11},{10,... | collective-permute-start | bytes 393224 | tf_op jit(solution)/shard_map/ppermute | solution.py:220
  265.9 11.9 %collective-permute-start.23 = (bf16[512,128]{1,0:T(8,128)(2,1)S(1)}, bf16[512,128]{1,0:T(8,128)(2,1)S(1)}, u32[]{:S(2)}, u32[]{:S(2)}) collective-permute-start(bf16[512,128]{1,0:T(8,128)(2,1)S(1)} %collective-permute-done.16.rest_2_), channel_id=1, source_target_pairs={{0,3},{1,2},{2,1},{3,0},{4,7},{5,6},{6,5},{7,4},{8,11},{9,10},{10,... | collective-permute-start | bytes 393224 | tf_op jit(solution)/shard_map/ppermute | solution.py:220
  (17 other events, 157.0 us)
Sparse Core Ops, SparseCore 0:
  25.0 77.3 all-gather.2

commit v9 on v5

--- a/solution.py
+++ b/solution.py
@@ -142,7 +142,7 @@
     out_ref[...] = (summed / jnp.sum(total, axis=1, keepdims=True)).astype(BF16)
 
 
-def attend(normed, matrix, where, stale, group):
+def attend(normed, matrix, where, stale, group, spot):
     patch, width = normed.shape
     heads, keys = len(group), stale.shape[1]
     first = group[0]
@@ -153,7 +153,7 @@
             grid=(heads,),
             in_specs=[
                 pl.BlockSpec((patch, width), lambda h, where: (0, 0)),
-                pl.BlockSpec((width, 3 * HD), lambda h, where: (0, h)),
+                pl.BlockSpec((width, 3 * HD), lambda h, where: (0, spot + h)),
                 pl.BlockSpec((2, keys, HD), lambda h, where: (0, 0, first + h)),
             ],
             out_specs=pl.BlockSpec((patch, HD), lambda h, where: (0, h)),
@@ -231,38 +231,48 @@
     tokens = lax.all_gather(inflow[0], "tp", axis=1, tiled=True)
 
     out_plan = [[(3, head) for head in range(lanes)]]
-    (to_out,) = split_blocks(rows, block_of((section_ids + sections - 1) % sections), out_plan, lanes)
+    before = block_of((section_ids + sections - 1) % sections)
+    (to_out,) = split_blocks(rows, before, out_plan, lanes)
     half = max(1, lanes // 2)
-    groups = [tuple(range(half))] + [(head,) for head in range(half, lanes)]
+    groups = [tuple(range(first, first + half)) for first in range(0, lanes, half)]
     plan = [[(kind, head) for head in group for kind in range(3)] for group in groups]
-    split = split_blocks(rows, block_of(section_ids), plan, lanes)
+    split = split_blocks(rows, after(block_of(section_ids), to_out), plan, lanes)
+
+    def waiting(block, *earlier):
+        return functools.reduce(after, earlier, block)
 
     to_out = relayed(to_out)
     normed = norm(tokens, modulation[0])
+    gate = handed_on(modulation[0, 2])
     matrices = []
     for distance in range(tp):
         held = lax.dynamic_slice_in_dim(to_out, (rank ^ distance) * share, share, 0)
-        if distance > 2:
-            held = after(held, matrices[distance - 2])
         matrices.append(swapped(held, "tp", distance) if distance else held)
-    gate = handed_on(modulation[0, 2])
-
-    waits = [[], [normed, gate, *matrices[1:3]], matrices[3:]]
+    ready = waiting(normed, gate)
+
     attended = [[] for _ in range(tp)]
-    ready = normed
+
+    def share_out(matrix, heads, spot, *earlier):
+        own = attend(waiting(ready, *earlier), matrix, patch_index, stale_cache[0], heads, spot)
+        moved = handed_on(own)
+        parts = [swapped(moved, "tp", distance) if distance else moved for distance in range(tp)]
+        parts.append(own)
+        for kept, part in zip(attended, parts):
+            kept.append(part)
+        return parts
+
+    parts = matrices[3:]
     for index, group in enumerate(groups):
         pieces = split[index]
-        for earlier in waits[index] if index < len(waits) else []:
-            pieces = after(pieces, earlier)
+        if index > 0:
+            pieces = waiting(pieces, normed, *matrices[1:3])
         matrix = relayed(pieces)
-        own = attend(ready, matrix, patch_index, stale_cache[0], group)
-        moved = handed_on(own)
-        for distance in range(tp):
-            attended[distance].append(swapped(moved, "tp", distance) if distance else moved)
-        if index + 2 < len(groups):
-            waits[index + 2] = [*waits[index + 2], *[own[-1] for own in attended]]
-        elif index + 1 < len(groups):
-            ready = functools.reduce(after, [own[-1] for own in attended], ready)
+        if index < len(groups) - 1:
+            parts = share_out(matrix, group, 0, *parts)
+            continue
+        for spot, head in enumerate(group):
+            parts = share_out(matrix, (head,), spot, *parts)
+            moved, parts = parts[0], parts[-1:]
     carried = handed_on(after(inflow[0], moved))
     gate = lax.dynamic_slice_in_dim(gate, rank * share, share, 0)[None]
     return output(carried, gate, attended, matrices)[None]

time: 277 us -> 285 us (1.029)
  waiting for transfers between devices: 149 us -> 166 us
  starting transfers between devices: 43.3 us -> 38.3 us
  local copies, waits for them, and re-layouts: 18.3 us -> 13.6 us
    ppermute x5, waiting for transfers between devices: 45.4 us -> 70.4 us  [handed_on(): lax.ppermute(block, 'section', [(i, (i + 1) % sections) for i in range(se...]
    ppermute x12, waiting for transfers between devices: 37.7 us -> 28.8 us  [swapped(): lax.ppermute(block, axis, [(i, i ^ distance) for i in range(lax.axis_size...]
    unnamed x47 -> x31, local copies, waits for them, and re-layouts: 16.5 us -> 11.8 us
    all_to_all x4 -> x3, starting transfers between devices: 18.5 us -> 14.4 us  [relayed(): lax.all_to_all(pieces, 'section', split_axis=0, concat_axis=0, tiled=True)]
    all_to_all x4 -> x3, waiting for transfers between devices: 23.2 us -> 23.7 us  [relayed(): lax.all_to_all(pieces, 'section', split_axis=0, concat_axis=0, tiled=True)]
  transfers between devices with their start and end apart: 22 -> 21, of which waited for: 13 -> 11; matrix products, arithmetic and copies ran while one was open for 1% -> 1% of each run, Pallas kernels for 11% -> 8%
where the time goes in v9:
time: 285 us; the launch traced here: 283 us
  waiting for transfers between devices  166 us (58%)
  Pallas kernels  50.3 us (18%)
  starting transfers between devices  38.3 us (13%)
  between operations  14.3 us (5%)
  local copies, waits for them, and re-layouts  13.6 us (5%)
    ppermute x5, waiting for transfers between devices, handed_on(): lax.ppermute(block, 'section', [(i, (i + 1) % sections) for i in range(se...  70.4 us
    all_gather x1, waiting for transfers between devices, local(): tokens = lax.all_gather(inflow[0], 'tp', axis=1, tiled=True)  42.2 us
    ppermute x12, waiting for transfers between devices, swapped(): lax.ppermute(block, axis, [(i, i ^ distance) for i in range(lax.axis_size...  28.8 us
    all_to_all x3, waiting for transfers between devices, relayed(): lax.all_to_all(pieces, 'section', split_axis=0, concat_axis=0, tiled=True)  23.7 us
    pallas_call x3, Pallas kernels, attend(): pl.pallas_call(attend_kernel, grid_spec=pltpu.PrefetchScalarGridSpec(num_...  23 us
    ppermute x12, starting transfers between devices, swapped(): lax.ppermute(block, axis, [(i, i ^ distance) for i in range(lax.axis_size...  22.5 us
    pallas_call x2, Pallas kernels, split_blocks(): pl.pallas_call(functools.partial(split_kernel, lanes, plan, kinds, depth_...  19.1 us
    all_to_all x3, starting transfers between devices, relayed(): lax.all_to_all(pieces, 'section', split_axis=0, concat_axis=0, tiled=True)  14.4 us
  transfers between devices with their start and end apart: 21, of which 11 were waited for; matrix products, arithmetic and copies ran while one was open for 1% of the time, Pallas kernels for 8%

profile of v9, /device:TPU:0, one launch (start us, length us, event | category | flops | bytes accessed | tf_op | source)
XLA Modules:
  0.0 283.0 jit_solution(3360931205467766426)
XLA Ops:
  7.4 10.1 %split_blocks.2 = bf16[8,384,512]{2,1,0:T(8,128)(2,1)} custom-call(s32[8]{0:T(128)S(1)} %get-tuple-element.36.order_ref, bf16[8,6144,128]{2,1,0:T(8,128)(2,1)} %bitcast.20), custom_call_target="tpu_custom_call" | custom-call | bytes 18874368 | tf_op jit(solution)/shard_map/split_blocks/pallas_call | solution.py:79
  17.5 5.2 %all-to-all-start = ((bf16[8,384,512]{2,1,0:T(8,128)(2,1)}), bf16[8,384,512]{2,1,0:T(8,128)(2,1)S(1)}, u32[]{:S(2)}, u32[]{:S(2)}) async-start(bf16[8,384,512]{2,1,0:T(8,128)(2,1)} %split_blocks.2), calls=%async_computation | async-start | bytes 6291456 | tf_op jit(solution)/shard_map/all_to_all | solution.py:213
  23.4 9.1 %split_blocks.3 = (bf16[8,384,768]{2,1,0:T(8,128)(2,1)S(1)}, bf16[8,384,768]{2,1,0:T(8,128)(2,1)S(1)}) custom-call(s32[8]{0:T(128)S(1)} %get-tuple-element.22.order_ref, bf16[8,6144,128]{2,1,0:T(8,128)(2,1)} %bitcast.21), custom_call_target="tpu_custom_call" | custom-call | bytes 18874368 | tf_op jit(solution)/shard_map/split_blocks/pallas_call | solution.py:79
  32.5 2.1 copy-done.2
  34.6 2.2 copy-done.3
  36.8 23.7 %all-to-all-done = bf16[8,384,512]{2,1,0:T(8,128)(2,1)S(1)} async-done(((bf16[8,384,512]{2,1,0:T(8,128)(2,1)}), bf16[8,384,512]{2,1,0:T(8,128)(2,1)S(1)}, u32[]{:S(2)}, u32[]{:S(2)}) %all-to-all-start) | async-done | bytes 3145760 | tf_op jit(solution)/shard_map/all_to_all | solution.py:213
  60.5 4.6 %all-to-all-start.1 = ((bf16[8,384,768]{2,1,0:T(8,128)(2,1)}), bf16[8,384,768]{2,1,0:T(8,128)(2,1)}, u32[]{:S(2)}, u32[]{:S(2)}) async-start(bf16[8,384,768]{2,1,0:T(8,128)(2,1)} %copy-done.3), calls=%async_computation.1 | async-start | bytes 9437184 | tf_op jit(solution)/shard_map/all_to_all | solution.py:213
  65.2 1.7 constant_dynamic-slice_fusion.3
  68.5 2.6 collective-permute-start.7
  71.1 42.2 %all-gather.3.cloned.1.call-done = bf16[1,512,3072]{2,1,0:T(8,128)(2,1)} async-done(((bf16[1,512,768]{2,1,0:T(8,128)(2,1)}), bf16[1,512,3072]{2,1,0:T(8,128)(2,1)}) %all-gather.3.cloned.1.call-update) | async-done | bytes 3145744 | tf_op jit(solution)/shard_map/all_gather | solution.py:231
  113.3 4.1 %norm.1.normed_ref = bf16[512,3072]{1,0:T(8,128)(2,1)S(1)} custom-call(bf16[512,3072]{1,0:T(8,128)(2,1)} %bitcast.23, f32[3,3072]{1,0:T(4,128)S(1)} %bitcast.19), custom_call_target="tpu_custom_call" | custom-call | flops 15728640 | bytes 6291456 | tf_op jit(solution)/shard_map/norm/pallas_call | solution.py:109
  117.4 4.5 %collective-permute-done.6.rest_13_ = bf16[768,512]{1,0:T(8,128)(2,1)} collective-permute-done((bf16[768,512]{1,0:T(8,128)(2,1)}, bf16[768,512]{1,0:T(8,128)(2,1)}, u32[]{:S(2)}, u32[]{:S(2)}) %collective-permute-start.6) | collective-permute-done | bytes 786464 | tf_op jit(solution)/shard_map/ppermute | solution.py:204
  121.9 4.6 %all-to-all-start.2 = ((bf16[8,384,768]{2,1,0:T(8,128)(2,1)}), bf16[8,384,768]{2,1,0:T(8,128)(2,1)}, u32[]{:S(2)}, u32[]{:S(2)}) async-start(bf16[8,384,768]{2,1,0:T(8,128)(2,1)} %copy-done.2), calls=%async_computation.2 | async-start | bytes 9437184 | tf_op jit(solution)/shard_map/all_to_all | solution.py:213
  126.5 2.4 collective-permute-start.1
  129.6 51.3 %collective-permute-done = f32[3072]{0:T(1024)S(1)} collective-permute-done((f32[3072]{0:T(1024)S(1)}, f32[3072]{0:T(1024)S(1)}, u32[]{:S(2)}, u32[]{:S(2)}) %collective-permute-start) | collective-permute-done | bytes 12320 | tf_op jit(solution)/shard_map/ppermute | solution.py:209
  181.8 2.2 copy-done
  184.0 10.6 %attend.3 = bf16[512,256]{1,0:T(8,128)(2,1)S(1)} custom-call(s32[1]{0:T(128)S(6)} %copy.12.where_ref, bf16[512,3072]{1,0:T(8,128)(2,1)S(1)} %norm.1.normed_ref, bf16[3072,768]{1,0:T(8,128)(2,1)} %bitcast.9.matrix_ref, bf16[2,2048,512]{2,1,0:T(8,128)(2,1)S(1)} %bitcast.16), custom_call_target="tpu_custom_call" | custom-call | flops 3489660928 | bytes 6815744 | tf_op jit(solution)/shard_map/attend/pallas_call | solution.py:149
  194.8 6.7 %collective-permute-done.2.rest_0_ = bf16[512,256]{1,0:T(8,128)(2,1)S(1)} collective-permute-done((bf16[512,256]{1,0:T(8,128)(2,1)S(1)}, bf16[512,256]{1,0:T(8,128)(2,1)S(1)}, u32[]{:S(2)}, u32[]{:S(2)}) %collective-permute-start.2) | collective-permute-done | bytes 262176 | tf_op jit(solution)/shard_map/ppermute | solution.py:209
  201.5 2.7 collective-permute-start.3
  204.5 2.2 collective-permute-start.5
  206.6 7.5 %collective-permute-done.3.rest_3_ = bf16[512,256]{1,0:T(8,128)(2,1)S(1)} collective-permute-done((bf16[512,256]{1,0:T(8,128)(2,1)S(1)}, bf16[512,256]{1,0:T(8,128)(2,1)S(1)}, u32[]{:S(2)}, u32[]{:S(2)}) %collective-permute-start.3) | collective-permute-done | bytes 262176 | tf_op jit(solution)/shard_map/ppermute | solution.py:204
  214.8 7.8 %collective-permute-done.4.rest_6_ = bf16[512,256]{1,0:T(8,128)(2,1)S(1)} collective-permute-done((bf16[512,256]{1,0:T(8,128)(2,1)S(1)}, bf16[512,256]{1,0:T(8,128)(2,1)S(1)}, u32[]{:S(2)}, u32[]{:S(2)}) %collective-permute-start.4) | collective-permute-done | bytes 262176 | tf_op jit(solution)/shard_map/ppermute | solution.py:204
  224.1 2.2 copy-done.1
  226.3 6.1 %attend.4 = bf16[512,128]{1,0:T(8,128)(2,1)S(1)} custom-call(s32[1]{0:T(128)S(6)} %copy.12.where_ref, bf16[512,3072]{1,0:T(8,128)(2,1)S(1)} %norm.1.normed_ref, bf16[3072,768]{1,0:T(8,128)(2,1)} %bitcast.11.matrix_ref, bf16[2,2048,512]{2,1,0:T(8,128)(2,1)S(1)} %bitcast.17), custom_call_target="tpu_custom_call" | custom-call | flops 1744830464 | bytes 3407872 | tf_op jit(solution)/shard_map/attend/pallas_call | solution.py:149
  232.4 6.3 %attend.5 = bf16[512,128]{1,0:T(8,128)(2,1)S(1)} custom-call(s32[1]{0:T(128)S(6)} %copy.12.where_ref, bf16[512,3072]{1,0:T(8,128)(2,1)S(1)} %norm.1.normed_ref, bf16[3072,768]{1,0:T(8,128)(2,1)} %bitcast.11.matrix_ref, bf16[2,2048,512]{2,1,0:T(8,128)(2,1)S(1)} %bitcast.18), custom_call_target="tpu_custom_call" | custom-call | flops 1744830464 | bytes 3407872 | tf_op jit(solution)/shard_map/attend/pallas_call | solution.py:149
  238.8 5.3 %collective-permute-done.8.rest_2_ = bf16[512,128]{1,0:T(8,128)(2,1)S(1)} collective-permute-done((bf16[512,128]{1,0:T(8,128)(2,1)S(1)}, bf16[512,128]{1,0:T(8,128)(2,1)S(1)}, u32[]{:S(2)}, u32[]{:S(2)}) %collective-permute-start.8) | collective-permute-done | bytes 131104 | tf_op jit(solution)/shard_map/ppermute | solution.py:209
  245.4 5.3 %collective-permute-start.14 = (bf16[512,128]{1,0:T(8,128)(2,1)S(1)}, bf16[512,128]{1,0:T(8,128)(2,1)S(1)}, u32[]{:S(2)}, u32[]{:S(2)}) collective-permute-start(bf16[512,128]{1,0:T(8,128)(2,1)S(1)} %collective-permute-done.8.rest_2_), channel_id=1, source_target_pairs={{0,2},{1,3},{2,0},{3,1},{4,6},{5,7},{6,4},{7,5},{8,10},{9,11},{10,... | collective-permute-start | bytes 393224 | tf_op jit(solution)/shard_map/ppermute | solution.py:204
  250.7 7.1 %collective-permute-done.10.rest_1_ = bf16[512,128]{1,0:T(8,128)(2,1)S(1)} collective-permute-done((bf16[512,128]{1,0:T(8,128)(2,1)S(1)}, bf16[512,128]{1,0:T(8,128)(2,1)S(1)}, u32[]{:S(2)}, u32[]{:S(2)}) %collective-permute-start.10) | collective-permute-done | bytes 131104 | tf_op jit(solution)/shard_map/ppermute | solution.py:209
  259.0 3.9 %collective-permute-start.13 = (bf16[512,128]{1,0:T(8,128)(2,1)S(1)}, bf16[512,128]{1,0:T(8,128)(2,1)S(1)}, u32[]{:S(2)}, u32[]{:S(2)}) collective-permute-start(bf16[512,128]{1,0:T(8,128)(2,1)S(1)} %collective-permute-done.10.rest_1_), channel_id=1, source_target_pairs={{0,2},{1,3},{2,0},{3,1},{4,6},{5,7},{6,4},{7,5},{8,10},{9,11},{10,... | collective-permute-start | bytes 393224 | tf_op jit(solution)/shard_map/ppermute | solution.py:204
  263.0 2.9 %collective-permute-done.15.rest_10_ = bf16[512,128]{1,0:T(8,128)(2,1)S(1)} collective-permute-done((bf16[512,128]{1,0:T(8,128)(2,1)S(1)}, bf16[512,128]{1,0:T(8,128)(2,1)S(1)}, u32[]{:S(2)}, u32[]{:S(2)}) %collective-permute-start.15) | collective-permute-done | bytes 131104 | tf_op jit(solution)/shard_map/ppermute | solution.py:204
  265.9 6.0 %collective-permute-done.13.rest_7_ = bf16[512,128]{1,0:T(8,128)(2,1)S(1)} collective-permute-done((bf16[512,128]{1,0:T(8,128)(2,1)S(1)}, bf16[512,128]{1,0:T(8,128)(2,1)S(1)}, u32[]{:S(2)}, u32[]{:S(2)}) %collective-permute-start.13) | collective-permute-done | bytes 131104 | tf_op jit(solution)/shard_map/ppermute | solution.py:204
  272.0 4.1 %output.1 = bf16[512,768]{1,0:T(8,128)(2,1)} custom-call(bf16[512,768]{1,0:T(8,128)(2,1)S(1)} %collective-permute-done.9.inflow_ref, f32[1,768]{1,0:T(1,128)S(1)} %broadcast_in_dim.4.gate_ref, bf16[512,256]{1,0:T(8,128)(2,1)S(1)} %collective-permute-done.2.rest_0_, bf16[512,128]{1,0:T(8,128)(2,1)S(1)} %collective-permute-done.10.rest_1_, ...), custom_call_target="tpu_custom_call" | custom-call | flops 1610612736 | bytes 5242880 | tf_op jit(solution)/shard_map/output/pallas_call | solution.py:187
  (55 shorter events, 9.4 us)
Async XLA Ops:
  17.5 43.1 %all-to-all-start = ((bf16[8,384,512]{2,1,0:T(8,128)(2,1)}), bf16[8,384,512]{2,1,0:T(8,128)(2,1)S(1)}, u32[]{:S(2)}, u32[]{:S(2)}) async-start(bf16[8,384,512]{2,1,0:T(8,128)(2,1)} %split_blocks.2), calls=%async_computation | async-start | bytes 6291456 | tf_op jit(solution)/shard_map/all_to_all | solution.py:213
  22.6 90.6 %all-gather.3.cloned.1.call-start = ((), (), s32[]{:S(2)}) async-start(), calls=%async_computation.3 | async-start | bytes 3932160 | tf_op jit(solution)/shard_map/all_gather | solution.py:231
  32.4 2.2 copy-start.2
  34.6 2.2 copy-start.3
  60.5 61.3 %all-to-all-start.1 = ((bf16[8,384,768]{2,1,0:T(8,128)(2,1)}), bf16[8,384,768]{2,1,0:T(8,128)(2,1)}, u32[]{:S(2)}, u32[]{:S(2)}) async-start(bf16[8,384,768]{2,1,0:T(8,128)(2,1)} %copy-done.3), calls=%async_computation.1 | async-start | bytes 9437184 | tf_op jit(solution)/shard_map/all_to_all | solution.py:213
  65.2 5.9 %copy-start.14 = (f32[1,3,3072]{2,0,1:T(1,128)S(1)}, f32[1,3,3072]{2,0,1:T(1,128)}, u32[]{:S(2)}) copy-start(f32[1,3,3072]{2,0,1:T(1,128)} %param.7) | copy-start | bytes 110596
  66.9 54.9 %collective-permute-start.6 = (bf16[768,512]{1,0:T(8,128)(2,1)}, bf16[768,512]{1,0:T(8,128)(2,1)}, u32[]{:S(2)}, u32[]{:S(2)}) collective-permute-start(bf16[768,512]{1,0:T(8,128)(2,1)} %get-tuple-element.39), channel_id=1, source_target_pairs={{0,1},{1,0},{2,3},{3,2},{4,5},{5,4},{6,7},{7,6},{8,9},{9,8},{10,11... | collective-permute-start | bytes 2359304 | tf_op jit(solution)/shard_map/ppermute | solution.py:204
  68.5 53.3 %collective-permute-start.7 = (bf16[768,512]{1,0:T(8,128)(2,1)}, bf16[768,512]{1,0:T(8,128)(2,1)}, u32[]{:S(2)}, u32[]{:S(2)}) collective-permute-start(bf16[768,512]{1,0:T(8,128)(2,1)} %get-tuple-element.38), channel_id=1, source_target_pairs={{0,2},{1,3},{2,0},{3,1},{4,6},{5,7},{6,4},{7,5},{8,10},{9,11},{10,... | collective-permute-start | bytes 2359304 | tf_op jit(solution)/shard_map/ppermute | solution.py:204
  121.9 102.2 %all-to-all-start.2 = ((bf16[8,384,768]{2,1,0:T(8,128)(2,1)}), bf16[8,384,768]{2,1,0:T(8,128)(2,1)}, u32[]{:S(2)}, u32[]{:S(2)}) async-start(bf16[8,384,768]{2,1,0:T(8,128)(2,1)} %copy-done.2), calls=%async_computation.2 | async-start | bytes 9437184 | tf_op jit(solution)/shard_map/all_to_all | solution.py:213
  126.5 54.4 %collective-permute-start.1 = (bf16[768,512]{1,0:T(8,128)(2,1)}, bf16[768,512]{1,0:T(8,128)(2,1)S(1)}, u32[]{:S(2)}, u32[]{:S(2)}) collective-permute-start(bf16[768,512]{1,0:T(8,128)(2,1)} %get-tuple-element.40), channel_id=1, source_target_pairs={{0,3},{1,2},{2,1},{3,0},{4,7},{5,6},{6,5},{7,4},{8,11},{9,10},{10,... | collective-permute-start | bytes 2359304 | tf_op jit(solution)/shard_map/ppermute | solution.py:204
  128.9 52.0 %collective-permute-start = (f32[3072]{0:T(1024)S(1)}, f32[3072]{0:T(1024)S(1)}, u32[]{:S(2)}, u32[]{:S(2)}) collective-permute-start(f32[3072]{0:T(1024)S(1)} %bitcast.25), channel_id=1, source_target_pairs={{0,4},{4,8},{8,12},{12,16},{16,20},{20,24},{24,28},{28,0},{1,5},{5... | collective-permute-start | bytes 36872 | tf_op jit(solution)/shard_map/ppermute | solution.py:209
  181.8 2.2 copy-start
  194.6 6.9 %collective-permute-start.2 = (bf16[512,256]{1,0:T(8,128)(2,1)S(1)}, bf16[512,256]{1,0:T(8,128)(2,1)S(1)}, u32[]{:S(2)}, u32[]{:S(2)}) collective-permute-start(bf16[512,256]{1,0:T(8,128)(2,1)S(1)} %attend.3), channel_id=1, source_target_pairs={{0,4},{4,8},{8,12},{12,16},{16,20},{20,24},{24,28},{28,0},{1,5},{5... | collective-permute-start | bytes 786440 | tf_op jit(solution)/shard_map/ppermute | solution.py:209
  201.5 12.6 %collective-permute-start.3 = (bf16[512,256]{1,0:T(8,128)(2,1)S(1)}, bf16[512,256]{1,0:T(8,128)(2,1)S(1)}, u32[]{:S(2)}, u32[]{:S(2)}) collective-permute-start(bf16[512,256]{1,0:T(8,128)(2,1)S(1)} %collective-permute-done.2.rest_0_), channel_id=1, source_target_pairs={{0,1},{1,0},{2,3},{3,2},{4,5},{5,4},{6,7},{7,6},{8,9},{9,8},{10,11... | collective-permute-start | bytes 786440 | tf_op jit(solution)/shard_map/ppermute | solution.py:204
  204.3 18.4 %collective-permute-start.4 = (bf16[512,256]{1,0:T(8,128)(2,1)S(1)}, bf16[512,256]{1,0:T(8,128)(2,1)S(1)}, u32[]{:S(2)}, u32[]{:S(2)}) collective-permute-start(bf16[512,256]{1,0:T(8,128)(2,1)S(1)} %collective-permute-done.2.rest_0_), channel_id=1, source_target_pairs={{0,2},{1,3},{2,0},{3,1},{4,6},{5,7},{6,4},{7,5},{8,10},{9,11},{10,... | collective-permute-start | bytes 786440 | tf_op jit(solution)/shard_map/ppermute | solution.py:204
  204.5 18.9 %collective-permute-start.5 = (bf16[512,256]{1,0:T(8,128)(2,1)S(1)}, bf16[512,256]{1,0:T(8,128)(2,1)S(1)}, u32[]{:S(2)}, u32[]{:S(2)}) collective-permute-start(bf16[512,256]{1,0:T(8,128)(2,1)S(1)} %collective-permute-done.2.rest_0_), channel_id=1, source_target_pairs={{0,3},{1,2},{2,1},{3,0},{4,7},{5,6},{6,5},{7,4},{8,11},{9,10},{10,... | collective-permute-start | bytes 786440 | tf_op jit(solution)/shard_map/ppermute | solution.py:204
  224.1 2.2 copy-start.1
  232.4 11.7 %copy-start.13 = (bf16[1,512,768]{2,1,0:T(8,128)(2,1)S(1)}, bf16[1,512,768]{2,1,0:T(8,128)(2,1)}, u32[]{:S(2)}) copy-start(bf16[1,512,768]{2,1,0:T(8,128)(2,1)} %param.8) | copy-start | bytes 2359300
  232.4 39.6 %copy-start.4 = (bf16[768,512]{1,0:T(8,128)(2,1)S(1)}, bf16[768,512]{1,0:T(8,128)(2,1)}, u32[]{:S(2)}) copy-start(bf16[768,512]{1,0:T(8,128)(2,1)} %get-tuple-element.37.rest_12_) | copy-start | bytes 2359300
  232.4 39.6 %copy-start.6 = (bf16[768,512]{1,0:T(8,128)(2,1)S(1)}, bf16[768,512]{1,0:T(8,128)(2,1)}, u32[]{:S(2)}) copy-start(bf16[768,512]{1,0:T(8,128)(2,1)} %copy-done.5) | copy-start | bytes 2359300
  232.4 39.6 %copy-start.8 = (bf16[512,256]{1,0:T(8,128)(2,1)S(1)}, bf16[512,256]{1,0:T(8,128)(2,1)}, u32[]{:S(2)}) copy-start(bf16[512,256]{1,0:T(8,128)(2,1)} %copy-done.7) | copy-start | bytes 786436
  232.4 39.6 %copy-start.10 = (bf16[512,256]{1,0:T(8,128)(2,1)S(1)}, bf16[512,256]{1,0:T(8,128)(2,1)}, u32[]{:S(2)}) copy-start(bf16[512,256]{1,0:T(8,128)(2,1)} %copy-done.9) | copy-start | bytes 786436
  232.4 39.6 %copy-start.12 = (bf16[512,256]{1,0:T(8,128)(2,1)S(1)}, bf16[512,256]{1,0:T(8,128)(2,1)}, u32[]{:S(2)}) copy-start(bf16[512,256]{1,0:T(8,128)(2,1)} %copy-done.11) | copy-start | bytes 786436
  238.7 5.3 %collective-permute-start.8 = (bf16[512,128]{1,0:T(8,128)(2,1)S(1)}, bf16[512,128]{1,0:T(8,128)(2,1)S(1)}, u32[]{:S(2)}, u32[]{:S(2)}) collective-permute-start(bf16[512,128]{1,0:T(8,128)(2,1)S(1)} %attend.5), channel_id=1, source_target_pairs={{0,4},{4,8},{8,12},{12,16},{16,20},{20,24},{24,28},{28,0},{1,5},{5... | collective-permute-start | bytes 393224 | tf_op jit(solution)/shard_map/ppermute | solution.py:209
  244.1 27.9 %collective-permute-start.9 = (bf16[512,768]{1,0:T(8,128)(2,1)S(1)}, bf16[512,768]{1,0:T(8,128)(2,1)S(1)}, u32[]{:S(2)}, u32[]{:S(2)}) collective-permute-start(bf16[512,768]{1,0:T(8,128)(2,1)S(1)} %bitcast.24), channel_id=1, source_target_pairs={{0,4},{4,8},{8,12},{12,16},{16,20},{20,24},{24,28},{28,0},{1,5},{5... | collective-permute-start | bytes 2359304 | tf_op jit(solution)/shard_map/ppermute | solution.py:209
  244.1 13.7 %collective-permute-start.10 = (bf16[512,128]{1,0:T(8,128)(2,1)S(1)}, bf16[512,128]{1,0:T(8,128)(2,1)S(1)}, u32[]{:S(2)}, u32[]{:S(2)}) collective-permute-start(bf16[512,128]{1,0:T(8,128)(2,1)S(1)} %attend.4), channel_id=1, source_target_pairs={{0,4},{4,8},{8,12},{12,16},{16,20},{20,24},{24,28},{28,0},{1,5},{5... | collective-permute-start | bytes 393224 | tf_op jit(solution)/shard_map/ppermute | solution.py:209
  245.1 13.9 %collective-permute-start.16 = (bf16[512,128]{1,0:T(8,128)(2,1)S(1)}, bf16[512,128]{1,0:T(8,128)(2,1)S(1)}, u32[]{:S(2)}, u32[]{:S(2)}) collective-permute-start(bf16[512,128]{1,0:T(8,128)(2,1)S(1)} %collective-permute-done.8.rest_2_), channel_id=1, source_target_pairs={{0,3},{1,2},{2,1},{3,0},{4,7},{5,6},{6,5},{7,4},{8,11},{9,10},{10,... | collective-permute-start | bytes 393224 | tf_op jit(solution)/shard_map/ppermute | solution.py:204
  245.4 17.5 %collective-permute-start.14 = (bf16[512,128]{1,0:T(8,128)(2,1)S(1)}, bf16[512,128]{1,0:T(8,128)(2,1)S(1)}, u32[]{:S(2)}, u32[]{:S(2)}) collective-permute-start(bf16[512,128]{1,0:T(8,128)(2,1)S(1)} %collective-permute-done.8.rest_2_), channel_id=1, source_target_pairs={{0,2},{1,3},{2,0},{3,1},{4,6},{5,7},{6,4},{7,5},{8,10},{9,11},{10,... | collective-permute-start | bytes 393224 | tf_op jit(solution)/shard_map/ppermute | solution.py:204
  250.7 12.3 %collective-permute-start.12 = (bf16[512,128]{1,0:T(8,128)(2,1)S(1)}, bf16[512,128]{1,0:T(8,128)(2,1)S(1)}, u32[]{:S(2)}, u32[]{:S(2)}) collective-permute-start(bf16[512,128]{1,0:T(8,128)(2,1)S(1)} %collective-permute-done.8.rest_2_), channel_id=1, source_target_pairs={{0,1},{1,0},{2,3},{3,2},{4,5},{5,4},{6,7},{7,6},{8,9},{9,8},{10,11... | collective-permute-start | bytes 393224 | tf_op jit(solution)/shard_map/ppermute | solution.py:204
  257.8 8.2 %collective-permute-start.15 = (bf16[512,128]{1,0:T(8,128)(2,1)S(1)}, bf16[512,128]{1,0:T(8,128)(2,1)S(1)}, u32[]{:S(2)}, u32[]{:S(2)}) collective-permute-start(bf16[512,128]{1,0:T(8,128)(2,1)S(1)} %collective-permute-done.10.rest_1_), channel_id=1, source_target_pairs={{0,3},{1,2},{2,1},{3,0},{4,7},{5,6},{6,5},{7,4},{8,11},{9,10},{10,... | collective-permute-start | bytes 393224 | tf_op jit(solution)/shard_map/ppermute | solution.py:204
  259.0 13.0 %collective-permute-start.13 = (bf16[512,128]{1,0:T(8,128)(2,1)S(1)}, bf16[512,128]{1,0:T(8,128)(2,1)S(1)}, u32[]{:S(2)}, u32[]{:S(2)}) collective-permute-start(bf16[512,128]{1,0:T(8,128)(2,1)S(1)} %collective-permute-done.10.rest_1_), channel_id=1, source_target_pairs={{0,2},{1,3},{2,0},{3,1},{4,6},{5,7},{6,4},{7,5},{8,10},{9,11},{10,... | collective-permute-start | bytes 393224 | tf_op jit(solution)/shard_map/ppermute | solution.py:204
  262.9 9.1 %collective-permute-start.11 = (bf16[512,128]{1,0:T(8,128)(2,1)S(1)}, bf16[512,128]{1,0:T(8,128)(2,1)S(1)}, u32[]{:S(2)}, u32[]{:S(2)}) collective-permute-start(bf16[512,128]{1,0:T(8,128)(2,1)S(1)} %collective-permute-done.10.rest_1_), channel_id=1, source_target_pairs={{0,1},{1,0},{2,3},{3,2},{4,5},{5,4},{6,7},{7,6},{8,9},{9,8},{10,11... | collective-permute-start | bytes 393224 | tf_op jit(solution)/shard_map/ppermute | solution.py:204
  (4 other events, 3.0 us)
Sparse Core Ops, SparseCore 0:
  25.0 88.2 all-gather.2

commit v10 on v9

--- a/solution.py
+++ b/solution.py
@@ -230,33 +230,28 @@
     rows = rows.transpose(0, 1, 3, 2, 4).reshape(blocks, depth * lanes * kinds, HD)
     tokens = lax.all_gather(inflow[0], "tp", axis=1, tiled=True)
 
-    out_plan = [[(3, head) for head in range(lanes)]]
-    before = block_of((section_ids + sections - 1) % sections)
-    (to_out,) = split_blocks(rows, before, out_plan, lanes)
+    order = block_of(section_ids)
+    (to_out,) = split_blocks(rows, order, [[(3, head) for head in range(lanes)]], lanes)
     half = max(1, lanes // 2)
     groups = [tuple(range(first, first + half)) for first in range(0, lanes, half)]
     plan = [[(kind, head) for head in group for kind in range(3)] for group in groups]
-    split = split_blocks(rows, after(block_of(section_ids), to_out), plan, lanes)
+    split = split_blocks(rows, after(order, to_out), plan, lanes)
 
     def waiting(block, *earlier):
         return functools.reduce(after, earlier, block)
 
     to_out = relayed(to_out)
     normed = norm(tokens, modulation[0])
-    gate = handed_on(modulation[0, 2])
     matrices = []
     for distance in range(tp):
         held = lax.dynamic_slice_in_dim(to_out, (rank ^ distance) * share, share, 0)
         matrices.append(swapped(held, "tp", distance) if distance else held)
-    ready = waiting(normed, gate)
 
     attended = [[] for _ in range(tp)]
 
     def share_out(matrix, heads, spot, *earlier):
-        own = attend(waiting(ready, *earlier), matrix, patch_index, stale_cache[0], heads, spot)
-        moved = handed_on(own)
-        parts = [swapped(moved, "tp", distance) if distance else moved for distance in range(tp)]
-        parts.append(own)
+        own = attend(waiting(normed, *earlier), matrix, patch_index, stale_cache[0], heads, spot)
+        parts = [swapped(own, "tp", distance) if distance else own for distance in range(tp)]
         for kept, part in zip(attended, parts):
             kept.append(part)
         return parts
@@ -271,11 +266,9 @@
             parts = share_out(matrix, group, 0, *parts)
             continue
         for spot, head in enumerate(group):
-            parts = share_out(matrix, (head,), spot, *parts)
-            moved, parts = parts[0], parts[-1:]
-    carried = handed_on(after(inflow[0], moved))
-    gate = lax.dynamic_slice_in_dim(gate, rank * share, share, 0)[None]
-    return output(carried, gate, attended, matrices)[None]
+            parts = share_out(matrix, (head,), spot, *parts)[:1]
+    gate = lax.dynamic_slice_in_dim(modulation[0, 2], rank * share, share, 0)[None]
+    return handed_on(output(inflow[0], gate, attended, matrices))[None]
 
 
 def solution(mesh):

time: 285 us -> 268 us (0.940)
  waiting for transfers between devices: 166 us -> 132 us
  starting transfers between devices: 38.3 us -> 56 us
    ppermute x5 -> x1, waiting for transfers between devices: 70.4 us -> 12.3 us  [handed_on(): lax.ppermute(block, 'section', [(i, (i + 1) % sections) for i in range(se...]
    ppermute x12, waiting for transfers between devices: 28.8 us -> 52.9 us  [swapped(): lax.ppermute(block, axis, [(i, i ^ distance) for i in range(lax.axis_size...]
    ppermute x12, starting transfers between devices: 22.5 us -> 41.5 us  [swapped(): lax.ppermute(block, axis, [(i, i ^ distance) for i in range(lax.axis_size...]
    unnamed x31 -> x32, local copies, waits for them, and re-layouts: 11.8 us -> 12.7 us
  transfers between devices with their start and end apart: 21 -> 17, of which waited for: 11 -> 9; matrix products, arithmetic and copies ran while one was open for 1% -> 1% of each run, Pallas kernels for 8% -> 9%
where the time goes in v10:
time: 268 us; the launch traced here: 267 us
  waiting for transfers between devices  132 us (49%)
  starting transfers between devices  56 us (21%)
  Pallas kernels  49.6 us (19%)
  local copies, waits for them, and re-layouts  14.4 us (5%)
  between operations  14.3 us (5%)
    ppermute x12, waiting for transfers between devices, swapped(): lax.ppermute(block, axis, [(i, i ^ distance) for i in range(lax.axis_size...  52.9 us
    all_gather x1, waiting for transfers between devices, local(): tokens = lax.all_gather(inflow[0], 'tp', axis=1, tiled=True)  42.2 us
    ppermute x12, starting transfers between devices, swapped(): lax.ppermute(block, axis, [(i, i ^ distance) for i in range(lax.axis_size...  41.5 us
    all_to_all x3, waiting for transfers between devices, relayed(): lax.all_to_all(pieces, 'section', split_axis=0, concat_axis=0, tiled=True)  23.7 us
    pallas_call x3, Pallas kernels, attend(): pl.pallas_call(attend_kernel, grid_spec=pltpu.PrefetchScalarGridSpec(num_...  23.2 us
    pallas_call x2, Pallas kernels, split_blocks(): pl.pallas_call(functools.partial(split_kernel, lanes, plan, kinds, depth_...  19.1 us
    all_to_all x3, starting transfers between devices, relayed(): lax.all_to_all(pieces, 'section', split_axis=0, concat_axis=0, tiled=True)  14.4 us
    unnamed x32, local copies, waits for them, and re-layouts  12.7 us
  transfers between devices with their start and end apart: 17, of which 9 were waited for; matrix products, arithmetic and copies ran while one was open for 1% of the time, Pallas kernels for 9%

profile of v10, /device:TPU:0, one launch (start us, length us, event | category | flops | bytes accessed | tf_op | source)
XLA Modules:
  0.0 266.8 jit_solution(10646576150268390831)
XLA Ops:
  7.3 10.1 %split_blocks.2 = bf16[8,384,512]{2,1,0:T(8,128)(2,1)} custom-call(s32[8]{0:T(128)S(1)} %select_reduce_fusion.order_ref, bf16[8,6144,128]{2,1,0:T(8,128)(2,1)} %bitcast.22), custom_call_target="tpu_custom_call" | custom-call | bytes 18874368 | tf_op jit(solution)/shard_map/split_blocks/pallas_call | solution.py:79
  17.4 5.2 %all-to-all-start = ((bf16[8,384,512]{2,1,0:T(8,128)(2,1)}), bf16[8,384,512]{2,1,0:T(8,128)(2,1)S(1)}, u32[]{:S(2)}, u32[]{:S(2)}) async-start(bf16[8,384,512]{2,1,0:T(8,128)(2,1)} %split_blocks.2), calls=%async_computation | async-start | bytes 6291456 | tf_op jit(solution)/shard_map/all_to_all | solution.py:213
  23.3 9.1 %split_blocks.3 = (bf16[8,384,768]{2,1,0:T(8,128)(2,1)S(1)}, bf16[8,384,768]{2,1,0:T(8,128)(2,1)S(1)}) custom-call(s32[8]{0:T(128)S(1)} %select_reduce_fusion.order_ref, bf16[8,6144,128]{2,1,0:T(8,128)(2,1)} %bitcast.23), custom_call_target="tpu_custom_call" | custom-call | bytes 18874368 | tf_op jit(solution)/shard_map/split_blocks/pallas_call | solution.py:79
  32.3 2.1 copy-done.2
  34.5 2.2 copy-done.3
  36.7 23.7 %all-to-all-done = bf16[8,384,512]{2,1,0:T(8,128)(2,1)S(1)} async-done(((bf16[8,384,512]{2,1,0:T(8,128)(2,1)}), bf16[8,384,512]{2,1,0:T(8,128)(2,1)S(1)}, u32[]{:S(2)}, u32[]{:S(2)}) %all-to-all-start) | async-done | bytes 3145760 | tf_op jit(solution)/shard_map/all_to_all | solution.py:213
  60.4 4.6 %all-to-all-start.1 = ((bf16[8,384,768]{2,1,0:T(8,128)(2,1)}), bf16[8,384,768]{2,1,0:T(8,128)(2,1)}, u32[]{:S(2)}, u32[]{:S(2)}) async-start(bf16[8,384,768]{2,1,0:T(8,128)(2,1)} %copy-done.3), calls=%async_computation.1 | async-start | bytes 9437184 | tf_op jit(solution)/shard_map/all_to_all | solution.py:213
  65.1 1.7 constant_dynamic-slice_fusion.3
  66.8 1.6 collective-permute-start.4
  68.4 2.6 collective-permute-start.5
  71.0 42.2 %all-gather.3.cloned.1.call-done = bf16[1,512,3072]{2,1,0:T(8,128)(2,1)} async-done(((bf16[1,512,768]{2,1,0:T(8,128)(2,1)}), bf16[1,512,3072]{2,1,0:T(8,128)(2,1)}) %all-gather.3.cloned.1.call-update) | async-done | bytes 3145744 | tf_op jit(solution)/shard_map/all_gather | solution.py:231
  113.2 4.1 %norm.1.normed_ref = bf16[512,3072]{1,0:T(8,128)(2,1)S(1)} custom-call(bf16[512,3072]{1,0:T(8,128)(2,1)} %bitcast.25, f32[3,3072]{1,0:T(4,128)S(1)} %bitcast.21), custom_call_target="tpu_custom_call" | custom-call | flops 15728640 | bytes 6291456 | tf_op jit(solution)/shard_map/norm/pallas_call | solution.py:109
  117.3 4.5 %collective-permute-done.4.rest_13_ = bf16[768,512]{1,0:T(8,128)(2,1)} collective-permute-done((bf16[768,512]{1,0:T(8,128)(2,1)}, bf16[768,512]{1,0:T(8,128)(2,1)}, u32[]{:S(2)}, u32[]{:S(2)}) %collective-permute-start.4) | collective-permute-done | bytes 786464 | tf_op jit(solution)/shard_map/ppermute | solution.py:204
  121.8 4.6 %all-to-all-start.2 = ((bf16[8,384,768]{2,1,0:T(8,128)(2,1)}), bf16[8,384,768]{2,1,0:T(8,128)(2,1)}, u32[]{:S(2)}, u32[]{:S(2)}) async-start(bf16[8,384,768]{2,1,0:T(8,128)(2,1)} %copy-done.2), calls=%async_computation.2 | async-start | bytes 9437184 | tf_op jit(solution)/shard_map/all_to_all | solution.py:213
  126.4 2.4 collective-permute-start
  129.5 18.8 %collective-permute-done.rest_15_ = bf16[768,512]{1,0:T(8,128)(2,1)S(1)} collective-permute-done((bf16[768,512]{1,0:T(8,128)(2,1)}, bf16[768,512]{1,0:T(8,128)(2,1)S(1)}, u32[]{:S(2)}, u32[]{:S(2)}) %collective-permute-start) | collective-permute-done | bytes 786464 | tf_op jit(solution)/shard_map/ppermute | solution.py:204
  149.2 2.2 copy-done
  151.4 10.8 %attend.3.rest_0_ = bf16[512,256]{1,0:T(8,128)(2,1)S(1)} custom-call(s32[1]{0:T(128)S(6)} %copy.13.where_ref, bf16[512,3072]{1,0:T(8,128)(2,1)S(1)} %norm.1.normed_ref, bf16[3072,768]{1,0:T(8,128)(2,1)} %bitcast.9.matrix_ref, bf16[2,2048,512]{2,1,0:T(8,128)(2,1)S(1)} %bitcast.17), custom_call_target="tpu_custom_call" | custom-call | flops 3489660928 | bytes 6815744 | tf_op jit(solution)/shard_map/attend/pallas_call | solution.py:149
  162.2 17.4 %collective-permute-start.1 = (bf16[512,256]{1,0:T(8,128)(2,1)S(1)}, bf16[512,256]{1,0:T(8,128)(2,1)S(1)}, u32[]{:S(2)}, u32[]{:S(2)}) collective-permute-start(bf16[512,256]{1,0:T(8,128)(2,1)S(1)} %attend.3.rest_0_), channel_id=1, source_target_pairs={{0,1},{1,0},{2,3},{3,2},{4,5},{5,4},{6,7},{7,6},{8,9},{9,8},{10,11... | collective-permute-start | bytes 786440 | tf_op jit(solution)/shard_map/ppermute | solution.py:204
  179.7 2.2 collective-permute-start.3
  182.0 8.6 %collective-permute-done.1.rest_3_ = bf16[512,256]{1,0:T(8,128)(2,1)S(1)} collective-permute-done((bf16[512,256]{1,0:T(8,128)(2,1)S(1)}, bf16[512,256]{1,0:T(8,128)(2,1)S(1)}, u32[]{:S(2)}, u32[]{:S(2)}) %collective-permute-start.1) | collective-permute-done | bytes 262176 | tf_op jit(solution)/shard_map/ppermute | solution.py:204
  191.2 9.6 %collective-permute-done.2.rest_6_ = bf16[512,256]{1,0:T(8,128)(2,1)S(1)} collective-permute-done((bf16[512,256]{1,0:T(8,128)(2,1)S(1)}, bf16[512,256]{1,0:T(8,128)(2,1)S(1)}, u32[]{:S(2)}, u32[]{:S(2)}) %collective-permute-start.2) | collective-permute-done | bytes 262176 | tf_op jit(solution)/shard_map/ppermute | solution.py:204
  202.3 2.2 copy-done.1
  204.5 6.1 %attend.4.rest_1_ = bf16[512,128]{1,0:T(8,128)(2,1)S(1)} custom-call(s32[1]{0:T(128)S(6)} %copy.13.where_ref, bf16[512,3072]{1,0:T(8,128)(2,1)S(1)} %norm.1.normed_ref, bf16[3072,768]{1,0:T(8,128)(2,1)} %bitcast.11.matrix_ref, bf16[2,2048,512]{2,1,0:T(8,128)(2,1)S(1)} %bitcast.18), custom_call_target="tpu_custom_call" | custom-call | flops 1744830464 | bytes 3407872 | tf_op jit(solution)/shard_map/attend/pallas_call | solution.py:149
  210.7 6.3 %attend.5.rest_2_ = bf16[512,128]{1,0:T(8,128)(2,1)S(1)} custom-call(s32[1]{0:T(128)S(6)} %copy.13.where_ref, bf16[512,3072]{1,0:T(8,128)(2,1)S(1)} %norm.1.normed_ref, bf16[3072,768]{1,0:T(8,128)(2,1)} %bitcast.11.matrix_ref, bf16[2,2048,512]{2,1,0:T(8,128)(2,1)S(1)} %bitcast.19), custom_call_target="tpu_custom_call" | custom-call | flops 1744830464 | bytes 3407872 | tf_op jit(solution)/shard_map/attend/pallas_call | solution.py:149
  216.9 1.7 collective-permute-start.11
  218.6 3.2 %collective-permute-start.7 = (bf16[512,128]{1,0:T(8,128)(2,1)S(1)}, bf16[512,128]{1,0:T(8,128)(2,1)S(1)}, u32[]{:S(2)}, u32[]{:S(2)}) collective-permute-start(bf16[512,128]{1,0:T(8,128)(2,1)S(1)} %attend.5.rest_2_), channel_id=1, source_target_pairs={{0,1},{1,0},{2,3},{3,2},{4,5},{5,4},{6,7},{7,6},{8,9},{9,8},{10,11... | collective-permute-start | bytes 393224 | tf_op jit(solution)/shard_map/ppermute | solution.py:204
  225.4 6.6 %collective-permute-start.8 = (bf16[512,128]{1,0:T(8,128)(2,1)S(1)}, bf16[512,128]{1,0:T(8,128)(2,1)S(1)}, u32[]{:S(2)}, u32[]{:S(2)}) collective-permute-start(bf16[512,128]{1,0:T(8,128)(2,1)S(1)} %attend.4.rest_1_), channel_id=1, source_target_pairs={{0,2},{1,3},{2,0},{3,1},{4,6},{5,7},{6,4},{7,5},{8,10},{9,11},{10,... | collective-permute-start | bytes 393224 | tf_op jit(solution)/shard_map/ppermute | solution.py:204
  232.0 6.5 %collective-permute-done.9.rest_8_ = bf16[512,128]{1,0:T(8,128)(2,1)S(1)} collective-permute-done((bf16[512,128]{1,0:T(8,128)(2,1)S(1)}, bf16[512,128]{1,0:T(8,128)(2,1)S(1)}, u32[]{:S(2)}, u32[]{:S(2)}) %collective-permute-start.9) | collective-permute-done | bytes 131104 | tf_op jit(solution)/shard_map/ppermute | solution.py:204
  238.5 4.9 %collective-permute-done.8.rest_7_ = bf16[512,128]{1,0:T(8,128)(2,1)S(1)} collective-permute-done((bf16[512,128]{1,0:T(8,128)(2,1)S(1)}, bf16[512,128]{1,0:T(8,128)(2,1)S(1)}, u32[]{:S(2)}, u32[]{:S(2)}) %collective-permute-start.8) | collective-permute-done | bytes 131104 | tf_op jit(solution)/shard_map/ppermute | solution.py:204
  243.5 3.2 %output.1 = bf16[512,768]{1,0:T(8,128)(2,1)S(1)} custom-call(bf16[512,768]{1,0:T(8,128)(2,1)S(1)} %bitcast.20, f32[1,768]{1,0:T(1,128)S(1)} %dynamic-slice_bitcast_fusion.gate_ref, bf16[512,256]{1,0:T(8,128)(2,1)S(1)} %attend.3.rest_0_, bf16[512,128]{1,0:T(8,128)(2,1)S(1)} %attend.4.rest_1_, bf16[512,128]{1,0:T(8,128)(2,1)S(1)} %attend.5.rest_2_, ...), custom_call_target="tpu_custom_call" | custom-call | flops 1610612736 | bytes 5242880 | tf_op jit(solution)/shard_map/output/pallas_call | solution.py:187
  246.8 12.3 %collective-permute-done.12 = bf16[512,768]{1,0:T(8,128)(2,1)S(1)} collective-permute-done((bf16[512,768]{1,0:T(8,128)(2,1)S(1)}, bf16[512,768]{1,0:T(8,128)(2,1)S(1)}, u32[]{:S(2)}, u32[]{:S(2)}) %collective-permute-start.12) | collective-permute-done | bytes 786464 | tf_op jit(solution)/shard_map/ppermute | solution.py:209
  (47 shorter events, 9.2 us)
Async XLA Ops:
  17.4 43.1 %all-to-all-start = ((bf16[8,384,512]{2,1,0:T(8,128)(2,1)}), bf16[8,384,512]{2,1,0:T(8,128)(2,1)S(1)}, u32[]{:S(2)}, u32[]{:S(2)}) async-start(bf16[8,384,512]{2,1,0:T(8,128)(2,1)} %split_blocks.2), calls=%async_computation | async-start | bytes 6291456 | tf_op jit(solution)/shard_map/all_to_all | solution.py:213
  22.5 90.6 %all-gather.3.cloned.1.call-start = ((), (), s32[]{:S(2)}) async-start(), calls=%async_computation.3 | async-start | bytes 3932160 | tf_op jit(solution)/shard_map/all_gather | solution.py:231
  32.3 2.2 copy-start.2
  34.5 2.2 copy-start.3
  60.4 61.3 %all-to-all-start.1 = ((bf16[8,384,768]{2,1,0:T(8,128)(2,1)}), bf16[8,384,768]{2,1,0:T(8,128)(2,1)}, u32[]{:S(2)}, u32[]{:S(2)}) async-start(bf16[8,384,768]{2,1,0:T(8,128)(2,1)} %copy-done.3), calls=%async_computation.1 | async-start | bytes 9437184 | tf_op jit(solution)/shard_map/all_to_all | solution.py:213
  65.1 5.9 %copy-start.14 = (f32[1,3,3072]{2,0,1:T(1,128)S(1)}, f32[1,3,3072]{2,0,1:T(1,128)}, u32[]{:S(2)}) copy-start(f32[1,3,3072]{2,0,1:T(1,128)} %param.7) | copy-start | bytes 110596
  66.8 54.9 %collective-permute-start.4 = (bf16[768,512]{1,0:T(8,128)(2,1)}, bf16[768,512]{1,0:T(8,128)(2,1)}, u32[]{:S(2)}, u32[]{:S(2)}) collective-permute-start(bf16[768,512]{1,0:T(8,128)(2,1)} %get-tuple-element.31), channel_id=1, source_target_pairs={{0,1},{1,0},{2,3},{3,2},{4,5},{5,4},{6,7},{7,6},{8,9},{9,8},{10,11... | collective-permute-start | bytes 2359304 | tf_op jit(solution)/shard_map/ppermute | solution.py:204
  68.4 53.3 %collective-permute-start.5 = (bf16[768,512]{1,0:T(8,128)(2,1)}, bf16[768,512]{1,0:T(8,128)(2,1)}, u32[]{:S(2)}, u32[]{:S(2)}) collective-permute-start(bf16[768,512]{1,0:T(8,128)(2,1)} %get-tuple-element.30), channel_id=1, source_target_pairs={{0,2},{1,3},{2,0},{3,1},{4,6},{5,7},{6,4},{7,5},{8,10},{9,11},{10,... | collective-permute-start | bytes 2359304 | tf_op jit(solution)/shard_map/ppermute | solution.py:204
  121.8 80.5 %all-to-all-start.2 = ((bf16[8,384,768]{2,1,0:T(8,128)(2,1)}), bf16[8,384,768]{2,1,0:T(8,128)(2,1)}, u32[]{:S(2)}, u32[]{:S(2)}) async-start(bf16[8,384,768]{2,1,0:T(8,128)(2,1)} %copy-done.2), calls=%async_computation.2 | async-start | bytes 9437184 | tf_op jit(solution)/shard_map/all_to_all | solution.py:213
  126.4 21.9 %collective-permute-start = (bf16[768,512]{1,0:T(8,128)(2,1)}, bf16[768,512]{1,0:T(8,128)(2,1)S(1)}, u32[]{:S(2)}, u32[]{:S(2)}) collective-permute-start(bf16[768,512]{1,0:T(8,128)(2,1)} %get-tuple-element.32), channel_id=1, source_target_pairs={{0,3},{1,2},{2,1},{3,0},{4,7},{5,6},{6,5},{7,4},{8,11},{9,10},{10,... | collective-permute-start | bytes 2359304 | tf_op jit(solution)/shard_map/ppermute | solution.py:204
  148.3 0.9 copy-start.6
  149.2 2.2 copy-start
  162.2 28.4 %collective-permute-start.1 = (bf16[512,256]{1,0:T(8,128)(2,1)S(1)}, bf16[512,256]{1,0:T(8,128)(2,1)S(1)}, u32[]{:S(2)}, u32[]{:S(2)}) collective-permute-start(bf16[512,256]{1,0:T(8,128)(2,1)S(1)} %attend.3.rest_0_), channel_id=1, source_target_pairs={{0,1},{1,0},{2,3},{3,2},{4,5},{5,4},{6,7},{7,6},{8,9},{9,8},{10,11... | collective-permute-start | bytes 786440 | tf_op jit(solution)/shard_map/ppermute | solution.py:204
  179.5 21.3 %collective-permute-start.2 = (bf16[512,256]{1,0:T(8,128)(2,1)S(1)}, bf16[512,256]{1,0:T(8,128)(2,1)S(1)}, u32[]{:S(2)}, u32[]{:S(2)}) collective-permute-start(bf16[512,256]{1,0:T(8,128)(2,1)S(1)} %attend.3.rest_0_), channel_id=1, source_target_pairs={{0,2},{1,3},{2,0},{3,1},{4,6},{5,7},{6,4},{7,5},{8,10},{9,11},{10,... | collective-permute-start | bytes 786440 | tf_op jit(solution)/shard_map/ppermute | solution.py:204
  179.7 21.8 %collective-permute-start.3 = (bf16[512,256]{1,0:T(8,128)(2,1)S(1)}, bf16[512,256]{1,0:T(8,128)(2,1)S(1)}, u32[]{:S(2)}, u32[]{:S(2)}) collective-permute-start(bf16[512,256]{1,0:T(8,128)(2,1)S(1)} %attend.3.rest_0_), channel_id=1, source_target_pairs={{0,3},{1,2},{2,1},{3,0},{4,7},{5,6},{6,5},{7,4},{8,11},{9,10},{10,... | collective-permute-start | bytes 786440 | tf_op jit(solution)/shard_map/ppermute | solution.py:204
  190.5 0.7 copy-start.8
  201.6 0.7 copy-start.12
  202.3 2.2 copy-start.1
  210.6 21.4 %slice-start = ((f32[1,3,3072]{2,0,1:T(1,128)}), f32[1,1,3072]{2,0,1:T(1,128)S(1)}, s32[]{:S(2)}) async-start(f32[1,3,3072]{2,0,1:T(1,128)} %param.7), calls=%async_computation.4 | async-start | bytes 24576 | tf_op jit(solution)/shard_map/slice | solution.py:270
  210.6 32.8 %copy-start.4 = (bf16[1,512,768]{2,1,0:T(8,128)(2,1)S(1)}, bf16[1,512,768]{2,1,0:T(8,128)(2,1)}, u32[]{:S(2)}) copy-start(bf16[1,512,768]{2,1,0:T(8,128)(2,1)} %param.8) | copy-start | bytes 2359300
  210.6 32.8 %copy-start.5 = (bf16[768,512]{1,0:T(8,128)(2,1)S(1)}, bf16[768,512]{1,0:T(8,128)(2,1)}, u32[]{:S(2)}) copy-start(bf16[768,512]{1,0:T(8,128)(2,1)} %get-tuple-element.29.rest_12_) | copy-start | bytes 2359300
  210.6 32.8 %copy-start.7 = (bf16[768,512]{1,0:T(8,128)(2,1)S(1)}, bf16[768,512]{1,0:T(8,128)(2,1)}, u32[]{:S(2)}) copy-start(bf16[768,512]{1,0:T(8,128)(2,1)} %copy-done.6) | copy-start | bytes 2359300
  210.6 32.8 %copy-start.9 = (bf16[512,256]{1,0:T(8,128)(2,1)S(1)}, bf16[512,256]{1,0:T(8,128)(2,1)}, u32[]{:S(2)}) copy-start(bf16[512,256]{1,0:T(8,128)(2,1)} %copy-done.8) | copy-start | bytes 786436
  210.6 32.8 %copy-start.11 = (bf16[512,256]{1,0:T(8,128)(2,1)S(1)}, bf16[512,256]{1,0:T(8,128)(2,1)}, u32[]{:S(2)}) copy-start(bf16[512,256]{1,0:T(8,128)(2,1)} %copy-done.10) | copy-start | bytes 786436
  210.6 32.8 %copy-start.13 = (bf16[512,256]{1,0:T(8,128)(2,1)S(1)}, bf16[512,256]{1,0:T(8,128)(2,1)}, u32[]{:S(2)}) copy-start(bf16[512,256]{1,0:T(8,128)(2,1)} %copy-done.12) | copy-start | bytes 786436
  216.9 8.4 %collective-permute-start.11 = (bf16[512,128]{1,0:T(8,128)(2,1)S(1)}, bf16[512,128]{1,0:T(8,128)(2,1)S(1)}, u32[]{:S(2)}, u32[]{:S(2)}) collective-permute-start(bf16[512,128]{1,0:T(8,128)(2,1)S(1)} %attend.5.rest_2_), channel_id=1, source_target_pairs={{0,3},{1,2},{2,1},{3,0},{4,7},{5,6},{6,5},{7,4},{8,11},{9,10},{10,... | collective-permute-start | bytes 393224 | tf_op jit(solution)/shard_map/ppermute | solution.py:204
  218.6 13.4 %collective-permute-start.7 = (bf16[512,128]{1,0:T(8,128)(2,1)S(1)}, bf16[512,128]{1,0:T(8,128)(2,1)S(1)}, u32[]{:S(2)}, u32[]{:S(2)}) collective-permute-start(bf16[512,128]{1,0:T(8,128)(2,1)S(1)} %attend.5.rest_2_), channel_id=1, source_target_pairs={{0,1},{1,0},{2,3},{3,2},{4,5},{5,4},{6,7},{7,6},{8,9},{9,8},{10,11... | collective-permute-start | bytes 393224 | tf_op jit(solution)/shard_map/ppermute | solution.py:204
  221.9 16.7 %collective-permute-start.9 = (bf16[512,128]{1,0:T(8,128)(2,1)S(1)}, bf16[512,128]{1,0:T(8,128)(2,1)S(1)}, u32[]{:S(2)}, u32[]{:S(2)}) collective-permute-start(bf16[512,128]{1,0:T(8,128)(2,1)S(1)} %attend.5.rest_2_), channel_id=1, source_target_pairs={{0,2},{1,3},{2,0},{3,1},{4,6},{5,7},{6,4},{7,5},{8,10},{9,11},{10,... | collective-permute-start | bytes 393224 | tf_op jit(solution)/shard_map/ppermute | solution.py:204
  222.9 15.6 %collective-permute-start.10 = (bf16[512,128]{1,0:T(8,128)(2,1)S(1)}, bf16[512,128]{1,0:T(8,128)(2,1)S(1)}, u32[]{:S(2)}, u32[]{:S(2)}) collective-permute-start(bf16[512,128]{1,0:T(8,128)(2,1)S(1)} %attend.4.rest_1_), channel_id=1, source_target_pairs={{0,3},{1,2},{2,1},{3,0},{4,7},{5,6},{6,5},{7,4},{8,11},{9,10},{10,... | collective-permute-start | bytes 393224 | tf_op jit(solution)/shard_map/ppermute | solution.py:204
  224.3 14.2 %collective-permute-start.6 = (bf16[512,128]{1,0:T(8,128)(2,1)S(1)}, bf16[512,128]{1,0:T(8,128)(2,1)S(1)}, u32[]{:S(2)}, u32[]{:S(2)}) collective-permute-start(bf16[512,128]{1,0:T(8,128)(2,1)S(1)} %attend.4.rest_1_), channel_id=1, source_target_pairs={{0,1},{1,0},{2,3},{3,2},{4,5},{5,4},{6,7},{7,6},{8,9},{9,8},{10,11... | collective-permute-start | bytes 393224 | tf_op jit(solution)/shard_map/ppermute | solution.py:204
  225.4 18.1 %collective-permute-start.8 = (bf16[512,128]{1,0:T(8,128)(2,1)S(1)}, bf16[512,128]{1,0:T(8,128)(2,1)S(1)}, u32[]{:S(2)}, u32[]{:S(2)}) collective-permute-start(bf16[512,128]{1,0:T(8,128)(2,1)S(1)} %attend.4.rest_1_), channel_id=1, source_target_pairs={{0,2},{1,3},{2,0},{3,1},{4,6},{5,7},{6,4},{7,5},{8,10},{9,11},{10,... | collective-permute-start | bytes 393224 | tf_op jit(solution)/shard_map/ppermute | solution.py:204
  246.7 12.4 %collective-permute-start.12 = (bf16[512,768]{1,0:T(8,128)(2,1)S(1)}, bf16[512,768]{1,0:T(8,128)(2,1)S(1)}, u32[]{:S(2)}, u32[]{:S(2)}) collective-permute-start(bf16[512,768]{1,0:T(8,128)(2,1)S(1)} %output.1), channel_id=1, source_target_pairs={{0,4},{4,8},{8,12},{12,16},{16,20},{20,24},{24,28},{28,0},{1,5},{5... | collective-permute-start | bytes 2359304 | tf_op jit(solution)/shard_map/ppermute | solution.py:209
  (1 other events, 0.7 us)
Sparse Core Ops, SparseCore 0:
  24.9 88.1 all-gather.2

commit v11 on v10

--- a/solution.py
+++ b/solution.py
@@ -169,31 +169,37 @@
     )(where, normed, matrix, stale)
 
 
-def output_kernel(tp, chunks, inflow_ref, gate_ref, *rest):
-    attended, matrices, out_ref = rest[: tp * chunks], rest[tp * chunks : -1], rest[-1]
+def output_kernel(tp, whole, rank_ref, inflow_ref, gate_ref, *rest):
+    shared, rest = rest[:whole], rest[whole:]
+    swaps, matrices, out_ref = rest[:tp], rest[tp:-1], rest[-1]
     mixed = 0.0
-    for index in range(tp):
-        own = attended[index * chunks : (index + 1) * chunks]
-        left = jnp.concatenate([piece[...] for piece in own], axis=1)
-        mixed += turned(left, matrices[index][...])
+    for distance in range(tp):
+        own = [every[rank_ref[0] ^ distance] for every in shared] + [swaps[distance][...]]
+        mixed += turned(jnp.concatenate(own, axis=1), matrices[distance][...])
     out_ref[...] = (inflow_ref[...].astype(F32) + gate_ref[...] * mixed).astype(BF16)
 
 
-def output(inflow, gate, attended, matrices):
-    tp, chunks = len(attended), len(attended[0])
+def output(rank, inflow, gate, shared, swaps, matrices):
+    tp = len(matrices)
     patch, share = inflow.shape
     inner = matrices[0].shape[1]
-    arrays = [inflow, gate] + [piece for own in attended for piece in own] + matrices
-    return pl.pallas_call(
-        functools.partial(output_kernel, tp, chunks),
-        grid=(1,),
-        in_specs=[pl.BlockSpec(array.shape, lambda i: (0, 0)) for array in arrays],
-        out_specs=pl.BlockSpec(inflow.shape, lambda i: (0, 0)),
+    arrays = [inflow, gate, *shared, *swaps, *matrices]
+    return pl.pallas_call(
+        functools.partial(output_kernel, tp, len(shared)),
+        grid_spec=pltpu.PrefetchScalarGridSpec(
+            num_scalar_prefetch=1,
+            grid=(1,),
+            in_specs=[
+                pl.BlockSpec(array.shape, lambda i, rank, zeros=(0,) * array.ndim: zeros)
+                for array in arrays
+            ],
+            out_specs=pl.BlockSpec(inflow.shape, lambda i, rank: (0, 0)),
+        ),
         out_shape=jax.ShapeDtypeStruct(inflow.shape, BF16),
-        compiler_params=params(20),
+        compiler_params=params(24),
         cost_estimate=cost(2 * patch * share * inner * tp, 2 * inner * tp * (share + patch)),
         name="output",
-    )(*arrays)
+    )(rank[None], *arrays)
 
 
 def after(block, earlier):
@@ -232,8 +238,7 @@
 
     order = block_of(section_ids)
     (to_out,) = split_blocks(rows, order, [[(3, head) for head in range(lanes)]], lanes)
-    half = max(1, lanes // 2)
-    groups = [tuple(range(first, first + half)) for first in range(0, lanes, half)]
+    groups = [tuple(range(max(1, lanes - 1)))] + [(lanes - 1,)] * (lanes > 1)
     plan = [[(kind, head) for head in group for kind in range(3)] for group in groups]
     split = split_blocks(rows, after(order, to_out), plan, lanes)
 
@@ -247,28 +252,23 @@
         held = lax.dynamic_slice_in_dim(to_out, (rank ^ distance) * share, share, 0)
         matrices.append(swapped(held, "tp", distance) if distance else held)
 
-    attended = [[] for _ in range(tp)]
-
-    def share_out(matrix, heads, spot, *earlier):
-        own = attend(waiting(normed, *earlier), matrix, patch_index, stale_cache[0], heads, spot)
-        parts = [swapped(own, "tp", distance) if distance else own for distance in range(tp)]
-        for kept, part in zip(attended, parts):
-            kept.append(part)
-        return parts
-
-    parts = matrices[3:]
-    for index, group in enumerate(groups):
-        pieces = split[index]
-        if index > 0:
-            pieces = waiting(pieces, normed, *matrices[1:3])
-        matrix = relayed(pieces)
-        if index < len(groups) - 1:
-            parts = share_out(matrix, group, 0, *parts)
-            continue
-        for spot, head in enumerate(group):
-            parts = share_out(matrix, (head,), spot, *parts)[:1]
+    def attended(matrix, head, spot, *earlier):
+        ready = waiting(normed, *earlier)
+        return attend(ready, matrix, patch_index, stale_cache[0], (head,), spot)
+
+    matrix = relayed(split[0])
+    shared, last = [], ()
+    if len(groups) > 1:
+        moved = relayed(waiting(split[1], normed, *matrices[1:]))
+        for spot, head in enumerate(groups[0]):
+            own = attended(matrix, head, spot, *last)
+            shared.append(lax.all_gather(own, "tp"))
+            last = (own,)
+        matrix, last = moved, (own, shared[0])
+    own = attended(matrix, lanes - 1, 0, *last)
+    swaps = [swapped(own, "tp", distance) if distance else own for distance in range(tp)]
     gate = lax.dynamic_slice_in_dim(modulation[0, 2], rank * share, share, 0)[None]
-    return handed_on(output(inflow[0], gate, attended, matrices))[None]
+    return handed_on(output(rank, inflow[0], gate, shared, swaps, matrices))[None]
 
 
 def solution(mesh):

time: 268 us -> 310 us (1.16)
  blocking collectives: 0 us -> 52 us
  starting transfers between devices: 56 us -> 23.5 us
  waiting for transfers between devices: 132 us -> 156 us
    all_gather x1, waiting for transfers between devices: 42.2 us -> 119 us  [local(): tokens = lax.all_gather(inflow[0], 'tp', axis=1, tiled=True)]
    ppermute x12 -> x6, waiting for transfers between devices: 52.9 us -> 0.02 us  [swapped(): lax.ppermute(block, axis, [(i, i ^ distance) for i in range(lax.axis_size...]
    all_gather x0 -> x3, blocking collectives: none -> 52 us  [local(): shared.append(lax.all_gather(own, 'tp'))]
    ppermute x12 -> x6, starting transfers between devices: 41.5 us -> 8.85 us  [swapped(): lax.ppermute(block, axis, [(i, i ^ distance) for i in range(lax.axis_size...]
    unnamed x32 -> x20, local copies, waits for them, and re-layouts: 12.7 us -> 9.53 us
    pallas_call x3 -> x4, Pallas kernels: 23.2 us -> 24.6 us  [attend(): pl.pallas_call(attend_kernel, grid_spec=pltpu.PrefetchScalarGridSpec(num_...]
  transfers between devices with their start and end apart: 17 -> 11, of which waited for: 9 -> 3; matrix products, arithmetic and copies ran while one was open for 1% -> 1% of each run, Pallas kernels for 9% -> 10%
where the time goes in v11:
time: 310 us
  waiting for transfers between devices  156 us (50%)
  blocking collectives  52 us (17%)
  Pallas kernels  51.3 us (17%)
  starting transfers between devices  23.5 us (8%)
  between operations  14.3 us (5%)
  local copies, waits for them, and re-layouts  11.3 us (4%)
    all_gather x1, waiting for transfers between devices, local(): tokens = lax.all_gather(inflow[0], 'tp', axis=1, tiled=True)  119 us
    all_gather x3, blocking collectives, local(): shared.append(lax.all_gather(own, 'tp'))  52 us
    pallas_call x4, Pallas kernels, attend(): pl.pallas_call(attend_kernel, grid_spec=pltpu.PrefetchScalarGridSpec(num_...  24.6 us
    all_to_all x3, waiting for transfers between devices, relayed(): lax.all_to_all(pieces, 'section', split_axis=0, concat_axis=0, tiled=True)  24.6 us
    pallas_call x2, Pallas kernels, split_blocks(): pl.pallas_call(functools.partial(split_kernel, lanes, plan, kinds, depth_...  19.1 us
    all_to_all x3, starting transfers between devices, relayed(): lax.all_to_all(pieces, 'section', split_axis=0, concat_axis=0, tiled=True)  14.6 us
    ppermute x1, waiting for transfers between devices, handed_on(): lax.ppermute(block, 'section', [(i, (i + 1) % sections) for i in range(se...  12.3 us
    unnamed x20, local copies, waits for them, and re-layouts  9.53 us
  transfers between devices with their start and end apart: 11, of which 3 were waited for; matrix products, arithmetic and copies ran while one was open for 1% of the time, Pallas kernels for 10%

profile of v11, /device:TPU:0, one launch (start us, length us, event | category | flops | bytes accessed | tf_op | source)
XLA Modules:
  0.0 309.5 jit_solution(4639317698691952096)
XLA Ops:
  6.5 0.8 select_reduce_fusion.order_ref
  7.3 10.1 %split_blocks.2 = bf16[8,384,512]{2,1,0:T(8,128)(2,1)} custom-call(s32[8]{0:T(128)S(1)} %select_reduce_fusion.order_ref, bf16[8,6144,128]{2,1,0:T(8,128)(2,1)} %bitcast.30), custom_call_target="tpu_custom_call" | custom-call | bytes 18874368 | tf_op jit(solution)/shard_map/split_blocks/pallas_call | solution.py:79
  17.4 5.2 %all-to-all-start.1 = ((bf16[8,384,512]{2,1,0:T(8,128)(2,1)}), bf16[8,384,512]{2,1,0:T(8,128)(2,1)S(1)}, u32[]{:S(2)}, u32[]{:S(2)}) async-start(bf16[8,384,512]{2,1,0:T(8,128)(2,1)} %split_blocks.2), calls=%async_computation.1 | async-start | bytes 6291456 | tf_op jit(solution)/shard_map/all_to_all | solution.py:219
  22.5 9.1 %split_blocks.3 = (bf16[8,384,1152]{2,1,0:T(8,128)(2,1)S(1)}, bf16[8,384,384]{2,1,0:T(8,128)(2,1)S(1)}) custom-call(s32[8]{0:T(128)S(1)} %select_reduce_fusion.order_ref, bf16[8,6144,128]{2,1,0:T(8,128)(2,1)} %bitcast.31), custom_call_target="tpu_custom_call" | custom-call | bytes 18874368 | tf_op jit(solution)/shard_map/split_blocks/pallas_call | solution.py:79
  31.6 2.8 copy-done.2
  34.5 1.4 copy-done.5
  35.9 24.6 %all-to-all-done.1 = bf16[8,384,512]{2,1,0:T(8,128)(2,1)S(1)} async-done(((bf16[8,384,512]{2,1,0:T(8,128)(2,1)}), bf16[8,384,512]{2,1,0:T(8,128)(2,1)S(1)}, u32[]{:S(2)}, u32[]{:S(2)}) %all-to-all-start.1) | async-done | bytes 3145760 | tf_op jit(solution)/shard_map/all_to_all | solution.py:219
  60.4 4.8 %all-to-all-start = ((bf16[8,384,1152]{2,1,0:T(8,128)(2,1)}), bf16[8,384,1152]{2,1,0:T(8,128)(2,1)}, u32[]{:S(2)}, u32[]{:S(2)}) async-start(bf16[8,384,1152]{2,1,0:T(8,128)(2,1)} %copy-done.2), calls=%async_computation | async-start | bytes 14155776 | tf_op jit(solution)/shard_map/all_to_all | solution.py:219
  65.3 0.7 all-gather.6.cloned.1.call-update
  66.0 1.7 constant_dynamic-slice_fusion.3
  67.8 1.6 collective-permute-start
  69.4 2.6 collective-permute-start.1
  72.0 0.2 collective-permute-start.2
  72.2 118.8 %all-gather.6.cloned.1.call-done = bf16[1,512,3072]{2,1,0:T(8,128)(2,1)} async-done(((bf16[1,512,768]{2,1,0:T(8,128)(2,1)}), bf16[1,512,3072]{2,1,0:T(8,128)(2,1)}) %all-gather.6.cloned.1.call-update) | async-done | bytes 3145744 | tf_op jit(solution)/shard_map/all_gather | solution.py:237
  191.0 4.1 %norm.1.normed_ref = bf16[512,3072]{1,0:T(8,128)(2,1)S(1)} custom-call(bf16[512,3072]{1,0:T(8,128)(2,1)} %bitcast.33, f32[3,3072]{1,0:T(4,128)S(1)} %bitcast.29), custom_call_target="tpu_custom_call" | custom-call | flops 15728640 | bytes 6291456 | tf_op jit(solution)/shard_map/norm/pallas_call | solution.py:109
  195.2 4.6 %all-to-all-start.2 = ((bf16[8,384,384]{2,1,0:T(8,128)(2,1)}), bf16[8,384,384]{2,1,0:T(8,128)(2,1)}, u32[]{:S(2)}, u32[]{:S(2)}) async-start(bf16[8,384,384]{2,1,0:T(8,128)(2,1)} %copy-done.5), calls=%async_computation.2 | async-start | bytes 4718592 | tf_op jit(solution)/shard_map/all_to_all | solution.py:219
  200.5 2.2 copy-done
  202.6 6.1 %attend.4 = bf16[512,128]{1,0:T(8,128)(2,1)S(1)} custom-call(s32[1]{0:T(128)S(6)} %copy.13.where_ref, bf16[512,3072]{1,0:T(8,128)(2,1)S(1)} %norm.1.normed_ref, bf16[3072,1152]{1,0:T(8,128)(2,1)} %bitcast.7.matrix_ref, bf16[2,2048,512]{2,1,0:T(8,128)(2,1)S(1)} %bitcast.21), custom_call_target="tpu_custom_call" | custom-call | flops 1744830464 | bytes 3407872 | tf_op jit(solution)/shard_map/attend/pallas_call | solution.py:149
  208.8 6.1 %attend.5 = bf16[512,128]{1,0:T(8,128)(2,1)S(1)} custom-call(s32[1]{0:T(128)S(6)} %copy.13.where_ref, bf16[512,3072]{1,0:T(8,128)(2,1)S(1)} %norm.1.normed_ref, bf16[3072,1152]{1,0:T(8,128)(2,1)} %bitcast.7.matrix_ref, bf16[2,2048,512]{2,1,0:T(8,128)(2,1)S(1)} %bitcast.22), custom_call_target="tpu_custom_call" | custom-call | flops 1744830464 | bytes 3407872 | tf_op jit(solution)/shard_map/attend/pallas_call | solution.py:149
  214.9 6.1 %attend.6 = bf16[512,128]{1,0:T(8,128)(2,1)S(1)} custom-call(s32[1]{0:T(128)S(6)} %copy.13.where_ref, bf16[512,3072]{1,0:T(8,128)(2,1)S(1)} %norm.1.normed_ref, bf16[3072,1152]{1,0:T(8,128)(2,1)} %bitcast.7.matrix_ref, bf16[2,2048,512]{2,1,0:T(8,128)(2,1)S(1)} %bitcast.23), custom_call_target="tpu_custom_call" | custom-call | flops 1744830464 | bytes 3407872 | tf_op jit(solution)/shard_map/attend/pallas_call | solution.py:149
  221.0 16.8 %all-gather.1 = bf16[2048,128]{1,0:T(8,128)(2,1)} all-gather(bf16[512,128]{1,0:T(8,128)(2,1)S(1)} %attend.4), channel_id=3, replica_groups=mesh['section'=8,'tp'=4] {'tp'}, dimensions={0}, use_global_device_ids=true | all-gather | bytes 655360 | tf_op jit(solution)/shard_map/all_gather | solution.py:265
  237.8 16.6 %all-gather.3 = bf16[2048,128]{1,0:T(8,128)(2,1)} all-gather(bf16[512,128]{1,0:T(8,128)(2,1)S(1)} %attend.6), channel_id=5, replica_groups=mesh['section'=8,'tp'=4] {'tp'}, dimensions={0}, use_global_device_ids=true | all-gather | bytes 655360 | tf_op jit(solution)/shard_map/all_gather | solution.py:265
  254.3 2.2 copy-done.1
  256.5 6.3 %attend.7.rest_3_ = bf16[512,128]{1,0:T(8,128)(2,1)S(1)} custom-call(s32[1]{0:T(128)S(6)} %copy.13.where_ref, bf16[512,3072]{1,0:T(8,128)(2,1)S(1)} %norm.1.normed_ref, bf16[3072,384]{1,0:T(8,128)(2,1)} %bitcast.13.matrix_ref, bf16[2,2048,512]{2,1,0:T(8,128)(2,1)S(1)} %bitcast.24), custom_call_target="tpu_custom_call" | custom-call | flops 1744830464 | bytes 3407872 | tf_op jit(solution)/shard_map/attend/pallas_call | solution.py:149
  262.8 0.1 collective-permute-start.3
  262.9 2.2 collective-permute-start.4
  265.1 2.1 collective-permute-start.5
  267.2 18.7 %all-gather.2 = bf16[2048,128]{1,0:T(8,128)(2,1)S(1)} all-gather(bf16[512,128]{1,0:T(8,128)(2,1)S(1)} %attend.5), channel_id=4, replica_groups=mesh['section'=8,'tp'=4] {'tp'}, dimensions={0}, use_global_device_ids=true | all-gather | bytes 655360 | tf_op jit(solution)/shard_map/all_gather | solution.py:265
  286.0 3.5 %output.1 = bf16[512,768]{1,0:T(8,128)(2,1)S(1)} custom-call(s32[1]{0:T(128)} %bitcast.rank_ref, bf16[512,768]{1,0:T(8,128)(2,1)S(1)} %bitcast.25, f32[1,768]{1,0:T(1,128)S(1)} %dynamic-slice_bitcast_fusion.gate_ref, bf16[4,512,128]{2,1,0:T(8,128)(2,1)S(1)} %bitcast.26, bf16[4,512,128]{2,1,0:T(8,128)(2,1)S(1)} %bitcast.28, ...), custom_call_target="tpu_custom_call" | custom-call | flops 1610612736 | bytes 5242880 | tf_op jit(solution)/shard_map/output/pallas_call | solution.py:187
  289.4 0.1 collective-permute-start.6
  289.5 12.3 %collective-permute-done.6 = bf16[512,768]{1,0:T(8,128)(2,1)S(1)} collective-permute-done((bf16[512,768]{1,0:T(8,128)(2,1)S(1)}, bf16[512,768]{1,0:T(8,128)(2,1)S(1)}, u32[]{:S(2)}, u32[]{:S(2)}) %collective-permute-start.6) | collective-permute-done | bytes 786464 | tf_op jit(solution)/shard_map/ppermute | solution.py:215
  301.8 0.9 copy.14
  (27 shorter events, 0.1 us)
Async XLA Ops:
  17.4 43.1 %all-to-all-start.1 = ((bf16[8,384,512]{2,1,0:T(8,128)(2,1)}), bf16[8,384,512]{2,1,0:T(8,128)(2,1)S(1)}, u32[]{:S(2)}, u32[]{:S(2)}) async-start(bf16[8,384,512]{2,1,0:T(8,128)(2,1)} %split_blocks.2), calls=%async_computation.1 | async-start | bytes 6291456 | tf_op jit(solution)/shard_map/all_to_all | solution.py:219
  31.6 2.9 copy-start.2
  34.5 1.4 copy-start.5
  60.4 134.8 %all-to-all-start = ((bf16[8,384,1152]{2,1,0:T(8,128)(2,1)}), bf16[8,384,1152]{2,1,0:T(8,128)(2,1)}, u32[]{:S(2)}, u32[]{:S(2)}) async-start(bf16[8,384,1152]{2,1,0:T(8,128)(2,1)} %copy-done.2), calls=%async_computation | async-start | bytes 14155776 | tf_op jit(solution)/shard_map/all_to_all | solution.py:219
  65.3 125.7 %all-gather.6.cloned.1.call-start = ((), (), s32[]{:S(2)}) async-start(), calls=%async_computation.3 | async-start | bytes 3932160 | tf_op jit(solution)/shard_map/all_gather | solution.py:237
  66.0 6.2 %copy-start.8 = (f32[1,3,3072]{2,0,1:T(1,128)S(1)}, f32[1,3,3072]{2,0,1:T(1,128)}, u32[]{:S(2)}) copy-start(f32[1,3,3072]{2,0,1:T(1,128)} %param.7) | copy-start | bytes 110596
  67.8 127.4 %collective-permute-start = (bf16[768,512]{1,0:T(8,128)(2,1)}, bf16[768,512]{1,0:T(8,128)(2,1)}, u32[]{:S(2)}, u32[]{:S(2)}) collective-permute-start(bf16[768,512]{1,0:T(8,128)(2,1)} %get-tuple-element.30), channel_id=1, source_target_pairs={{0,1},{1,0},{2,3},{3,2},{4,5},{5,4},{6,7},{7,6},{8,9},{9,8},{10,11... | collective-permute-start | bytes 2359304 | tf_op jit(solution)/shard_map/ppermute | solution.py:210
  69.4 125.8 %collective-permute-start.1 = (bf16[768,512]{1,0:T(8,128)(2,1)}, bf16[768,512]{1,0:T(8,128)(2,1)}, u32[]{:S(2)}, u32[]{:S(2)}) collective-permute-start(bf16[768,512]{1,0:T(8,128)(2,1)} %get-tuple-element.29), channel_id=1, source_target_pairs={{0,2},{1,3},{2,0},{3,1},{4,6},{5,7},{6,4},{7,5},{8,10},{9,11},{10,... | collective-permute-start | bytes 2359304 | tf_op jit(solution)/shard_map/ppermute | solution.py:210
  72.0 123.2 %collective-permute-start.2 = (bf16[768,512]{1,0:T(8,128)(2,1)}, bf16[768,512]{1,0:T(8,128)(2,1)}, u32[]{:S(2)}, u32[]{:S(2)}) collective-permute-start(bf16[768,512]{1,0:T(8,128)(2,1)} %get-tuple-element.28), channel_id=1, source_target_pairs={{0,3},{1,2},{2,1},{3,0},{4,7},{5,6},{6,5},{7,4},{8,11},{9,10},{10,... | collective-permute-start | bytes 2359304 | tf_op jit(solution)/shard_map/ppermute | solution.py:210
  195.1 5.3 %slice-start = ((f32[1,3,3072]{2,0,1:T(1,128)}), f32[1,1,3072]{2,0,1:T(1,128)S(1)}, s32[]{:S(2)}) async-start(f32[1,3,3072]{2,0,1:T(1,128)} %param.7), calls=%async_computation.4 | async-start | bytes 24576 | tf_op jit(solution)/shard_map/slice | solution.py:270
  195.2 59.1 %all-to-all-start.2 = ((bf16[8,384,384]{2,1,0:T(8,128)(2,1)}), bf16[8,384,384]{2,1,0:T(8,128)(2,1)}, u32[]{:S(2)}, u32[]{:S(2)}) async-start(bf16[8,384,384]{2,1,0:T(8,128)(2,1)} %copy-done.5), calls=%async_computation.2 | async-start | bytes 4718592 | tf_op jit(solution)/shard_map/all_to_all | solution.py:219
  200.4 2.2 copy-start
  254.3 2.2 copy-start.1
  256.5 29.4 %copy-start.3 = (bf16[1,512,768]{2,1,0:T(8,128)(2,1)S(1)}, bf16[1,512,768]{2,1,0:T(8,128)(2,1)}, u32[]{:S(2)}) copy-start(bf16[1,512,768]{2,1,0:T(8,128)(2,1)} %param.8) | copy-start | bytes 2359300
  256.5 29.4 %copy-start.4 = (bf16[768,512]{1,0:T(8,128)(2,1)S(1)}, bf16[768,512]{1,0:T(8,128)(2,1)}, u32[]{:S(2)}) copy-start(bf16[768,512]{1,0:T(8,128)(2,1)} %get-tuple-element.27.rest_7_) | copy-start | bytes 2359300
  256.5 29.4 %copy-start.6 = (bf16[2048,128]{1,0:T(8,128)(2,1)S(1)}, bf16[2048,128]{1,0:T(8,128)(2,1)}, u32[]{:S(2)}) copy-start(bf16[2048,128]{1,0:T(8,128)(2,1)} %all-gather.1) | copy-start | bytes 1572868
  256.5 29.4 %copy-start.7 = (bf16[2048,128]{1,0:T(8,128)(2,1)S(1)}, bf16[2048,128]{1,0:T(8,128)(2,1)}, u32[]{:S(2)}) copy-start(bf16[2048,128]{1,0:T(8,128)(2,1)} %all-gather.3) | copy-start | bytes 1572868
  262.8 23.1 %collective-permute-start.3 = (bf16[512,128]{1,0:T(8,128)(2,1)S(1)}, bf16[512,128]{1,0:T(8,128)(2,1)S(1)}, u32[]{:S(2)}, u32[]{:S(2)}) collective-permute-start(bf16[512,128]{1,0:T(8,128)(2,1)S(1)} %attend.7.rest_3_), channel_id=1, source_target_pairs={{0,1},{1,0},{2,3},{3,2},{4,5},{5,4},{6,7},{7,6},{8,9},{9,8},{10,11... | collective-permute-start | bytes 393224 | tf_op jit(solution)/shard_map/ppermute | solution.py:210
  262.9 23.0 %collective-permute-start.4 = (bf16[512,128]{1,0:T(8,128)(2,1)S(1)}, bf16[512,128]{1,0:T(8,128)(2,1)S(1)}, u32[]{:S(2)}, u32[]{:S(2)}) collective-permute-start(bf16[512,128]{1,0:T(8,128)(2,1)S(1)} %attend.7.rest_3_), channel_id=1, source_target_pairs={{0,2},{1,3},{2,0},{3,1},{4,6},{5,7},{6,4},{7,5},{8,10},{9,11},{10,... | collective-permute-start | bytes 393224 | tf_op jit(solution)/shard_map/ppermute | solution.py:210
  265.1 20.8 %collective-permute-start.5 = (bf16[512,128]{1,0:T(8,128)(2,1)S(1)}, bf16[512,128]{1,0:T(8,128)(2,1)S(1)}, u32[]{:S(2)}, u32[]{:S(2)}) collective-permute-start(bf16[512,128]{1,0:T(8,128)(2,1)S(1)} %attend.7.rest_3_), channel_id=1, source_target_pairs={{0,3},{1,2},{2,1},{3,0},{4,7},{5,6},{6,5},{7,4},{8,11},{9,10},{10,... | collective-permute-start | bytes 393224 | tf_op jit(solution)/shard_map/ppermute | solution.py:210
  289.4 12.4 %collective-permute-start.6 = (bf16[512,768]{1,0:T(8,128)(2,1)S(1)}, bf16[512,768]{1,0:T(8,128)(2,1)S(1)}, u32[]{:S(2)}, u32[]{:S(2)}) collective-permute-start(bf16[512,768]{1,0:T(8,128)(2,1)S(1)} %output.1), channel_id=1, source_target_pairs={{0,4},{4,8},{8,12},{12,16},{16,20},{20,24},{24,28},{28,0},{1,5},{5... | collective-permute-start | bytes 2359304 | tf_op jit(solution)/shard_map/ppermute | solution.py:215
Sparse Core Ops, SparseCore 0:
  67.7 123.2 all-gather.5

commit v12 on v10

--- a/solution.py
+++ b/solution.py
@@ -233,7 +233,7 @@
     order = block_of(section_ids)
     (to_out,) = split_blocks(rows, order, [[(3, head) for head in range(lanes)]], lanes)
     half = max(1, lanes // 2)
-    groups = [tuple(range(first, first + half)) for first in range(0, lanes, half)]
+    groups = [tuple(range(half))] + [(head,) for head in range(half, lanes)]
     plan = [[(kind, head) for head in group for kind in range(3)] for group in groups]
     split = split_blocks(rows, after(order, to_out), plan, lanes)
 
@@ -247,26 +247,23 @@
         held = lax.dynamic_slice_in_dim(to_out, (rank ^ distance) * share, share, 0)
         matrices.append(swapped(held, "tp", distance) if distance else held)
 
-    attended = [[] for _ in range(tp)]
-
-    def share_out(matrix, heads, spot, *earlier):
-        own = attend(waiting(normed, *earlier), matrix, patch_index, stale_cache[0], heads, spot)
-        parts = [swapped(own, "tp", distance) if distance else own for distance in range(tp)]
-        for kept, part in zip(attended, parts):
-            kept.append(part)
-        return parts
-
-    parts = matrices[3:]
+    waits, parts = [(), (normed, *matrices[1:3]), tuple(matrices[3:])], []
+    owns, final = [], len(groups) - 1
     for index, group in enumerate(groups):
-        pieces = split[index]
+        if index > 1:
+            waits[index] += (owns[index - 2], moved)
+        pieces = waiting(split[index], *(waits[index] if index < len(waits) else ()))
+        moved = relayed(pieces)
         if index > 0:
-            pieces = waiting(pieces, normed, *matrices[1:3])
-        matrix = relayed(pieces)
-        if index < len(groups) - 1:
-            parts = share_out(matrix, group, 0, *parts)
+            owns.append(attend(normed, matrix, patch_index, stale_cache[0], groups[index - 1], 0))
+        matrix = moved
+        if index < final:
             continue
-        for spot, head in enumerate(group):
-            parts = share_out(matrix, (head,), spot, *parts)[:1]
+        parts = [[swapped(own, "tp", distance) for distance in range(1, tp)] for own in owns]
+        ready = waiting(normed, *[part for own in parts[:1] for part in own], *owns[1:])
+        owns.append(attend(ready, matrix, patch_index, stale_cache[0], group, 0))
+        parts.append([swapped(owns[-1], "tp", distance) for distance in range(1, tp)])
+    attended = [owns] + [[own[distance] for own in parts] for distance in range(tp - 1)]
     gate = lax.dynamic_slice_in_dim(modulation[0, 2], rank * share, share, 0)[None]
     return handed_on(output(inflow[0], gate, attended, matrices))[None]
 

time: 268 us -> 267 us (level)
  waiting for transfers between devices: 132 us -> 129 us
  local copies, waits for them, and re-layouts: 14.4 us -> 17.2 us
    ppermute x12, starting transfers between devices: 41.5 us -> 36.8 us  [swapped(): lax.ppermute(block, axis, [(i, i ^ distance) for i in range(lax.axis_size...]
    all_to_all x3 -> x4, starting transfers between devices: 14.4 us -> 18.7 us  [relayed(): lax.all_to_all(pieces, 'section', split_axis=0, concat_axis=0, tiled=True)]
    unnamed x32 -> x36, local copies, waits for them, and re-layouts: 12.7 us -> 15.4 us
    all_to_all x3 -> x4, waiting for transfers between devices: 23.7 us -> 23.2 us  [relayed(): lax.all_to_all(pieces, 'section', split_axis=0, concat_axis=0, tiled=True)]
  transfers between devices with their start and end apart: 17 -> 18, of which waited for: 9 -> 10; matrix products, arithmetic and copies ran while one was open for 1% -> 1% of each run, Pallas kernels for 9% -> 14%
where the time goes in v12:
time: 267 us; the launch traced here: 266 us
  waiting for transfers between devices  129 us (48%)
  starting transfers between devices  55.6 us (21%)
  Pallas kernels  49.6 us (19%)
  local copies, waits for them, and re-layouts  17.2 us (6%)
  between operations  14.3 us (5%)
    ppermute x12, waiting for transfers between devices, swapped(): lax.ppermute(block, axis, [(i, i ^ distance) for i in range(lax.axis_size...  50.6 us
    all_gather x1, waiting for transfers between devices, local(): tokens = lax.all_gather(inflow[0], 'tp', axis=1, tiled=True)  42.2 us
    ppermute x12, starting transfers between devices, swapped(): lax.ppermute(block, axis, [(i, i ^ distance) for i in range(lax.axis_size...  36.8 us
    all_to_all x4, waiting for transfers between devices, relayed(): lax.all_to_all(pieces, 'section', split_axis=0, concat_axis=0, tiled=True)  23.2 us
    pallas_call x3, Pallas kernels, attend(): pl.pallas_call(attend_kernel, grid_spec=pltpu.PrefetchScalarGridSpec(num_...  23 us
    pallas_call x2, Pallas kernels, split_blocks(): pl.pallas_call(functools.partial(split_kernel, lanes, plan, kinds, depth_...  19.1 us
    all_to_all x4, starting transfers between devices, relayed(): lax.all_to_all(pieces, 'section', split_axis=0, concat_axis=0, tiled=True)  18.7 us
    unnamed x36, local copies, waits for them, and re-layouts  15.4 us
  transfers between devices with their start and end apart: 18, of which 10 were waited for; matrix products, arithmetic and copies ran while one was open for 1% of the time, Pallas kernels for 14%

profile of v12, /device:TPU:0, one launch (start us, length us, event | category | flops | bytes accessed | tf_op | source)
XLA Modules:
  0.0 266.4 jit_solution(16363543535793305367)
XLA Ops:
  7.3 10.1 %split_blocks.2 = bf16[8,384,512]{2,1,0:T(8,128)(2,1)} custom-call(s32[8]{0:T(128)S(1)} %select_reduce_fusion.order_ref, bf16[8,6144,128]{2,1,0:T(8,128)(2,1)} %bitcast.23), custom_call_target="tpu_custom_call" | custom-call | bytes 18874368 | tf_op jit(solution)/shard_map/split_blocks/pallas_call | solution.py:79
  17.4 5.2 %all-to-all-start.1 = ((bf16[8,384,512]{2,1,0:T(8,128)(2,1)}), bf16[8,384,512]{2,1,0:T(8,128)(2,1)S(1)}, u32[]{:S(2)}, u32[]{:S(2)}) async-start(bf16[8,384,512]{2,1,0:T(8,128)(2,1)} %split_blocks.2), calls=%async_computation.1 | async-start | bytes 6291456 | tf_op jit(solution)/shard_map/all_to_all | solution.py:213
  23.3 9.1 %split_blocks.3 = (bf16[8,384,768]{2,1,0:T(8,128)(2,1)S(1)}, bf16[8,384,384]{2,1,0:T(8,128)(2,1)S(1)}, bf16[8,384,384]{2,1,0:T(8,128)(2,1)S(1)}) custom-call(s32[8]{0:T(128)S(1)} %select_reduce_fusion.order_ref, bf16[8,6144,128]{2,1,0:T(8,128)(2,1)} %bitcast.24), custom_call_target="tpu_custom_call" | custom-call | bytes 18874368 | tf_op jit(solution)/shard_map/split_blocks/pallas_call | solution.py:79
  32.3 2.1 copy-done.3
  37.3 23.2 %all-to-all-done.1 = bf16[8,384,512]{2,1,0:T(8,128)(2,1)S(1)} async-done(((bf16[8,384,512]{2,1,0:T(8,128)(2,1)}), bf16[8,384,512]{2,1,0:T(8,128)(2,1)S(1)}, u32[]{:S(2)}, u32[]{:S(2)}) %all-to-all-start.1) | async-done | bytes 3145760 | tf_op jit(solution)/shard_map/all_to_all | solution.py:213
  60.4 4.6 %all-to-all-start = ((bf16[8,384,768]{2,1,0:T(8,128)(2,1)}), bf16[8,384,768]{2,1,0:T(8,128)(2,1)}, u32[]{:S(2)}, u32[]{:S(2)}) async-start(bf16[8,384,768]{2,1,0:T(8,128)(2,1)} %copy-done.3), calls=%async_computation | async-start | bytes 9437184 | tf_op jit(solution)/shard_map/all_to_all | solution.py:213
  65.1 1.7 constant_dynamic-slice_fusion.3
  68.4 2.6 collective-permute-start.1
  71.0 42.2 %all-gather.3.cloned.1.call-done = bf16[1,512,3072]{2,1,0:T(8,128)(2,1)} async-done(((bf16[1,512,768]{2,1,0:T(8,128)(2,1)}), bf16[1,512,3072]{2,1,0:T(8,128)(2,1)}) %all-gather.3.cloned.1.call-update) | async-done | bytes 3145744 | tf_op jit(solution)/shard_map/all_gather | solution.py:231
  113.2 4.1 %norm.1.normed_ref = bf16[512,3072]{1,0:T(8,128)(2,1)S(1)} custom-call(bf16[512,3072]{1,0:T(8,128)(2,1)} %bitcast.26, f32[3,3072]{1,0:T(4,128)S(1)} %bitcast.22), custom_call_target="tpu_custom_call" | custom-call | flops 15728640 | bytes 6291456 | tf_op jit(solution)/shard_map/norm/pallas_call | solution.py:109
  117.3 4.4 %collective-permute-done.rest_13_ = bf16[768,512]{1,0:T(8,128)(2,1)} collective-permute-done((bf16[768,512]{1,0:T(8,128)(2,1)}, bf16[768,512]{1,0:T(8,128)(2,1)}, u32[]{:S(2)}, u32[]{:S(2)}) %collective-permute-start) | collective-permute-done | bytes 786464 | tf_op jit(solution)/shard_map/ppermute | solution.py:204
  121.8 4.4 %all-to-all-start.2 = ((bf16[8,384,384]{2,1,0:T(8,128)(2,1)}), bf16[8,384,384]{2,1,0:T(8,128)(2,1)}, u32[]{:S(2)}, u32[]{:S(2)}) async-start(bf16[8,384,384]{2,1,0:T(8,128)(2,1)} %copy-done.7), calls=%async_computation.2 | async-start | bytes 4718592 | tf_op jit(solution)/shard_map/all_to_all | solution.py:213
  126.2 2.4 collective-permute-start.5
  129.3 18.8 %collective-permute-done.5.rest_15_ = bf16[768,512]{1,0:T(8,128)(2,1)S(1)} collective-permute-done((bf16[768,512]{1,0:T(8,128)(2,1)}, bf16[768,512]{1,0:T(8,128)(2,1)S(1)}, u32[]{:S(2)}, u32[]{:S(2)}) %collective-permute-start.5) | collective-permute-done | bytes 786464 | tf_op jit(solution)/shard_map/ppermute | solution.py:204
  149.0 2.2 copy-done
  151.2 10.6 %attend.3.rest_0_ = bf16[512,256]{1,0:T(8,128)(2,1)S(1)} custom-call(s32[1]{0:T(128)S(6)} %copy.13.where_ref, bf16[512,3072]{1,0:T(8,128)(2,1)S(1)} %norm.1.normed_ref, bf16[3072,768]{1,0:T(8,128)(2,1)} %bitcast.6.matrix_ref, bf16[2,2048,512]{2,1,0:T(8,128)(2,1)S(1)} %bitcast.18), custom_call_target="tpu_custom_call" | custom-call | flops 3489660928 | bytes 6815744 | tf_op jit(solution)/shard_map/attend/pallas_call | solution.py:149
  161.8 4.6 %all-to-all-start.3 = ((bf16[8,384,384]{2,1,0:T(8,128)(2,1)}), bf16[8,384,384]{2,1,0:T(8,128)(2,1)}, u32[]{:S(2)}, u32[]{:S(2)}) async-start(bf16[8,384,384]{2,1,0:T(8,128)(2,1)} %copy-done.6), calls=%async_computation.3 | async-start | bytes 4718592 | tf_op jit(solution)/shard_map/all_to_all | solution.py:213
  166.4 17.4 %collective-permute-start.2 = (bf16[512,256]{1,0:T(8,128)(2,1)S(1)}, bf16[512,256]{1,0:T(8,128)(2,1)S(1)}, u32[]{:S(2)}, u32[]{:S(2)}) collective-permute-start(bf16[512,256]{1,0:T(8,128)(2,1)S(1)} %attend.3.rest_0_), channel_id=1, source_target_pairs={{0,1},{1,0},{2,3},{3,2},{4,5},{5,4},{6,7},{7,6},{8,9},{9,8},{10,11... | collective-permute-start | bytes 786440 | tf_op jit(solution)/shard_map/ppermute | solution.py:204
  184.0 2.2 collective-permute-start.4
  186.2 8.7 %collective-permute-done.2.rest_3_ = bf16[512,256]{1,0:T(8,128)(2,1)S(1)} collective-permute-done((bf16[512,256]{1,0:T(8,128)(2,1)S(1)}, bf16[512,256]{1,0:T(8,128)(2,1)S(1)}, u32[]{:S(2)}, u32[]{:S(2)}) %collective-permute-start.2) | collective-permute-done | bytes 262176 | tf_op jit(solution)/shard_map/ppermute | solution.py:204
  195.7 9.5 %collective-permute-done.3.rest_6_ = bf16[512,256]{1,0:T(8,128)(2,1)S(1)} collective-permute-done((bf16[512,256]{1,0:T(8,128)(2,1)S(1)}, bf16[512,256]{1,0:T(8,128)(2,1)S(1)}, u32[]{:S(2)}, u32[]{:S(2)}) %collective-permute-start.3) | collective-permute-done | bytes 262176 | tf_op jit(solution)/shard_map/ppermute | solution.py:204
  206.5 2.2 copy-done.1
  208.7 6.1 %attend.4.rest_1_ = bf16[512,128]{1,0:T(8,128)(2,1)S(1)} custom-call(s32[1]{0:T(128)S(6)} %copy.13.where_ref, bf16[512,3072]{1,0:T(8,128)(2,1)S(1)} %norm.1.normed_ref, bf16[3072,384]{1,0:T(8,128)(2,1)} %bitcast.9.matrix_ref, bf16[2,2048,512]{2,1,0:T(8,128)(2,1)S(1)} %bitcast.19), custom_call_target="tpu_custom_call" | custom-call | flops 1744830464 | bytes 3407872 | tf_op jit(solution)/shard_map/attend/pallas_call | solution.py:149
  216.5 3.5 %collective-permute-start.6 = (bf16[512,128]{1,0:T(8,128)(2,1)S(1)}, bf16[512,128]{1,0:T(8,128)(2,1)}, u32[]{:S(2)}, u32[]{:S(2)}) collective-permute-start(bf16[512,128]{1,0:T(8,128)(2,1)S(1)} %attend.4.rest_1_), channel_id=1, source_target_pairs={{0,1},{1,0},{2,3},{3,2},{4,5},{5,4},{6,7},{7,6},{8,9},{9,8},{10,11... | collective-permute-start | bytes 393224 | tf_op jit(solution)/shard_map/ppermute | solution.py:204
  220.8 2.2 copy-done.2
  223.0 6.3 %attend.5.rest_2_ = bf16[512,128]{1,0:T(8,128)(2,1)S(1)} custom-call(s32[1]{0:T(128)S(6)} %copy.13.where_ref, bf16[512,3072]{1,0:T(8,128)(2,1)S(1)} %norm.1.normed_ref, bf16[3072,384]{1,0:T(8,128)(2,1)} %bitcast.10.matrix_ref, bf16[2,2048,512]{2,1,0:T(8,128)(2,1)S(1)} %bitcast.20), custom_call_target="tpu_custom_call" | custom-call | flops 1744830464 | bytes 3407872 | tf_op jit(solution)/shard_map/attend/pallas_call | solution.py:149
  229.3 1.6 collective-permute-start.11
  232.0 1.7 collective-permute-start.9
  233.7 3.9 %collective-permute-done.11.rest_11_ = bf16[512,128]{1,0:T(8,128)(2,1)S(1)} collective-permute-done((bf16[512,128]{1,0:T(8,128)(2,1)S(1)}, bf16[512,128]{1,0:T(8,128)(2,1)S(1)}, u32[]{:S(2)}, u32[]{:S(2)}) %collective-permute-start.11) | collective-permute-done | bytes 131104 | tf_op jit(solution)/shard_map/ppermute | solution.py:204
  237.8 5.1 %collective-permute-done.9.rest_8_ = bf16[512,128]{1,0:T(8,128)(2,1)S(1)} collective-permute-done((bf16[512,128]{1,0:T(8,128)(2,1)S(1)}, bf16[512,128]{1,0:T(8,128)(2,1)S(1)}, u32[]{:S(2)}, u32[]{:S(2)}) %collective-permute-start.9) | collective-permute-done | bytes 131104 | tf_op jit(solution)/shard_map/ppermute | solution.py:204
  242.9 3.4 %output.1 = bf16[512,768]{1,0:T(8,128)(2,1)S(1)} custom-call(bf16[512,768]{1,0:T(8,128)(2,1)S(1)} %bitcast.21, f32[1,768]{1,0:T(1,128)S(1)} %dynamic-slice_bitcast_fusion.gate_ref, bf16[512,256]{1,0:T(8,128)(2,1)S(1)} %attend.3.rest_0_, bf16[512,128]{1,0:T(8,128)(2,1)S(1)} %attend.4.rest_1_, bf16[512,128]{1,0:T(8,128)(2,1)S(1)} %attend.5.rest_2_, ...), custom_call_target="tpu_custom_call" | custom-call | flops 1610612736 | bytes 5242880 | tf_op jit(solution)/shard_map/output/pallas_call | solution.py:187
  246.4 12.3 %collective-permute-done.12 = bf16[512,768]{1,0:T(8,128)(2,1)S(1)} collective-permute-done((bf16[512,768]{1,0:T(8,128)(2,1)S(1)}, bf16[512,768]{1,0:T(8,128)(2,1)S(1)}, u32[]{:S(2)}, u32[]{:S(2)}) %collective-permute-start.12) | collective-permute-done | bytes 786464 | tf_op jit(solution)/shard_map/ppermute | solution.py:209
  (53 shorter events, 13.7 us)
Async XLA Ops:
  17.4 43.1 %all-to-all-start.1 = ((bf16[8,384,512]{2,1,0:T(8,128)(2,1)}), bf16[8,384,512]{2,1,0:T(8,128)(2,1)S(1)}, u32[]{:S(2)}, u32[]{:S(2)}) async-start(bf16[8,384,512]{2,1,0:T(8,128)(2,1)} %split_blocks.2), calls=%async_computation.1 | async-start | bytes 6291456 | tf_op jit(solution)/shard_map/all_to_all | solution.py:213
  22.5 90.7 %all-gather.3.cloned.1.call-start = ((), (), s32[]{:S(2)}) async-start(), calls=%async_computation.4 | async-start | bytes 3932160 | tf_op jit(solution)/shard_map/all_gather | solution.py:231
  32.3 2.2 copy-start.3
  34.5 1.4 copy-start.6
  35.9 1.4 copy-start.7
  60.4 61.3 %all-to-all-start = ((bf16[8,384,768]{2,1,0:T(8,128)(2,1)}), bf16[8,384,768]{2,1,0:T(8,128)(2,1)}, u32[]{:S(2)}, u32[]{:S(2)}) async-start(bf16[8,384,768]{2,1,0:T(8,128)(2,1)} %copy-done.3), calls=%async_computation | async-start | bytes 9437184 | tf_op jit(solution)/shard_map/all_to_all | solution.py:213
  65.1 5.9 %copy-start.16 = (f32[1,3,3072]{2,0,1:T(1,128)S(1)}, f32[1,3,3072]{2,0,1:T(1,128)}, u32[]{:S(2)}) copy-start(f32[1,3,3072]{2,0,1:T(1,128)} %param.7) | copy-start | bytes 110596
  66.8 55.0 %collective-permute-start = (bf16[768,512]{1,0:T(8,128)(2,1)}, bf16[768,512]{1,0:T(8,128)(2,1)}, u32[]{:S(2)}, u32[]{:S(2)}) collective-permute-start(bf16[768,512]{1,0:T(8,128)(2,1)} %get-tuple-element.36), channel_id=1, source_target_pairs={{0,1},{1,0},{2,3},{3,2},{4,5},{5,4},{6,7},{7,6},{8,9},{9,8},{10,11... | collective-permute-start | bytes 2359304 | tf_op jit(solution)/shard_map/ppermute | solution.py:204
  68.4 53.4 %collective-permute-start.1 = (bf16[768,512]{1,0:T(8,128)(2,1)}, bf16[768,512]{1,0:T(8,128)(2,1)}, u32[]{:S(2)}, u32[]{:S(2)}) collective-permute-start(bf16[768,512]{1,0:T(8,128)(2,1)} %get-tuple-element.35), channel_id=1, source_target_pairs={{0,2},{1,3},{2,0},{3,1},{4,6},{5,7},{6,4},{7,5},{8,10},{9,11},{10,... | collective-permute-start | bytes 2359304 | tf_op jit(solution)/shard_map/ppermute | solution.py:204
  121.8 40.1 %all-to-all-start.2 = ((bf16[8,384,384]{2,1,0:T(8,128)(2,1)}), bf16[8,384,384]{2,1,0:T(8,128)(2,1)}, u32[]{:S(2)}, u32[]{:S(2)}) async-start(bf16[8,384,384]{2,1,0:T(8,128)(2,1)} %copy-done.7), calls=%async_computation.2 | async-start | bytes 4718592 | tf_op jit(solution)/shard_map/all_to_all | solution.py:213
  126.2 21.9 %collective-permute-start.5 = (bf16[768,512]{1,0:T(8,128)(2,1)}, bf16[768,512]{1,0:T(8,128)(2,1)S(1)}, u32[]{:S(2)}, u32[]{:S(2)}) collective-permute-start(bf16[768,512]{1,0:T(8,128)(2,1)} %get-tuple-element.34), channel_id=1, source_target_pairs={{0,3},{1,2},{2,1},{3,0},{4,7},{5,6},{6,5},{7,4},{8,11},{9,10},{10,... | collective-permute-start | bytes 2359304 | tf_op jit(solution)/shard_map/ppermute | solution.py:204
  149.0 2.2 copy-start
  161.8 58.9 %all-to-all-start.3 = ((bf16[8,384,384]{2,1,0:T(8,128)(2,1)}), bf16[8,384,384]{2,1,0:T(8,128)(2,1)}, u32[]{:S(2)}, u32[]{:S(2)}) async-start(bf16[8,384,384]{2,1,0:T(8,128)(2,1)} %copy-done.6), calls=%async_computation.3 | async-start | bytes 4718592 | tf_op jit(solution)/shard_map/all_to_all | solution.py:213
  166.4 28.5 %collective-permute-start.2 = (bf16[512,256]{1,0:T(8,128)(2,1)S(1)}, bf16[512,256]{1,0:T(8,128)(2,1)S(1)}, u32[]{:S(2)}, u32[]{:S(2)}) collective-permute-start(bf16[512,256]{1,0:T(8,128)(2,1)S(1)} %attend.3.rest_0_), channel_id=1, source_target_pairs={{0,1},{1,0},{2,3},{3,2},{4,5},{5,4},{6,7},{7,6},{8,9},{9,8},{10,11... | collective-permute-start | bytes 786440 | tf_op jit(solution)/shard_map/ppermute | solution.py:204
  183.8 21.3 %collective-permute-start.3 = (bf16[512,256]{1,0:T(8,128)(2,1)S(1)}, bf16[512,256]{1,0:T(8,128)(2,1)S(1)}, u32[]{:S(2)}, u32[]{:S(2)}) collective-permute-start(bf16[512,256]{1,0:T(8,128)(2,1)S(1)} %attend.3.rest_0_), channel_id=1, source_target_pairs={{0,2},{1,3},{2,0},{3,1},{4,6},{5,7},{6,4},{7,5},{8,10},{9,11},{10,... | collective-permute-start | bytes 786440 | tf_op jit(solution)/shard_map/ppermute | solution.py:204
  184.0 21.8 %collective-permute-start.4 = (bf16[512,256]{1,0:T(8,128)(2,1)S(1)}, bf16[512,256]{1,0:T(8,128)(2,1)S(1)}, u32[]{:S(2)}, u32[]{:S(2)}) collective-permute-start(bf16[512,256]{1,0:T(8,128)(2,1)S(1)} %attend.3.rest_0_), channel_id=1, source_target_pairs={{0,3},{1,2},{2,1},{3,0},{4,7},{5,6},{6,5},{7,4},{8,11},{9,10},{10,... | collective-permute-start | bytes 786440 | tf_op jit(solution)/shard_map/ppermute | solution.py:204
  206.5 2.2 copy-start.1
  214.8 17.2 %collective-permute-start.10 = (bf16[512,128]{1,0:T(8,128)(2,1)S(1)}, bf16[512,128]{1,0:T(8,128)(2,1)}, u32[]{:S(2)}, u32[]{:S(2)}) collective-permute-start(bf16[512,128]{1,0:T(8,128)(2,1)S(1)} %attend.4.rest_1_), channel_id=1, source_target_pairs={{0,3},{1,2},{2,1},{3,0},{4,7},{5,6},{6,5},{7,4},{8,11},{9,10},{10,... | collective-permute-start | bytes 393224 | tf_op jit(solution)/shard_map/ppermute | solution.py:204
  216.5 17.3 %collective-permute-start.6 = (bf16[512,128]{1,0:T(8,128)(2,1)S(1)}, bf16[512,128]{1,0:T(8,128)(2,1)}, u32[]{:S(2)}, u32[]{:S(2)}) collective-permute-start(bf16[512,128]{1,0:T(8,128)(2,1)S(1)} %attend.4.rest_1_), channel_id=1, source_target_pairs={{0,1},{1,0},{2,3},{3,2},{4,5},{5,4},{6,7},{7,6},{8,9},{9,8},{10,11... | collective-permute-start | bytes 393224 | tf_op jit(solution)/shard_map/ppermute | solution.py:204
  220.0 13.8 %collective-permute-start.8 = (bf16[512,128]{1,0:T(8,128)(2,1)S(1)}, bf16[512,128]{1,0:T(8,128)(2,1)}, u32[]{:S(2)}, u32[]{:S(2)}) collective-permute-start(bf16[512,128]{1,0:T(8,128)(2,1)S(1)} %attend.4.rest_1_), channel_id=1, source_target_pairs={{0,2},{1,3},{2,0},{3,1},{4,6},{5,7},{6,4},{7,5},{8,10},{9,11},{10,... | collective-permute-start | bytes 393224 | tf_op jit(solution)/shard_map/ppermute | solution.py:204
  220.8 2.2 copy-start.2
  222.9 10.8 %slice-start = ((f32[1,3,3072]{2,0,1:T(1,128)}), f32[1,1,3072]{2,0,1:T(1,128)S(1)}, s32[]{:S(2)}) async-start(f32[1,3,3072]{2,0,1:T(1,128)} %param.7), calls=%async_computation.5 | async-start | bytes 24576 | tf_op jit(solution)/shard_map/slice | solution.py:267
  222.9 20.0 %copy-start.4 = (bf16[1,512,768]{2,1,0:T(8,128)(2,1)S(1)}, bf16[1,512,768]{2,1,0:T(8,128)(2,1)}, u32[]{:S(2)}) copy-start(bf16[1,512,768]{2,1,0:T(8,128)(2,1)} %param.8) | copy-start | bytes 2359300
  222.9 20.0 %copy-start.5 = (bf16[768,512]{1,0:T(8,128)(2,1)S(1)}, bf16[768,512]{1,0:T(8,128)(2,1)}, u32[]{:S(2)}) copy-start(bf16[768,512]{1,0:T(8,128)(2,1)} %get-tuple-element.33.rest_12_) | copy-start | bytes 2359300
  223.0 20.0 %copy-start.9 = (bf16[768,512]{1,0:T(8,128)(2,1)S(1)}, bf16[768,512]{1,0:T(8,128)(2,1)}, u32[]{:S(2)}) copy-start(bf16[768,512]{1,0:T(8,128)(2,1)} %copy-done.8) | copy-start | bytes 2359300
  223.0 20.0 %copy-start.11 = (bf16[512,256]{1,0:T(8,128)(2,1)S(1)}, bf16[512,256]{1,0:T(8,128)(2,1)}, u32[]{:S(2)}) copy-start(bf16[512,256]{1,0:T(8,128)(2,1)} %copy-done.10) | copy-start | bytes 786436
  223.0 20.0 %copy-start.13 = (bf16[512,256]{1,0:T(8,128)(2,1)S(1)}, bf16[512,256]{1,0:T(8,128)(2,1)}, u32[]{:S(2)}) copy-start(bf16[512,256]{1,0:T(8,128)(2,1)} %copy-done.12) | copy-start | bytes 786436
  223.0 20.0 %copy-start.15 = (bf16[512,256]{1,0:T(8,128)(2,1)S(1)}, bf16[512,256]{1,0:T(8,128)(2,1)}, u32[]{:S(2)}) copy-start(bf16[512,256]{1,0:T(8,128)(2,1)} %copy-done.14) | copy-start | bytes 786436
  229.3 8.4 %collective-permute-start.11 = (bf16[512,128]{1,0:T(8,128)(2,1)S(1)}, bf16[512,128]{1,0:T(8,128)(2,1)S(1)}, u32[]{:S(2)}, u32[]{:S(2)}) collective-permute-start(bf16[512,128]{1,0:T(8,128)(2,1)S(1)} %attend.5.rest_2_), channel_id=1, source_target_pairs={{0,3},{1,2},{2,1},{3,0},{4,7},{5,6},{6,5},{7,4},{8,11},{9,10},{10,... | collective-permute-start | bytes 393224 | tf_op jit(solution)/shard_map/ppermute | solution.py:204
  230.9 6.9 %collective-permute-start.7 = (bf16[512,128]{1,0:T(8,128)(2,1)S(1)}, bf16[512,128]{1,0:T(8,128)(2,1)S(1)}, u32[]{:S(2)}, u32[]{:S(2)}) collective-permute-start(bf16[512,128]{1,0:T(8,128)(2,1)S(1)} %attend.5.rest_2_), channel_id=1, source_target_pairs={{0,1},{1,0},{2,3},{3,2},{4,5},{5,4},{6,7},{7,6},{8,9},{9,8},{10,11... | collective-permute-start | bytes 393224 | tf_op jit(solution)/shard_map/ppermute | solution.py:204
  232.0 10.9 %collective-permute-start.9 = (bf16[512,128]{1,0:T(8,128)(2,1)S(1)}, bf16[512,128]{1,0:T(8,128)(2,1)S(1)}, u32[]{:S(2)}, u32[]{:S(2)}) collective-permute-start(bf16[512,128]{1,0:T(8,128)(2,1)S(1)} %attend.5.rest_2_), channel_id=1, source_target_pairs={{0,2},{1,3},{2,0},{3,1},{4,6},{5,7},{6,4},{7,5},{8,10},{9,11},{10,... | collective-permute-start | bytes 393224 | tf_op jit(solution)/shard_map/ppermute | solution.py:204
  246.3 12.4 %collective-permute-start.12 = (bf16[512,768]{1,0:T(8,128)(2,1)S(1)}, bf16[512,768]{1,0:T(8,128)(2,1)S(1)}, u32[]{:S(2)}, u32[]{:S(2)}) collective-permute-start(bf16[512,768]{1,0:T(8,128)(2,1)S(1)} %output.1), channel_id=1, source_target_pairs={{0,4},{4,8},{8,12},{12,16},{16,20},{20,24},{24,28},{28,0},{1,5},{5... | collective-permute-start | bytes 2359304 | tf_op jit(solution)/shard_map/ppermute | solution.py:209
  (4 other events, 3.1 us)
Sparse Core Ops, SparseCore 0:
  24.9 88.2 all-gather.2

commit v13 on v12

--- a/solution.py
+++ b/solution.py
@@ -166,7 +166,7 @@
             patch * heads * keys,
         ),
         name="attend",
-    )(where, normed, matrix, stale)
+    )(where, normed, matrix, in_hbm(stale))
 
 
 def output_kernel(tp, chunks, inflow_ref, gate_ref, *rest):
@@ -247,7 +247,7 @@
         held = lax.dynamic_slice_in_dim(to_out, (rank ^ distance) * share, share, 0)
         matrices.append(swapped(held, "tp", distance) if distance else held)
 
-    waits, parts = [(), (normed, *matrices[1:3]), tuple(matrices[3:])], []
+    waits, parts = [(), (normed, *matrices[1:3]), ()], []
     owns, final = [], len(groups) - 1
     for index, group in enumerate(groups):
         if index > 1:
@@ -259,10 +259,13 @@
         matrix = moved
         if index < final:
             continue
-        parts = [[swapped(own, "tp", distance) for distance in range(1, tp)] for own in owns]
-        ready = waiting(normed, *[part for own in parts[:1] for part in own], *owns[1:])
+        early = [waiting(own, *owns[1:]) for own in owns[:1]] + owns[1:]
+        parts = [[swapped(own, "tp", distance) for distance in range(1, tp)] for own in early]
+        first = [part for own in parts[:1] for part in own]
+        ready = waiting(normed, *first[:1], *owns[1:], *matrices[3:])
         owns.append(attend(ready, matrix, patch_index, stale_cache[0], group, 0))
-        parts.append([swapped(owns[-1], "tp", distance) for distance in range(1, tp)])
+        ready = waiting(owns[-1], *first[1:])
+        parts.append([swapped(ready, "tp", distance) for distance in range(1, tp)])
     attended = [owns] + [[own[distance] for own in parts] for distance in range(tp - 1)]
     gate = lax.dynamic_slice_in_dim(modulation[0, 2], rank * share, share, 0)[None]
     return handed_on(output(inflow[0], gate, attended, matrices))[None]

time: 267 us -> 268 us (level)
  starting transfers between devices: 55.6 us -> 69.3 us
  local copies, waits for them, and re-layouts: 17.2 us -> 9.09 us
  waiting for transfers between devices: 129 us -> 123 us
    ppermute x12, waiting for transfers between devices: 50.6 us -> 27.1 us  [swapped(): lax.ppermute(block, axis, [(i, i ^ distance) for i in range(lax.axis_size...]
    all_to_all x4, waiting for transfers between devices: 23.2 us -> 41.1 us  [relayed(): lax.all_to_all(pieces, 'section', split_axis=0, concat_axis=0, tiled=True)]
    ppermute x12, starting transfers between devices: 36.8 us -> 50.4 us  [swapped(): lax.ppermute(block, axis, [(i, i ^ distance) for i in range(lax.axis_size...]
    unnamed x36 -> x22, local copies, waits for them, and re-layouts: 15.4 us -> 7.37 us
  transfers between devices with their start and end apart: 18 -> 18, of which waited for: 10 -> 9; matrix products, arithmetic and copies ran while one was open for 1% -> 1% of each run, Pallas kernels for 14% -> 14%
where the time goes in v13:
time: 268 us; the launch traced here: 267 us
  waiting for transfers between devices  123 us (46%)
  starting transfers between devices  69.3 us (26%)
  Pallas kernels  50.6 us (19%)
  between operations  14.2 us (5%)
  local copies, waits for them, and re-layouts  9.09 us (3%)
    ppermute x12, starting transfers between devices, swapped(): lax.ppermute(block, axis, [(i, i ^ distance) for i in range(lax.axis_size...  50.4 us
    all_gather x1, waiting for transfers between devices, local(): tokens = lax.all_gather(inflow[0], 'tp', axis=1, tiled=True)  42.2 us
    all_to_all x4, waiting for transfers between devices, relayed(): lax.all_to_all(pieces, 'section', split_axis=0, concat_axis=0, tiled=True)  41.1 us
    ppermute x12, waiting for transfers between devices, swapped(): lax.ppermute(block, axis, [(i, i ^ distance) for i in range(lax.axis_size...  27.1 us
    pallas_call x3, Pallas kernels, attend(): pl.pallas_call(attend_kernel, grid_spec=pltpu.PrefetchScalarGridSpec(num_...  23.8 us
    pallas_call x2, Pallas kernels, split_blocks(): pl.pallas_call(functools.partial(split_kernel, lanes, plan, kinds, depth_...  19.1 us
    all_to_all x4, starting transfers between devices, relayed(): lax.all_to_all(pieces, 'section', split_axis=0, concat_axis=0, tiled=True)  18.7 us
    ppermute x1, waiting for transfers between devices, handed_on(): lax.ppermute(block, 'section', [(i, (i + 1) % sections) for i in range(se...  12.3 us
  transfers between devices with their start and end apart: 18, of which 9 were waited for; matrix products, arithmetic and copies ran while one was open for 1% of the time, Pallas kernels for 14%

profile of v13, /device:TPU:0, one launch (start us, length us, event | category | flops | bytes accessed | tf_op | source)
XLA Modules:
  0.0 267.3 jit_solution(7550370378345917948)
XLA Ops:
  7.3 10.1 %split_blocks.2 = bf16[8,384,512]{2,1,0:T(8,128)(2,1)} custom-call(s32[8]{0:T(128)S(1)} %select_reduce_fusion.order_ref, bf16[8,6144,128]{2,1,0:T(8,128)(2,1)} %bitcast.20), custom_call_target="tpu_custom_call" | custom-call | bytes 18874368 | tf_op jit(solution)/shard_map/split_blocks/pallas_call | solution.py:79
  17.4 5.2 %all-to-all-start.1 = ((bf16[8,384,512]{2,1,0:T(8,128)(2,1)}), bf16[8,384,512]{2,1,0:T(8,128)(2,1)S(1)}, u32[]{:S(2)}, u32[]{:S(2)}) async-start(bf16[8,384,512]{2,1,0:T(8,128)(2,1)} %split_blocks.2), calls=%async_computation.1 | async-start | bytes 6291456 | tf_op jit(solution)/shard_map/all_to_all | solution.py:213
  23.3 9.1 %split_blocks.3 = (bf16[8,384,768]{2,1,0:T(8,128)(2,1)S(1)}, bf16[8,384,384]{2,1,0:T(8,128)(2,1)S(1)}, bf16[8,384,384]{2,1,0:T(8,128)(2,1)S(1)}) custom-call(s32[8]{0:T(128)S(1)} %select_reduce_fusion.order_ref, bf16[8,6144,128]{2,1,0:T(8,128)(2,1)} %bitcast.21), custom_call_target="tpu_custom_call" | custom-call | bytes 18874368 | tf_op jit(solution)/shard_map/split_blocks/pallas_call | solution.py:79
  32.4 2.1 copy-done
  37.2 23.2 %all-to-all-done.1 = bf16[8,384,512]{2,1,0:T(8,128)(2,1)S(1)} async-done(((bf16[8,384,512]{2,1,0:T(8,128)(2,1)}), bf16[8,384,512]{2,1,0:T(8,128)(2,1)S(1)}, u32[]{:S(2)}, u32[]{:S(2)}) %all-to-all-start.1) | async-done | bytes 3145760 | tf_op jit(solution)/shard_map/all_to_all | solution.py:213
  60.4 4.6 %all-to-all-start = ((bf16[8,384,768]{2,1,0:T(8,128)(2,1)}), bf16[8,384,768]{2,1,0:T(8,128)(2,1)}, u32[]{:S(2)}, u32[]{:S(2)}) async-start(bf16[8,384,768]{2,1,0:T(8,128)(2,1)} %copy-done), calls=%async_computation | async-start | bytes 9437184 | tf_op jit(solution)/shard_map/all_to_all | solution.py:213
  65.1 1.7 constant_dynamic-slice_fusion.3
  66.8 1.6 collective-permute-start
  68.4 2.6 collective-permute-start.1
  71.0 42.2 %all-gather.3.cloned.1.call-done = bf16[1,512,3072]{2,1,0:T(8,128)(2,1)} async-done(((bf16[1,512,768]{2,1,0:T(8,128)(2,1)}), bf16[1,512,3072]{2,1,0:T(8,128)(2,1)}) %all-gather.3.cloned.1.call-update) | async-done | bytes 3145744 | tf_op jit(solution)/shard_map/all_gather | solution.py:231
  113.2 4.1 %norm.1.normed_ref = bf16[512,3072]{1,0:T(8,128)(2,1)S(1)} custom-call(bf16[512,3072]{1,0:T(8,128)(2,1)} %bitcast.26, f32[3,3072]{1,0:T(4,128)S(1)} %bitcast.19), custom_call_target="tpu_custom_call" | custom-call | flops 15728640 | bytes 6291456 | tf_op jit(solution)/shard_map/norm/pallas_call | solution.py:109
  117.3 4.4 %collective-permute-done.rest_13_ = bf16[768,512]{1,0:T(8,128)(2,1)} collective-permute-done((bf16[768,512]{1,0:T(8,128)(2,1)}, bf16[768,512]{1,0:T(8,128)(2,1)}, u32[]{:S(2)}, u32[]{:S(2)}) %collective-permute-start) | collective-permute-done | bytes 786464 | tf_op jit(solution)/shard_map/ppermute | solution.py:204
  121.8 4.4 %all-to-all-start.2 = ((bf16[8,384,384]{2,1,0:T(8,128)(2,1)}), bf16[8,384,384]{2,1,0:T(8,128)(2,1)}, u32[]{:S(2)}, u32[]{:S(2)}) async-start(bf16[8,384,384]{2,1,0:T(8,128)(2,1)} %copy-done.4), calls=%async_computation.2 | async-start | bytes 4718592 | tf_op jit(solution)/shard_map/all_to_all | solution.py:213
  126.8 10.9 %attend.3.rest_0_ = bf16[512,256]{1,0:T(8,128)(2,1)S(1)} custom-call(s32[1]{0:T(128)S(6)} %copy.13.where_ref, bf16[512,3072]{1,0:T(8,128)(2,1)S(1)} %norm.1.normed_ref, bf16[3072,768]{1,0:T(8,128)(2,1)} %bitcast.6.matrix_ref, bf16[2,2048,512]{2,1,0:T(8,128)(2,1)} %bitcast.22), custom_call_target="tpu_custom_call" | custom-call | flops 3489660928 | bytes 6815744 | tf_op jit(solution)/shard_map/attend/pallas_call | solution.py:149
  137.7 17.9 %all-to-all-done.2 = bf16[8,384,384]{2,1,0:T(8,128)(2,1)} async-done(((bf16[8,384,384]{2,1,0:T(8,128)(2,1)}), bf16[8,384,384]{2,1,0:T(8,128)(2,1)}, u32[]{:S(2)}, u32[]{:S(2)}) %all-to-all-start.2) | async-done | bytes 2359328 | tf_op jit(solution)/shard_map/all_to_all | solution.py:213
  155.6 4.5 %all-to-all-start.3 = ((bf16[8,384,384]{2,1,0:T(8,128)(2,1)}), bf16[8,384,384]{2,1,0:T(8,128)(2,1)}, u32[]{:S(2)}, u32[]{:S(2)}) async-start(bf16[8,384,384]{2,1,0:T(8,128)(2,1)} %copy-done.3), calls=%async_computation.3 | async-start | bytes 4718592 | tf_op jit(solution)/shard_map/all_to_all | solution.py:213
  160.2 2.4 collective-permute-start.3
  162.6 6.4 %attend.4.rest_1_ = bf16[512,128]{1,0:T(8,128)(2,1)S(1)} custom-call(s32[1]{0:T(128)S(6)} %copy.13.where_ref, bf16[512,3072]{1,0:T(8,128)(2,1)S(1)} %norm.1.normed_ref, bf16[3072,384]{1,0:T(8,128)(2,1)} %bitcast.9.matrix_ref, bf16[2,2048,512]{2,1,0:T(8,128)(2,1)} %bitcast.23), custom_call_target="tpu_custom_call" | custom-call | flops 1744830464 | bytes 3407872 | tf_op jit(solution)/shard_map/attend/pallas_call | solution.py:149
  169.5 1.6 collective-permute-start.5
  171.1 2.4 collective-permute-start.6
  173.5 1.4 collective-permute-start.10
  174.9 12.6 %collective-permute-done.2.rest_3_ = bf16[512,256]{1,0:T(8,128)(2,1)S(1)} collective-permute-done((bf16[512,256]{1,0:T(8,128)(2,1)S(1)}, bf16[512,256]{1,0:T(8,128)(2,1)S(1)}, u32[]{:S(2)}, u32[]{:S(2)}) %collective-permute-start.2) | collective-permute-done | bytes 262176 | tf_op jit(solution)/shard_map/ppermute | solution.py:204
  188.3 1.4 collective-permute-start.4
  190.5 24.3 %collective-permute-start.8 = (bf16[512,128]{1,0:T(8,128)(2,1)S(1)}, bf16[512,128]{1,0:T(8,128)(2,1)}, u32[]{:S(2)}, u32[]{:S(2)}) collective-permute-start(bf16[512,128]{1,0:T(8,128)(2,1)S(1)} %attend.4.rest_1_), channel_id=1, source_target_pairs={{0,2},{1,3},{2,0},{3,1},{4,6},{5,7},{6,4},{7,5},{8,10},{9,11},{10,... | collective-permute-start | bytes 393224 | tf_op jit(solution)/shard_map/ppermute | solution.py:204
  214.8 6.5 %attend.5.rest_2_ = bf16[512,128]{1,0:T(8,128)(2,1)S(1)} custom-call(s32[1]{0:T(128)S(6)} %copy.13.where_ref, bf16[512,3072]{1,0:T(8,128)(2,1)S(1)} %norm.1.normed_ref, bf16[3072,384]{1,0:T(8,128)(2,1)} %bitcast.10.matrix_ref, bf16[2,2048,512]{2,1,0:T(8,128)(2,1)} %bitcast.24), custom_call_target="tpu_custom_call" | custom-call | flops 1744830464 | bytes 3407872 | tf_op jit(solution)/shard_map/attend/pallas_call | solution.py:149
  221.4 1.9 collective-permute-start.11
  223.3 8.1 %collective-permute-start.7 = (bf16[512,128]{1,0:T(8,128)(2,1)S(1)}, bf16[512,128]{1,0:T(8,128)(2,1)S(1)}, u32[]{:S(2)}, u32[]{:S(2)}) collective-permute-start(bf16[512,128]{1,0:T(8,128)(2,1)S(1)} %attend.5.rest_2_), channel_id=1, source_target_pairs={{0,1},{1,0},{2,3},{3,2},{4,5},{5,4},{6,7},{7,6},{8,9},{9,8},{10,11... | collective-permute-start | bytes 393224 | tf_op jit(solution)/shard_map/ppermute | solution.py:204
  231.4 2.2 collective-permute-start.9
  233.7 1.8 collective-permute-done.8.rest_7_
  236.8 6.9 %collective-permute-done.9.rest_8_ = bf16[512,128]{1,0:T(8,128)(2,1)S(1)} collective-permute-done((bf16[512,128]{1,0:T(8,128)(2,1)S(1)}, bf16[512,128]{1,0:T(8,128)(2,1)S(1)}, u32[]{:S(2)}, u32[]{:S(2)}) %collective-permute-start.9) | collective-permute-done | bytes 131104 | tf_op jit(solution)/shard_map/ppermute | solution.py:204
  243.7 3.5 %output.1 = bf16[512,768]{1,0:T(8,128)(2,1)S(1)} custom-call(bf16[512,768]{1,0:T(8,128)(2,1)S(1)} %bitcast.18, f32[1,768]{1,0:T(1,128)S(1)} %dynamic-slice_bitcast_fusion.gate_ref, bf16[512,256]{1,0:T(8,128)(2,1)S(1)} %attend.3.rest_0_, bf16[512,128]{1,0:T(8,128)(2,1)S(1)} %attend.4.rest_1_, bf16[512,128]{1,0:T(8,128)(2,1)S(1)} %attend.5.rest_2_, ...), custom_call_target="tpu_custom_call" | custom-call | flops 1610612736 | bytes 5242880 | tf_op jit(solution)/shard_map/output/pallas_call | solution.py:187
  247.3 12.3 %collective-permute-done.12 = bf16[512,768]{1,0:T(8,128)(2,1)S(1)} collective-permute-done((bf16[512,768]{1,0:T(8,128)(2,1)S(1)}, bf16[512,768]{1,0:T(8,128)(2,1)S(1)}, u32[]{:S(2)}, u32[]{:S(2)}) %collective-permute-start.12) | collective-permute-done | bytes 786464 | tf_op jit(solution)/shard_map/ppermute | solution.py:209
  (39 shorter events, 8.6 us)
Async XLA Ops:
  17.4 43.1 %all-to-all-start.1 = ((bf16[8,384,512]{2,1,0:T(8,128)(2,1)}), bf16[8,384,512]{2,1,0:T(8,128)(2,1)S(1)}, u32[]{:S(2)}, u32[]{:S(2)}) async-start(bf16[8,384,512]{2,1,0:T(8,128)(2,1)} %split_blocks.2), calls=%async_computation.1 | async-start | bytes 6291456 | tf_op jit(solution)/shard_map/all_to_all | solution.py:213
  22.5 90.7 %all-gather.3.cloned.1.call-start = ((), (), s32[]{:S(2)}) async-start(), calls=%async_computation.4 | async-start | bytes 3932160 | tf_op jit(solution)/shard_map/all_gather | solution.py:231
  32.4 2.1 copy-start
  34.5 1.4 copy-start.3
  35.9 1.4 copy-start.4
  60.4 61.3 %all-to-all-start = ((bf16[8,384,768]{2,1,0:T(8,128)(2,1)}), bf16[8,384,768]{2,1,0:T(8,128)(2,1)}, u32[]{:S(2)}, u32[]{:S(2)}) async-start(bf16[8,384,768]{2,1,0:T(8,128)(2,1)} %copy-done), calls=%async_computation | async-start | bytes 9437184 | tf_op jit(solution)/shard_map/all_to_all | solution.py:213
  65.1 5.9 %copy-start.9 = (f32[1,3,3072]{2,0,1:T(1,128)S(1)}, f32[1,3,3072]{2,0,1:T(1,128)}, u32[]{:S(2)}) copy-start(f32[1,3,3072]{2,0,1:T(1,128)} %param.7) | copy-start | bytes 110596
  66.8 55.0 %collective-permute-start = (bf16[768,512]{1,0:T(8,128)(2,1)}, bf16[768,512]{1,0:T(8,128)(2,1)}, u32[]{:S(2)}, u32[]{:S(2)}) collective-permute-start(bf16[768,512]{1,0:T(8,128)(2,1)} %get-tuple-element.38), channel_id=1, source_target_pairs={{0,1},{1,0},{2,3},{3,2},{4,5},{5,4},{6,7},{7,6},{8,9},{9,8},{10,11... | collective-permute-start | bytes 2359304 | tf_op jit(solution)/shard_map/ppermute | solution.py:204
  68.4 53.4 %collective-permute-start.1 = (bf16[768,512]{1,0:T(8,128)(2,1)}, bf16[768,512]{1,0:T(8,128)(2,1)}, u32[]{:S(2)}, u32[]{:S(2)}) collective-permute-start(bf16[768,512]{1,0:T(8,128)(2,1)} %get-tuple-element.37), channel_id=1, source_target_pairs={{0,2},{1,3},{2,0},{3,1},{4,6},{5,7},{6,4},{7,5},{8,10},{9,11},{10,... | collective-permute-start | bytes 2359304 | tf_op jit(solution)/shard_map/ppermute | solution.py:204
  121.8 33.9 %all-to-all-start.2 = ((bf16[8,384,384]{2,1,0:T(8,128)(2,1)}), bf16[8,384,384]{2,1,0:T(8,128)(2,1)}, u32[]{:S(2)}, u32[]{:S(2)}) async-start(bf16[8,384,384]{2,1,0:T(8,128)(2,1)} %copy-done.4), calls=%async_computation.2 | async-start | bytes 4718592 | tf_op jit(solution)/shard_map/all_to_all | solution.py:213
  155.6 59.2 %all-to-all-start.3 = ((bf16[8,384,384]{2,1,0:T(8,128)(2,1)}), bf16[8,384,384]{2,1,0:T(8,128)(2,1)}, u32[]{:S(2)}, u32[]{:S(2)}) async-start(bf16[8,384,384]{2,1,0:T(8,128)(2,1)} %copy-done.3), calls=%async_computation.3 | async-start | bytes 4718592 | tf_op jit(solution)/shard_map/all_to_all | solution.py:213
  160.2 29.4 %collective-permute-start.3 = (bf16[768,512]{1,0:T(8,128)(2,1)}, bf16[768,512]{1,0:T(8,128)(2,1)S(1)}, u32[]{:S(2)}, u32[]{:S(2)}) collective-permute-start(bf16[768,512]{1,0:T(8,128)(2,1)} %get-tuple-element.36), channel_id=1, source_target_pairs={{0,3},{1,2},{2,1},{3,0},{4,7},{5,6},{6,5},{7,4},{8,11},{9,10},{10,... | collective-permute-start | bytes 2359304 | tf_op jit(solution)/shard_map/ppermute | solution.py:204
  169.0 18.5 %collective-permute-start.2 = (bf16[512,256]{1,0:T(8,128)(2,1)S(1)}, bf16[512,256]{1,0:T(8,128)(2,1)S(1)}, u32[]{:S(2)}, u32[]{:S(2)}) collective-permute-start(bf16[512,256]{1,0:T(8,128)(2,1)S(1)} %attend.3.rest_0_), channel_id=1, source_target_pairs={{0,1},{1,0},{2,3},{3,2},{4,5},{5,4},{6,7},{7,6},{8,9},{9,8},{10,11... | collective-permute-start | bytes 786440 | tf_op jit(solution)/shard_map/ppermute | solution.py:204
  169.5 51.9 %collective-permute-start.5 = (bf16[512,256]{1,0:T(8,128)(2,1)S(1)}, bf16[512,256]{1,0:T(8,128)(2,1)}, u32[]{:S(2)}, u32[]{:S(2)}) collective-permute-start(bf16[512,256]{1,0:T(8,128)(2,1)S(1)} %attend.3.rest_0_), channel_id=1, source_target_pairs={{0,2},{1,3},{2,0},{3,1},{4,6},{5,7},{6,4},{7,5},{8,10},{9,11},{10,... | collective-permute-start | bytes 786440 | tf_op jit(solution)/shard_map/ppermute | solution.py:204
  171.1 50.3 %collective-permute-start.6 = (bf16[512,256]{1,0:T(8,128)(2,1)S(1)}, bf16[512,256]{1,0:T(8,128)(2,1)}, u32[]{:S(2)}, u32[]{:S(2)}) collective-permute-start(bf16[512,256]{1,0:T(8,128)(2,1)S(1)} %attend.3.rest_0_), channel_id=1, source_target_pairs={{0,3},{1,2},{2,1},{3,0},{4,7},{5,6},{6,5},{7,4},{8,11},{9,10},{10,... | collective-permute-start | bytes 786440 | tf_op jit(solution)/shard_map/ppermute | solution.py:204
  173.5 58.0 %collective-permute-start.10 = (bf16[512,128]{1,0:T(8,128)(2,1)S(1)}, bf16[512,128]{1,0:T(8,128)(2,1)}, u32[]{:S(2)}, u32[]{:S(2)}) collective-permute-start(bf16[512,128]{1,0:T(8,128)(2,1)S(1)} %attend.4.rest_1_), channel_id=1, source_target_pairs={{0,3},{1,2},{2,1},{3,0},{4,7},{5,6},{6,5},{7,4},{8,11},{9,10},{10,... | collective-permute-start | bytes 393224 | tf_op jit(solution)/shard_map/ppermute | solution.py:204
  187.6 0.7 copy-start.7
  188.3 45.4 %collective-permute-start.4 = (bf16[512,128]{1,0:T(8,128)(2,1)S(1)}, bf16[512,128]{1,0:T(8,128)(2,1)}, u32[]{:S(2)}, u32[]{:S(2)}) collective-permute-start(bf16[512,128]{1,0:T(8,128)(2,1)S(1)} %attend.4.rest_1_), channel_id=1, source_target_pairs={{0,1},{1,0},{2,3},{3,2},{4,5},{5,4},{6,7},{7,6},{8,9},{9,8},{10,11... | collective-permute-start | bytes 393224 | tf_op jit(solution)/shard_map/ppermute | solution.py:204
  189.6 0.9 copy-start.5
  190.5 44.9 %collective-permute-start.8 = (bf16[512,128]{1,0:T(8,128)(2,1)S(1)}, bf16[512,128]{1,0:T(8,128)(2,1)}, u32[]{:S(2)}, u32[]{:S(2)}) collective-permute-start(bf16[512,128]{1,0:T(8,128)(2,1)S(1)} %attend.4.rest_1_), channel_id=1, source_target_pairs={{0,2},{1,3},{2,0},{3,1},{4,6},{5,7},{6,4},{7,5},{8,10},{9,11},{10,... | collective-permute-start | bytes 393224 | tf_op jit(solution)/shard_map/ppermute | solution.py:204
  214.8 18.9 %slice-start = ((f32[1,3,3072]{2,0,1:T(1,128)}), f32[1,1,3072]{2,0,1:T(1,128)S(1)}, s32[]{:S(2)}) async-start(f32[1,3,3072]{2,0,1:T(1,128)} %param.7), calls=%async_computation.5 | async-start | bytes 24576 | tf_op jit(solution)/shard_map/slice | solution.py:270
  214.8 28.9 %copy-start.1 = (bf16[1,512,768]{2,1,0:T(8,128)(2,1)S(1)}, bf16[1,512,768]{2,1,0:T(8,128)(2,1)}, u32[]{:S(2)}) copy-start(bf16[1,512,768]{2,1,0:T(8,128)(2,1)} %param.8) | copy-start | bytes 2359300
  214.8 28.9 %copy-start.2 = (bf16[768,512]{1,0:T(8,128)(2,1)S(1)}, bf16[768,512]{1,0:T(8,128)(2,1)}, u32[]{:S(2)}) copy-start(bf16[768,512]{1,0:T(8,128)(2,1)} %get-tuple-element.35.rest_12_) | copy-start | bytes 2359300
  214.8 28.9 %copy-start.6 = (bf16[768,512]{1,0:T(8,128)(2,1)S(1)}, bf16[768,512]{1,0:T(8,128)(2,1)}, u32[]{:S(2)}) copy-start(bf16[768,512]{1,0:T(8,128)(2,1)} %copy-done.5) | copy-start | bytes 2359300
  214.8 28.9 %copy-start.8 = (bf16[512,256]{1,0:T(8,128)(2,1)S(1)}, bf16[512,256]{1,0:T(8,128)(2,1)}, u32[]{:S(2)}) copy-start(bf16[512,256]{1,0:T(8,128)(2,1)} %copy-done.7) | copy-start | bytes 786436
  221.4 14.1 %collective-permute-start.11 = (bf16[512,128]{1,0:T(8,128)(2,1)S(1)}, bf16[512,128]{1,0:T(8,128)(2,1)S(1)}, u32[]{:S(2)}, u32[]{:S(2)}) collective-permute-start(bf16[512,128]{1,0:T(8,128)(2,1)S(1)} %attend.5.rest_2_), channel_id=1, source_target_pairs={{0,3},{1,2},{2,1},{3,0},{4,7},{5,6},{6,5},{7,4},{8,11},{9,10},{10,... | collective-permute-start | bytes 393224 | tf_op jit(solution)/shard_map/ppermute | solution.py:204
  223.3 13.4 %collective-permute-start.7 = (bf16[512,128]{1,0:T(8,128)(2,1)S(1)}, bf16[512,128]{1,0:T(8,128)(2,1)S(1)}, u32[]{:S(2)}, u32[]{:S(2)}) collective-permute-start(bf16[512,128]{1,0:T(8,128)(2,1)S(1)} %attend.5.rest_2_), channel_id=1, source_target_pairs={{0,1},{1,0},{2,3},{3,2},{4,5},{5,4},{6,7},{7,6},{8,9},{9,8},{10,11... | collective-permute-start | bytes 393224 | tf_op jit(solution)/shard_map/ppermute | solution.py:204
  231.4 12.3 %collective-permute-start.9 = (bf16[512,128]{1,0:T(8,128)(2,1)S(1)}, bf16[512,128]{1,0:T(8,128)(2,1)S(1)}, u32[]{:S(2)}, u32[]{:S(2)}) collective-permute-start(bf16[512,128]{1,0:T(8,128)(2,1)S(1)} %attend.5.rest_2_), channel_id=1, source_target_pairs={{0,2},{1,3},{2,0},{3,1},{4,6},{5,7},{6,4},{7,5},{8,10},{9,11},{10,... | collective-permute-start | bytes 393224 | tf_op jit(solution)/shard_map/ppermute | solution.py:204
  247.2 12.4 %collective-permute-start.12 = (bf16[512,768]{1,0:T(8,128)(2,1)S(1)}, bf16[512,768]{1,0:T(8,128)(2,1)S(1)}, u32[]{:S(2)}, u32[]{:S(2)}) collective-permute-start(bf16[512,768]{1,0:T(8,128)(2,1)S(1)} %output.1), channel_id=1, source_target_pairs={{0,4},{4,8},{8,12},{12,16},{16,20},{20,24},{24,28},{28,0},{1,5},{5... | collective-permute-start | bytes 2359304 | tf_op jit(solution)/shard_map/ppermute | solution.py:209
Sparse Core Ops, SparseCore 0:
  25.0 88.2 all-gather.2

commit v14 on v13

--- a/solution.py
+++ b/solution.py
@@ -247,7 +247,7 @@
         held = lax.dynamic_slice_in_dim(to_out, (rank ^ distance) * share, share, 0)
         matrices.append(swapped(held, "tp", distance) if distance else held)
 
-    waits, parts = [(), (normed, *matrices[1:3]), ()], []
+    waits, parts = [(), (normed, *matrices[1:3]), tuple(matrices[3:])], []
     owns, final = [], len(groups) - 1
     for index, group in enumerate(groups):
         if index > 1:

time: 268 us -> 261 us (0.974)
  starting transfers between devices: 69.3 us -> 61.6 us
    ppermute x12, waiting for transfers between devices: 27.1 us -> 45.5 us  [swapped(): lax.ppermute(block, axis, [(i, i ^ distance) for i in range(lax.axis_size...]
    all_to_all x4, waiting for transfers between devices: 41.1 us -> 23.1 us  [relayed(): lax.all_to_all(pieces, 'section', split_axis=0, concat_axis=0, tiled=True)]
    ppermute x12, starting transfers between devices: 50.4 us -> 42.9 us  [swapped(): lax.ppermute(block, axis, [(i, i ^ distance) for i in range(lax.axis_size...]
where the time goes in v14:
time: 261 us; the launch traced here: 260 us
  waiting for transfers between devices  124 us (48%)
  starting transfers between devices  61.6 us (24%)
  Pallas kernels  50.5 us (19%)
  between operations  14.2 us (5%)
  local copies, waits for them, and re-layouts  9.2 us (4%)
    ppermute x12, waiting for transfers between devices, swapped(): lax.ppermute(block, axis, [(i, i ^ distance) for i in range(lax.axis_size...  45.5 us
    ppermute x12, starting transfers between devices, swapped(): lax.ppermute(block, axis, [(i, i ^ distance) for i in range(lax.axis_size...  42.9 us
    all_gather x1, waiting for transfers between devices, local(): tokens = lax.all_gather(inflow[0], 'tp', axis=1, tiled=True)  42.3 us
    pallas_call x3, Pallas kernels, attend(): pl.pallas_call(attend_kernel, grid_spec=pltpu.PrefetchScalarGridSpec(num_...  23.8 us
    all_to_all x4, waiting for transfers between devices, relayed(): lax.all_to_all(pieces, 'section', split_axis=0, concat_axis=0, tiled=True)  23.1 us
    pallas_call x2, Pallas kernels, split_blocks(): pl.pallas_call(functools.partial(split_kernel, lanes, plan, kinds, depth_...  19.1 us
    all_to_all x4, starting transfers between devices, relayed(): lax.all_to_all(pieces, 'section', split_axis=0, concat_axis=0, tiled=True)  18.7 us
    ppermute x1, waiting for transfers between devices, handed_on(): lax.ppermute(block, 'section', [(i, (i + 1) % sections) for i in range(se...  12.3 us
  transfers between devices with their start and end apart: 18, of which 9 were waited for; matrix products, arithmetic and copies ran while one was open for 1% of the time, Pallas kernels for 14%

profile of v14, /device:TPU:0, one launch (start us, length us, event | category | flops | bytes accessed | tf_op | source)
XLA Modules:
  0.0 260.3 jit_solution(7686650581568283256)
XLA Ops:
  7.3 10.0 %split_blocks.2 = bf16[8,384,512]{2,1,0:T(8,128)(2,1)} custom-call(s32[8]{0:T(128)S(1)} %select_reduce_fusion.order_ref, bf16[8,6144,128]{2,1,0:T(8,128)(2,1)} %bitcast.20), custom_call_target="tpu_custom_call" | custom-call | bytes 18874368 | tf_op jit(solution)/shard_map/split_blocks/pallas_call | solution.py:79
  17.3 5.2 %all-to-all-start.1 = ((bf16[8,384,512]{2,1,0:T(8,128)(2,1)}), bf16[8,384,512]{2,1,0:T(8,128)(2,1)S(1)}, u32[]{:S(2)}, u32[]{:S(2)}) async-start(bf16[8,384,512]{2,1,0:T(8,128)(2,1)} %split_blocks.2), calls=%async_computation.1 | async-start | bytes 6291456 | tf_op jit(solution)/shard_map/all_to_all | solution.py:213
  23.2 9.1 %split_blocks.3 = (bf16[8,384,768]{2,1,0:T(8,128)(2,1)S(1)}, bf16[8,384,384]{2,1,0:T(8,128)(2,1)S(1)}, bf16[8,384,384]{2,1,0:T(8,128)(2,1)S(1)}) custom-call(s32[8]{0:T(128)S(1)} %select_reduce_fusion.order_ref, bf16[8,6144,128]{2,1,0:T(8,128)(2,1)} %bitcast.21), custom_call_target="tpu_custom_call" | custom-call | bytes 18874368 | tf_op jit(solution)/shard_map/split_blocks/pallas_call | solution.py:79
  32.3 2.2 copy-done
  34.5 1.4 copy-done.3
  37.3 23.1 %all-to-all-done.1 = bf16[8,384,512]{2,1,0:T(8,128)(2,1)S(1)} async-done(((bf16[8,384,512]{2,1,0:T(8,128)(2,1)}), bf16[8,384,512]{2,1,0:T(8,128)(2,1)S(1)}, u32[]{:S(2)}, u32[]{:S(2)}) %all-to-all-start.1) | async-done | bytes 3145760 | tf_op jit(solution)/shard_map/all_to_all | solution.py:213
  60.4 4.6 %all-to-all-start = ((bf16[8,384,768]{2,1,0:T(8,128)(2,1)}), bf16[8,384,768]{2,1,0:T(8,128)(2,1)}, u32[]{:S(2)}, u32[]{:S(2)}) async-start(bf16[8,384,768]{2,1,0:T(8,128)(2,1)} %copy-done), calls=%async_computation | async-start | bytes 9437184 | tf_op jit(solution)/shard_map/all_to_all | solution.py:213
  65.0 1.7 constant_dynamic-slice_fusion.3
  66.7 1.6 collective-permute-start
  68.3 2.6 collective-permute-start.1
  70.9 42.3 %all-gather.3.cloned.1.call-done = bf16[1,512,3072]{2,1,0:T(8,128)(2,1)} async-done(((bf16[1,512,768]{2,1,0:T(8,128)(2,1)}), bf16[1,512,3072]{2,1,0:T(8,128)(2,1)}) %all-gather.3.cloned.1.call-update) | async-done | bytes 3145744 | tf_op jit(solution)/shard_map/all_gather | solution.py:231
  113.2 4.1 %norm.1.normed_ref = bf16[512,3072]{1,0:T(8,128)(2,1)S(1)} custom-call(bf16[512,3072]{1,0:T(8,128)(2,1)} %bitcast.26, f32[3,3072]{1,0:T(4,128)S(1)} %bitcast.19), custom_call_target="tpu_custom_call" | custom-call | flops 15728640 | bytes 6291456 | tf_op jit(solution)/shard_map/norm/pallas_call | solution.py:109
  117.3 4.4 %collective-permute-done.rest_13_ = bf16[768,512]{1,0:T(8,128)(2,1)} collective-permute-done((bf16[768,512]{1,0:T(8,128)(2,1)}, bf16[768,512]{1,0:T(8,128)(2,1)}, u32[]{:S(2)}, u32[]{:S(2)}) %collective-permute-start) | collective-permute-done | bytes 786464 | tf_op jit(solution)/shard_map/ppermute | solution.py:204
  121.7 4.4 %all-to-all-start.2 = ((bf16[8,384,384]{2,1,0:T(8,128)(2,1)}), bf16[8,384,384]{2,1,0:T(8,128)(2,1)}, u32[]{:S(2)}, u32[]{:S(2)}) async-start(bf16[8,384,384]{2,1,0:T(8,128)(2,1)} %copy-done.4), calls=%async_computation.2 | async-start | bytes 4718592 | tf_op jit(solution)/shard_map/all_to_all | solution.py:213
  126.1 2.4 collective-permute-start.3
  129.2 18.8 %collective-permute-done.3.rest_15_ = bf16[768,512]{1,0:T(8,128)(2,1)S(1)} collective-permute-done((bf16[768,512]{1,0:T(8,128)(2,1)}, bf16[768,512]{1,0:T(8,128)(2,1)S(1)}, u32[]{:S(2)}, u32[]{:S(2)}) %collective-permute-start.3) | collective-permute-done | bytes 786464 | tf_op jit(solution)/shard_map/ppermute | solution.py:204
  149.0 10.9 %attend.3.rest_0_ = bf16[512,256]{1,0:T(8,128)(2,1)S(1)} custom-call(s32[1]{0:T(128)S(6)} %copy.13.where_ref, bf16[512,3072]{1,0:T(8,128)(2,1)S(1)} %norm.1.normed_ref, bf16[3072,768]{1,0:T(8,128)(2,1)} %bitcast.6.matrix_ref, bf16[2,2048,512]{2,1,0:T(8,128)(2,1)} %bitcast.22), custom_call_target="tpu_custom_call" | custom-call | flops 3489660928 | bytes 6815744 | tf_op jit(solution)/shard_map/attend/pallas_call | solution.py:149
  159.9 4.6 %all-to-all-start.3 = ((bf16[8,384,384]{2,1,0:T(8,128)(2,1)}), bf16[8,384,384]{2,1,0:T(8,128)(2,1)}, u32[]{:S(2)}, u32[]{:S(2)}) async-start(bf16[8,384,384]{2,1,0:T(8,128)(2,1)} %copy-done.3), calls=%async_computation.3 | async-start | bytes 4718592 | tf_op jit(solution)/shard_map/all_to_all | solution.py:213
  164.4 6.4 %attend.4.rest_1_ = bf16[512,128]{1,0:T(8,128)(2,1)S(1)} custom-call(s32[1]{0:T(128)S(6)} %copy.13.where_ref, bf16[512,3072]{1,0:T(8,128)(2,1)S(1)} %norm.1.normed_ref, bf16[3072,384]{1,0:T(8,128)(2,1)} %bitcast.9.matrix_ref, bf16[2,2048,512]{2,1,0:T(8,128)(2,1)} %bitcast.23), custom_call_target="tpu_custom_call" | custom-call | flops 1744830464 | bytes 3407872 | tf_op jit(solution)/shard_map/attend/pallas_call | solution.py:149
  170.8 17.4 %collective-permute-start.2 = (bf16[512,256]{1,0:T(8,128)(2,1)S(1)}, bf16[512,256]{1,0:T(8,128)(2,1)S(1)}, u32[]{:S(2)}, u32[]{:S(2)}) collective-permute-start(bf16[512,256]{1,0:T(8,128)(2,1)S(1)} %attend.3.rest_0_), channel_id=1, source_target_pairs={{0,1},{1,0},{2,3},{3,2},{4,5},{5,4},{6,7},{7,6},{8,9},{9,8},{10,11... | collective-permute-start | bytes 786440 | tf_op jit(solution)/shard_map/ppermute | solution.py:204
  188.4 2.3 collective-permute-start.6
  190.6 1.6 collective-permute-start.10
  192.4 7.5 %collective-permute-done.2.rest_3_ = bf16[512,256]{1,0:T(8,128)(2,1)S(1)} collective-permute-done((bf16[512,256]{1,0:T(8,128)(2,1)S(1)}, bf16[512,256]{1,0:T(8,128)(2,1)S(1)}, u32[]{:S(2)}, u32[]{:S(2)}) %collective-permute-start.2) | collective-permute-done | bytes 262176 | tf_op jit(solution)/shard_map/ppermute | solution.py:204
  200.6 6.5 %attend.5.rest_2_ = bf16[512,128]{1,0:T(8,128)(2,1)S(1)} custom-call(s32[1]{0:T(128)S(6)} %copy.13.where_ref, bf16[512,3072]{1,0:T(8,128)(2,1)S(1)} %norm.1.normed_ref, bf16[3072,384]{1,0:T(8,128)(2,1)} %bitcast.10.matrix_ref, bf16[2,2048,512]{2,1,0:T(8,128)(2,1)} %bitcast.24), custom_call_target="tpu_custom_call" | custom-call | flops 1744830464 | bytes 3407872 | tf_op jit(solution)/shard_map/attend/pallas_call | solution.py:149
  207.2 5.3 %collective-permute-done.5.rest_6_ = bf16[512,256]{1,0:T(8,128)(2,1)} collective-permute-done((bf16[512,256]{1,0:T(8,128)(2,1)S(1)}, bf16[512,256]{1,0:T(8,128)(2,1)}, u32[]{:S(2)}, u32[]{:S(2)}) %collective-permute-start.5) | collective-permute-done | bytes 262176 | tf_op jit(solution)/shard_map/ppermute | solution.py:204
  212.5 1.5 collective-permute-start.11
  214.0 10.9 %collective-permute-start.7 = (bf16[512,128]{1,0:T(8,128)(2,1)S(1)}, bf16[512,128]{1,0:T(8,128)(2,1)S(1)}, u32[]{:S(2)}, u32[]{:S(2)}) collective-permute-start(bf16[512,128]{1,0:T(8,128)(2,1)S(1)} %attend.5.rest_2_), channel_id=1, source_target_pairs={{0,1},{1,0},{2,3},{3,2},{4,5},{5,4},{6,7},{7,6},{8,9},{9,8},{10,11... | collective-permute-start | bytes 393224 | tf_op jit(solution)/shard_map/ppermute | solution.py:204
  224.9 2.2 collective-permute-start.9
  227.2 3.6 %collective-permute-done.8.rest_7_ = bf16[512,128]{1,0:T(8,128)(2,1)} collective-permute-done((bf16[512,128]{1,0:T(8,128)(2,1)S(1)}, bf16[512,128]{1,0:T(8,128)(2,1)}, u32[]{:S(2)}, u32[]{:S(2)}) %collective-permute-start.8) | collective-permute-done | bytes 131104 | tf_op jit(solution)/shard_map/ppermute | solution.py:204
  230.7 5.9 %collective-permute-done.9.rest_8_ = bf16[512,128]{1,0:T(8,128)(2,1)S(1)} collective-permute-done((bf16[512,128]{1,0:T(8,128)(2,1)S(1)}, bf16[512,128]{1,0:T(8,128)(2,1)S(1)}, u32[]{:S(2)}, u32[]{:S(2)}) %collective-permute-start.9) | collective-permute-done | bytes 131104 | tf_op jit(solution)/shard_map/ppermute | solution.py:204
  236.7 3.5 %output.1 = bf16[512,768]{1,0:T(8,128)(2,1)S(1)} custom-call(bf16[512,768]{1,0:T(8,128)(2,1)S(1)} %bitcast.18, f32[1,768]{1,0:T(1,128)S(1)} %dynamic-slice_bitcast_fusion.gate_ref, bf16[512,256]{1,0:T(8,128)(2,1)S(1)} %attend.3.rest_0_, bf16[512,128]{1,0:T(8,128)(2,1)S(1)} %attend.4.rest_1_, bf16[512,128]{1,0:T(8,128)(2,1)S(1)} %attend.5.rest_2_, ...), custom_call_target="tpu_custom_call" | custom-call | flops 1610612736 | bytes 5242880 | tf_op jit(solution)/shard_map/output/pallas_call | solution.py:187
  240.2 12.3 %collective-permute-done.12 = bf16[512,768]{1,0:T(8,128)(2,1)S(1)} collective-permute-done((bf16[512,768]{1,0:T(8,128)(2,1)S(1)}, bf16[512,768]{1,0:T(8,128)(2,1)S(1)}, u32[]{:S(2)}, u32[]{:S(2)}) %collective-permute-start.12) | collective-permute-done | bytes 786464 | tf_op jit(solution)/shard_map/ppermute | solution.py:209
  (39 shorter events, 5.8 us)
Async XLA Ops:
  17.3 43.1 %all-to-all-start.1 = ((bf16[8,384,512]{2,1,0:T(8,128)(2,1)}), bf16[8,384,512]{2,1,0:T(8,128)(2,1)S(1)}, u32[]{:S(2)}, u32[]{:S(2)}) async-start(bf16[8,384,512]{2,1,0:T(8,128)(2,1)} %split_blocks.2), calls=%async_computation.1 | async-start | bytes 6291456 | tf_op jit(solution)/shard_map/all_to_all | solution.py:213
  22.5 90.7 %all-gather.3.cloned.1.call-start = ((), (), s32[]{:S(2)}) async-start(), calls=%async_computation.4 | async-start | bytes 3932160 | tf_op jit(solution)/shard_map/all_gather | solution.py:231
  32.3 2.2 copy-start
  34.5 1.4 copy-start.3
  35.9 1.4 copy-start.4
  60.4 61.3 %all-to-all-start = ((bf16[8,384,768]{2,1,0:T(8,128)(2,1)}), bf16[8,384,768]{2,1,0:T(8,128)(2,1)}, u32[]{:S(2)}, u32[]{:S(2)}) async-start(bf16[8,384,768]{2,1,0:T(8,128)(2,1)} %copy-done), calls=%async_computation | async-start | bytes 9437184 | tf_op jit(solution)/shard_map/all_to_all | solution.py:213
  65.0 5.9 %copy-start.9 = (f32[1,3,3072]{2,0,1:T(1,128)S(1)}, f32[1,3,3072]{2,0,1:T(1,128)}, u32[]{:S(2)}) copy-start(f32[1,3,3072]{2,0,1:T(1,128)} %param.7) | copy-start | bytes 110596
  66.7 55.0 %collective-permute-start = (bf16[768,512]{1,0:T(8,128)(2,1)}, bf16[768,512]{1,0:T(8,128)(2,1)}, u32[]{:S(2)}, u32[]{:S(2)}) collective-permute-start(bf16[768,512]{1,0:T(8,128)(2,1)} %get-tuple-element.40), channel_id=1, source_target_pairs={{0,1},{1,0},{2,3},{3,2},{4,5},{5,4},{6,7},{7,6},{8,9},{9,8},{10,11... | collective-permute-start | bytes 2359304 | tf_op jit(solution)/shard_map/ppermute | solution.py:204
  68.3 53.4 %collective-permute-start.1 = (bf16[768,512]{1,0:T(8,128)(2,1)}, bf16[768,512]{1,0:T(8,128)(2,1)}, u32[]{:S(2)}, u32[]{:S(2)}) collective-permute-start(bf16[768,512]{1,0:T(8,128)(2,1)} %get-tuple-element.39), channel_id=1, source_target_pairs={{0,2},{1,3},{2,0},{3,1},{4,6},{5,7},{6,4},{7,5},{8,10},{9,11},{10,... | collective-permute-start | bytes 2359304 | tf_op jit(solution)/shard_map/ppermute | solution.py:204
  121.7 38.1 %all-to-all-start.2 = ((bf16[8,384,384]{2,1,0:T(8,128)(2,1)}), bf16[8,384,384]{2,1,0:T(8,128)(2,1)}, u32[]{:S(2)}, u32[]{:S(2)}) async-start(bf16[8,384,384]{2,1,0:T(8,128)(2,1)} %copy-done.4), calls=%async_computation.2 | async-start | bytes 4718592 | tf_op jit(solution)/shard_map/all_to_all | solution.py:213
  126.1 21.9 %collective-permute-start.3 = (bf16[768,512]{1,0:T(8,128)(2,1)}, bf16[768,512]{1,0:T(8,128)(2,1)S(1)}, u32[]{:S(2)}, u32[]{:S(2)}) collective-permute-start(bf16[768,512]{1,0:T(8,128)(2,1)} %get-tuple-element.38), channel_id=1, source_target_pairs={{0,3},{1,2},{2,1},{3,0},{4,7},{5,6},{6,5},{7,4},{8,11},{9,10},{10,... | collective-permute-start | bytes 2359304 | tf_op jit(solution)/shard_map/ppermute | solution.py:204
  148.0 0.9 copy-start.5
  159.9 40.7 %all-to-all-start.3 = ((bf16[8,384,384]{2,1,0:T(8,128)(2,1)}), bf16[8,384,384]{2,1,0:T(8,128)(2,1)}, u32[]{:S(2)}, u32[]{:S(2)}) async-start(bf16[8,384,384]{2,1,0:T(8,128)(2,1)} %copy-done.3), calls=%async_computation.3 | async-start | bytes 4718592 | tf_op jit(solution)/shard_map/all_to_all | solution.py:213
  170.8 29.1 %collective-permute-start.2 = (bf16[512,256]{1,0:T(8,128)(2,1)S(1)}, bf16[512,256]{1,0:T(8,128)(2,1)S(1)}, u32[]{:S(2)}, u32[]{:S(2)}) collective-permute-start(bf16[512,256]{1,0:T(8,128)(2,1)S(1)} %attend.3.rest_0_), channel_id=1, source_target_pairs={{0,1},{1,0},{2,3},{3,2},{4,5},{5,4},{6,7},{7,6},{8,9},{9,8},{10,11... | collective-permute-start | bytes 786440 | tf_op jit(solution)/shard_map/ppermute | solution.py:204
  188.2 24.3 %collective-permute-start.5 = (bf16[512,256]{1,0:T(8,128)(2,1)S(1)}, bf16[512,256]{1,0:T(8,128)(2,1)}, u32[]{:S(2)}, u32[]{:S(2)}) collective-permute-start(bf16[512,256]{1,0:T(8,128)(2,1)S(1)} %attend.3.rest_0_), channel_id=1, source_target_pairs={{0,2},{1,3},{2,0},{3,1},{4,6},{5,7},{6,4},{7,5},{8,10},{9,11},{10,... | collective-permute-start | bytes 786440 | tf_op jit(solution)/shard_map/ppermute | solution.py:204
  188.4 24.1 %collective-permute-start.6 = (bf16[512,256]{1,0:T(8,128)(2,1)S(1)}, bf16[512,256]{1,0:T(8,128)(2,1)}, u32[]{:S(2)}, u32[]{:S(2)}) collective-permute-start(bf16[512,256]{1,0:T(8,128)(2,1)S(1)} %attend.3.rest_0_), channel_id=1, source_target_pairs={{0,3},{1,2},{2,1},{3,0},{4,7},{5,6},{6,5},{7,4},{8,11},{9,10},{10,... | collective-permute-start | bytes 786440 | tf_op jit(solution)/shard_map/ppermute | solution.py:204
  190.6 34.3 %collective-permute-start.10 = (bf16[512,128]{1,0:T(8,128)(2,1)S(1)}, bf16[512,128]{1,0:T(8,128)(2,1)}, u32[]{:S(2)}, u32[]{:S(2)}) collective-permute-start(bf16[512,128]{1,0:T(8,128)(2,1)S(1)} %attend.4.rest_1_), channel_id=1, source_target_pairs={{0,3},{1,2},{2,1},{3,0},{4,7},{5,6},{6,5},{7,4},{8,11},{9,10},{10,... | collective-permute-start | bytes 393224 | tf_op jit(solution)/shard_map/ppermute | solution.py:204
  192.2 35.0 %collective-permute-start.4 = (bf16[512,128]{1,0:T(8,128)(2,1)S(1)}, bf16[512,128]{1,0:T(8,128)(2,1)}, u32[]{:S(2)}, u32[]{:S(2)}) collective-permute-start(bf16[512,128]{1,0:T(8,128)(2,1)S(1)} %attend.4.rest_1_), channel_id=1, source_target_pairs={{0,1},{1,0},{2,3},{3,2},{4,5},{5,4},{6,7},{7,6},{8,9},{9,8},{10,11... | collective-permute-start | bytes 393224 | tf_op jit(solution)/shard_map/ppermute | solution.py:204
  199.9 0.7 copy-start.7
  200.6 30.1 %collective-permute-start.8 = (bf16[512,128]{1,0:T(8,128)(2,1)S(1)}, bf16[512,128]{1,0:T(8,128)(2,1)}, u32[]{:S(2)}, u32[]{:S(2)}) collective-permute-start(bf16[512,128]{1,0:T(8,128)(2,1)S(1)} %attend.4.rest_1_), channel_id=1, source_target_pairs={{0,2},{1,3},{2,0},{3,1},{4,6},{5,7},{6,4},{7,5},{8,10},{9,11},{10,... | collective-permute-start | bytes 393224 | tf_op jit(solution)/shard_map/ppermute | solution.py:204
  200.6 26.6 %slice-start = ((f32[1,3,3072]{2,0,1:T(1,128)}), f32[1,1,3072]{2,0,1:T(1,128)S(1)}, s32[]{:S(2)}) async-start(f32[1,3,3072]{2,0,1:T(1,128)} %param.7), calls=%async_computation.5 | async-start | bytes 24576 | tf_op jit(solution)/shard_map/slice | solution.py:270
  200.6 36.0 %copy-start.1 = (bf16[1,512,768]{2,1,0:T(8,128)(2,1)S(1)}, bf16[1,512,768]{2,1,0:T(8,128)(2,1)}, u32[]{:S(2)}) copy-start(bf16[1,512,768]{2,1,0:T(8,128)(2,1)} %param.8) | copy-start | bytes 2359300
  200.6 36.0 %copy-start.2 = (bf16[768,512]{1,0:T(8,128)(2,1)S(1)}, bf16[768,512]{1,0:T(8,128)(2,1)}, u32[]{:S(2)}) copy-start(bf16[768,512]{1,0:T(8,128)(2,1)} %get-tuple-element.37.rest_12_) | copy-start | bytes 2359300
  200.6 36.0 %copy-start.6 = (bf16[768,512]{1,0:T(8,128)(2,1)S(1)}, bf16[768,512]{1,0:T(8,128)(2,1)}, u32[]{:S(2)}) copy-start(bf16[768,512]{1,0:T(8,128)(2,1)} %copy-done.5) | copy-start | bytes 2359300
  200.6 36.0 %copy-start.8 = (bf16[512,256]{1,0:T(8,128)(2,1)S(1)}, bf16[512,256]{1,0:T(8,128)(2,1)}, u32[]{:S(2)}) copy-start(bf16[512,256]{1,0:T(8,128)(2,1)} %copy-done.7) | copy-start | bytes 786436
  212.5 18.3 %collective-permute-start.11 = (bf16[512,128]{1,0:T(8,128)(2,1)S(1)}, bf16[512,128]{1,0:T(8,128)(2,1)S(1)}, u32[]{:S(2)}, u32[]{:S(2)}) collective-permute-start(bf16[512,128]{1,0:T(8,128)(2,1)S(1)} %attend.5.rest_2_), channel_id=1, source_target_pairs={{0,3},{1,2},{2,1},{3,0},{4,7},{5,6},{6,5},{7,4},{8,11},{9,10},{10,... | collective-permute-start | bytes 393224 | tf_op jit(solution)/shard_map/ppermute | solution.py:204
  214.0 16.7 %collective-permute-start.7 = (bf16[512,128]{1,0:T(8,128)(2,1)S(1)}, bf16[512,128]{1,0:T(8,128)(2,1)S(1)}, u32[]{:S(2)}, u32[]{:S(2)}) collective-permute-start(bf16[512,128]{1,0:T(8,128)(2,1)S(1)} %attend.5.rest_2_), channel_id=1, source_target_pairs={{0,1},{1,0},{2,3},{3,2},{4,5},{5,4},{6,7},{7,6},{8,9},{9,8},{10,11... | collective-permute-start | bytes 393224 | tf_op jit(solution)/shard_map/ppermute | solution.py:204
  224.9 11.7 %collective-permute-start.9 = (bf16[512,128]{1,0:T(8,128)(2,1)S(1)}, bf16[512,128]{1,0:T(8,128)(2,1)S(1)}, u32[]{:S(2)}, u32[]{:S(2)}) collective-permute-start(bf16[512,128]{1,0:T(8,128)(2,1)S(1)} %attend.5.rest_2_), channel_id=1, source_target_pairs={{0,2},{1,3},{2,0},{3,1},{4,6},{5,7},{6,4},{7,5},{8,10},{9,11},{10,... | collective-permute-start | bytes 393224 | tf_op jit(solution)/shard_map/ppermute | solution.py:204
  240.2 12.4 %collective-permute-start.12 = (bf16[512,768]{1,0:T(8,128)(2,1)S(1)}, bf16[512,768]{1,0:T(8,128)(2,1)S(1)}, u32[]{:S(2)}, u32[]{:S(2)}) collective-permute-start(bf16[512,768]{1,0:T(8,128)(2,1)S(1)} %output.1), channel_id=1, source_target_pairs={{0,4},{4,8},{8,12},{12,16},{16,20},{20,24},{24,28},{28,0},{1,5},{5... | collective-permute-start | bytes 2359304 | tf_op jit(solution)/shard_map/ppermute | solution.py:209
Sparse Core Ops, SparseCore 0:
  24.9 88.2 all-gather.2

commit v15 on v12

--- a/solution.py
+++ b/solution.py
@@ -61,8 +61,11 @@
             pick[...], jnp.concatenate(chunks, axis=1), preferred_element_type=F32
         ).astype(BF16)
         for i in range(beside):
-            to = slice(first + i * depth_step, first + (i + 1) * depth_step)
-            for out, columns in zip(outs, plan):
+            begin = first + i * depth_step
+            for out, (start, stop, columns) in zip(outs, plan):
+                if not start <= begin < stop:
+                    continue
+                to = slice(begin - start, begin - start + depth_step)
                 for column, (kind, lane) in enumerate(columns):
                     at = (kinds.index(kind) * lanes + lane) * depth_step
                     out[0, to, column * HD : (column + 1) * HD] = sorted_rows[
@@ -73,9 +76,9 @@
 def split_blocks(rows, order, plan, lanes):
     depth = rows.shape[1] // (4 * lanes)
     depth_step = max(n for n in (16, 32, 64) if depth % n == 0 and n * 4 * lanes <= 256)
-    kinds = sorted({kind for columns in plan for kind, _ in columns})
+    kinds = sorted({kind for _, _, columns in plan for kind, _ in columns})
     blocks = order.shape[0]
-    shapes = [(blocks, depth, len(columns) * HD) for columns in plan]
+    shapes = [(blocks, stop - start, len(columns) * HD) for start, stop, columns in plan]
     return pl.pallas_call(
         functools.partial(split_kernel, lanes, plan, kinds, depth_step),
         grid_spec=pltpu.PrefetchScalarGridSpec(
@@ -166,42 +169,34 @@
             patch * heads * keys,
         ),
         name="attend",
-    )(where, normed, matrix, stale)
-
-
-def output_kernel(tp, chunks, inflow_ref, gate_ref, *rest):
-    attended, matrices, out_ref = rest[: tp * chunks], rest[tp * chunks : -1], rest[-1]
-    mixed = 0.0
-    for index in range(tp):
-        own = attended[index * chunks : (index + 1) * chunks]
-        left = jnp.concatenate([piece[...] for piece in own], axis=1)
-        mixed += turned(left, matrices[index][...])
-    out_ref[...] = (inflow_ref[...].astype(F32) + gate_ref[...] * mixed).astype(BF16)
-
-
-def output(inflow, gate, attended, matrices):
-    tp, chunks = len(attended), len(attended[0])
-    patch, share = inflow.shape
-    inner = matrices[0].shape[1]
-    arrays = [inflow, gate] + [piece for own in attended for piece in own] + matrices
-    return pl.pallas_call(
-        functools.partial(output_kernel, tp, chunks),
-        grid=(1,),
-        in_specs=[pl.BlockSpec(array.shape, lambda i: (0, 0)) for array in arrays],
-        out_specs=pl.BlockSpec(inflow.shape, lambda i: (0, 0)),
-        out_shape=jax.ShapeDtypeStruct(inflow.shape, BF16),
-        compiler_params=params(20),
-        cost_estimate=cost(2 * patch * share * inner * tp, 2 * inner * tp * (share + patch)),
+    )(where, normed, matrix, in_hbm(stale))
+
+
+def output_kernel(attended_ref, matrix_ref, out_ref):
+    out_ref[...] = turned(attended_ref[...], matrix_ref[...]).astype(BF16)
+
+
+def output(attended, matrix):
+    patch, inner = attended.shape
+    rows = matrix.shape[0]
+    step = 512 if rows % 512 == 0 else rows
+    return pl.pallas_call(
+        output_kernel,
+        grid=(rows // step,),
+        in_specs=[
+            pl.BlockSpec((patch, inner), lambda i: (0, 0)),
+            pl.BlockSpec((step, inner), lambda i: (i, 0)),
+        ],
+        out_specs=pl.BlockSpec((patch, step), lambda i: (0, i)),
+        out_shape=jax.ShapeDtypeStruct((patch, rows), BF16),
+        compiler_params=params(24),
+        cost_estimate=cost(2 * patch * rows * inner, 2 * rows * (inner + patch)),
         name="output",
-    )(*arrays)
+    )(attended, matrix)
 
 
 def after(block, earlier):
     return lax.optimization_barrier((block, earlier))[0]
-
-
-def swapped(block, axis, distance):
-    return lax.ppermute(block, axis, [(i, i ^ distance) for i in range(lax.axis_size(axis))])
 
 
 def handed_on(block):
@@ -230,42 +225,36 @@
     rows = rows.transpose(0, 1, 3, 2, 4).reshape(blocks, depth * lanes * kinds, HD)
     tokens = lax.all_gather(inflow[0], "tp", axis=1, tiled=True)
 
-    order = block_of(section_ids)
-    (to_out,) = split_blocks(rows, order, [[(3, head) for head in range(lanes)]], lanes)
-    half = max(1, lanes // 2)
-    groups = [tuple(range(half))] + [(head,) for head in range(half, lanes)]
-    plan = [[(kind, head) for head in group for kind in range(3)] for group in groups]
-    split = split_blocks(rows, after(order, to_out), plan, lanes)
-
     def waiting(block, *earlier):
         return functools.reduce(after, earlier, block)
 
-    to_out = relayed(to_out)
+    order = block_of(section_ids)
+    every = [(kind, head) for head in range(lanes) for kind in range(3)]
+    (pieces,) = split_blocks(rows, order, [(0, depth, every)], lanes)
+    part = depth * 2 // 3 // 16 * 16
+    out_columns = [(3, head) for head in range(lanes)]
+    out_plan = [(0, part, out_columns), (part, depth, out_columns)]
+    first, second = split_blocks(rows, after(order, pieces), out_plan, lanes)
+
+    matrix = relayed(pieces)
     normed = norm(tokens, modulation[0])
-    matrices = []
-    for distance in range(tp):
-        held = lax.dynamic_slice_in_dim(to_out, (rank ^ distance) * share, share, 0)
-        matrices.append(swapped(held, "tp", distance) if distance else held)
-
-    waits, parts = [(), (normed, *matrices[1:3]), tuple(matrices[3:])], []
-    owns, final = [], len(groups) - 1
-    for index, group in enumerate(groups):
-        if index > 1:
-            waits[index] += (owns[index - 2], moved)
-        pieces = waiting(split[index], *(waits[index] if index < len(waits) else ()))
-        moved = relayed(pieces)
-        if index > 0:
-            owns.append(attend(normed, matrix, patch_index, stale_cache[0], groups[index - 1], 0))
-        matrix = moved
-        if index < final:
-            continue
-        parts = [[swapped(own, "tp", distance) for distance in range(1, tp)] for own in owns]
-        ready = waiting(normed, *[part for own in parts[:1] for part in own], *owns[1:])
-        owns.append(attend(ready, matrix, patch_index, stale_cache[0], group, 0))
-        parts.append([swapped(owns[-1], "tp", distance) for distance in range(1, tp)])
-    attended = [owns] + [[own[distance] for own in parts] for distance in range(tp - 1)]
-    gate = lax.dynamic_slice_in_dim(modulation[0, 2], rank * share, share, 0)[None]
-    return handed_on(output(inflow[0], gate, attended, matrices))[None]
+    to_out = relayed(after(first, matrix))
+    own = attend(normed, matrix, patch_index, stale_cache[0], tuple(range(lanes)), 0)
+    rest = relayed(waiting(second, to_out, own))
+
+    per = sections // tp
+    gate = lax.dynamic_slice_in_dim(modulation[0, 2], rank * share, share, 0)
+
+    def result(matrix, start, stop):
+        columns = [slice(r * depth + start, r * depth + stop) for r in range(per)]
+        mixed = lax.psum_scatter(output(own, matrix), "tp", scatter_dimension=1, tiled=True)
+        patch = jnp.concatenate([inflow[0][:, cols] for cols in columns], axis=1)
+        gates = jnp.concatenate([gate[cols] for cols in columns])
+        made = handed_on((patch.astype(F32) + gates * mixed.astype(F32)).astype(BF16))
+        return jnp.split(made, per, axis=1)
+
+    results = zip(result(to_out, 0, part), result(rest, part, depth))
+    return jnp.concatenate([piece for both in results for piece in both], axis=1)[None]
 
 
 def solution(mesh):

time: 267 us -> 254 us (0.951)
  starting transfers between devices: 55.6 us -> 9.14 us
  waiting for transfers between devices: 129 us -> 155 us
  blocking collectives: 0 us -> 17.8 us
  local copies, waits for them, and re-layouts: 17.2 us -> 7.36 us
  other arithmetic: 0.77 us -> 3.97 us
  Pallas kernels: 49.6 us -> 46.6 us
    all_to_all x4 -> x2, waiting for transfers between devices: 23.2 us -> 96 us  [relayed(): lax.all_to_all(pieces, 'section', split_axis=0, concat_axis=0, tiled=True)]
    reduce_scatter x0 -> x2, waiting for transfers between devices: none -> 51.2 us  [result(): lax.psum_scatter(output(own, matrix), 'tp', scatter_dimension=1, tiled=True)]
    ppermute x12 -> x0, waiting for transfers between devices: 50.6 us -> none  [swapped(): lax.ppermute(block, axis, [(i, i ^ distance) for i in range(lax.axis_size...]
    all_gather x1, waiting for transfers between devices: 42.2 us -> 0.02 us  [local(): tokens = lax.all_gather(inflow[0], 'tp', axis=1, tiled=True)]
    ppermute x12 -> x0, starting transfers between devices: 36.8 us -> none  [swapped(): lax.ppermute(block, axis, [(i, i ^ distance) for i in range(lax.axis_size...]
    all_to_all x0 -> x1, blocking collectives: none -> 17.8 us  [relayed(): lax.all_to_all(pieces, 'section', split_axis=0, concat_axis=0, tiled=True)]
    all_to_all x4 -> x2, starting transfers between devices: 18.7 us -> 8.91 us  [relayed(): lax.all_to_all(pieces, 'section', split_axis=0, concat_axis=0, tiled=True)]
    unnamed x36 -> x13, local copies, waits for them, and re-layouts: 15.4 us -> 7.22 us
  transfers between devices with their start and end apart: 18 -> 7, of which waited for: 10 -> 5; matrix products, arithmetic and copies ran while one was open for 1% -> 1% of each run, Pallas kernels for 14% -> 14%
where the time goes in v15:
time: 254 us; the launch traced here: 253 us
  waiting for transfers between devices  155 us (61%)
  Pallas kernels  46.6 us (18%)
  blocking collectives  17.8 us (7%)
  between operations  14 us (6%)
  starting transfers between devices  9.14 us (4%)
  local copies, waits for them, and re-layouts  7.36 us (3%)
  other arithmetic  3.97 us (2%)
    all_to_all x2, waiting for transfers between devices, relayed(): lax.all_to_all(pieces, 'section', split_axis=0, concat_axis=0, tiled=True)  96 us
    reduce_scatter x2, waiting for transfers between devices, result(): lax.psum_scatter(output(own, matrix), 'tp', scatter_dimension=1, tiled=True)  51.2 us
    pallas_call x1, Pallas kernels, attend(): pl.pallas_call(attend_kernel, grid_spec=pltpu.PrefetchScalarGridSpec(num_...  19.8 us
    all_to_all x1, blocking collectives, relayed(): lax.all_to_all(pieces, 'section', split_axis=0, concat_axis=0, tiled=True)  17.8 us
    pallas_call x2, Pallas kernels, split_blocks(): pl.pallas_call(functools.partial(split_kernel, lanes, plan, kinds, depth_...  17.7 us
    all_to_all x2, starting transfers between devices, relayed(): lax.all_to_all(pieces, 'section', split_axis=0, concat_axis=0, tiled=True)  8.91 us
    unnamed x13, local copies, waits for them, and re-layouts  7.22 us
    ppermute x2, waiting for transfers between devices, handed_on(): lax.ppermute(block, 'section', [(i, (i + 1) % sections) for i in range(se...  6.69 us
  transfers between devices with their start and end apart: 7, of which 5 were waited for; matrix products, arithmetic and copies ran while one was open for 1% of the time, Pallas kernels for 14%

profile of v15, /device:TPU:0, one launch (start us, length us, event | category | flops | bytes accessed | tf_op | source)
XLA Modules:
  0.0 253.4 jit_solution(3844356514593845201)
XLA Ops:
  6.5 0.8 select_reduce_fusion.order_ref
  7.3 9.1 %split_blocks.2 = bf16[8,384,1536]{2,1,0:T(8,128)(2,1)S(1)} custom-call(s32[8]{0:T(128)S(1)} %select_reduce_fusion.order_ref, bf16[8,6144,128]{2,1,0:T(8,128)(2,1)} %bitcast.25), custom_call_target="tpu_custom_call" | custom-call | bytes 18874368 | tf_op jit(solution)/shard_map/split_blocks/pallas_call | solution.py:82
  16.4 3.7 %copy-done = bf16[8,384,1536]{2,1,0:T(8,128)(2,1)} copy-done((bf16[8,384,1536]{2,1,0:T(8,128)(2,1)}, bf16[8,384,1536]{2,1,0:T(8,128)(2,1)S(1)}, u32[]{:S(2)}) %copy-start) | copy-done | bytes 9437208
  20.1 5.2 %all-to-all-start = ((bf16[8,384,1536]{2,1,0:T(8,128)(2,1)}), bf16[8,384,1536]{2,1,0:T(8,128)(2,1)}, u32[]{:S(2)}, u32[]{:S(2)}) async-start(bf16[8,384,1536]{2,1,0:T(8,128)(2,1)} %copy-done), calls=%async_computation | async-start | bytes 18874368 | tf_op jit(solution)/shard_map/all_to_all | solution.py:208
  25.2 0.0 all-gather.3.cloned.1.call-start
  25.3 0.7 all-gather.3.cloned.1.call-update
  26.0 8.6 %split_blocks.3 = (bf16[8,256,512]{2,1,0:T(8,128)(2,1)S(1)}, bf16[8,128,512]{2,1,0:T(8,128)(2,1)S(1)}) custom-call(s32[8]{0:T(128)S(1)} %select_reduce_fusion.order_ref, bf16[8,6144,128]{2,1,0:T(8,128)(2,1)} %bitcast.26), custom_call_target="tpu_custom_call" | custom-call | bytes 18874368 | tf_op jit(solution)/shard_map/split_blocks/pallas_call | solution.py:82
  34.6 1.3 copy-done.1
  35.9 1.0 copy-done.2
  37.0 94.1 %all-to-all-done = bf16[8,384,1536]{2,1,0:T(8,128)(2,1)} async-done(((bf16[8,384,1536]{2,1,0:T(8,128)(2,1)}), bf16[8,384,1536]{2,1,0:T(8,128)(2,1)}, u32[]{:S(2)}, u32[]{:S(2)}) %all-to-all-start) | async-done | bytes 9437216 | tf_op jit(solution)/shard_map/all_to_all | solution.py:208
  131.1 3.7 %all-to-all-start.1 = ((bf16[8,256,512]{2,1,0:T(8,128)(2,1)}), bf16[8,256,512]{2,1,0:T(8,128)(2,1)S(1)}, u32[]{:S(2)}, u32[]{:S(2)}) async-start(bf16[8,256,512]{2,1,0:T(8,128)(2,1)} %copy-done.1), calls=%async_computation.1 | async-start | bytes 4194304 | tf_op jit(solution)/shard_map/all_to_all | solution.py:208
  134.9 0.0 reduce-scatter.3.cloned.1.call-start
  135.6 0.0 all-gather.3.cloned.1.call-done
  135.6 4.1 %norm.1.normed_ref = bf16[512,3072]{1,0:T(8,128)(2,1)S(1)} custom-call(bf16[512,3072]{1,0:T(8,128)(2,1)} %bitcast.27, f32[3,3072]{1,0:T(4,128)S(1)} %bitcast.24), custom_call_target="tpu_custom_call" | custom-call | flops 15728640 | bytes 6291456 | tf_op jit(solution)/shard_map/norm/pallas_call | solution.py:112
  139.8 19.8 %attend.1.attended_ref = bf16[512,512]{1,0:T(8,128)(2,1)S(1)} custom-call(s32[1]{0:T(128)S(6)} %copy.12.where_ref, bf16[512,3072]{1,0:T(8,128)(2,1)S(1)} %norm.1.normed_ref, bf16[3072,1536]{1,0:T(8,128)(2,1)} %bitcast.7.matrix_ref, bf16[2,2048,512]{2,1,0:T(8,128)(2,1)} %bitcast.32), custom_call_target="tpu_custom_call" | custom-call | flops 6979321856 | bytes 13631488 | tf_op jit(solution)/shard_map/attend/pallas_call | solution.py:152
  159.6 1.8 all-to-all-done.1
  161.5 3.1 %output.2 = bf16[512,2048]{1,0:T(8,128)(2,1)} custom-call(bf16[512,512]{1,0:T(8,128)(2,1)S(1)} %attend.1.attended_ref, bf16[2048,512]{1,0:T(8,128)(2,1)S(1)} %bitcast.22), custom_call_target="tpu_custom_call" | custom-call | flops 1073741824 | bytes 4194304 | tf_op jit(solution)/shard_map/output/pallas_call | solution.py:183
  164.6 0.0 reduce-scatter.3.cloned.1.call-update
  164.6 0.0 reduce-scatter.5.cloned.1.call-start
  164.7 1.1 copy-done.3
  165.8 17.8 %all_to_all.15 = bf16[8,128,512]{2,1,0:T(8,128)(2,1)S(1)} all-to-all(bf16[8,128,512]{2,1,0:T(8,128)(2,1)S(1)} %copy-done.3), channel_id=1, replica_groups=mesh['section'=8,'tp'=4] {'section'}, dimensions={0} | all-to-all | bytes 2097152 | tf_op jit(solution)/shard_map/all_to_all | solution.py:208
  183.6 1.8 output.3
  185.4 0.0 reduce-scatter.5.cloned.1.call-update
  185.6 23.6 %reduce-scatter.3.cloned.1.call-done = bf16[512,512]{1,0:T(8,128)(2,1)} async-done(((bf16[512,2048]{1,0:T(8,128)(2,1)}), bf16[512,512]{1,0:T(8,128)(2,1)}) %reduce-scatter.3.cloned.1.call-update) | async-done | bytes 524304 | tf_op jit(solution)/shard_map/reduce_scatter | solution.py:250
  209.2 1.2 add_convert_fusion
  210.4 0.1 collective-permute-start
  210.5 27.6 %reduce-scatter.5.cloned.1.call-done = bf16[512,256]{1,0:T(8,128)(2,1)} async-done(((bf16[512,1024]{1,0:T(8,128)(2,1)}), bf16[512,256]{1,0:T(8,128)(2,1)}) %reduce-scatter.5.cloned.1.call-update) | async-done | bytes 262160 | tf_op jit(solution)/shard_map/reduce_scatter | solution.py:250
  238.1 1.0 add_convert_fusion.1
  239.1 0.1 collective-permute-start.1
  239.2 6.7 %collective-permute-done.1 = bf16[512,256]{1,0:T(8,128)(2,1)S(1)} collective-permute-done((bf16[512,256]{1,0:T(8,128)(2,1)S(1)}, bf16[512,256]{1,0:T(8,128)(2,1)S(1)}, u32[]{:S(2)}, u32[]{:S(2)}) %collective-permute-start.1) | collective-permute-done | bytes 262176 | tf_op jit(solution)/shard_map/ppermute | solution.py:204
  245.9 0.0 collective-permute-done
  246.0 1.0 maximum_bitcast_fusion
  (18 shorter events, 0.2 us)
Async XLA Ops:
  16.4 3.7 %copy-start = (bf16[8,384,1536]{2,1,0:T(8,128)(2,1)}, bf16[8,384,1536]{2,1,0:T(8,128)(2,1)S(1)}, u32[]{:S(2)}) copy-start(bf16[8,384,1536]{2,1,0:T(8,128)(2,1)S(1)} %split_blocks.2) | copy-start | bytes 28311556
  20.1 111.1 %all-to-all-start = ((bf16[8,384,1536]{2,1,0:T(8,128)(2,1)}), bf16[8,384,1536]{2,1,0:T(8,128)(2,1)}, u32[]{:S(2)}, u32[]{:S(2)}) async-start(bf16[8,384,1536]{2,1,0:T(8,128)(2,1)} %copy-done), calls=%async_computation | async-start | bytes 18874368 | tf_op jit(solution)/shard_map/all_to_all | solution.py:208
  25.2 110.4 %all-gather.3.cloned.1.call-start = ((), (), s32[]{:S(2)}) async-start(), calls=%async_computation.7 | async-start | bytes 3932160 | tf_op jit(solution)/shard_map/all_gather | solution.py:226
  34.6 1.4 copy-start.1
  35.9 1.0 copy-start.2
  131.1 3.8 %copy-start.5 = (f32[1,3,3072]{2,0,1:T(1,128)S(1)}, f32[1,3,3072]{2,0,1:T(1,128)}, u32[]{:S(2)}) copy-start(f32[1,3,3072]{2,0,1:T(1,128)} %param.7) | copy-start | bytes 110596
  131.1 30.3 %all-to-all-start.1 = ((bf16[8,256,512]{2,1,0:T(8,128)(2,1)}), bf16[8,256,512]{2,1,0:T(8,128)(2,1)S(1)}, u32[]{:S(2)}, u32[]{:S(2)}) async-start(bf16[8,256,512]{2,1,0:T(8,128)(2,1)} %copy-done.1), calls=%async_computation.1 | async-start | bytes 4194304 | tf_op jit(solution)/shard_map/all_to_all | solution.py:208
  134.9 74.3 %reduce-scatter.3.cloned.1.call-start = ((), (), s32[]{:S(2)}) async-start(), calls=%async_computation.5 | async-start | bytes 2621440 | tf_op jit(solution)/shard_map/reduce_scatter | solution.py:250
  164.6 1.2 copy-start.3
  164.6 73.5 %reduce-scatter.5.cloned.1.call-start = ((), (), s32[]{:S(2)}) async-start(), calls=%async_computation.6 | async-start | bytes 1310720 | tf_op jit(solution)/shard_map/reduce_scatter | solution.py:250
  183.6 1.9 copy-start.4
  210.4 35.5 %collective-permute-start = (bf16[512,512]{1,0:T(8,128)(2,1)S(1)}, bf16[512,512]{1,0:T(8,128)(2,1)S(1)}, u32[]{:S(2)}, u32[]{:S(2)}) collective-permute-start(bf16[512,512]{1,0:T(8,128)(2,1)S(1)} %add_convert_fusion), channel_id=1, source_target_pairs={{0,4},{4,8},{8,12},{12,16},{16,20},{20,24},{24,28},{28,0},{1,5},{5... | collective-permute-start | bytes 1572872 | tf_op jit(solution)/shard_map/ppermute | solution.py:204
  239.1 6.7 %collective-permute-start.1 = (bf16[512,256]{1,0:T(8,128)(2,1)S(1)}, bf16[512,256]{1,0:T(8,128)(2,1)S(1)}, u32[]{:S(2)}, u32[]{:S(2)}) collective-permute-start(bf16[512,256]{1,0:T(8,128)(2,1)S(1)} %add_convert_fusion.1), channel_id=1, source_target_pairs={{0,4},{4,8},{8,12},{12,16},{16,20},{20,24},{24,28},{28,0},{1,5},{5... | collective-permute-start | bytes 786440 | tf_op jit(solution)/shard_map/ppermute | solution.py:204
Sparse Core Ops, SparseCore 0:
  27.6 66.4 all-gather.2
  164.8 44.4 reduce-scatter.2
  211.6 26.4 reduce-scatter.4

commit v16 on v15

--- a/solution.py
+++ b/solution.py
@@ -90,7 +90,7 @@
                 pltpu.VMEM((len(kinds) * lanes * depth_step, depth_step * 4 * lanes), BF16)
             ],
         ),
-        out_shape=[jax.ShapeDtypeStruct(shape, BF16) for shape in shapes],
+        out_shape=[pltpu.HBM(shape, BF16) for shape in shapes],
         compiler_params=params(16),
         cost_estimate=cost(0, 3 * blocks * rows.shape[1] * HD),
         name="split_blocks",
@@ -231,14 +231,14 @@
     order = block_of(section_ids)
     every = [(kind, head) for head in range(lanes) for kind in range(3)]
     (pieces,) = split_blocks(rows, order, [(0, depth, every)], lanes)
-    part = depth * 2 // 3 // 16 * 16
+    part = depth // 3 // 16 * 16
     out_columns = [(3, head) for head in range(lanes)]
     out_plan = [(0, part, out_columns), (part, depth, out_columns)]
     first, second = split_blocks(rows, after(order, pieces), out_plan, lanes)
 
     matrix = relayed(pieces)
     normed = norm(tokens, modulation[0])
-    to_out = relayed(after(first, matrix))
+    to_out = relayed(waiting(first, matrix, normed))
     own = attend(normed, matrix, patch_index, stale_cache[0], tuple(range(lanes)), 0)
     rest = relayed(waiting(second, to_out, own))
 

time: 254 us -> 280 us (1.10)
  blocking collectives: 17.8 us -> 30.7 us
  waiting for transfers between devices: 155 us -> 167 us
  Pallas kernels: 46.6 us -> 51.1 us
  local copies, waits for them, and re-layouts: 7.36 us -> 3.71 us
    all_to_all x2, waiting for transfers between devices: 96 us -> 31.2 us  [relayed(): lax.all_to_all(pieces, 'section', split_axis=0, concat_axis=0, tiled=True)]
    all_gather x1, waiting for transfers between devices: 0.02 us -> 58.2 us  [local(): tokens = lax.all_gather(inflow[0], 'tp', axis=1, tiled=True)]
    reduce_scatter x2, waiting for transfers between devices: 51.2 us -> 69.7 us  [result(): lax.psum_scatter(output(own, matrix), 'tp', scatter_dimension=1, tiled=True)]
    all_to_all x1, blocking collectives: 17.8 us -> 30.7 us  [relayed(): lax.all_to_all(pieces, 'section', split_axis=0, concat_axis=0, tiled=True)]
    pallas_call x2, Pallas kernels: 17.7 us -> 22.2 us  [split_blocks(): pl.pallas_call(functools.partial(split_kernel, lanes, plan, kinds, depth_...]
    unnamed x13 -> x9, local copies, waits for them, and re-layouts: 7.22 us -> 3.57 us
  transfers between devices with their start and end apart: 7 -> 7, of which waited for: 5 -> 5; matrix products, arithmetic and copies ran while one was open for 1% -> 1% of each run, Pallas kernels for 14% -> 13%
where the time goes in v16:
time: 280 us; the launch traced here: 279 us
  waiting for transfers between devices  167 us (60%)
  Pallas kernels  51.1 us (18%)
  blocking collectives  30.7 us (11%)
  between operations  13.9 us (5%)
  starting transfers between devices  8.96 us (3%)
  other arithmetic  3.97 us (1%)
  local copies, waits for them, and re-layouts  3.71 us (1%)
    reduce_scatter x2, waiting for transfers between devices, result(): lax.psum_scatter(output(own, matrix), 'tp', scatter_dimension=1, tiled=True)  69.7 us
    all_gather x1, waiting for transfers between devices, local(): tokens = lax.all_gather(inflow[0], 'tp', axis=1, tiled=True)  58.2 us
    all_to_all x2, waiting for transfers between devices, relayed(): lax.all_to_all(pieces, 'section', split_axis=0, concat_axis=0, tiled=True)  31.2 us
    all_to_all x1, blocking collectives, relayed(): lax.all_to_all(pieces, 'section', split_axis=0, concat_axis=0, tiled=True)  30.7 us
    pallas_call x2, Pallas kernels, split_blocks(): pl.pallas_call(functools.partial(split_kernel, lanes, plan, kinds, depth_...  22.2 us
    pallas_call x1, Pallas kernels, attend(): pl.pallas_call(attend_kernel, grid_spec=pltpu.PrefetchScalarGridSpec(num_...  19.8 us
    all_to_all x2, starting transfers between devices, relayed(): lax.all_to_all(pieces, 'section', split_axis=0, concat_axis=0, tiled=True)  8.73 us
    ppermute x2, waiting for transfers between devices, handed_on(): lax.ppermute(block, 'section', [(i, (i + 1) % sections) for i in range(se...  6.69 us
  transfers between devices with their start and end apart: 7, of which 5 were waited for; matrix products, arithmetic and copies ran while one was open for 1% of the time, Pallas kernels for 13%

profile of v16, /device:TPU:0, one launch (start us, length us, event | category | flops | bytes accessed | tf_op | source)
XLA Modules:
  0.0 279.0 jit_solution(2273142970572430687)
XLA Ops:
  6.5 0.8 select_reduce_fusion.order_ref
  7.3 12.3 %split_blocks.2 = bf16[8,384,1536]{2,1,0:T(8,128)(2,1)} custom-call(s32[8]{0:T(128)S(1)} %select_reduce_fusion.order_ref, bf16[8,6144,128]{2,1,0:T(8,128)(2,1)} %bitcast.25), custom_call_target="tpu_custom_call" | custom-call | bytes 18874368 | tf_op jit(solution)/shard_map/split_blocks/pallas_call | solution.py:82
  19.6 5.2 %all-to-all-start = ((bf16[8,384,1536]{2,1,0:T(8,128)(2,1)}), bf16[8,384,1536]{2,1,0:T(8,128)(2,1)}, u32[]{:S(2)}, u32[]{:S(2)}) async-start(bf16[8,384,1536]{2,1,0:T(8,128)(2,1)} %split_blocks.2), calls=%async_computation | async-start | bytes 18874368 | tf_op jit(solution)/shard_map/all_to_all | solution.py:208
  24.8 0.0 all-gather.3.cloned.1.call-start
  24.9 0.7 all-gather.3.cloned.1.call-update
  25.6 0.0 copy-start.3
  25.6 9.9 %split_blocks.3 = (bf16[8,128,512]{2,1,0:T(8,128)(2,1)}, bf16[8,256,512]{2,1,0:T(8,128)(2,1)}) custom-call(s32[8]{0:T(128)S(1)} %select_reduce_fusion.order_ref, bf16[8,6144,128]{2,1,0:T(8,128)(2,1)} %bitcast.26), custom_call_target="tpu_custom_call" | custom-call | bytes 18874368 | tf_op jit(solution)/shard_map/split_blocks/pallas_call | solution.py:82
  35.4 58.2 %all-gather.3.cloned.1.call-done = bf16[1,512,3072]{2,1,0:T(8,128)(2,1)} async-done(((bf16[1,512,768]{2,1,0:T(8,128)(2,1)}), bf16[1,512,3072]{2,1,0:T(8,128)(2,1)}) %all-gather.3.cloned.1.call-update) | async-done | bytes 3145744 | tf_op jit(solution)/shard_map/all_gather | solution.py:226
  93.7 4.1 %norm.1.normed_ref = bf16[512,3072]{1,0:T(8,128)(2,1)S(1)} custom-call(bf16[512,3072]{1,0:T(8,128)(2,1)} %bitcast.27, f32[3,3072]{1,0:T(4,128)S(1)} %bitcast.24), custom_call_target="tpu_custom_call" | custom-call | flops 15728640 | bytes 6291456 | tf_op jit(solution)/shard_map/norm/pallas_call | solution.py:112
  97.8 1.7 copy-done
  99.5 31.2 %all-to-all-done = bf16[8,384,1536]{2,1,0:T(8,128)(2,1)} async-done(((bf16[8,384,1536]{2,1,0:T(8,128)(2,1)}), bf16[8,384,1536]{2,1,0:T(8,128)(2,1)}, u32[]{:S(2)}, u32[]{:S(2)}) %all-to-all-start) | async-done | bytes 9437216 | tf_op jit(solution)/shard_map/all_to_all | solution.py:208
  130.7 3.6 %all-to-all-start.1 = ((bf16[8,128,512]{2,1,0:T(8,128)(2,1)}), bf16[8,128,512]{2,1,0:T(8,128)(2,1)S(1)}, u32[]{:S(2)}, u32[]{:S(2)}) async-start(bf16[8,128,512]{2,1,0:T(8,128)(2,1)} %get-tuple-element.15), calls=%async_computation.1 | async-start | bytes 2097152 | tf_op jit(solution)/shard_map/all_to_all | solution.py:208
  134.3 0.0 reduce-scatter.5.cloned.1.call-start
  135.0 1.9 copy-done.1
  136.9 19.8 %attend.1.attended_ref = bf16[512,512]{1,0:T(8,128)(2,1)S(1)} custom-call(s32[1]{0:T(128)S(6)} %copy.12.where_ref, bf16[512,3072]{1,0:T(8,128)(2,1)S(1)} %copy-done.1, bf16[3072,1536]{1,0:T(8,128)(2,1)} %bitcast.7.matrix_ref, bf16[2,2048,512]{2,1,0:T(8,128)(2,1)} %bitcast.32), custom_call_target="tpu_custom_call" | custom-call | flops 6979321856 | bytes 13631488 | tf_op jit(solution)/shard_map/attend/pallas_call | solution.py:152
  156.7 0.0 all-to-all-done.1
  156.7 30.7 %all_to_all.15 = bf16[8,256,512]{2,1,0:T(8,128)(2,1)S(1)} all-to-all(bf16[8,256,512]{2,1,0:T(8,128)(2,1)} %get-tuple-element.18), channel_id=1, replica_groups=mesh['section'=8,'tp'=4] {'section'}, dimensions={0} | all-to-all | bytes 4194304 | tf_op jit(solution)/shard_map/all_to_all | solution.py:208
  187.4 3.2 %output.3 = bf16[512,2048]{1,0:T(8,128)(2,1)} custom-call(bf16[512,512]{1,0:T(8,128)(2,1)S(1)} %attend.1.attended_ref, bf16[2048,512]{1,0:T(8,128)(2,1)S(1)} %bitcast.22), custom_call_target="tpu_custom_call" | custom-call | flops 1073741824 | bytes 4194304 | tf_op jit(solution)/shard_map/output/pallas_call | solution.py:183
  190.6 0.0 reduce-scatter.5.cloned.1.call-update
  190.6 0.0 copy-start.2
  190.6 0.0 reduce-scatter.3.cloned.1.call-start
  190.7 1.8 output.2
  192.5 0.0 reduce-scatter.3.cloned.1.call-update
  192.7 42.1 %reduce-scatter.5.cloned.1.call-done = bf16[512,512]{1,0:T(8,128)(2,1)} async-done(((bf16[512,2048]{1,0:T(8,128)(2,1)}), bf16[512,512]{1,0:T(8,128)(2,1)}) %reduce-scatter.5.cloned.1.call-update) | async-done | bytes 524304 | tf_op jit(solution)/shard_map/reduce_scatter | solution.py:250
  234.8 1.2 add_convert_fusion
  236.0 0.1 collective-permute-start.1
  236.0 27.6 %reduce-scatter.3.cloned.1.call-done = bf16[512,256]{1,0:T(8,128)(2,1)} async-done(((bf16[512,1024]{1,0:T(8,128)(2,1)}), bf16[512,256]{1,0:T(8,128)(2,1)}) %reduce-scatter.3.cloned.1.call-update) | async-done | bytes 262160 | tf_op jit(solution)/shard_map/reduce_scatter | solution.py:250
  263.7 1.0 add_convert_fusion.1
  264.7 0.1 collective-permute-start
  264.8 6.7 %collective-permute-done = bf16[512,256]{1,0:T(8,128)(2,1)S(1)} collective-permute-done((bf16[512,256]{1,0:T(8,128)(2,1)S(1)}, bf16[512,256]{1,0:T(8,128)(2,1)S(1)}, u32[]{:S(2)}, u32[]{:S(2)}) %collective-permute-start) | collective-permute-done | bytes 262176 | tf_op jit(solution)/shard_map/ppermute | solution.py:204
  271.5 0.0 collective-permute-done.1
  271.5 1.0 maximum_bitcast_fusion
  (14 shorter events, 0.2 us)
Async XLA Ops:
  19.6 111.1 %all-to-all-start = ((bf16[8,384,1536]{2,1,0:T(8,128)(2,1)}), bf16[8,384,1536]{2,1,0:T(8,128)(2,1)}, u32[]{:S(2)}, u32[]{:S(2)}) async-start(bf16[8,384,1536]{2,1,0:T(8,128)(2,1)} %split_blocks.2), calls=%async_computation | async-start | bytes 18874368 | tf_op jit(solution)/shard_map/all_to_all | solution.py:208
  24.8 68.9 %all-gather.3.cloned.1.call-start = ((), (), s32[]{:S(2)}) async-start(), calls=%async_computation.7 | async-start | bytes 3932160 | tf_op jit(solution)/shard_map/all_gather | solution.py:226
  25.6 9.9 %copy-start.3 = (f32[1,3,3072]{2,0,1:T(1,128)S(1)}, f32[1,3,3072]{2,0,1:T(1,128)}, u32[]{:S(2)}) copy-start(f32[1,3,3072]{2,0,1:T(1,128)} %param.7) | copy-start | bytes 110596
  97.8 1.7 copy-start
  130.7 26.0 %all-to-all-start.1 = ((bf16[8,128,512]{2,1,0:T(8,128)(2,1)}), bf16[8,128,512]{2,1,0:T(8,128)(2,1)S(1)}, u32[]{:S(2)}, u32[]{:S(2)}) async-start(bf16[8,128,512]{2,1,0:T(8,128)(2,1)} %get-tuple-element.15), calls=%async_computation.1 | async-start | bytes 2097152 | tf_op jit(solution)/shard_map/all_to_all | solution.py:208
  134.3 100.5 %reduce-scatter.5.cloned.1.call-start = ((), (), s32[]{:S(2)}) async-start(), calls=%async_computation.6 | async-start | bytes 2621440 | tf_op jit(solution)/shard_map/reduce_scatter | solution.py:250
  135.0 1.9 copy-start.1
  190.6 2.0 copy-start.2
  190.6 73.0 %reduce-scatter.3.cloned.1.call-start = ((), (), s32[]{:S(2)}) async-start(), calls=%async_computation.5 | async-start | bytes 1310720 | tf_op jit(solution)/shard_map/reduce_scatter | solution.py:250
  236.0 35.5 %collective-permute-start.1 = (bf16[512,512]{1,0:T(8,128)(2,1)S(1)}, bf16[512,512]{1,0:T(8,128)(2,1)S(1)}, u32[]{:S(2)}, u32[]{:S(2)}) collective-permute-start(bf16[512,512]{1,0:T(8,128)(2,1)S(1)} %add_convert_fusion), channel_id=1, source_target_pairs={{0,4},{4,8},{8,12},{12,16},{16,20},{20,24},{24,28},{28,0},{1,5},{5... | collective-permute-start | bytes 1572872 | tf_op jit(solution)/shard_map/ppermute | solution.py:204
  264.7 6.7 %collective-permute-start = (bf16[512,256]{1,0:T(8,128)(2,1)S(1)}, bf16[512,256]{1,0:T(8,128)(2,1)S(1)}, u32[]{:S(2)}, u32[]{:S(2)}) collective-permute-start(bf16[512,256]{1,0:T(8,128)(2,1)S(1)} %add_convert_fusion.1), channel_id=1, source_target_pairs={{0,4},{4,8},{8,12},{12,16},{16,20},{20,24},{24,28},{28,0},{1,5},{5... | collective-permute-start | bytes 786440 | tf_op jit(solution)/shard_map/ppermute | solution.py:204
Sparse Core Ops, SparseCore 0:
  27.2 66.4 all-gather.2
  190.7 43.9 reduce-scatter.4
  237.2 26.4 reduce-scatter.2

commit v17 on v15

--- a/solution.py
+++ b/solution.py
@@ -75,7 +75,10 @@
 
 def split_blocks(rows, order, plan, lanes):
     depth = rows.shape[1] // (4 * lanes)
-    depth_step = max(n for n in (16, 32, 64) if depth % n == 0 and n * 4 * lanes <= 256)
+    ends = [depth] + [stop for _, stop, _ in plan]
+    depth_step = max(
+        n for n in (16, 32, 64) if n * 4 * lanes <= 256 and all(end % n == 0 for end in ends)
+    )
     kinds = sorted({kind for _, _, columns in plan for kind, _ in columns})
     blocks = order.shape[0]
     shapes = [(blocks, stop - start, len(columns) * HD) for start, stop, columns in plan]
@@ -169,7 +172,7 @@
             patch * heads * keys,
         ),
         name="attend",
-    )(where, normed, matrix, in_hbm(stale))
+    )(where, in_hbm(normed), matrix, in_hbm(stale))
 
 
 def output_kernel(attended_ref, matrix_ref, out_ref):
@@ -238,22 +241,23 @@
 
     matrix = relayed(pieces)
     normed = norm(tokens, modulation[0])
-    to_out = relayed(after(first, matrix))
+    to_out = relayed(waiting(first, matrix, normed))
     own = attend(normed, matrix, patch_index, stale_cache[0], tuple(range(lanes)), 0)
-    rest = relayed(waiting(second, to_out, own))
+    product = output(own, to_out)
+    rest = relayed(waiting(second, product))
 
     per = sections // tp
     gate = lax.dynamic_slice_in_dim(modulation[0, 2], rank * share, share, 0)
 
-    def result(matrix, start, stop):
+    def result(partial, start, stop):
         columns = [slice(r * depth + start, r * depth + stop) for r in range(per)]
-        mixed = lax.psum_scatter(output(own, matrix), "tp", scatter_dimension=1, tiled=True)
+        mixed = lax.psum_scatter(partial, "tp", scatter_dimension=1, tiled=True)
         patch = jnp.concatenate([inflow[0][:, cols] for cols in columns], axis=1)
         gates = jnp.concatenate([gate[cols] for cols in columns])
         made = handed_on((patch.astype(F32) + gates * mixed.astype(F32)).astype(BF16))
         return jnp.split(made, per, axis=1)
 
-    results = zip(result(to_out, 0, part), result(rest, part, depth))
+    results = zip(result(product, 0, part), result(output(own, rest), part, depth))
     return jnp.concatenate([piece for both in results for piece in both], axis=1)[None]
 
 

time: 254 us -> 253 us (level)
  waiting for transfers between devices: 155 us -> 151 us
    all_to_all x2, waiting for transfers between devices: 96 us -> 36.2 us  [relayed(): lax.all_to_all(pieces, 'section', split_axis=0, concat_axis=0, tiled=True)]
    all_gather x1, waiting for transfers between devices: 0.02 us -> 57.1 us  [local(): tokens = lax.all_gather(inflow[0], 'tp', axis=1, tiled=True)]
    unnamed x13 -> x15, local copies, waits for them, and re-layouts: 7.22 us -> 8.89 us
  transfers between devices with their start and end apart: 7 -> 7, of which waited for: 5 -> 6; matrix products, arithmetic and copies ran while one was open for 1% -> 1% of each run, Pallas kernels for 14% -> 14%
where the time goes in v17:
time: 253 us
  waiting for transfers between devices  151 us (60%)
  Pallas kernels  47.7 us (19%)
  blocking collectives  17.8 us (7%)
  between operations  14 us (6%)
  local copies, waits for them, and re-layouts  9.03 us (4%)
  starting transfers between devices  9.01 us (4%)
  other arithmetic  3.97 us (2%)
    all_gather x1, waiting for transfers between devices, local(): tokens = lax.all_gather(inflow[0], 'tp', axis=1, tiled=True)  57.1 us
    reduce_scatter x2, waiting for transfers between devices, result(): mixed = lax.psum_scatter(partial, 'tp', scatter_dimension=1, tiled=True)  50.8 us
    all_to_all x2, waiting for transfers between devices, relayed(): lax.all_to_all(pieces, 'section', split_axis=0, concat_axis=0, tiled=True)  36.2 us
    pallas_call x1, Pallas kernels, attend(): pl.pallas_call(attend_kernel, grid_spec=pltpu.PrefetchScalarGridSpec(num_...  20.9 us
    all_to_all x1, blocking collectives, relayed(): lax.all_to_all(pieces, 'section', split_axis=0, concat_axis=0, tiled=True)  17.8 us
    pallas_call x2, Pallas kernels, split_blocks(): pl.pallas_call(functools.partial(split_kernel, lanes, plan, kinds, depth_...  17.7 us
    unnamed x15, local copies, waits for them, and re-layouts  8.89 us
    all_to_all x2, starting transfers between devices, relayed(): lax.all_to_all(pieces, 'section', split_axis=0, concat_axis=0, tiled=True)  8.77 us
  transfers between devices with their start and end apart: 7, of which 6 were waited for; matrix products, arithmetic and copies ran while one was open for 1% of the time, Pallas kernels for 14%

profile of v17, /device:TPU:0, one launch (start us, length us, event | category | flops | bytes accessed | tf_op | source)
XLA Modules:
  0.0 252.9 jit_solution(6369925322089112602)
XLA Ops:
  6.5 0.8 select_reduce_fusion.order_ref
  7.3 9.1 %split_blocks.2 = bf16[8,384,1536]{2,1,0:T(8,128)(2,1)S(1)} custom-call(s32[8]{0:T(128)S(1)} %select_reduce_fusion.order_ref, bf16[8,6144,128]{2,1,0:T(8,128)(2,1)} %bitcast.25), custom_call_target="tpu_custom_call" | custom-call | bytes 18874368 | tf_op jit(solution)/shard_map/split_blocks/pallas_call | solution.py:85
  16.4 3.7 %copy-done = bf16[8,384,1536]{2,1,0:T(8,128)(2,1)} copy-done((bf16[8,384,1536]{2,1,0:T(8,128)(2,1)}, bf16[8,384,1536]{2,1,0:T(8,128)(2,1)S(1)}, u32[]{:S(2)}) %copy-start) | copy-done | bytes 9437208
  20.0 5.2 %all-to-all-start = ((bf16[8,384,1536]{2,1,0:T(8,128)(2,1)}), bf16[8,384,1536]{2,1,0:T(8,128)(2,1)}, u32[]{:S(2)}, u32[]{:S(2)}) async-start(bf16[8,384,1536]{2,1,0:T(8,128)(2,1)} %copy-done), calls=%async_computation | async-start | bytes 18874368 | tf_op jit(solution)/shard_map/all_to_all | solution.py:211
  25.2 0.0 all-gather.3.cloned.1.call-start
  25.3 0.7 all-gather.3.cloned.1.call-update
  26.0 8.6 %split_blocks.3 = (bf16[8,256,512]{2,1,0:T(8,128)(2,1)S(1)}, bf16[8,128,512]{2,1,0:T(8,128)(2,1)S(1)}) custom-call(s32[8]{0:T(128)S(1)} %select_reduce_fusion.order_ref, bf16[8,6144,128]{2,1,0:T(8,128)(2,1)} %bitcast.26), custom_call_target="tpu_custom_call" | custom-call | bytes 18874368 | tf_op jit(solution)/shard_map/split_blocks/pallas_call | solution.py:85
  34.6 1.3 copy-done.2
  36.0 1.0 copy-done.3
  37.0 57.1 %all-gather.3.cloned.1.call-done = bf16[1,512,3072]{2,1,0:T(8,128)(2,1)} async-done(((bf16[1,512,768]{2,1,0:T(8,128)(2,1)}), bf16[1,512,3072]{2,1,0:T(8,128)(2,1)}) %all-gather.3.cloned.1.call-update) | async-done | bytes 3145744 | tf_op jit(solution)/shard_map/all_gather | solution.py:229
  94.1 4.1 %norm.1.normed_ref = bf16[512,3072]{1,0:T(8,128)(2,1)S(1)} custom-call(bf16[512,3072]{1,0:T(8,128)(2,1)} %bitcast.27, f32[3,3072]{1,0:T(4,128)S(1)} %bitcast.24), custom_call_target="tpu_custom_call" | custom-call | flops 15728640 | bytes 6291456 | tf_op jit(solution)/shard_map/norm/pallas_call | solution.py:115
  98.2 1.7 copy-done.1
  99.9 31.2 %all-to-all-done = bf16[8,384,1536]{2,1,0:T(8,128)(2,1)} async-done(((bf16[8,384,1536]{2,1,0:T(8,128)(2,1)}), bf16[8,384,1536]{2,1,0:T(8,128)(2,1)}, u32[]{:S(2)}, u32[]{:S(2)}) %all-to-all-start) | async-done | bytes 9437216 | tf_op jit(solution)/shard_map/all_to_all | solution.py:211
  131.1 3.6 %all-to-all-start.1 = ((bf16[8,256,512]{2,1,0:T(8,128)(2,1)}), bf16[8,256,512]{2,1,0:T(8,128)(2,1)S(1)}, u32[]{:S(2)}, u32[]{:S(2)}) async-start(bf16[8,256,512]{2,1,0:T(8,128)(2,1)} %copy-done.2), calls=%async_computation.1 | async-start | bytes 4194304 | tf_op jit(solution)/shard_map/all_to_all | solution.py:211
  134.8 0.0 reduce-scatter.3.cloned.1.call-start
  135.4 20.9 %attend.1.attended_ref = bf16[512,512]{1,0:T(8,128)(2,1)S(1)} custom-call(s32[1]{0:T(128)S(6)} %copy.12.where_ref, bf16[512,3072]{1,0:T(8,128)(2,1)} %copy-done.1, bf16[3072,1536]{1,0:T(8,128)(2,1)} %bitcast.7.matrix_ref, bf16[2,2048,512]{2,1,0:T(8,128)(2,1)} %bitcast.32), custom_call_target="tpu_custom_call" | custom-call | flops 6979321856 | bytes 13631488 | tf_op jit(solution)/shard_map/attend/pallas_call | solution.py:155
  156.4 4.9 %all-to-all-done.1 = bf16[8,256,512]{2,1,0:T(8,128)(2,1)S(1)} async-done(((bf16[8,256,512]{2,1,0:T(8,128)(2,1)}), bf16[8,256,512]{2,1,0:T(8,128)(2,1)S(1)}, u32[]{:S(2)}, u32[]{:S(2)}) %all-to-all-start.1) | async-done | bytes 2097184 | tf_op jit(solution)/shard_map/all_to_all | solution.py:211
  161.3 3.1 %output.2 = bf16[512,2048]{1,0:T(8,128)(2,1)} custom-call(bf16[512,512]{1,0:T(8,128)(2,1)S(1)} %attend.1.attended_ref, bf16[2048,512]{1,0:T(8,128)(2,1)S(1)} %bitcast.22), custom_call_target="tpu_custom_call" | custom-call | flops 1073741824 | bytes 4194304 | tf_op jit(solution)/shard_map/output/pallas_call | solution.py:186
  164.4 0.0 reduce-scatter.3.cloned.1.call-update
  164.5 0.0 reduce-scatter.5.cloned.1.call-start
  164.5 1.1 copy-done.4
  165.7 17.8 %all_to_all.15 = bf16[8,128,512]{2,1,0:T(8,128)(2,1)S(1)} all-to-all(bf16[8,128,512]{2,1,0:T(8,128)(2,1)S(1)} %copy-done.4), channel_id=1, replica_groups=mesh['section'=8,'tp'=4] {'section'}, dimensions={0} | all-to-all | bytes 2097152 | tf_op jit(solution)/shard_map/all_to_all | solution.py:211
  183.4 1.8 output.3
  185.2 0.0 reduce-scatter.5.cloned.1.call-update
  185.4 23.2 %reduce-scatter.3.cloned.1.call-done = bf16[512,512]{1,0:T(8,128)(2,1)} async-done(((bf16[512,2048]{1,0:T(8,128)(2,1)}), bf16[512,512]{1,0:T(8,128)(2,1)}) %reduce-scatter.3.cloned.1.call-update) | async-done | bytes 524304 | tf_op jit(solution)/shard_map/reduce_scatter | solution.py:254
  208.6 1.2 add_convert_fusion
  209.8 0.1 collective-permute-start
  209.9 27.6 %reduce-scatter.5.cloned.1.call-done = bf16[512,256]{1,0:T(8,128)(2,1)} async-done(((bf16[512,1024]{1,0:T(8,128)(2,1)}), bf16[512,256]{1,0:T(8,128)(2,1)}) %reduce-scatter.5.cloned.1.call-update) | async-done | bytes 262160 | tf_op jit(solution)/shard_map/reduce_scatter | solution.py:254
  237.5 1.0 add_convert_fusion.1
  238.6 0.1 collective-permute-start.1
  238.6 6.7 %collective-permute-done.1 = bf16[512,256]{1,0:T(8,128)(2,1)S(1)} collective-permute-done((bf16[512,256]{1,0:T(8,128)(2,1)S(1)}, bf16[512,256]{1,0:T(8,128)(2,1)S(1)}, u32[]{:S(2)}, u32[]{:S(2)}) %collective-permute-start.1) | collective-permute-done | bytes 262176 | tf_op jit(solution)/shard_map/ppermute | solution.py:207
  245.4 1.0 maximum_bitcast_fusion
  (20 shorter events, 0.2 us)
Async XLA Ops:
  16.4 3.7 %copy-start = (bf16[8,384,1536]{2,1,0:T(8,128)(2,1)}, bf16[8,384,1536]{2,1,0:T(8,128)(2,1)S(1)}, u32[]{:S(2)}) copy-start(bf16[8,384,1536]{2,1,0:T(8,128)(2,1)S(1)} %split_blocks.2) | copy-start | bytes 28311556
  20.0 111.1 %all-to-all-start = ((bf16[8,384,1536]{2,1,0:T(8,128)(2,1)}), bf16[8,384,1536]{2,1,0:T(8,128)(2,1)}, u32[]{:S(2)}, u32[]{:S(2)}) async-start(bf16[8,384,1536]{2,1,0:T(8,128)(2,1)} %copy-done), calls=%async_computation | async-start | bytes 18874368 | tf_op jit(solution)/shard_map/all_to_all | solution.py:211
  25.2 68.9 %all-gather.3.cloned.1.call-start = ((), (), s32[]{:S(2)}) async-start(), calls=%async_computation.7 | async-start | bytes 3932160 | tf_op jit(solution)/shard_map/all_gather | solution.py:229
  25.9 11.0 %copy-start.6 = (f32[1,3,3072]{2,0,1:T(1,128)S(1)}, f32[1,3,3072]{2,0,1:T(1,128)}, u32[]{:S(2)}) copy-start(f32[1,3,3072]{2,0,1:T(1,128)} %param.7) | copy-start | bytes 110596
  34.6 1.3 copy-start.2
  36.0 1.0 copy-start.3
  98.2 1.7 copy-start.1
  131.1 30.2 %all-to-all-start.1 = ((bf16[8,256,512]{2,1,0:T(8,128)(2,1)}), bf16[8,256,512]{2,1,0:T(8,128)(2,1)S(1)}, u32[]{:S(2)}, u32[]{:S(2)}) async-start(bf16[8,256,512]{2,1,0:T(8,128)(2,1)} %copy-done.2), calls=%async_computation.1 | async-start | bytes 4194304 | tf_op jit(solution)/shard_map/all_to_all | solution.py:211
  134.8 73.9 %reduce-scatter.3.cloned.1.call-start = ((), (), s32[]{:S(2)}) async-start(), calls=%async_computation.5 | async-start | bytes 2621440 | tf_op jit(solution)/shard_map/reduce_scatter | solution.py:254
  164.4 1.2 copy-start.4
  164.5 73.0 %reduce-scatter.5.cloned.1.call-start = ((), (), s32[]{:S(2)}) async-start(), calls=%async_computation.6 | async-start | bytes 1310720 | tf_op jit(solution)/shard_map/reduce_scatter | solution.py:254
  183.4 1.9 copy-start.5
  209.8 35.5 %collective-permute-start = (bf16[512,512]{1,0:T(8,128)(2,1)S(1)}, bf16[512,512]{1,0:T(8,128)(2,1)S(1)}, u32[]{:S(2)}, u32[]{:S(2)}) collective-permute-start(bf16[512,512]{1,0:T(8,128)(2,1)S(1)} %add_convert_fusion), channel_id=1, source_target_pairs={{0,4},{4,8},{8,12},{12,16},{16,20},{20,24},{24,28},{28,0},{1,5},{5... | collective-permute-start | bytes 1572872 | tf_op jit(solution)/shard_map/ppermute | solution.py:207
  238.6 6.7 %collective-permute-start.1 = (bf16[512,256]{1,0:T(8,128)(2,1)S(1)}, bf16[512,256]{1,0:T(8,128)(2,1)S(1)}, u32[]{:S(2)}, u32[]{:S(2)}) collective-permute-start(bf16[512,256]{1,0:T(8,128)(2,1)S(1)} %add_convert_fusion.1), channel_id=1, source_target_pairs={{0,4},{4,8},{8,12},{12,16},{16,20},{20,24},{24,28},{28,0},{1,5},{5... | collective-permute-start | bytes 786440 | tf_op jit(solution)/shard_map/ppermute | solution.py:207
Sparse Core Ops, SparseCore 0:
  27.6 66.4 all-gather.2
  164.6 43.9 reduce-scatter.2
  211.0 26.4 reduce-scatter.4

commit v18 on v17

--- a/solution.py
+++ b/solution.py
@@ -202,6 +202,10 @@
     return lax.optimization_barrier((block, earlier))[0]
 
 
+def swapped(block, axis, distance):
+    return lax.ppermute(block, axis, [(i, i ^ distance) for i in range(lax.axis_size(axis))])
+
+
 def handed_on(block):
     sections = lax.axis_size("section")
     return lax.ppermute(block, "section", [(i, (i + 1) % sections) for i in range(sections)])
@@ -249,15 +253,25 @@
     per = sections // tp
     gate = lax.dynamic_slice_in_dim(modulation[0, 2], rank * share, share, 0)
 
-    def result(partial, start, stop):
+    mixed = lax.psum_scatter(product, "tp", scatter_dimension=1, tiled=True)
+    product = output(own, rest)
+    share = product.shape[1] // tp
+    wanted = [
+        lax.dynamic_slice_in_dim(product, (rank ^ distance) * share, share, 1)
+        for distance in range(tp)
+    ]
+    wanted[1:] = [swapped(wanted[distance], "tp", distance) for distance in range(1, tp)]
+    mixed = waiting(mixed, *wanted[1:])
+    mixed_rest = sum(chunk.astype(F32) for chunk in wanted)
+
+    def result(mixed, start, stop):
         columns = [slice(r * depth + start, r * depth + stop) for r in range(per)]
-        mixed = lax.psum_scatter(partial, "tp", scatter_dimension=1, tiled=True)
         patch = jnp.concatenate([inflow[0][:, cols] for cols in columns], axis=1)
         gates = jnp.concatenate([gate[cols] for cols in columns])
         made = handed_on((patch.astype(F32) + gates * mixed.astype(F32)).astype(BF16))
         return jnp.split(made, per, axis=1)
 
-    results = zip(result(product, 0, part), result(output(own, rest), part, depth))
+    results = zip(result(mixed, 0, part), result(mixed_rest, part, depth))
     return jnp.concatenate([piece for both in results for piece in both], axis=1)[None]
 
 

time: 253 us -> 249 us (0.984)
  blocking collectives: 17.8 us -> 0 us
  starting transfers between devices: 9.01 us -> 19.2 us
  waiting for transfers between devices: 151 us -> 154 us
    reduce_scatter x2 -> x1, waiting for transfers between devices: 50.8 us -> 13.9 us  [local(): mixed = lax.psum_scatter(product, 'tp', scatter_dimension=1, tiled=True)]
    ppermute x0 -> x3, waiting for transfers between devices: none -> 20.7 us  [swapped(): lax.ppermute(block, axis, [(i, i ^ distance) for i in range(lax.axis_size...]
    all_to_all x1 -> x0, blocking collectives: 17.8 us -> none  [relayed(): lax.all_to_all(pieces, 'section', split_axis=0, concat_axis=0, tiled=True)]
    all_to_all x2 -> x3, waiting for transfers between devices: 36.2 us -> 50.8 us  [relayed(): lax.all_to_all(pieces, 'section', split_axis=0, concat_axis=0, tiled=True)]
    ppermute x0 -> x3, starting transfers between devices: none -> 4.88 us  [swapped(): lax.ppermute(block, axis, [(i, i ^ distance) for i in range(lax.axis_size...]
    ppermute x2, waiting for transfers between devices: 6.69 us -> 10.4 us  [handed_on(): lax.ppermute(block, 'section', [(i, (i + 1) % sections) for i in range(se...]
    all_to_all x2 -> x3, starting transfers between devices: 8.77 us -> 12.5 us  [relayed(): lax.all_to_all(pieces, 'section', split_axis=0, concat_axis=0, tiled=True)]
    unnamed x15 -> x13, local copies, waits for them, and re-layouts: 8.89 us -> 6.7 us
  transfers between devices with their start and end apart: 7 -> 10, of which waited for: 6 -> 7; matrix products, arithmetic and copies ran while one was open for 1% -> 1% of each run, Pallas kernels for 14% -> 14%
where the time goes in v18:
time: 249 us; the launch traced here: 246 us
  waiting for transfers between devices  154 us (62%)
  Pallas kernels  47.8 us (19%)
  starting transfers between devices  19.2 us (8%)
  between operations  14.3 us (6%)
  local copies, waits for them, and re-layouts  8.39 us (3%)
  other arithmetic  3.14 us (1%)
    all_gather x1, waiting for transfers between devices, local(): tokens = lax.all_gather(inflow[0], 'tp', axis=1, tiled=True)  57.2 us
    all_to_all x3, waiting for transfers between devices, relayed(): lax.all_to_all(pieces, 'section', split_axis=0, concat_axis=0, tiled=True)  50.8 us
    pallas_call x1, Pallas kernels, attend(): pl.pallas_call(attend_kernel, grid_spec=pltpu.PrefetchScalarGridSpec(num_...  20.9 us
    ppermute x3, waiting for transfers between devices, swapped(): lax.ppermute(block, axis, [(i, i ^ distance) for i in range(lax.axis_size...  20.7 us
    pallas_call x2, Pallas kernels, split_blocks(): pl.pallas_call(functools.partial(split_kernel, lanes, plan, kinds, depth_...  18.6 us
    reduce_scatter x1, waiting for transfers between devices, local(): mixed = lax.psum_scatter(product, 'tp', scatter_dimension=1, tiled=True)  13.9 us
    all_to_all x3, starting transfers between devices, relayed(): lax.all_to_all(pieces, 'section', split_axis=0, concat_axis=0, tiled=True)  12.5 us
    ppermute x2, waiting for transfers between devices, handed_on(): lax.ppermute(block, 'section', [(i, (i + 1) % sections) for i in range(se...  10.4 us
  transfers between devices with their start and end apart: 10, of which 7 were waited for; matrix products, arithmetic and copies ran while one was open for 1% of the time, Pallas kernels for 14%

profile of v18, /device:TPU:0, one launch (start us, length us, event | category | flops | bytes accessed | tf_op | source)
XLA Modules:
  0.0 246.5 jit_solution(9562535665986350339)
XLA Ops:
  6.5 0.8 select_reduce_fusion.order_ref
  7.3 9.1 %split_blocks.2 = bf16[8,384,1536]{2,1,0:T(8,128)(2,1)S(1)} custom-call(s32[8]{0:T(128)S(1)} %select_reduce_fusion.order_ref, bf16[8,6144,128]{2,1,0:T(8,128)(2,1)} %bitcast.25), custom_call_target="tpu_custom_call" | custom-call | bytes 18874368 | tf_op jit(solution)/shard_map/split_blocks/pallas_call | solution.py:85
  16.4 3.6 %copy-done = bf16[8,384,1536]{2,1,0:T(8,128)(2,1)} copy-done((bf16[8,384,1536]{2,1,0:T(8,128)(2,1)}, bf16[8,384,1536]{2,1,0:T(8,128)(2,1)S(1)}, u32[]{:S(2)}) %copy-start) | copy-done | bytes 9437208
  20.0 5.2 %all-to-all-start = ((bf16[8,384,1536]{2,1,0:T(8,128)(2,1)}), bf16[8,384,1536]{2,1,0:T(8,128)(2,1)}, u32[]{:S(2)}, u32[]{:S(2)}) async-start(bf16[8,384,1536]{2,1,0:T(8,128)(2,1)} %copy-done), calls=%async_computation | async-start | bytes 18874368 | tf_op jit(solution)/shard_map/all_to_all | solution.py:215
  25.2 0.0 all-gather.3.cloned.1.call-start
  25.2 0.7 all-gather.3.cloned.1.call-update
  25.9 9.5 %split_blocks.3 = (bf16[8,256,512]{2,1,0:T(8,128)(2,1)S(1)}, bf16[8,128,512]{2,1,0:T(8,128)(2,1)}) custom-call(s32[8]{0:T(128)S(1)} %select_reduce_fusion.order_ref, bf16[8,6144,128]{2,1,0:T(8,128)(2,1)} %bitcast.26), custom_call_target="tpu_custom_call" | custom-call | bytes 18874368 | tf_op jit(solution)/shard_map/split_blocks/pallas_call | solution.py:85
  35.5 1.3 copy-done.2
  36.8 57.2 %all-gather.3.cloned.1.call-done = bf16[1,512,3072]{2,1,0:T(8,128)(2,1)} async-done(((bf16[1,512,768]{2,1,0:T(8,128)(2,1)}), bf16[1,512,3072]{2,1,0:T(8,128)(2,1)}) %all-gather.3.cloned.1.call-update) | async-done | bytes 3145744 | tf_op jit(solution)/shard_map/all_gather | solution.py:233
  94.1 4.1 %norm.1.normed_ref = bf16[512,3072]{1,0:T(8,128)(2,1)S(1)} custom-call(bf16[512,3072]{1,0:T(8,128)(2,1)} %bitcast.27, f32[3,3072]{1,0:T(4,128)S(1)} %bitcast.24), custom_call_target="tpu_custom_call" | custom-call | flops 15728640 | bytes 6291456 | tf_op jit(solution)/shard_map/norm/pallas_call | solution.py:115
  98.2 1.7 copy-done.1
  99.9 31.2 %all-to-all-done = bf16[8,384,1536]{2,1,0:T(8,128)(2,1)} async-done(((bf16[8,384,1536]{2,1,0:T(8,128)(2,1)}), bf16[8,384,1536]{2,1,0:T(8,128)(2,1)}, u32[]{:S(2)}, u32[]{:S(2)}) %all-to-all-start) | async-done | bytes 9437216 | tf_op jit(solution)/shard_map/all_to_all | solution.py:215
  131.1 3.6 %all-to-all-start.1 = ((bf16[8,256,512]{2,1,0:T(8,128)(2,1)}), bf16[8,256,512]{2,1,0:T(8,128)(2,1)S(1)}, u32[]{:S(2)}, u32[]{:S(2)}) async-start(bf16[8,256,512]{2,1,0:T(8,128)(2,1)} %copy-done.2), calls=%async_computation.1 | async-start | bytes 4194304 | tf_op jit(solution)/shard_map/all_to_all | solution.py:215
  134.7 0.0 reduce-scatter.2.cloned.1.call-start
  135.4 20.9 %attend.1.attended_ref = bf16[512,512]{1,0:T(8,128)(2,1)S(1)} custom-call(s32[1]{0:T(128)S(6)} %copy.12.where_ref, bf16[512,3072]{1,0:T(8,128)(2,1)} %copy-done.1, bf16[3072,1536]{1,0:T(8,128)(2,1)} %bitcast.7.matrix_ref, bf16[2,2048,512]{2,1,0:T(8,128)(2,1)} %bitcast.32), custom_call_target="tpu_custom_call" | custom-call | flops 6979321856 | bytes 13631488 | tf_op jit(solution)/shard_map/attend/pallas_call | solution.py:155
  156.3 5.0 %all-to-all-done.1 = bf16[8,256,512]{2,1,0:T(8,128)(2,1)S(1)} async-done(((bf16[8,256,512]{2,1,0:T(8,128)(2,1)}), bf16[8,256,512]{2,1,0:T(8,128)(2,1)S(1)}, u32[]{:S(2)}, u32[]{:S(2)}) %all-to-all-start.1) | async-done | bytes 2097184 | tf_op jit(solution)/shard_map/all_to_all | solution.py:215
  161.3 3.2 %output.2 = bf16[512,2048]{1,0:T(8,128)(2,1)} custom-call(bf16[512,512]{1,0:T(8,128)(2,1)S(1)} %attend.1.attended_ref, bf16[2048,512]{1,0:T(8,128)(2,1)S(1)} %bitcast.22), custom_call_target="tpu_custom_call" | custom-call | flops 1073741824 | bytes 4194304 | tf_op jit(solution)/shard_map/output/pallas_call | solution.py:186
  164.5 3.7 %all-to-all-start.2 = ((bf16[8,128,512]{2,1,0:T(8,128)(2,1)}), bf16[8,128,512]{2,1,0:T(8,128)(2,1)S(1)}, u32[]{:S(2)}, u32[]{:S(2)}) async-start(bf16[8,128,512]{2,1,0:T(8,128)(2,1)} %get-tuple-element.19), calls=%async_computation.3 | async-start | bytes 2097152 | tf_op jit(solution)/shard_map/all_to_all | solution.py:215
  168.3 0.7 fusion.3
  169.0 14.6 %all-to-all-done.2 = bf16[8,128,512]{2,1,0:T(8,128)(2,1)S(1)} async-done(((bf16[8,128,512]{2,1,0:T(8,128)(2,1)}), bf16[8,128,512]{2,1,0:T(8,128)(2,1)S(1)}, u32[]{:S(2)}, u32[]{:S(2)}) %all-to-all-start.2) | async-done | bytes 1048608 | tf_op jit(solution)/shard_map/all_to_all | solution.py:215
  183.5 1.0 output.3
  184.6 0.9 constant_dynamic-slice_fusion.4
  185.5 2.3 collective-permute-start
  187.8 2.6 %collective-permute-start.1 = (bf16[512,256]{1,0:T(8,128)(2,1)}, bf16[512,256]{1,0:T(8,128)(2,1)S(1)}, u32[]{:S(2)}, u32[]{:S(2)}) collective-permute-start(bf16[512,256]{1,0:T(8,128)(2,1)} %get-tuple-element.25), channel_id=1, source_target_pairs={{0,2},{1,3},{2,0},{3,1},{4,6},{5,7},{6,4},{7,5},{8,10},{9,11},{10,... | collective-permute-start | bytes 786440 | tf_op jit(solution)/shard_map/ppermute | solution.py:206
  190.4 20.7 %collective-permute-done = bf16[512,256]{1,0:T(8,128)(2,1)S(1)} collective-permute-done((bf16[512,256]{1,0:T(8,128)(2,1)}, bf16[512,256]{1,0:T(8,128)(2,1)S(1)}, u32[]{:S(2)}, u32[]{:S(2)}) %collective-permute-start) | collective-permute-done | bytes 262176 | tf_op jit(solution)/shard_map/ppermute | solution.py:206
  211.2 13.9 %reduce-scatter.2.cloned.1.call-done = bf16[512,512]{1,0:T(8,128)(2,1)} async-done(((bf16[512,2048]{1,0:T(8,128)(2,1)}), bf16[512,512]{1,0:T(8,128)(2,1)}) %reduce-scatter.2.cloned.1.call-update) | async-done | bytes 524304 | tf_op jit(solution)/shard_map/reduce_scatter | solution.py:256
  225.0 1.2 add_convert_fusion
  226.2 0.1 collective-permute-start.3
  226.3 0.2 add_convert_fusion.1
  226.5 1.7 collective-permute-start.4
  228.2 10.4 %collective-permute-done.4 = bf16[512,256]{1,0:T(8,128)(2,1)S(1)} collective-permute-done((bf16[512,256]{1,0:T(8,128)(2,1)S(1)}, bf16[512,256]{1,0:T(8,128)(2,1)S(1)}, u32[]{:S(2)}, u32[]{:S(2)}) %collective-permute-start.4) | collective-permute-done | bytes 262176 | tf_op jit(solution)/shard_map/ppermute | solution.py:211
  238.7 1.0 maximum_bitcast_fusion
  (23 shorter events, 0.2 us)
Async XLA Ops:
  16.4 3.6 %copy-start = (bf16[8,384,1536]{2,1,0:T(8,128)(2,1)}, bf16[8,384,1536]{2,1,0:T(8,128)(2,1)S(1)}, u32[]{:S(2)}) copy-start(bf16[8,384,1536]{2,1,0:T(8,128)(2,1)S(1)} %split_blocks.2) | copy-start | bytes 28311556
  20.0 111.1 %all-to-all-start = ((bf16[8,384,1536]{2,1,0:T(8,128)(2,1)}), bf16[8,384,1536]{2,1,0:T(8,128)(2,1)}, u32[]{:S(2)}, u32[]{:S(2)}) async-start(bf16[8,384,1536]{2,1,0:T(8,128)(2,1)} %copy-done), calls=%async_computation | async-start | bytes 18874368 | tf_op jit(solution)/shard_map/all_to_all | solution.py:215
  25.2 68.9 %all-gather.3.cloned.1.call-start = ((), (), s32[]{:S(2)}) async-start(), calls=%async_computation.5 | async-start | bytes 3932160 | tf_op jit(solution)/shard_map/all_gather | solution.py:233
  25.9 10.9 %copy-start.5 = (f32[1,3,3072]{2,0,1:T(1,128)S(1)}, f32[1,3,3072]{2,0,1:T(1,128)}, u32[]{:S(2)}) copy-start(f32[1,3,3072]{2,0,1:T(1,128)} %param.7) | copy-start | bytes 110596
  35.5 1.3 copy-start.2
  98.2 1.7 copy-start.1
  131.1 30.2 %all-to-all-start.1 = ((bf16[8,256,512]{2,1,0:T(8,128)(2,1)}), bf16[8,256,512]{2,1,0:T(8,128)(2,1)S(1)}, u32[]{:S(2)}, u32[]{:S(2)}) async-start(bf16[8,256,512]{2,1,0:T(8,128)(2,1)} %copy-done.2), calls=%async_computation.1 | async-start | bytes 4194304 | tf_op jit(solution)/shard_map/all_to_all | solution.py:215
  134.7 90.3 %reduce-scatter.2.cloned.1.call-start = ((), (), s32[]{:S(2)}) async-start(), calls=%async_computation.4 | async-start | bytes 2621440 | tf_op jit(solution)/shard_map/reduce_scatter | solution.py:256
  164.5 3.8 %copy-start.3 = (bf16[1,512,768]{2,1,0:T(8,128)(2,1)S(1)}, bf16[1,512,768]{2,1,0:T(8,128)(2,1)}, u32[]{:S(2)}) copy-start(bf16[1,512,768]{2,1,0:T(8,128)(2,1)} %param.8) | copy-start | bytes 2359300
  164.5 19.0 %all-to-all-start.2 = ((bf16[8,128,512]{2,1,0:T(8,128)(2,1)}), bf16[8,128,512]{2,1,0:T(8,128)(2,1)S(1)}, u32[]{:S(2)}, u32[]{:S(2)}) async-start(bf16[8,128,512]{2,1,0:T(8,128)(2,1)} %get-tuple-element.19), calls=%async_computation.3 | async-start | bytes 2097152 | tf_op jit(solution)/shard_map/all_to_all | solution.py:215
  184.6 41.7 %copy-start.4 = (bf16[512,128]{1,0:T(8,128)(2,1)S(1)}, bf16[512,128]{1,0:T(8,128)(2,1)}, u32[]{:S(2)}) copy-start(bf16[512,128]{1,0:T(8,128)(2,1)} %get-tuple-element.29) | copy-start | bytes 393220
  185.5 25.7 %collective-permute-start = (bf16[512,256]{1,0:T(8,128)(2,1)}, bf16[512,256]{1,0:T(8,128)(2,1)S(1)}, u32[]{:S(2)}, u32[]{:S(2)}) collective-permute-start(bf16[512,256]{1,0:T(8,128)(2,1)} %get-tuple-element.23), channel_id=1, source_target_pairs={{0,1},{1,0},{2,3},{3,2},{4,5},{5,4},{6,7},{7,6},{8,9},{9,8},{10,11... | collective-permute-start | bytes 786440 | tf_op jit(solution)/shard_map/ppermute | solution.py:206
  187.8 37.3 %collective-permute-start.1 = (bf16[512,256]{1,0:T(8,128)(2,1)}, bf16[512,256]{1,0:T(8,128)(2,1)S(1)}, u32[]{:S(2)}, u32[]{:S(2)}) collective-permute-start(bf16[512,256]{1,0:T(8,128)(2,1)} %get-tuple-element.25), channel_id=1, source_target_pairs={{0,2},{1,3},{2,0},{3,1},{4,6},{5,7},{6,4},{7,5},{8,10},{9,11},{10,... | collective-permute-start | bytes 786440 | tf_op jit(solution)/shard_map/ppermute | solution.py:206
  190.4 34.7 %collective-permute-start.2 = (bf16[512,256]{1,0:T(8,128)(2,1)}, bf16[512,256]{1,0:T(8,128)(2,1)S(1)}, u32[]{:S(2)}, u32[]{:S(2)}) collective-permute-start(bf16[512,256]{1,0:T(8,128)(2,1)} %get-tuple-element.24), channel_id=1, source_target_pairs={{0,3},{1,2},{2,1},{3,0},{4,7},{5,6},{6,5},{7,4},{8,11},{9,10},{10,... | collective-permute-start | bytes 786440 | tf_op jit(solution)/shard_map/ppermute | solution.py:206
  226.2 12.4 %collective-permute-start.3 = (bf16[512,512]{1,0:T(8,128)(2,1)S(1)}, bf16[512,512]{1,0:T(8,128)(2,1)S(1)}, u32[]{:S(2)}, u32[]{:S(2)}) collective-permute-start(bf16[512,512]{1,0:T(8,128)(2,1)S(1)} %add_convert_fusion), channel_id=1, source_target_pairs={{0,4},{4,8},{8,12},{12,16},{16,20},{20,24},{24,28},{28,0},{1,5},{5... | collective-permute-start | bytes 1572872 | tf_op jit(solution)/shard_map/ppermute | solution.py:211
  226.5 12.1 %collective-permute-start.4 = (bf16[512,256]{1,0:T(8,128)(2,1)S(1)}, bf16[512,256]{1,0:T(8,128)(2,1)S(1)}, u32[]{:S(2)}, u32[]{:S(2)}) collective-permute-start(bf16[512,256]{1,0:T(8,128)(2,1)S(1)} %add_convert_fusion.1), channel_id=1, source_target_pairs={{0,4},{4,8},{8,12},{12,16},{16,20},{20,24},{24,28},{28,0},{1,5},{5... | collective-permute-start | bytes 786440 | tf_op jit(solution)/shard_map/ppermute | solution.py:211
Sparse Core Ops, SparseCore 0:
  27.6 66.4 all-gather.2
  164.6 60.3 reduce-scatter.1

commit v19 on v18

--- a/solution.py
+++ b/solution.py
@@ -261,7 +261,6 @@
         for distance in range(tp)
     ]
     wanted[1:] = [swapped(wanted[distance], "tp", distance) for distance in range(1, tp)]
-    mixed = waiting(mixed, *wanted[1:])
     mixed_rest = sum(chunk.astype(F32) for chunk in wanted)
 
     def result(mixed, start, stop):
@@ -269,9 +268,11 @@
         patch = jnp.concatenate([inflow[0][:, cols] for cols in columns], axis=1)
         gates = jnp.concatenate([gate[cols] for cols in columns])
         made = handed_on((patch.astype(F32) + gates * mixed.astype(F32)).astype(BF16))
-        return jnp.split(made, per, axis=1)
-
-    results = zip(result(mixed, 0, part), result(mixed_rest, part, depth))
+        return made
+
+    second = result(mixed_rest, part, depth)
+    first = result(waiting(mixed, second), 0, part)
+    results = zip(jnp.split(first, per, axis=1), jnp.split(second, per, axis=1))
     return jnp.concatenate([piece for both in results for piece in both], axis=1)[None]
 
 

time: 249 us -> 253 us (1.016)
  waiting for transfers between devices: 154 us -> 159 us
    reduce_scatter x1, waiting for transfers between devices: 13.9 us -> 0.01 us  [local(): mixed = lax.psum_scatter(product, 'tp', scatter_dimension=1, tiled=True)]
    ppermute x3, waiting for transfers between devices: 20.7 us -> 34 us  [swapped(): lax.ppermute(block, axis, [(i, i ^ distance) for i in range(lax.axis_size...]
    ppermute x2, waiting for transfers between devices: 10.4 us -> 16.1 us  [handed_on(): lax.ppermute(block, 'section', [(i, (i + 1) % sections) for i in range(se...]
    unnamed x13 -> x11, local copies, waits for them, and re-layouts: 6.7 us -> 6.71 us
  transfers between devices with their start and end apart: 10 -> 10, of which waited for: 7 -> 9; matrix products, arithmetic and copies ran while one was open for 1% -> 0% of each run, Pallas kernels for 14% -> 14%
where the time goes in v19:
time: 253 us; the launch traced here: 249 us
  waiting for transfers between devices  159 us (63%)
  Pallas kernels  47.7 us (19%)
  starting transfers between devices  17.5 us (7%)
  between operations  14.3 us (6%)
  local copies, waits for them, and re-layouts  6.96 us (3%)
  other arithmetic  3.13 us (1%)
    all_gather x1, waiting for transfers between devices, local(): tokens = lax.all_gather(inflow[0], 'tp', axis=1, tiled=True)  57.2 us
    all_to_all x3, waiting for transfers between devices, relayed(): lax.all_to_all(pieces, 'section', split_axis=0, concat_axis=0, tiled=True)  51.5 us
    ppermute x3, waiting for transfers between devices, swapped(): lax.ppermute(block, axis, [(i, i ^ distance) for i in range(lax.axis_size...  34 us
    pallas_call x1, Pallas kernels, attend(): pl.pallas_call(attend_kernel, grid_spec=pltpu.PrefetchScalarGridSpec(num_...  20.9 us
    pallas_call x2, Pallas kernels, split_blocks(): pl.pallas_call(functools.partial(split_kernel, lanes, plan, kinds, depth_...  18.6 us
    ppermute x2, waiting for transfers between devices, handed_on(): lax.ppermute(block, 'section', [(i, (i + 1) % sections) for i in range(se...  16.1 us
    all_to_all x3, starting transfers between devices, relayed(): lax.all_to_all(pieces, 'section', split_axis=0, concat_axis=0, tiled=True)  12.3 us
    unnamed x11, local copies, waits for them, and re-layouts  6.71 us
  transfers between devices with their start and end apart: 10, of which 9 were waited for; matrix products, arithmetic and copies ran while one was open for 0% of the time, Pallas kernels for 14%

profile of v19, /device:TPU:0, one launch (start us, length us, event | category | flops | bytes accessed | tf_op | source)
XLA Modules:
  0.0 249.0 jit_solution(17370642388755158978)
XLA Ops:
  6.5 0.8 select_reduce_fusion.order_ref
  7.3 9.1 %split_blocks.2 = bf16[8,384,1536]{2,1,0:T(8,128)(2,1)S(1)} custom-call(s32[8]{0:T(128)S(1)} %select_reduce_fusion.order_ref, bf16[8,6144,128]{2,1,0:T(8,128)(2,1)} %bitcast.25), custom_call_target="tpu_custom_call" | custom-call | bytes 18874368 | tf_op jit(solution)/shard_map/split_blocks/pallas_call | solution.py:85
  16.4 3.6 %copy-done = bf16[8,384,1536]{2,1,0:T(8,128)(2,1)} copy-done((bf16[8,384,1536]{2,1,0:T(8,128)(2,1)}, bf16[8,384,1536]{2,1,0:T(8,128)(2,1)S(1)}, u32[]{:S(2)}) %copy-start) | copy-done | bytes 9437208
  20.0 5.2 %all-to-all-start = ((bf16[8,384,1536]{2,1,0:T(8,128)(2,1)}), bf16[8,384,1536]{2,1,0:T(8,128)(2,1)}, u32[]{:S(2)}, u32[]{:S(2)}) async-start(bf16[8,384,1536]{2,1,0:T(8,128)(2,1)} %copy-done), calls=%async_computation | async-start | bytes 18874368 | tf_op jit(solution)/shard_map/all_to_all | solution.py:215
  25.2 0.7 all-gather.3.cloned.1.call-update
  25.9 9.5 %split_blocks.3 = (bf16[8,256,512]{2,1,0:T(8,128)(2,1)S(1)}, bf16[8,128,512]{2,1,0:T(8,128)(2,1)}) custom-call(s32[8]{0:T(128)S(1)} %select_reduce_fusion.order_ref, bf16[8,6144,128]{2,1,0:T(8,128)(2,1)} %bitcast.26), custom_call_target="tpu_custom_call" | custom-call | bytes 18874368 | tf_op jit(solution)/shard_map/split_blocks/pallas_call | solution.py:85
  35.5 1.3 copy-done.2
  36.8 57.2 %all-gather.3.cloned.1.call-done = bf16[1,512,3072]{2,1,0:T(8,128)(2,1)} async-done(((bf16[1,512,768]{2,1,0:T(8,128)(2,1)}), bf16[1,512,3072]{2,1,0:T(8,128)(2,1)}) %all-gather.3.cloned.1.call-update) | async-done | bytes 3145744 | tf_op jit(solution)/shard_map/all_gather | solution.py:233
  94.1 4.1 %norm.1.normed_ref = bf16[512,3072]{1,0:T(8,128)(2,1)S(1)} custom-call(bf16[512,3072]{1,0:T(8,128)(2,1)} %bitcast.27, f32[3,3072]{1,0:T(4,128)S(1)} %bitcast.24), custom_call_target="tpu_custom_call" | custom-call | flops 15728640 | bytes 6291456 | tf_op jit(solution)/shard_map/norm/pallas_call | solution.py:115
  98.2 1.7 copy-done.1
  99.9 31.2 %all-to-all-done = bf16[8,384,1536]{2,1,0:T(8,128)(2,1)} async-done(((bf16[8,384,1536]{2,1,0:T(8,128)(2,1)}), bf16[8,384,1536]{2,1,0:T(8,128)(2,1)}, u32[]{:S(2)}, u32[]{:S(2)}) %all-to-all-start) | async-done | bytes 9437216 | tf_op jit(solution)/shard_map/all_to_all | solution.py:215
  131.1 3.6 %all-to-all-start.1 = ((bf16[8,256,512]{2,1,0:T(8,128)(2,1)}), bf16[8,256,512]{2,1,0:T(8,128)(2,1)S(1)}, u32[]{:S(2)}, u32[]{:S(2)}) async-start(bf16[8,256,512]{2,1,0:T(8,128)(2,1)} %copy-done.2), calls=%async_computation.1 | async-start | bytes 4194304 | tf_op jit(solution)/shard_map/all_to_all | solution.py:215
  134.7 0.0 reduce-scatter.2.cloned.1.call-start
  135.4 20.9 %attend.1.attended_ref = bf16[512,512]{1,0:T(8,128)(2,1)S(1)} custom-call(s32[1]{0:T(128)S(6)} %copy.12.where_ref, bf16[512,3072]{1,0:T(8,128)(2,1)} %copy-done.1, bf16[3072,1536]{1,0:T(8,128)(2,1)} %bitcast.7.matrix_ref, bf16[2,2048,512]{2,1,0:T(8,128)(2,1)} %bitcast.32), custom_call_target="tpu_custom_call" | custom-call | flops 6979321856 | bytes 13631488 | tf_op jit(solution)/shard_map/attend/pallas_call | solution.py:155
  156.3 5.0 %all-to-all-done.1 = bf16[8,256,512]{2,1,0:T(8,128)(2,1)S(1)} async-done(((bf16[8,256,512]{2,1,0:T(8,128)(2,1)}), bf16[8,256,512]{2,1,0:T(8,128)(2,1)S(1)}, u32[]{:S(2)}, u32[]{:S(2)}) %all-to-all-start.1) | async-done | bytes 2097184 | tf_op jit(solution)/shard_map/all_to_all | solution.py:215
  161.3 3.1 %output.2 = bf16[512,2048]{1,0:T(8,128)(2,1)} custom-call(bf16[512,512]{1,0:T(8,128)(2,1)S(1)} %attend.1.attended_ref, bf16[2048,512]{1,0:T(8,128)(2,1)S(1)} %bitcast.22), custom_call_target="tpu_custom_call" | custom-call | flops 1073741824 | bytes 4194304 | tf_op jit(solution)/shard_map/output/pallas_call | solution.py:186
  164.4 3.6 %all-to-all-start.2 = ((bf16[8,128,512]{2,1,0:T(8,128)(2,1)}), bf16[8,128,512]{2,1,0:T(8,128)(2,1)S(1)}, u32[]{:S(2)}, u32[]{:S(2)}) async-start(bf16[8,128,512]{2,1,0:T(8,128)(2,1)} %get-tuple-element.17), calls=%async_computation.3 | async-start | bytes 2097152 | tf_op jit(solution)/shard_map/all_to_all | solution.py:215
  168.1 15.3 %all-to-all-done.2 = bf16[8,128,512]{2,1,0:T(8,128)(2,1)S(1)} async-done(((bf16[8,128,512]{2,1,0:T(8,128)(2,1)}), bf16[8,128,512]{2,1,0:T(8,128)(2,1)S(1)}, u32[]{:S(2)}, u32[]{:S(2)}) %all-to-all-start.2) | async-done | bytes 1048608 | tf_op jit(solution)/shard_map/all_to_all | solution.py:215
  183.4 1.0 output.3
  184.4 0.1 constant_dynamic-slice_fusion.4
  184.5 2.4 collective-permute-start
  186.9 2.6 %collective-permute-start.1 = (bf16[512,256]{1,0:T(8,128)(2,1)S(1)}, bf16[512,256]{1,0:T(8,128)(2,1)S(1)}, u32[]{:S(2)}, u32[]{:S(2)}) collective-permute-start(bf16[512,256]{1,0:T(8,128)(2,1)S(1)} %get-tuple-element.21), channel_id=1, source_target_pairs={{0,2},{1,3},{2,0},{3,1},{4,6},{5,7},{6,4},{7,5},{8,10},{9,11},{10,... | collective-permute-start | bytes 786440 | tf_op jit(solution)/shard_map/ppermute | solution.py:206
  189.5 20.4 %collective-permute-done = bf16[512,256]{1,0:T(8,128)(2,1)S(1)} collective-permute-done((bf16[512,256]{1,0:T(8,128)(2,1)S(1)}, bf16[512,256]{1,0:T(8,128)(2,1)S(1)}, u32[]{:S(2)}, u32[]{:S(2)}) %collective-permute-start) | collective-permute-done | bytes 262176 | tf_op jit(solution)/shard_map/ppermute | solution.py:206
  209.9 10.3 %collective-permute-done.1 = bf16[512,256]{1,0:T(8,128)(2,1)S(1)} collective-permute-done((bf16[512,256]{1,0:T(8,128)(2,1)S(1)}, bf16[512,256]{1,0:T(8,128)(2,1)S(1)}, u32[]{:S(2)}, u32[]{:S(2)}) %collective-permute-start.1) | collective-permute-done | bytes 262176 | tf_op jit(solution)/shard_map/ppermute | solution.py:206
  220.2 3.2 %collective-permute-done.2 = bf16[512,256]{1,0:T(8,128)(2,1)S(1)} collective-permute-done((bf16[512,256]{1,0:T(8,128)(2,1)S(1)}, bf16[512,256]{1,0:T(8,128)(2,1)S(1)}, u32[]{:S(2)}, u32[]{:S(2)}) %collective-permute-start.2) | collective-permute-done | bytes 262176 | tf_op jit(solution)/shard_map/ppermute | solution.py:206
  223.5 0.2 add_convert_fusion.1
  223.7 0.1 collective-permute-start.3
  223.8 6.6 %collective-permute-done.3 = bf16[512,256]{1,0:T(8,128)(2,1)S(1)} collective-permute-done((bf16[512,256]{1,0:T(8,128)(2,1)S(1)}, bf16[512,256]{1,0:T(8,128)(2,1)S(1)}, u32[]{:S(2)}, u32[]{:S(2)}) %collective-permute-start.3) | collective-permute-done | bytes 262176 | tf_op jit(solution)/shard_map/ppermute | solution.py:211
  230.4 1.2 add_convert_fusion
  231.6 0.1 collective-permute-start.4
  231.7 9.5 %collective-permute-done.4 = bf16[512,512]{1,0:T(8,128)(2,1)S(1)} collective-permute-done((bf16[512,512]{1,0:T(8,128)(2,1)S(1)}, bf16[512,512]{1,0:T(8,128)(2,1)S(1)}, u32[]{:S(2)}, u32[]{:S(2)}) %collective-permute-start.4) | collective-permute-done | bytes 524320 | tf_op jit(solution)/shard_map/ppermute | solution.py:211
  241.2 1.0 maximum_bitcast_fusion
  (21 shorter events, 0.2 us)
Async XLA Ops:
  16.4 3.6 %copy-start = (bf16[8,384,1536]{2,1,0:T(8,128)(2,1)}, bf16[8,384,1536]{2,1,0:T(8,128)(2,1)S(1)}, u32[]{:S(2)}) copy-start(bf16[8,384,1536]{2,1,0:T(8,128)(2,1)S(1)} %split_blocks.2) | copy-start | bytes 28311556
  20.0 111.1 %all-to-all-start = ((bf16[8,384,1536]{2,1,0:T(8,128)(2,1)}), bf16[8,384,1536]{2,1,0:T(8,128)(2,1)}, u32[]{:S(2)}, u32[]{:S(2)}) async-start(bf16[8,384,1536]{2,1,0:T(8,128)(2,1)} %copy-done), calls=%async_computation | async-start | bytes 18874368 | tf_op jit(solution)/shard_map/all_to_all | solution.py:215
  25.2 68.9 %all-gather.3.cloned.1.call-start = ((), (), s32[]{:S(2)}) async-start(), calls=%async_computation.5 | async-start | bytes 3932160 | tf_op jit(solution)/shard_map/all_gather | solution.py:233
  25.9 10.9 %copy-start.4 = (f32[1,3,3072]{2,0,1:T(1,128)S(1)}, f32[1,3,3072]{2,0,1:T(1,128)}, u32[]{:S(2)}) copy-start(f32[1,3,3072]{2,0,1:T(1,128)} %param.7) | copy-start | bytes 110596
  35.5 1.3 copy-start.2
  98.2 1.7 copy-start.1
  131.1 30.2 %all-to-all-start.1 = ((bf16[8,256,512]{2,1,0:T(8,128)(2,1)}), bf16[8,256,512]{2,1,0:T(8,128)(2,1)S(1)}, u32[]{:S(2)}, u32[]{:S(2)}) async-start(bf16[8,256,512]{2,1,0:T(8,128)(2,1)} %copy-done.2), calls=%async_computation.1 | async-start | bytes 4194304 | tf_op jit(solution)/shard_map/all_to_all | solution.py:215
  134.7 95.7 %reduce-scatter.2.cloned.1.call-start = ((), (), s32[]{:S(2)}) async-start(), calls=%async_computation.4 | async-start | bytes 2621440 | tf_op jit(solution)/shard_map/reduce_scatter | solution.py:256
  164.4 18.9 %all-to-all-start.2 = ((bf16[8,128,512]{2,1,0:T(8,128)(2,1)}), bf16[8,128,512]{2,1,0:T(8,128)(2,1)S(1)}, u32[]{:S(2)}, u32[]{:S(2)}) async-start(bf16[8,128,512]{2,1,0:T(8,128)(2,1)} %get-tuple-element.17), calls=%async_computation.3 | async-start | bytes 2097152 | tf_op jit(solution)/shard_map/all_to_all | solution.py:215
  183.4 6.1 %copy-start.3 = (bf16[1,512,768]{2,1,0:T(8,128)(2,1)S(1)}, bf16[1,512,768]{2,1,0:T(8,128)(2,1)}, u32[]{:S(2)}) copy-start(bf16[1,512,768]{2,1,0:T(8,128)(2,1)} %param.8) | copy-start | bytes 2359300
  184.5 25.4 %collective-permute-start = (bf16[512,256]{1,0:T(8,128)(2,1)S(1)}, bf16[512,256]{1,0:T(8,128)(2,1)S(1)}, u32[]{:S(2)}, u32[]{:S(2)}) collective-permute-start(bf16[512,256]{1,0:T(8,128)(2,1)S(1)} %get-tuple-element.19), channel_id=1, source_target_pairs={{0,1},{1,0},{2,3},{3,2},{4,5},{5,4},{6,7},{7,6},{8,9},{9,8},{10,11... | collective-permute-start | bytes 786440 | tf_op jit(solution)/shard_map/ppermute | solution.py:206
  186.9 33.4 %collective-permute-start.1 = (bf16[512,256]{1,0:T(8,128)(2,1)S(1)}, bf16[512,256]{1,0:T(8,128)(2,1)S(1)}, u32[]{:S(2)}, u32[]{:S(2)}) collective-permute-start(bf16[512,256]{1,0:T(8,128)(2,1)S(1)} %get-tuple-element.21), channel_id=1, source_target_pairs={{0,2},{1,3},{2,0},{3,1},{4,6},{5,7},{6,4},{7,5},{8,10},{9,11},{10,... | collective-permute-start | bytes 786440 | tf_op jit(solution)/shard_map/ppermute | solution.py:206
  189.4 34.0 %collective-permute-start.2 = (bf16[512,256]{1,0:T(8,128)(2,1)S(1)}, bf16[512,256]{1,0:T(8,128)(2,1)S(1)}, u32[]{:S(2)}, u32[]{:S(2)}) collective-permute-start(bf16[512,256]{1,0:T(8,128)(2,1)S(1)} %get-tuple-element.20), channel_id=1, source_target_pairs={{0,3},{1,2},{2,1},{3,0},{4,7},{5,6},{6,5},{7,4},{8,11},{9,10},{10,... | collective-permute-start | bytes 786440 | tf_op jit(solution)/shard_map/ppermute | solution.py:206
  223.7 6.7 %collective-permute-start.3 = (bf16[512,256]{1,0:T(8,128)(2,1)S(1)}, bf16[512,256]{1,0:T(8,128)(2,1)S(1)}, u32[]{:S(2)}, u32[]{:S(2)}) collective-permute-start(bf16[512,256]{1,0:T(8,128)(2,1)S(1)} %add_convert_fusion.1), channel_id=1, source_target_pairs={{0,4},{4,8},{8,12},{12,16},{16,20},{20,24},{24,28},{28,0},{1,5},{5... | collective-permute-start | bytes 786440 | tf_op jit(solution)/shard_map/ppermute | solution.py:211
  231.6 9.6 %collective-permute-start.4 = (bf16[512,512]{1,0:T(8,128)(2,1)S(1)}, bf16[512,512]{1,0:T(8,128)(2,1)S(1)}, u32[]{:S(2)}, u32[]{:S(2)}) collective-permute-start(bf16[512,512]{1,0:T(8,128)(2,1)S(1)} %add_convert_fusion), channel_id=1, source_target_pairs={{0,4},{4,8},{8,12},{12,16},{16,20},{20,24},{24,28},{28,0},{1,5},{5... | collective-permute-start | bytes 1572872 | tf_op jit(solution)/shard_map/ppermute | solution.py:211
Sparse Core Ops, SparseCore 0:
  27.6 66.4 all-gather.2
  164.6 60.5 reduce-scatter.1

commit v20 on v18

--- a/solution.py
+++ b/solution.py
@@ -182,7 +182,7 @@
 def output(attended, matrix):
     patch, inner = attended.shape
     rows = matrix.shape[0]
-    step = 512 if rows % 512 == 0 else rows
+    step = 256 if rows % 256 == 0 else rows
     return pl.pallas_call(
         output_kernel,
         grid=(rows // step,),

time: 249 us -> 251 us (level)
  transfers between devices with their start and end apart: 10 -> 10, of which waited for: 7 -> 8; matrix products, arithmetic and copies ran while one was open for 1% -> 1% of each run, Pallas kernels for 14% -> 15%
where the time goes in v20:
time: 251 us; the launch traced here: 248 us
  waiting for transfers between devices  153 us (61%)
  Pallas kernels  49.7 us (20%)
  starting transfers between devices  19.1 us (8%)
  between operations  14.3 us (6%)
  local copies, waits for them, and re-layouts  8.39 us (3%)
  other arithmetic  3.14 us (1%)
    all_gather x1, waiting for transfers between devices, local(): tokens = lax.all_gather(inflow[0], 'tp', axis=1, tiled=True)  57.2 us
    all_to_all x3, waiting for transfers between devices, relayed(): lax.all_to_all(pieces, 'section', split_axis=0, concat_axis=0, tiled=True)  50.8 us
    ppermute x3, waiting for transfers between devices, swapped(): lax.ppermute(block, axis, [(i, i ^ distance) for i in range(lax.axis_size...  21.1 us
    pallas_call x1, Pallas kernels, attend(): pl.pallas_call(attend_kernel, grid_spec=pltpu.PrefetchScalarGridSpec(num_...  20.9 us
    pallas_call x2, Pallas kernels, split_blocks(): pl.pallas_call(functools.partial(split_kernel, lanes, plan, kinds, depth_...  18.6 us
    reduce_scatter x1, waiting for transfers between devices, local(): mixed = lax.psum_scatter(product, 'tp', scatter_dimension=1, tiled=True)  13 us
    all_to_all x3, starting transfers between devices, relayed(): lax.all_to_all(pieces, 'section', split_axis=0, concat_axis=0, tiled=True)  12.5 us
    ppermute x2, waiting for transfers between devices, handed_on(): lax.ppermute(block, 'section', [(i, (i + 1) % sections) for i in range(se...  10.5 us
  transfers between devices with their start and end apart: 10, of which 8 were waited for; matrix products, arithmetic and copies ran while one was open for 1% of the time, Pallas kernels for 15%

profile of v20, /device:TPU:0, one launch (start us, length us, event | category | flops | bytes accessed | tf_op | source)
XLA Modules:
  0.0 247.9 jit_solution(9353852774626754196)
XLA Ops:
  6.5 0.8 select_reduce_fusion.order_ref
  7.3 9.1 %split_blocks.2 = bf16[8,384,1536]{2,1,0:T(8,128)(2,1)S(1)} custom-call(s32[8]{0:T(128)S(1)} %select_reduce_fusion.order_ref, bf16[8,6144,128]{2,1,0:T(8,128)(2,1)} %bitcast.25), custom_call_target="tpu_custom_call" | custom-call | bytes 18874368 | tf_op jit(solution)/shard_map/split_blocks/pallas_call | solution.py:85
  16.4 3.6 %copy-done = bf16[8,384,1536]{2,1,0:T(8,128)(2,1)} copy-done((bf16[8,384,1536]{2,1,0:T(8,128)(2,1)}, bf16[8,384,1536]{2,1,0:T(8,128)(2,1)S(1)}, u32[]{:S(2)}) %copy-start) | copy-done | bytes 9437208
  20.0 5.2 %all-to-all-start = ((bf16[8,384,1536]{2,1,0:T(8,128)(2,1)}), bf16[8,384,1536]{2,1,0:T(8,128)(2,1)}, u32[]{:S(2)}, u32[]{:S(2)}) async-start(bf16[8,384,1536]{2,1,0:T(8,128)(2,1)} %copy-done), calls=%async_computation | async-start | bytes 18874368 | tf_op jit(solution)/shard_map/all_to_all | solution.py:215
  25.2 0.7 all-gather.3.cloned.1.call-update
  25.9 9.5 %split_blocks.3 = (bf16[8,256,512]{2,1,0:T(8,128)(2,1)S(1)}, bf16[8,128,512]{2,1,0:T(8,128)(2,1)}) custom-call(s32[8]{0:T(128)S(1)} %select_reduce_fusion.order_ref, bf16[8,6144,128]{2,1,0:T(8,128)(2,1)} %bitcast.26), custom_call_target="tpu_custom_call" | custom-call | bytes 18874368 | tf_op jit(solution)/shard_map/split_blocks/pallas_call | solution.py:85
  35.5 1.3 copy-done.2
  36.8 57.2 %all-gather.3.cloned.1.call-done = bf16[1,512,3072]{2,1,0:T(8,128)(2,1)} async-done(((bf16[1,512,768]{2,1,0:T(8,128)(2,1)}), bf16[1,512,3072]{2,1,0:T(8,128)(2,1)}) %all-gather.3.cloned.1.call-update) | async-done | bytes 3145744 | tf_op jit(solution)/shard_map/all_gather | solution.py:233
  94.1 4.1 %norm.1.normed_ref = bf16[512,3072]{1,0:T(8,128)(2,1)S(1)} custom-call(bf16[512,3072]{1,0:T(8,128)(2,1)} %bitcast.27, f32[3,3072]{1,0:T(4,128)S(1)} %bitcast.24), custom_call_target="tpu_custom_call" | custom-call | flops 15728640 | bytes 6291456 | tf_op jit(solution)/shard_map/norm/pallas_call | solution.py:115
  98.2 1.7 copy-done.1
  99.9 31.2 %all-to-all-done = bf16[8,384,1536]{2,1,0:T(8,128)(2,1)} async-done(((bf16[8,384,1536]{2,1,0:T(8,128)(2,1)}), bf16[8,384,1536]{2,1,0:T(8,128)(2,1)}, u32[]{:S(2)}, u32[]{:S(2)}) %all-to-all-start) | async-done | bytes 9437216 | tf_op jit(solution)/shard_map/all_to_all | solution.py:215
  131.1 3.6 %all-to-all-start.1 = ((bf16[8,256,512]{2,1,0:T(8,128)(2,1)}), bf16[8,256,512]{2,1,0:T(8,128)(2,1)S(1)}, u32[]{:S(2)}, u32[]{:S(2)}) async-start(bf16[8,256,512]{2,1,0:T(8,128)(2,1)} %copy-done.2), calls=%async_computation.1 | async-start | bytes 4194304 | tf_op jit(solution)/shard_map/all_to_all | solution.py:215
  134.7 0.0 reduce-scatter.2.cloned.1.call-start
  135.4 20.9 %attend.1.attended_ref = bf16[512,512]{1,0:T(8,128)(2,1)S(1)} custom-call(s32[1]{0:T(128)S(6)} %copy.12.where_ref, bf16[512,3072]{1,0:T(8,128)(2,1)} %copy-done.1, bf16[3072,1536]{1,0:T(8,128)(2,1)} %bitcast.7.matrix_ref, bf16[2,2048,512]{2,1,0:T(8,128)(2,1)} %bitcast.32), custom_call_target="tpu_custom_call" | custom-call | flops 6979321856 | bytes 13631488 | tf_op jit(solution)/shard_map/attend/pallas_call | solution.py:155
  156.3 5.0 %all-to-all-done.1 = bf16[8,256,512]{2,1,0:T(8,128)(2,1)S(1)} async-done(((bf16[8,256,512]{2,1,0:T(8,128)(2,1)}), bf16[8,256,512]{2,1,0:T(8,128)(2,1)S(1)}, u32[]{:S(2)}, u32[]{:S(2)}) %all-to-all-start.1) | async-done | bytes 2097184 | tf_op jit(solution)/shard_map/all_to_all | solution.py:215
  161.3 4.6 %output.2 = bf16[512,2048]{1,0:T(8,128)(2,1)} custom-call(bf16[512,512]{1,0:T(8,128)(2,1)S(1)} %attend.1.attended_ref, bf16[2048,512]{1,0:T(8,128)(2,1)S(1)} %bitcast.22), custom_call_target="tpu_custom_call" | custom-call | flops 1073741824 | bytes 4194304 | tf_op jit(solution)/shard_map/output/pallas_call | solution.py:186
  166.0 3.7 %all-to-all-start.2 = ((bf16[8,128,512]{2,1,0:T(8,128)(2,1)}), bf16[8,128,512]{2,1,0:T(8,128)(2,1)S(1)}, u32[]{:S(2)}, u32[]{:S(2)}) async-start(bf16[8,128,512]{2,1,0:T(8,128)(2,1)} %get-tuple-element.19), calls=%async_computation.3 | async-start | bytes 2097152 | tf_op jit(solution)/shard_map/all_to_all | solution.py:215
  169.8 0.7 fusion.3
  170.5 14.6 %all-to-all-done.2 = bf16[8,128,512]{2,1,0:T(8,128)(2,1)S(1)} async-done(((bf16[8,128,512]{2,1,0:T(8,128)(2,1)}), bf16[8,128,512]{2,1,0:T(8,128)(2,1)S(1)}, u32[]{:S(2)}, u32[]{:S(2)}) %all-to-all-start.2) | async-done | bytes 1048608 | tf_op jit(solution)/shard_map/all_to_all | solution.py:215
  185.0 1.4 output.3
  186.5 0.9 constant_dynamic-slice_fusion.4
  187.4 2.3 collective-permute-start
  189.7 2.6 %collective-permute-start.1 = (bf16[512,256]{1,0:T(8,128)(2,1)}, bf16[512,256]{1,0:T(8,128)(2,1)S(1)}, u32[]{:S(2)}, u32[]{:S(2)}) collective-permute-start(bf16[512,256]{1,0:T(8,128)(2,1)} %get-tuple-element.25), channel_id=1, source_target_pairs={{0,2},{1,3},{2,0},{3,1},{4,6},{5,7},{6,4},{7,5},{8,10},{9,11},{10,... | collective-permute-start | bytes 786440 | tf_op jit(solution)/shard_map/ppermute | solution.py:206
  192.3 20.9 %collective-permute-done = bf16[512,256]{1,0:T(8,128)(2,1)S(1)} collective-permute-done((bf16[512,256]{1,0:T(8,128)(2,1)}, bf16[512,256]{1,0:T(8,128)(2,1)S(1)}, u32[]{:S(2)}, u32[]{:S(2)}) %collective-permute-start) | collective-permute-done | bytes 262176 | tf_op jit(solution)/shard_map/ppermute | solution.py:206
  213.3 13.0 %reduce-scatter.2.cloned.1.call-done = bf16[512,512]{1,0:T(8,128)(2,1)} async-done(((bf16[512,2048]{1,0:T(8,128)(2,1)}), bf16[512,512]{1,0:T(8,128)(2,1)}) %reduce-scatter.2.cloned.1.call-update) | async-done | bytes 524304 | tf_op jit(solution)/shard_map/reduce_scatter | solution.py:256
  226.3 0.1 collective-permute-done.2
  226.4 1.2 add_convert_fusion
  227.6 0.1 collective-permute-start.3
  227.7 0.2 add_convert_fusion.1
  227.9 1.6 collective-permute-start.4
  229.5 10.5 %collective-permute-done.4 = bf16[512,256]{1,0:T(8,128)(2,1)S(1)} collective-permute-done((bf16[512,256]{1,0:T(8,128)(2,1)S(1)}, bf16[512,256]{1,0:T(8,128)(2,1)S(1)}, u32[]{:S(2)}, u32[]{:S(2)}) %collective-permute-start.4) | collective-permute-done | bytes 262176 | tf_op jit(solution)/shard_map/ppermute | solution.py:211
  240.1 1.0 maximum_bitcast_fusion
  (23 shorter events, 0.2 us)
Async XLA Ops:
  16.4 3.6 %copy-start = (bf16[8,384,1536]{2,1,0:T(8,128)(2,1)}, bf16[8,384,1536]{2,1,0:T(8,128)(2,1)S(1)}, u32[]{:S(2)}) copy-start(bf16[8,384,1536]{2,1,0:T(8,128)(2,1)S(1)} %split_blocks.2) | copy-start | bytes 28311556
  20.0 111.1 %all-to-all-start = ((bf16[8,384,1536]{2,1,0:T(8,128)(2,1)}), bf16[8,384,1536]{2,1,0:T(8,128)(2,1)}, u32[]{:S(2)}, u32[]{:S(2)}) async-start(bf16[8,384,1536]{2,1,0:T(8,128)(2,1)} %copy-done), calls=%async_computation | async-start | bytes 18874368 | tf_op jit(solution)/shard_map/all_to_all | solution.py:215
  25.2 68.9 %all-gather.3.cloned.1.call-start = ((), (), s32[]{:S(2)}) async-start(), calls=%async_computation.5 | async-start | bytes 3932160 | tf_op jit(solution)/shard_map/all_gather | solution.py:233
  25.9 10.9 %copy-start.5 = (f32[1,3,3072]{2,0,1:T(1,128)S(1)}, f32[1,3,3072]{2,0,1:T(1,128)}, u32[]{:S(2)}) copy-start(f32[1,3,3072]{2,0,1:T(1,128)} %param.7) | copy-start | bytes 110596
  35.5 1.3 copy-start.2
  98.2 1.7 copy-start.1
  131.1 30.2 %all-to-all-start.1 = ((bf16[8,256,512]{2,1,0:T(8,128)(2,1)}), bf16[8,256,512]{2,1,0:T(8,128)(2,1)S(1)}, u32[]{:S(2)}, u32[]{:S(2)}) async-start(bf16[8,256,512]{2,1,0:T(8,128)(2,1)} %copy-done.2), calls=%async_computation.1 | async-start | bytes 4194304 | tf_op jit(solution)/shard_map/all_to_all | solution.py:215
  134.7 91.6 %reduce-scatter.2.cloned.1.call-start = ((), (), s32[]{:S(2)}) async-start(), calls=%async_computation.4 | async-start | bytes 2621440 | tf_op jit(solution)/shard_map/reduce_scatter | solution.py:256
  166.0 3.8 %copy-start.3 = (bf16[1,512,768]{2,1,0:T(8,128)(2,1)S(1)}, bf16[1,512,768]{2,1,0:T(8,128)(2,1)}, u32[]{:S(2)}) copy-start(bf16[1,512,768]{2,1,0:T(8,128)(2,1)} %param.8) | copy-start | bytes 2359300
  166.0 19.0 %all-to-all-start.2 = ((bf16[8,128,512]{2,1,0:T(8,128)(2,1)}), bf16[8,128,512]{2,1,0:T(8,128)(2,1)S(1)}, u32[]{:S(2)}, u32[]{:S(2)}) async-start(bf16[8,128,512]{2,1,0:T(8,128)(2,1)} %get-tuple-element.19), calls=%async_computation.3 | async-start | bytes 2097152 | tf_op jit(solution)/shard_map/all_to_all | solution.py:215
  186.5 41.2 %copy-start.4 = (bf16[512,128]{1,0:T(8,128)(2,1)S(1)}, bf16[512,128]{1,0:T(8,128)(2,1)}, u32[]{:S(2)}) copy-start(bf16[512,128]{1,0:T(8,128)(2,1)} %get-tuple-element.29) | copy-start | bytes 393220
  187.4 25.9 %collective-permute-start = (bf16[512,256]{1,0:T(8,128)(2,1)}, bf16[512,256]{1,0:T(8,128)(2,1)S(1)}, u32[]{:S(2)}, u32[]{:S(2)}) collective-permute-start(bf16[512,256]{1,0:T(8,128)(2,1)} %get-tuple-element.23), channel_id=1, source_target_pairs={{0,1},{1,0},{2,3},{3,2},{4,5},{5,4},{6,7},{7,6},{8,9},{9,8},{10,11... | collective-permute-start | bytes 786440 | tf_op jit(solution)/shard_map/ppermute | solution.py:206
  189.7 36.6 %collective-permute-start.1 = (bf16[512,256]{1,0:T(8,128)(2,1)}, bf16[512,256]{1,0:T(8,128)(2,1)S(1)}, u32[]{:S(2)}, u32[]{:S(2)}) collective-permute-start(bf16[512,256]{1,0:T(8,128)(2,1)} %get-tuple-element.25), channel_id=1, source_target_pairs={{0,2},{1,3},{2,0},{3,1},{4,6},{5,7},{6,4},{7,5},{8,10},{9,11},{10,... | collective-permute-start | bytes 786440 | tf_op jit(solution)/shard_map/ppermute | solution.py:206
  192.3 34.2 %collective-permute-start.2 = (bf16[512,256]{1,0:T(8,128)(2,1)}, bf16[512,256]{1,0:T(8,128)(2,1)S(1)}, u32[]{:S(2)}, u32[]{:S(2)}) collective-permute-start(bf16[512,256]{1,0:T(8,128)(2,1)} %get-tuple-element.24), channel_id=1, source_target_pairs={{0,3},{1,2},{2,1},{3,0},{4,7},{5,6},{6,5},{7,4},{8,11},{9,10},{10,... | collective-permute-start | bytes 786440 | tf_op jit(solution)/shard_map/ppermute | solution.py:206
  227.6 12.4 %collective-permute-start.3 = (bf16[512,512]{1,0:T(8,128)(2,1)S(1)}, bf16[512,512]{1,0:T(8,128)(2,1)S(1)}, u32[]{:S(2)}, u32[]{:S(2)}) collective-permute-start(bf16[512,512]{1,0:T(8,128)(2,1)S(1)} %add_convert_fusion), channel_id=1, source_target_pairs={{0,4},{4,8},{8,12},{12,16},{16,20},{20,24},{24,28},{28,0},{1,5},{5... | collective-permute-start | bytes 1572872 | tf_op jit(solution)/shard_map/ppermute | solution.py:211
  227.9 12.1 %collective-permute-start.4 = (bf16[512,256]{1,0:T(8,128)(2,1)S(1)}, bf16[512,256]{1,0:T(8,128)(2,1)S(1)}, u32[]{:S(2)}, u32[]{:S(2)}) collective-permute-start(bf16[512,256]{1,0:T(8,128)(2,1)S(1)} %add_convert_fusion.1), channel_id=1, source_target_pairs={{0,4},{4,8},{8,12},{12,16},{16,20},{20,24},{24,28},{28,0},{1,5},{5... | collective-permute-start | bytes 786440 | tf_op jit(solution)/shard_map/ppermute | solution.py:211
Sparse Core Ops, SparseCore 0:
  27.6 66.4 all-gather.2
  166.1 60.1 reduce-scatter.1
